TPU v7x, 768 devices: a whole 4x8x12 slice. The times are simulated.
768 devices in a mesh: dp: 48 (over y_lo, z, core), mp: 16 (over y_hi, x).
Axes of the slice: x: 4, y: 8 (y_hi: 4, y_lo: 2; y = y_hi * 2 + y_lo), z: 12, core: 2. Of those that a mesh axis runs over, the one named last changes fastest.
Arguments:
- layer_entry_matrix: bfloat16 [12288, 8192], P('dp', 'mp'), may hold values from -6 to 6
- stored_projector: bfloat16 [8448, 1024], P(('dp', 'mp')), may hold values from -0.0625 to 0.0625
- projection_adjoint: bfloat16 [12288, 1024], P('dp', 'mp'), may hold values from -2 to 2
- active_mask: int32 [96], P('dp'), may hold values from 0 to 1, as said below
Outputs:
- kv_values: bfloat16 [12288, 1024], P('dp', 'mp')
- activation_grad: bfloat16 [12288, 8192], P('dp', 'mp')
- weight_grad: float32 [8448, 1024], P(('dp', 'mp'))
Inputs may be any that keep to these rules, and one draw needn't show every extreme that they name: `active_mask`: sequence j of the dp index i is entry 2 * i + j. The dp indices i and i + 24 together hold exactly 2 surviving sequences, and some dp index holds 2 survivors.
All inputs are finite; a program needn't handle non-finite values.
Results may differ from a plain program's by a relative error of at most 0.018.
Values may be sent and summed in bfloat16 or wider, within the bound.
No kernel may reach another device: no remote copies, remote signals or barrier semaphores. Data moves between devices by JAX's collectives and lax.ppermute only.
A program may use at most 32 MiB of HBM per device.

v0:
```python
import jax
import jax.numpy as jnp
from jax import lax
from jax.sharding import PartitionSpec as P


def on_device(layer_entry_matrix, stored_projector, projection_adjoint, active_mask):
    context_count = active_mask.shape[0]
    rows_dev = layer_entry_matrix.shape[0]
    feat_width = layer_entry_matrix.shape[1]
    context_line_group = rows_dev // context_count
    gathered = lax.all_gather(stored_projector, "dp", axis=0, tiled=True)
    padded_rows = gathered.shape[0]
    w_used = gathered[:feat_width]
    kept_lines = jnp.repeat(active_mask, context_line_group)[:, None]
    work_g = projection_adjoint * kept_lines.astype(jnp.bfloat16)
    partial_value = jnp.dot(layer_entry_matrix, w_used, preferred_element_type=jnp.float32).astype(
        jnp.bfloat16
    )
    kv_work = lax.psum_scatter(partial_value, "mp", scatter_dimension=1, tiled=True).astype(
        jnp.float32
    )
    grad_full = lax.all_gather(work_g, "mp", axis=1, tiled=True)
    dx_work = lax.dot_general(
        grad_full, w_used, (((1,), (1,)), ((), ())), preferred_element_type=jnp.float32
    ).astype(jnp.bfloat16)
    input_widened = jnp.pad(layer_entry_matrix, ((0, 0), (0, padded_rows - feat_width)))
    weight_grad = lax.psum_scatter(
        lax.dot_general(
            input_widened, grad_full, (((0,), (0,)), ((), ())), preferred_element_type=jnp.float32
        ),
        "dp",
        scatter_dimension=0,
        tiled=True,
    )
    kv_values = (kv_work * kept_lines.astype(jnp.float32)).astype(jnp.bfloat16)
    return (kv_values, dx_work, weight_grad)


def solution(mesh):
    return jax.shard_map(
        on_device,
        mesh=mesh,
        in_specs=(P("dp", "mp"), P(("dp", "mp"), None), P("dp", "mp"), P("dp")),
        out_specs=(P("dp", "mp"), P("dp", "mp"), P(("dp", "mp"), None)),
        check_vma=False,
    )
```

profile of v0, /device:TPU:1, one launch (start us, length us, event | category | flops | bytes accessed | tf_op | source)
XLA Modules:
  0.0 305.2 jit_solution(5302946416725261901)
XLA Ops:
  7.2 0.0 all-gather.3.cloned.1.call-start
  7.2 0.7 all-gather.3.cloned.1.call-update
  7.9 0.0 reduce-scatter.4.cloned.1.call-start
  7.9 0.7 fusion.6
  8.7 0.1 broadcast_bitcast_fusion.1
  8.8 0.8 broadcast_multiply_fusion
  9.5 41.3 %all_gather.7 = bf16[256,1024]{0,1:T(8,128)(2,1)S(1)} all-gather(bf16[256,64]{0,1:T(8,128)(2,1)S(1)} %broadcast_multiply_fusion), channel_id=1, replica_groups=mesh['dp'=48,'mp'=16] {'mp'}, dimensions={1}, use_global_device_ids=true | all-gather | bytes 557056 | tf_op jit(solution)/shard_map/all_gather | solution.py:23
  50.8 1.4 fusion.3
  52.2 0.0 copy-start.1
  52.2 63.2 %all-gather.3.cloned.1.call-done = bf16[48,11,1024]{2,1,0:T(8,128)(2,1)} async-done(((bf16[1,11,1024]{2,1,0:T(8,128)(2,1)}), bf16[48,11,1024]{2,1,0:T(8,128)(2,1)}) %all-gather.3.cloned.1.call-update) | async-done | bytes 1081360 | tf_op jit(solution)/shard_map/all_gather | solution.py:12
  115.4 2.4 reshape.23
  117.8 2.6 convolution_convert_fusion
  120.4 0.0 reduce-scatter.4.cloned.1.call-update
  120.4 95.9 %fusion = f32[16,1024]{1,0:T(8,128)S(1)} fusion(f32[528,1024]{1,0:T(8,128)S(1)} %fusion.3), kind=kCustom, calls=%all-reduce-scatter | all-reduce-scatter fusion | flops 786433 | bytes 2232320
  216.4 1.4 collective-permute-start.13
  217.8 5.5 %collective-permute-start.12 = (f32[16,1024]{1,0:T(8,128)S(1)}, f32[16,1024]{1,0:T(8,128)S(1)}, u32[]{:S(2)}, u32[]{:S(2)}) collective-permute-start(f32[16,1024]{1,0:T(8,128)S(1)} %fusion), channel_id=1, source_target_pairs={{0,208},{16,224},{32,240},{48,256},{64,272},{80,288},{96,304},{112... | collective-permute-start | bytes 196616
  223.3 6.1 %collective-permute-start.11 = (f32[16,1024]{1,0:T(8,128)S(1)}, f32[16,1024]{1,0:T(8,128)S(1)}, u32[]{:S(2)}, u32[]{:S(2)}) collective-permute-start(f32[16,1024]{1,0:T(8,128)S(1)} %fusion), channel_id=1, source_target_pairs={{0,192},{16,208},{32,224},{48,240},{64,256},{80,272},{96,288},{112... | collective-permute-start | bytes 196616
  229.4 7.0 %collective-permute-start.10 = (f32[16,1024]{1,0:T(8,128)S(1)}, f32[16,1024]{1,0:T(8,128)S(1)}, u32[]{:S(2)}, u32[]{:S(2)}) collective-permute-start(f32[16,1024]{1,0:T(8,128)S(1)} %fusion), channel_id=1, source_target_pairs={{0,176},{16,192},{32,208},{48,224},{64,240},{80,256},{96,272},{112... | collective-permute-start | bytes 196616
  236.4 1.3 collective-permute-start.14
  237.7 7.6 %collective-permute-done.14 = f32[11,1024]{1,0:T(8,128)S(1)} collective-permute-done((f32[11,1024]{1,0:T(8,128)S(1)}, f32[11,1024]{1,0:T(8,128)S(1)}, u32[]{:S(2)}, u32[]{:S(2)}) %collective-permute-start.14) | collective-permute-done | bytes 45088
  245.4 2.0 collective-permute-start.9
  247.4 0.0 collective-permute-done.13
  247.4 12.9 %collective-permute-start.8 = (f32[16,1024]{1,0:T(8,128)S(1)}, f32[16,1024]{1,0:T(8,128)S(1)}, u32[]{:S(2)}, u32[]{:S(2)}) collective-permute-start(f32[16,1024]{1,0:T(8,128)S(1)} %fusion), channel_id=1, source_target_pairs={{0,144},{16,160},{32,176},{48,192},{64,208},{80,224},{96,240},{112... | collective-permute-start | bytes 196616
  260.2 0.0 collective-permute-done.12
  260.3 1.3 collective-permute-start.7
  261.6 0.0 collective-permute-done.11
  261.6 2.4 collective-permute-start.6
  264.0 0.0 collective-permute-done.10
  264.0 4.9 %collective-permute-start.5 = (f32[16,1024]{1,0:T(8,128)S(1)}, f32[16,1024]{1,0:T(8,128)S(1)}, u32[]{:S(2)}, u32[]{:S(2)}) collective-permute-start(f32[16,1024]{1,0:T(8,128)S(1)} %fusion), channel_id=1, source_target_pairs={{0,96},{16,112},{32,128},{48,144},{64,160},{80,176},{96,192},{112,... | collective-permute-start | bytes 196616
  268.8 0.0 collective-permute-done.9
  268.9 1.9 collective-permute-start.4
  270.8 0.0 collective-permute-done.8
  270.8 5.0 %collective-permute-start.3 = (f32[16,1024]{1,0:T(8,128)S(1)}, f32[16,1024]{1,0:T(8,128)S(1)}, u32[]{:S(2)}, u32[]{:S(2)}) collective-permute-start(f32[16,1024]{1,0:T(8,128)S(1)} %fusion), channel_id=1, source_target_pairs={{0,64},{16,80},{32,96},{48,112},{64,128},{80,144},{96,160},{112,17... | collective-permute-start | bytes 196616
  275.8 0.0 collective-permute-done.7
  275.8 1.9 collective-permute-start.2
  277.7 0.0 collective-permute-done.6
  277.7 8.3 %collective-permute-start.1 = (f32[16,1024]{1,0:T(8,128)S(1)}, f32[16,1024]{1,0:T(8,128)}, u32[]{:S(2)}, u32[]{:S(2)}) collective-permute-start(f32[16,1024]{1,0:T(8,128)S(1)} %fusion), channel_id=1, source_target_pairs={{0,32},{16,48},{32,64},{48,80},{64,96},{80,112},{96,128},{112,144}... | collective-permute-start | bytes 196616
  286.0 0.0 collective-permute-done.5
  286.1 1.9 collective-permute-start
  288.0 0.1 broadcast_bitcast_fusion
  288.0 1.3 dynamic-slice.4
  290.0 0.0 collective-permute-done.3
  290.0 0.0 collective-permute-done.2
  290.0 0.7 collective-permute-done
  290.7 4.4 %concatenate = f32[251,1024]{1,0:T(8,128)S(1)} concatenate(f32[11,1024]{1,0:T(8,128)S(1)} %collective-permute-done.14, f32[16,1024]{1,0:T(8,128)S(1)} %collective-permute-done.13, f32[16,1024]{1,0:T(8,128)S(1)} %collective-permute-done.12, f32[16,1024]{1,0:T(8,128)S(1)} %collective-permute-done.11, f32[16,1024]{1,0:T(8,128)S(1)} %collective-permute-done.10, ...), dimensions={0} | concatenate | bytes 2056192
  295.1 0.6 constant_dynamic-slice_fusion
  295.8 1.2 convolution_convert_fusion.1
  297.0 1.4 multiply_convert_fusion
  (7 shorter events, 0.0 us)
Async XLA Ops:
  7.2 108.3 %all-gather.3.cloned.1.call-start = ((), (), s32[]{:S(2)}) async-start(), calls=%async_computation.2 | async-start | bytes 1605632 | tf_op jit(solution)/shard_map/all_gather | solution.py:12
  7.9 289.1 %reduce-scatter.4.cloned.1.call-start = ((), (), s32[]{:S(2)}) async-start(), calls=%async_computation.1 | async-start | bytes 557056 | tf_op jit(solution)/shard_map/reduce_scatter | solution.py:20
  52.2 65.6 %copy-start.1 = (bf16[256,512]{1,0:T(8,128)(2,1)S(1)}, bf16[256,512]{1,0:T(8,128)(2,1)}, u32[]{:S(2)}) copy-start(bf16[256,512]{1,0:T(8,128)(2,1)} %param.4) | copy-start | bytes 786436
  216.4 79.4 %copy-start = (bf16[528,1024]{1,0:T(8,128)(2,1)S(1)}, bf16[528,1024]{1,0:T(8,128)(2,1)}, u32[]{:S(2)}) copy-start(bf16[528,1024]{1,0:T(8,128)(2,1)} %reshape.23) | copy-start | bytes 3244036
  216.4 31.0 %collective-permute-start.13 = (f32[16,1024]{1,0:T(8,128)S(1)}, f32[16,1024]{1,0:T(8,128)S(1)}, u32[]{:S(2)}, u32[]{:S(2)}) collective-permute-start(f32[16,1024]{1,0:T(8,128)S(1)} %fusion), channel_id=1, source_target_pairs={{0,224},{16,240},{32,256},{48,272},{64,288},{80,304},{96,320},{112... | collective-permute-start | bytes 196616
  217.8 42.4 %collective-permute-start.12 = (f32[16,1024]{1,0:T(8,128)S(1)}, f32[16,1024]{1,0:T(8,128)S(1)}, u32[]{:S(2)}, u32[]{:S(2)}) collective-permute-start(f32[16,1024]{1,0:T(8,128)S(1)} %fusion), channel_id=1, source_target_pairs={{0,208},{16,224},{32,240},{48,256},{64,272},{80,288},{96,304},{112... | collective-permute-start | bytes 196616
  223.3 38.2 %collective-permute-start.11 = (f32[16,1024]{1,0:T(8,128)S(1)}, f32[16,1024]{1,0:T(8,128)S(1)}, u32[]{:S(2)}, u32[]{:S(2)}) collective-permute-start(f32[16,1024]{1,0:T(8,128)S(1)} %fusion), channel_id=1, source_target_pairs={{0,192},{16,208},{32,224},{48,240},{64,256},{80,272},{96,288},{112... | collective-permute-start | bytes 196616
  229.4 34.5 %collective-permute-start.10 = (f32[16,1024]{1,0:T(8,128)S(1)}, f32[16,1024]{1,0:T(8,128)S(1)}, u32[]{:S(2)}, u32[]{:S(2)}) collective-permute-start(f32[16,1024]{1,0:T(8,128)S(1)} %fusion), channel_id=1, source_target_pairs={{0,176},{16,192},{32,208},{48,224},{64,240},{80,256},{96,272},{112... | collective-permute-start | bytes 196616
  236.4 8.9 %collective-permute-start.14 = (f32[11,1024]{1,0:T(8,128)S(1)}, f32[11,1024]{1,0:T(8,128)S(1)}, u32[]{:S(2)}, u32[]{:S(2)}) collective-permute-start(f32[11,1024]{1,0:T(8,128)S(1)} %slice.5), channel_id=1, source_target_pairs={{0,240},{16,256},{32,272},{48,288},{64,304},{80,320},{96,336},{112... | collective-permute-start | bytes 135176
  245.4 23.5 %collective-permute-start.9 = (f32[16,1024]{1,0:T(8,128)S(1)}, f32[16,1024]{1,0:T(8,128)S(1)}, u32[]{:S(2)}, u32[]{:S(2)}) collective-permute-start(f32[16,1024]{1,0:T(8,128)S(1)} %fusion), channel_id=1, source_target_pairs={{0,160},{16,176},{32,192},{48,208},{64,224},{80,240},{96,256},{112... | collective-permute-start | bytes 196616
  247.4 23.4 %collective-permute-start.8 = (f32[16,1024]{1,0:T(8,128)S(1)}, f32[16,1024]{1,0:T(8,128)S(1)}, u32[]{:S(2)}, u32[]{:S(2)}) collective-permute-start(f32[16,1024]{1,0:T(8,128)S(1)} %fusion), channel_id=1, source_target_pairs={{0,144},{16,160},{32,176},{48,192},{64,208},{80,224},{96,240},{112... | collective-permute-start | bytes 196616
  260.3 15.5 %collective-permute-start.7 = (f32[16,1024]{1,0:T(8,128)S(1)}, f32[16,1024]{1,0:T(8,128)S(1)}, u32[]{:S(2)}, u32[]{:S(2)}) collective-permute-start(f32[16,1024]{1,0:T(8,128)S(1)} %fusion), channel_id=1, source_target_pairs={{0,128},{16,144},{32,160},{48,176},{64,192},{80,208},{96,224},{112... | collective-permute-start | bytes 196616
  261.6 16.2 %collective-permute-start.6 = (f32[16,1024]{1,0:T(8,128)S(1)}, f32[16,1024]{1,0:T(8,128)S(1)}, u32[]{:S(2)}, u32[]{:S(2)}) collective-permute-start(f32[16,1024]{1,0:T(8,128)S(1)} %fusion), channel_id=1, source_target_pairs={{0,112},{16,128},{32,144},{48,160},{64,176},{80,192},{96,208},{112... | collective-permute-start | bytes 196616
  264.0 22.1 %collective-permute-start.5 = (f32[16,1024]{1,0:T(8,128)S(1)}, f32[16,1024]{1,0:T(8,128)S(1)}, u32[]{:S(2)}, u32[]{:S(2)}) collective-permute-start(f32[16,1024]{1,0:T(8,128)S(1)} %fusion), channel_id=1, source_target_pairs={{0,96},{16,112},{32,128},{48,144},{64,160},{80,176},{96,192},{112,... | collective-permute-start | bytes 196616
  268.9 21.1 %collective-permute-start.4 = (f32[16,1024]{1,0:T(8,128)S(1)}, f32[16,1024]{1,0:T(8,128)S(1)}, u32[]{:S(2)}, u32[]{:S(2)}) collective-permute-start(f32[16,1024]{1,0:T(8,128)S(1)} %fusion), channel_id=1, source_target_pairs={{0,80},{16,96},{32,112},{48,128},{64,144},{80,160},{96,176},{112,1... | collective-permute-start | bytes 196616
  270.8 19.2 %collective-permute-start.3 = (f32[16,1024]{1,0:T(8,128)S(1)}, f32[16,1024]{1,0:T(8,128)S(1)}, u32[]{:S(2)}, u32[]{:S(2)}) collective-permute-start(f32[16,1024]{1,0:T(8,128)S(1)} %fusion), channel_id=1, source_target_pairs={{0,64},{16,80},{32,96},{48,112},{64,128},{80,144},{96,160},{112,17... | collective-permute-start | bytes 196616
  275.8 14.2 %collective-permute-start.2 = (f32[16,1024]{1,0:T(8,128)S(1)}, f32[16,1024]{1,0:T(8,128)}, u32[]{:S(2)}, u32[]{:S(2)}) collective-permute-start(f32[16,1024]{1,0:T(8,128)S(1)} %fusion), channel_id=1, source_target_pairs={{0,48},{16,64},{32,80},{48,96},{64,112},{80,128},{96,144},{112,160... | collective-permute-start | bytes 196616
  277.7 12.3 %collective-permute-start.1 = (f32[16,1024]{1,0:T(8,128)S(1)}, f32[16,1024]{1,0:T(8,128)}, u32[]{:S(2)}, u32[]{:S(2)}) collective-permute-start(f32[16,1024]{1,0:T(8,128)S(1)} %fusion), channel_id=1, source_target_pairs={{0,32},{16,48},{32,64},{48,80},{64,96},{80,112},{96,128},{112,144}... | collective-permute-start | bytes 196616
  286.1 4.7 %collective-permute-start = (f32[16,1024]{1,0:T(8,128)S(1)}, f32[16,1024]{1,0:T(8,128)}, u32[]{:S(2)}, u32[]{:S(2)}) collective-permute-start(f32[16,1024]{1,0:T(8,128)S(1)} %fusion), channel_id=1, source_target_pairs={{0,16},{16,32},{32,48},{48,64},{64,80},{80,96},{96,112},{112,128},... | collective-permute-start | bytes 196616
Sparse Core Ops, SparseCore 0:
  10.5 104.9 all-gather.2
  120.6 91.4 reduce-scatter.3
where the time goes:
time: 309 us; the launch traced here: 305 us
  blocking collectives  137 us (44%)
  waiting for transfers between devices  72.3 us (23%)
  starting transfers between devices  63.8 us (21%)
  between operations  14.9 us (5%)
  local copies, waits for them, and re-layouts  8.85 us (3%)
  matrix products  5.22 us (2%)
    unnamed x1, blocking collectives  95.9 us
    unnamed x15, starting transfers between devices  63.8 us
    all_gather x1, waiting for transfers between devices, on_device(): gathered = lax.all_gather(stored_projector, 'dp', axis=0, tiled=True)  63.2 us
    all_gather x1, blocking collectives, on_device(): grad_full = lax.all_gather(work_g, 'mp', axis=1, tiled=True)  41.3 us
    unnamed x17, waiting for transfers between devices  9.08 us
    unnamed x9, local copies, waits for them, and re-layouts  8.71 us
  transfers between devices with their start and end apart: 17, of which 3 were waited for; matrix products, arithmetic and copies ran while one was open for 35% of the time, Pallas kernels for 0%

commit v1 on v0

v1 whole, which is shorter than its diff:
```python
import jax
import jax.numpy as jnp
from jax import lax
from jax.sharding import Mesh, PartitionSpec as P

BF16 = jnp.bfloat16
F32 = jnp.float32
SWAP = [(0, 1), (1, 0)]


def swap_pair(value):
    return lax.ppermute(value, "pair", SWAP)


def swap_core(value):
    return lax.ppermute(value, "core", SWAP)


def on_device(x, w, adjoint, mask):
    seqs = mask.shape[0]
    tokens, feats = x.shape
    span = tokens // seqs
    wrows, cols = w.shape
    n_z = lax.axis_size("z")
    n_mp = lax.axis_size("mp")
    own_cols = cols // n_mp
    half = own_cols // 2
    side = lax.axis_index("pair")
    core = lax.axis_index("core")

    alive = mask != 0
    count = jnp.sum(mask)
    first_count = jnp.where(side == 0, count, 2 - count)
    skip_first = jnp.logical_not(alive[0])

    def survivor_first(value):
        return jnp.where(skip_first, value[::-1], value)

    def compact(own, other):
        a0 = jnp.where(side == 0, own[0], other[0])
        a1 = jnp.where(side == 0, own[1], other[1])
        b0 = jnp.where(side == 0, other[0], own[0])
        b1 = jnp.where(side == 0, other[1], own[1])
        slot0 = jnp.where(first_count >= 1, a0, b0)
        slot1 = jnp.where(first_count == 2, a1, jnp.where(first_count == 1, b0, b1))
        return jnp.stack([slot0, slot1])

    start = jnp.where(side == 0, 0, 2 - count)

    def home(slots):
        second = start + mask[0]
        rows0 = jnp.where(start == 0, slots[0], slots[1])
        rows1 = jnp.where(second == 0, slots[0], slots[1])
        zero = jnp.zeros_like(rows0)
        return jnp.stack([jnp.where(alive[0], rows0, zero), jnp.where(alive[1], rows1, zero)])

    w_parts = w.reshape(wrows, n_mp, 2, half)
    w_mine = jnp.where(side == 0, w_parts[:, :, 0], w_parts[:, :, 1]).reshape(wrows, n_mp * half)
    w_theirs = jnp.where(side == 0, w_parts[:, :, 1], w_parts[:, :, 0]).reshape(wrows, n_mp * half)
    g = survivor_first(adjoint.T.reshape(2, half, seqs, span).transpose(2, 0, 1, 3))
    g_mine = jnp.where(side == 0, g[:, 0], g[:, 1])
    g_theirs = jnp.where(side == 0, g[:, 1], g[:, 0])
    xs = survivor_first(x.reshape(seqs, span, feats))

    w_other = swap_pair(w_theirs)
    g_other = swap_pair(g_theirs)
    x_other = swap_pair(xs)

    w_block = jnp.where(side == 0, jnp.stack([w_mine, w_other]), jnp.stack([w_other, w_mine]))
    w_block = w_block.reshape(1, 2 * wrows, n_mp * half)
    w_z = lax.all_to_all(jnp.broadcast_to(w_block, (n_z,) + w_block.shape[1:]), "z", 0, 0, tiled=True)
    w_z_other = swap_core(w_z)

    g_pair = compact(g_mine, g_other)
    g_cols = g_pair.transpose(1, 0, 2).reshape(1, half, tokens)
    g_all = lax.all_to_all(jnp.broadcast_to(g_cols, (n_mp, half, tokens)), "mp", 0, 0, tiled=True)
    g_all = g_all.reshape(n_mp * half, tokens)
    x_pair = compact(xs, x_other).reshape(tokens, feats)

    w_cores = jnp.where(core == 0, jnp.stack([w_z, w_z_other]), jnp.stack([w_z_other, w_z]))
    w_full = w_cores.reshape(2, n_z, 2, wrows, n_mp * half).transpose(2, 1, 0, 3, 4)
    w_full = w_full.reshape(4 * n_z * wrows, n_mp * half)[:feats]

    dw = lax.dot_general(x_pair, g_all, (((0,), (1,)), ((), ())), preferred_element_type=F32)
    dw = jnp.pad(dw, ((0, 4 * n_z * wrows - feats), (0, 0)))
    dw = dw.reshape(2, n_z, 2, wrows, n_mp * half).transpose(2, 1, 0, 3, 4)
    dw_mine = jnp.where(core == 0, dw[0], dw[1])
    dw_theirs = jnp.where(core == 0, dw[1], dw[0]).astype(BF16)
    dw_sum = dw_mine + swap_core(dw_theirs).astype(F32)
    dw_z = dw_sum.astype(BF16).reshape(n_z, 2 * wrows, n_mp * half)
    dw_z = lax.all_to_all(dw_z, "z", 0, 0, tiled=True)
    dw_rows = jnp.sum(dw_z.astype(F32), axis=0).reshape(2, wrows, n_mp * half)
    dw_own = jnp.where(side == 0, dw_rows[0], dw_rows[1])
    dw_send = jnp.where(side == 0, dw_rows[1], dw_rows[0])
    dw_other = swap_pair(dw_send)
    dw_own = dw_own.reshape(wrows, n_mp, 1, half)
    dw_other = dw_other.reshape(wrows, n_mp, 1, half)
    weight_grad = jnp.where(
        side == 0,
        jnp.concatenate([dw_own, dw_other], axis=2),
        jnp.concatenate([dw_other, dw_own], axis=2),
    ).reshape(wrows, cols)

    kv = lax.dot_general(w_full, x_pair, (((0,), (1,)), ((), ())), preferred_element_type=F32)
    kv = lax.all_to_all(kv.astype(BF16).reshape(n_mp, half, tokens), "mp", 0, 0, tiled=True)
    kv = jnp.sum(kv.astype(F32), axis=0).astype(BF16)
    kv_other = swap_pair(kv)
    kv_cols = jnp.where(side == 0, jnp.concatenate([kv, kv_other]), jnp.concatenate([kv_other, kv]))
    kv_home = home(kv_cols.reshape(own_cols, seqs, span).transpose(1, 0, 2))
    kv_values = kv_home.transpose(0, 2, 1).reshape(tokens, own_cols)

    dx = lax.dot_general(g_all, w_full, (((0,), (1,)), ((), ())), preferred_element_type=F32)
    dx_other = swap_pair(dx.astype(BF16))
    dx = (dx + dx_other.astype(F32)).astype(BF16)
    activation_grad = home(dx.reshape(seqs, span, feats)).reshape(tokens, feats)
    return kv_values, activation_grad, weight_grad


def solution(mesh):
    n_dp, n_mp = mesh.devices.shape
    names = ("pair", "z", "core", "mp")
    split = Mesh(mesh.devices.reshape(2, n_dp // 4, 2, n_mp), names)
    dp = ("pair", "z", "core")
    return jax.shard_map(
        on_device,
        mesh=split,
        in_specs=(P(dp, "mp"), P((*dp, "mp"), None), P(dp, "mp"), P(dp)),
        out_specs=(P(dp, "mp"), P(dp, "mp"), P((*dp, "mp"), None)),
        check_vma=False,
    )
```

time: 309 us -> 113 us (0.37)
  the two profiles are of different devices: /device:TPU:1 before, /device:TPU:8 now
where the time goes in v1:
time: 113 us; the launch traced here: 112 us
  starting transfers between devices  55.3 us (49%)
  waiting for transfers between devices  36.1 us (32%)
  local copies, waits for them, and re-layouts  8.23 us (7%)
  other arithmetic  7.94 us (7%)
  between operations  3.12 us (3%)
  matrix products  1.75 us (2%)
    ppermute x6, starting transfers between devices, swap_pair(): return lax.ppermute(value, 'pair', SWAP)  26.4 us
    all_to_all x1, waiting for transfers between devices, on_device(): dw_z = lax.all_to_all(dw_z, 'z', 0, 0, tiled=True)  10.8 us
    all_to_all x1, starting transfers between devices, on_device(): lax.all_to_all(jnp.broadcast_to(g_cols, (n_mp, half, tokens)), 'mp', 0, 0...  9.63 us
    all_to_all x1, waiting for transfers between devices, on_device(): lax.all_to_all(jnp.broadcast_to(g_cols, (n_mp, half, tokens)), 'mp', 0, 0...  8.87 us
    all_to_all x1, waiting for transfers between devices, on_device(): lax.all_to_all(jnp.broadcast_to(w_block, (n_z,) + w_block.shape[1:]), 'z'...  8.44 us
    all_to_all x1, waiting for transfers between devices, on_device(): lax.all_to_all(kv.astype(BF16).reshape(n_mp, half, tokens), 'mp', 0, 0, t...  7.21 us
    all_to_all x1, starting transfers between devices, on_device(): lax.all_to_all(jnp.broadcast_to(w_block, (n_z,) + w_block.shape[1:]), 'z'...  6.41 us
    all_to_all x1, starting transfers between devices, on_device(): dw_z = lax.all_to_all(dw_z, 'z', 0, 0, tiled=True)  5.33 us
  transfers between devices with their start and end apart: 12, of which 5 were waited for; matrix products, arithmetic and copies ran while one was open for 12% of the time, Pallas kernels for 0%

profile of v1, /device:TPU:8, one launch (start us, length us, event | category | flops | bytes accessed | tf_op | source)
XLA Modules:
  0.0 112.4 jit_solution(16257674159595556976)
XLA Ops:
  0.7 0.9 reshape.123
  1.6 0.1 fusion.10
  1.8 0.1 select_n.295
  1.9 11.4 %collective-permute-start = (bf16[11,512]{1,0:T(8,128)(2,1)S(1)}, bf16[11,512]{1,0:T(8,128)(2,1)S(1)}, u32[]{:S(2)}, u32[]{:S(2)}) collective-permute-start(bf16[11,512]{1,0:T(8,128)(2,1)S(1)} %select_n.295), channel_id=1, source_target_pairs={{0,384},{384,0},{1,385},{385,1},{2,386},{386,2},{3,387},{387,3},{4... | collective-permute-start | bytes 33800 | tf_op jit(solution)/shard_map/ppermute | solution.py:12
  13.2 0.7 broadcast_compare_fusion
  13.9 0.6 fusion.11
  15.1 0.8 reshape.129
  15.9 0.2 rev.7
  16.1 0.1 select_n.293
  16.3 0.7 broadcast_in_dim.18
  17.0 6.4 %all-to-all-start = ((bf16[12,22,512]{2,1,0:T(8,128)(2,1)}), bf16[12,22,512]{2,1,0:T(8,128)(2,1)S(1)}, u32[]{:S(2)}, u32[]{:S(2)}) async-start(bf16[12,22,512]{2,1,0:T(8,128)(2,1)} %broadcast_in_dim.18), calls=%async_computation | async-start | bytes 589824 | tf_op jit(solution)/shard_map/all_to_all | solution.py:71
  23.5 3.2 %collective-permute-start.4 = (bf16[2,32,128]{2,0,1:T(2,128)(2,1)S(1)}, bf16[2,32,128]{2,0,1:T(2,128)(2,1)S(1)}, u32[]{:S(2)}, u32[]{:S(2)}) collective-permute-start(bf16[2,32,128]{2,0,1:T(2,128)(2,1)S(1)} %get-tuple-element.16), channel_id=1, source_target_pairs={{0,384},{384,0},{1,385},{385,1},{2,386},{386,2},{3,387},{387,3},{4... | collective-permute-start | bytes 49160 | tf_op jit(solution)/shard_map/ppermute | solution.py:12
  26.8 2.6 %collective-permute-start.2 = (bf16[2,128,512]{2,1,0:T(8,128)(2,1)S(1)}, bf16[2,128,512]{2,1,0:T(8,128)(2,1)S(1)}, u32[]{:S(2)}, u32[]{:S(2)}) collective-permute-start(bf16[2,128,512]{2,1,0:T(8,128)(2,1)S(1)} %reverse_select_fusion), channel_id=1, source_target_pairs={{0,384},{384,0},{1,385},{385,1},{2,386},{386,2},{3,387},{387,3},{4... | collective-permute-start | bytes 786440 | tf_op jit(solution)/shard_map/ppermute | solution.py:12
  29.4 0.6 reduce_sum.30
  31.4 0.1 broadcast_select_fusion.17
  31.5 8.4 %all-to-all-done = bf16[12,22,512]{2,1,0:T(8,128)(2,1)S(1)} async-done(((bf16[12,22,512]{2,1,0:T(8,128)(2,1)}), bf16[12,22,512]{2,1,0:T(8,128)(2,1)S(1)}, u32[]{:S(2)}, u32[]{:S(2)}) %all-to-all-start) | async-done | bytes 270368 | tf_op jit(solution)/shard_map/all_to_all | solution.py:71
  39.9 0.7 broadcast_in_dim.21
  40.7 9.6 %all-to-all-start.2 = ((bf16[16,32,256]{2,1,0:T(8,128)(2,1)}), bf16[16,32,256]{2,1,0:T(8,128)(2,1)S(1)}, u32[]{:S(2)}, u32[]{:S(2)}) async-start(bf16[16,32,256]{2,1,0:T(8,128)(2,1)} %broadcast_in_dim.21), calls=%async_computation.2 | async-start | bytes 524288 | tf_op jit(solution)/shard_map/all_to_all | solution.py:76
  50.4 1.9 %collective-permute-start.1 = (bf16[12,22,512]{2,1,0:T(8,128)(2,1)S(1)}, bf16[12,22,512]{2,1,0:T(8,128)(2,1)S(1)}, u32[]{:S(2)}, u32[]{:S(2)}) collective-permute-start(bf16[12,22,512]{2,1,0:T(8,128)(2,1)S(1)} %all-to-all-done), channel_id=1, source_target_pairs={{0,16},{16,0},{1,17},{17,1},{2,18},{18,2},{3,19},{19,3},{4,20},{20... | collective-permute-start | bytes 811016 | tf_op jit(solution)/shard_map/ppermute | solution.py:16
  52.3 8.9 %all-to-all-done.2 = bf16[16,32,256]{2,1,0:T(8,128)(2,1)S(1)} async-done(((bf16[16,32,256]{2,1,0:T(8,128)(2,1)}), bf16[16,32,256]{2,1,0:T(8,128)(2,1)S(1)}, u32[]{:S(2)}, u32[]{:S(2)}) %all-to-all-start.2) | async-done | bytes 262176 | tf_op jit(solution)/shard_map/all_to_all | solution.py:76
  61.2 0.3 fusion.13
  61.7 0.2 reshape.132
  61.8 0.8 fusion.7
  62.7 1.9 %collective-permute-start.6 = (bf16[12,2,11,512]{3,2,0,1:T(8,128)(2,1)}, bf16[12,2,11,512]{3,2,0,1:T(8,128)(2,1)}, u32[]{:S(2)}, u32[]{:S(2)}) collective-permute-start(bf16[12,2,11,512]{3,2,0,1:T(8,128)(2,1)} %fusion.7), channel_id=1, source_target_pairs={{0,16},{16,0},{1,17},{17,1},{2,18},{18,2},{3,19},{19,3},{4,20},{20... | collective-permute-start | bytes 811016 | tf_op jit(solution)/shard_map/ppermute | solution.py:16
  64.7 0.2 fusion
  65.0 0.2 reshape.124
  65.2 0.7 copy-done.1
  65.9 1.1 convolution_convert_fusion
  66.9 3.7 %all-to-all-start.1 = ((bf16[16,32,256]{2,1,0:T(8,128)(2,1)}), bf16[16,32,256]{2,1,0:T(8,128)(2,1)S(1)}, u32[]{:S(2)}, u32[]{:S(2)}) async-start(bf16[16,32,256]{2,1,0:T(8,128)(2,1)} %bitcast.5), calls=%async_computation.1 | async-start | bytes 524288 | tf_op jit(solution)/shard_map/all_to_all | solution.py:105
  70.6 0.4 fusion.12
  71.0 3.1 %collective-permute-start.5 = (bf16[256,512]{1,0:T(8,128)(2,1)S(1)}, bf16[256,512]{1,0:T(8,128)(2,1)S(1)}, u32[]{:S(2)}, u32[]{:S(2)}) collective-permute-start(bf16[256,512]{1,0:T(8,128)(2,1)S(1)} %get-tuple-element.21), channel_id=1, source_target_pairs={{0,384},{384,0},{1,385},{385,1},{2,386},{386,2},{3,387},{387,3},{4... | collective-permute-start | bytes 786440 | tf_op jit(solution)/shard_map/ppermute | solution.py:12
  74.1 1.2 %fusion.3 = bf16[12,2,11,512]{3,2,0,1:T(8,128)(2,1)S(1)} fusion(bf16[12,2,11,512]{3,2,0,1:T(8,128)(2,1)} %collective-permute-done.6, f32[2,12,2,11,512]{4,3,0,1,2:T(8,128)S(1)} %bitcast.89, pred[]{:T(512)S(6)} %eq.14), kind=kLoop, calls=%fused_computation.6 | loop fusion | flops 540672 | bytes 1622017 | tf_op jit(solution)/shard_map/convert_element_type | solution.py:90
  75.4 0.8 reshape.133
  76.2 7.2 %all-to-all-done.1 = bf16[16,32,256]{2,1,0:T(8,128)(2,1)S(1)} async-done(((bf16[16,32,256]{2,1,0:T(8,128)(2,1)}), bf16[16,32,256]{2,1,0:T(8,128)(2,1)S(1)}, u32[]{:S(2)}, u32[]{:S(2)}) %all-to-all-start.1) | async-done | bytes 262176 | tf_op jit(solution)/shard_map/all_to_all | solution.py:105
  83.4 5.3 %all-to-all-start.3 = ((bf16[12,22,512]{2,1,0:T(8,128)(2,1)}), bf16[12,22,512]{2,1,0:T(8,128)(2,1)S(1)}, u32[]{:S(2)}, u32[]{:S(2)}) async-start(bf16[12,22,512]{2,1,0:T(8,128)(2,1)} %reshape.133), calls=%async_computation.3 | async-start | bytes 589824 | tf_op jit(solution)/shard_map/all_to_all | solution.py:91
  88.8 1.3 %select_bitcast_fusion.1 = (bf16[1,128,512]{2,1,0:T(8,128)(2,1)S(1)}, bf16[1,128,512]{2,1,0:T(8,128)(2,1)S(1)}) fusion(pred[]{:T(512)S(6)} %eq.13, pred[]{:T(512)} %bitcast, bf16[256,512]{1,0:T(8,128)(2,1)S(1)} %add_convert_fusion, pred[]{:T(512)S(6)} %eq.17, pred[]{:T(512)} %bitcast.7), kind=kLoop, calls=%fused_computation.19 | loop fusion | flops 262144 | bytes 524292 | tf_op jit(solution)/shard_map/stack | solution.py:55
  90.2 0.7 pad_maximum_fusion.1
  91.0 3.4 %collective-permute-start.3 = (bf16[32,256]{1,0:T(8,128)(2,1)S(1)}, bf16[32,256]{1,0:T(8,128)(2,1)S(1)}, u32[]{:S(2)}, u32[]{:S(2)}) collective-permute-start(bf16[32,256]{1,0:T(8,128)(2,1)S(1)} %reduce_sum.31), channel_id=1, source_target_pairs={{0,384},{384,0},{1,385},{385,1},{2,386},{386,2},{3,387},{387,3},{4... | collective-permute-start | bytes 49160 | tf_op jit(solution)/shard_map/ppermute | solution.py:12
  94.3 10.8 %all-to-all-done.3 = bf16[12,22,512]{2,1,0:T(8,128)(2,1)S(1)} async-done(((bf16[12,22,512]{2,1,0:T(8,128)(2,1)}), bf16[12,22,512]{2,1,0:T(8,128)(2,1)S(1)}, u32[]{:S(2)}, u32[]{:S(2)}) %all-to-all-start.3) | async-done | bytes 270368 | tf_op jit(solution)/shard_map/all_to_all | solution.py:91
  105.2 2.7 %collective-permute-start.7 = (f32[11,512]{1,0:T(8,128)S(1)}, f32[11,512]{1,0:T(8,128)S(1)}, u32[]{:S(2)}, u32[]{:S(2)}) collective-permute-start(f32[11,512]{1,0:T(8,128)S(1)} %get-tuple-element.12), channel_id=1, source_target_pairs={{0,384},{384,0},{1,385},{385,1},{2,386},{386,2},{3,387},{387,3},{4... | collective-permute-start | bytes 67592 | tf_op jit(solution)/shard_map/ppermute | solution.py:12
  107.9 0.2 reshape.134
  108.2 1.4 %broadcast_select_fusion.6 = (bf16[1,64,128]{2,0,1:T(2,128)(2,1)S(1)}, bf16[1,64,128]{2,0,1:T(2,128)(2,1)S(1)}) fusion(pred[]{:T(512)} %bitcast, pred[]{:T(512)S(6)} %eq.13, bf16[2,64,128]{2,0,1:T(2,128)(2,1)S(1)} %fusion.8, pred[]{:T(512)S(6)} %eq.17, pred[]{:T(512)} %bitcast.7), kind=kLoop, calls=%fused_computation.28 | loop fusion | flops 32768 | bytes 65540 | tf_op jit(solution)/shard_map/jit(_where)/select_n | solution.py:55
  109.6 0.1 pad_maximum_fusion.2
  109.7 0.6 copy.46
  110.3 0.8 collective-permute-done.7
  111.0 0.2 reshape.135
  111.2 0.4 maximum_select_fusion.1
  111.6 0.9 select_n.354
  (36 shorter events, 0.9 us)
Async XLA Ops:
  0.6 28.8 %copy-start.3 = (s32[2]{0:T(128)S(1)}, s32[2]{0:T(128)}, u32[]{:S(2)}) copy-start(s32[2]{0:T(128)} %param.7) | copy-start | bytes 28
  0.6 26.1 %copy-start.2 = (bf16[256,512]{1,0:T(8,128)(2,1)S(1)}, bf16[256,512]{1,0:T(8,128)(2,1)}, u32[]{:S(2)}) copy-start(bf16[256,512]{1,0:T(8,128)(2,1)} %param.4) | copy-start | bytes 786436
  1.9 14.4 %collective-permute-start = (bf16[11,512]{1,0:T(8,128)(2,1)S(1)}, bf16[11,512]{1,0:T(8,128)(2,1)S(1)}, u32[]{:S(2)}, u32[]{:S(2)}) collective-permute-start(bf16[11,512]{1,0:T(8,128)(2,1)S(1)} %select_n.295), channel_id=1, source_target_pairs={{0,384},{384,0},{1,385},{385,1},{2,386},{386,2},{3,387},{387,3},{4... | collective-permute-start | bytes 33800 | tf_op jit(solution)/shard_map/ppermute | solution.py:12
  17.0 22.9 %all-to-all-start = ((bf16[12,22,512]{2,1,0:T(8,128)(2,1)}), bf16[12,22,512]{2,1,0:T(8,128)(2,1)S(1)}, u32[]{:S(2)}, u32[]{:S(2)}) async-start(bf16[12,22,512]{2,1,0:T(8,128)(2,1)} %broadcast_in_dim.18), calls=%async_computation | async-start | bytes 589824 | tf_op jit(solution)/shard_map/all_to_all | solution.py:71
  23.5 7.9 %collective-permute-start.4 = (bf16[2,32,128]{2,0,1:T(2,128)(2,1)S(1)}, bf16[2,32,128]{2,0,1:T(2,128)(2,1)S(1)}, u32[]{:S(2)}, u32[]{:S(2)}) collective-permute-start(bf16[2,32,128]{2,0,1:T(2,128)(2,1)S(1)} %get-tuple-element.16), channel_id=1, source_target_pairs={{0,384},{384,0},{1,385},{385,1},{2,386},{386,2},{3,387},{387,3},{4... | collective-permute-start | bytes 49160 | tf_op jit(solution)/shard_map/ppermute | solution.py:12
  26.8 23.5 %collective-permute-start.2 = (bf16[2,128,512]{2,1,0:T(8,128)(2,1)S(1)}, bf16[2,128,512]{2,1,0:T(8,128)(2,1)S(1)}, u32[]{:S(2)}, u32[]{:S(2)}) collective-permute-start(bf16[2,128,512]{2,1,0:T(8,128)(2,1)S(1)} %reverse_select_fusion), channel_id=1, source_target_pairs={{0,384},{384,0},{1,385},{385,1},{2,386},{386,2},{3,387},{387,3},{4... | collective-permute-start | bytes 786440 | tf_op jit(solution)/shard_map/ppermute | solution.py:12
  40.7 20.6 %all-to-all-start.2 = ((bf16[16,32,256]{2,1,0:T(8,128)(2,1)}), bf16[16,32,256]{2,1,0:T(8,128)(2,1)S(1)}, u32[]{:S(2)}, u32[]{:S(2)}) async-start(bf16[16,32,256]{2,1,0:T(8,128)(2,1)} %broadcast_in_dim.21), calls=%async_computation.2 | async-start | bytes 524288 | tf_op jit(solution)/shard_map/all_to_all | solution.py:76
  50.4 11.2 %copy-start = (bf16[2,128,512]{2,1,0:T(8,128)(2,1)}, bf16[2,128,512]{2,1,0:T(8,128)(2,1)S(1)}, u32[]{:S(2)}) copy-start(bf16[2,128,512]{2,1,0:T(8,128)(2,1)S(1)} %pad_maximum_fusion) | copy-start | bytes 786436
  50.4 14.2 %collective-permute-start.1 = (bf16[12,22,512]{2,1,0:T(8,128)(2,1)S(1)}, bf16[12,22,512]{2,1,0:T(8,128)(2,1)S(1)}, u32[]{:S(2)}, u32[]{:S(2)}) collective-permute-start(bf16[12,22,512]{2,1,0:T(8,128)(2,1)S(1)} %all-to-all-done), channel_id=1, source_target_pairs={{0,16},{16,0},{1,17},{17,1},{2,18},{18,2},{3,19},{19,3},{4,20},{20... | collective-permute-start | bytes 811016 | tf_op jit(solution)/shard_map/ppermute | solution.py:16
  62.7 11.5 %collective-permute-start.6 = (bf16[12,2,11,512]{3,2,0,1:T(8,128)(2,1)}, bf16[12,2,11,512]{3,2,0,1:T(8,128)(2,1)}, u32[]{:S(2)}, u32[]{:S(2)}) collective-permute-start(bf16[12,2,11,512]{3,2,0,1:T(8,128)(2,1)} %fusion.7), channel_id=1, source_target_pairs={{0,16},{16,0},{1,17},{17,1},{2,18},{18,2},{3,19},{19,3},{4,20},{20... | collective-permute-start | bytes 811016 | tf_op jit(solution)/shard_map/ppermute | solution.py:16
  64.9 1.0 copy-start.1
  66.9 16.5 %all-to-all-start.1 = ((bf16[16,32,256]{2,1,0:T(8,128)(2,1)}), bf16[16,32,256]{2,1,0:T(8,128)(2,1)S(1)}, u32[]{:S(2)}, u32[]{:S(2)}) async-start(bf16[16,32,256]{2,1,0:T(8,128)(2,1)} %bitcast.5), calls=%async_computation.1 | async-start | bytes 524288 | tf_op jit(solution)/shard_map/all_to_all | solution.py:105
  71.0 17.7 %collective-permute-start.5 = (bf16[256,512]{1,0:T(8,128)(2,1)S(1)}, bf16[256,512]{1,0:T(8,128)(2,1)S(1)}, u32[]{:S(2)}, u32[]{:S(2)}) collective-permute-start(bf16[256,512]{1,0:T(8,128)(2,1)S(1)} %get-tuple-element.21), channel_id=1, source_target_pairs={{0,384},{384,0},{1,385},{385,1},{2,386},{386,2},{3,387},{387,3},{4... | collective-permute-start | bytes 786440 | tf_op jit(solution)/shard_map/ppermute | solution.py:12
  83.4 21.8 %all-to-all-start.3 = ((bf16[12,22,512]{2,1,0:T(8,128)(2,1)}), bf16[12,22,512]{2,1,0:T(8,128)(2,1)S(1)}, u32[]{:S(2)}, u32[]{:S(2)}) async-start(bf16[12,22,512]{2,1,0:T(8,128)(2,1)} %reshape.133), calls=%async_computation.3 | async-start | bytes 589824 | tf_op jit(solution)/shard_map/all_to_all | solution.py:91
  91.0 17.2 %collective-permute-start.3 = (bf16[32,256]{1,0:T(8,128)(2,1)S(1)}, bf16[32,256]{1,0:T(8,128)(2,1)S(1)}, u32[]{:S(2)}, u32[]{:S(2)}) collective-permute-start(bf16[32,256]{1,0:T(8,128)(2,1)S(1)} %reduce_sum.31), channel_id=1, source_target_pairs={{0,384},{384,0},{1,385},{385,1},{2,386},{386,2},{3,387},{387,3},{4... | collective-permute-start | bytes 49160 | tf_op jit(solution)/shard_map/ppermute | solution.py:12
  105.2 5.8 %collective-permute-start.7 = (f32[11,512]{1,0:T(8,128)S(1)}, f32[11,512]{1,0:T(8,128)S(1)}, u32[]{:S(2)}, u32[]{:S(2)}) collective-permute-start(f32[11,512]{1,0:T(8,128)S(1)} %get-tuple-element.12), channel_id=1, source_target_pairs={{0,384},{384,0},{1,385},{385,1},{2,386},{386,2},{3,387},{387,3},{4... | collective-permute-start | bytes 67592 | tf_op jit(solution)/shard_map/ppermute | solution.py:12

commit v2 on v1

--- a/solution.py
+++ b/solution.py
@@ -67,13 +67,15 @@
     x_other = swap_pair(xs)
 
     w_block = jnp.where(side == 0, jnp.stack([w_mine, w_other]), jnp.stack([w_other, w_mine]))
-    w_block = w_block.reshape(1, 2 * wrows, n_mp * half)
-    w_z = lax.all_to_all(jnp.broadcast_to(w_block, (n_z,) + w_block.shape[1:]), "z", 0, 0, tiled=True)
-    w_z_other = swap_core(w_z)
 
     g_pair = compact(g_mine, g_other)
     g_cols = g_pair.transpose(1, 0, 2).reshape(1, half, tokens)
-    g_all = lax.all_to_all(jnp.broadcast_to(g_cols, (n_mp, half, tokens)), "mp", 0, 0, tiled=True)
+    g_send = jnp.broadcast_to(g_cols, (n_mp, half, tokens))
+    w_block = w_block.reshape(1, 2 * wrows, n_mp * half)
+    g_send, w_block = lax.optimization_barrier((g_send, w_block))
+    g_all = lax.all_to_all(g_send, "mp", 0, 0, tiled=True)
+    w_z = lax.all_gather(w_block, "z", axis=0, tiled=True)
+    w_z_other = swap_core(w_z)
     g_all = g_all.reshape(n_mp * half, tokens)
     x_pair = compact(xs, x_other).reshape(tokens, feats)
 

time: 113 us -> 122 us (1.080)
  blocking collectives: 0 us -> 31 us
  waiting for transfers between devices: 36.1 us -> 23.3 us
  starting transfers between devices: 55.3 us -> 45.5 us
  local copies, waits for them, and re-layouts: 8.23 us -> 6.77 us
    all_gather x0 -> x1, blocking collectives: none -> 31 us  [on_device(): w_z = lax.all_gather(w_block, 'z', axis=0, tiled=True)]
    all_to_all x2 -> x1, waiting for transfers between devices: 17.3 us -> 0.01 us  [on_device(): g_all = lax.all_to_all(g_send, 'mp', 0, 0, tiled=True)]
    all_to_all x2 -> x1, starting transfers between devices: 16 us -> 3.53 us  [on_device(): g_all = lax.all_to_all(g_send, 'mp', 0, 0, tiled=True)]
    all_to_all x1, starting transfers between devices: 3.73 us -> 9.63 us  [on_device(): lax.all_to_all(kv.astype(BF16).reshape(n_mp, half, tokens), 'mp', 0, 0, t...]
    ppermute x6, waiting for transfers between devices: 0.76 us -> 4.8 us  [swap_pair(): return lax.ppermute(value, 'pair', SWAP)]
    all_to_all x1, starting transfers between devices: 5.33 us -> 3.55 us  [on_device(): dw_z = lax.all_to_all(dw_z, 'z', 0, 0, tiled=True)]
    all_to_all x1, waiting for transfers between devices: 10.8 us -> 9.06 us  [on_device(): dw_z = lax.all_to_all(dw_z, 'z', 0, 0, tiled=True)]
    ppermute x6, starting transfers between devices: 26.4 us -> 24.8 us  [swap_pair(): return lax.ppermute(value, 'pair', SWAP)]
  transfers between devices with their start and end apart: 12 -> 11, of which waited for: 5 -> 5; matrix products, arithmetic and copies ran while one was open for 12% -> 11% of each run, Pallas kernels for 0% -> 0%
where the time goes in v2:
time: 122 us; the launch traced here: 121 us
  starting transfers between devices  45.5 us (37%)
  blocking collectives  31 us (25%)
  waiting for transfers between devices  23.3 us (19%)
  other arithmetic  9.05 us (7%)
  local copies, waits for them, and re-layouts  6.77 us (6%)
  between operations  3.06 us (3%)
  matrix products  2.72 us (2%)
    all_gather x1, blocking collectives, on_device(): w_z = lax.all_gather(w_block, 'z', axis=0, tiled=True)  31 us
    ppermute x6, starting transfers between devices, swap_pair(): return lax.ppermute(value, 'pair', SWAP)  24.8 us
    all_to_all x1, starting transfers between devices, on_device(): lax.all_to_all(kv.astype(BF16).reshape(n_mp, half, tokens), 'mp', 0, 0, t...  9.63 us
    all_to_all x1, waiting for transfers between devices, on_device(): dw_z = lax.all_to_all(dw_z, 'z', 0, 0, tiled=True)  9.06 us
    all_to_all x1, waiting for transfers between devices, on_device(): lax.all_to_all(kv.astype(BF16).reshape(n_mp, half, tokens), 'mp', 0, 0, t...  8.11 us
    ppermute x6, waiting for transfers between devices, swap_pair(): return lax.ppermute(value, 'pair', SWAP)  4.8 us
    ppermute x2, starting transfers between devices, swap_core(): return lax.ppermute(value, 'core', SWAP)  3.94 us
    all_to_all x1, starting transfers between devices, on_device(): dw_z = lax.all_to_all(dw_z, 'z', 0, 0, tiled=True)  3.55 us
  transfers between devices with their start and end apart: 11, of which 5 were waited for; matrix products, arithmetic and copies ran while one was open for 11% of the time, Pallas kernels for 0%

profile of v2, /device:TPU:8, one launch (start us, length us, event | category | flops | bytes accessed | tf_op | source)
XLA Modules:
  0.0 121.4 jit_solution(9683497074455613822)
XLA Ops:
  0.6 0.7 broadcast_compare_fusion
  1.4 0.6 fusion.11
  2.6 0.8 reshape.131
  3.4 0.2 rev.6
  3.6 11.4 %collective-permute-start = (bf16[2,32,128]{2,0,1:T(2,128)(2,1)S(1)}, bf16[2,32,128]{2,0,1:T(2,128)(2,1)S(1)}, u32[]{:S(2)}, u32[]{:S(2)}) collective-permute-start(bf16[2,32,128]{2,0,1:T(2,128)(2,1)S(1)} %get-tuple-element.22), channel_id=1, source_target_pairs={{0,384},{384,0},{1,385},{385,1},{2,386},{386,2},{3,387},{387,3},{4... | collective-permute-start | bytes 49160 | tf_op jit(solution)/shard_map/ppermute | solution.py:12
  15.0 0.9 reshape.132
  15.9 0.1 fusion.10
  16.1 0.1 select_n.316
  16.2 1.9 %collective-permute-start.1 = (bf16[11,512]{1,0:T(8,128)(2,1)S(1)}, bf16[11,512]{1,0:T(8,128)(2,1)S(1)}, u32[]{:S(2)}, u32[]{:S(2)}) collective-permute-start(bf16[11,512]{1,0:T(8,128)(2,1)S(1)} %select_n.316), channel_id=1, source_target_pairs={{0,384},{384,0},{1,385},{385,1},{2,386},{386,2},{3,387},{387,3},{4... | collective-permute-start | bytes 33800 | tf_op jit(solution)/shard_map/ppermute | solution.py:12
  18.1 1.1 reverse_select_fusion
  19.2 3.9 %collective-permute-start.3 = (bf16[2,128,512]{2,1,0:T(8,128)(2,1)S(1)}, bf16[2,128,512]{2,1,0:T(8,128)(2,1)S(1)}, u32[]{:S(2)}, u32[]{:S(2)}) collective-permute-start(bf16[2,128,512]{2,1,0:T(8,128)(2,1)S(1)} %reverse_select_fusion), channel_id=1, source_target_pairs={{0,384},{384,0},{1,385},{385,1},{2,386},{386,2},{3,387},{387,3},{4... | collective-permute-start | bytes 786440 | tf_op jit(solution)/shard_map/ppermute | solution.py:12
  23.1 0.6 reduce_sum.30
  25.1 0.1 select_n.314
  25.3 0.1 broadcast_select_fusion.17
  25.4 0.7 broadcast_in_dim.14
  26.2 3.5 %all-to-all-start.1 = ((bf16[16,32,256]{2,1,0:T(8,128)(2,1)}), bf16[16,32,256]{2,1,0:T(8,128)(2,1)S(1)}, u32[]{:S(2)}, u32[]{:S(2)}) async-start(bf16[16,32,256]{2,1,0:T(8,128)(2,1)} %broadcast_in_dim.14), calls=%async_computation.1 | async-start | bytes 524288 | tf_op jit(solution)/shard_map/all_to_all | solution.py:76
  29.7 31.0 %all_gather.3 = bf16[12,22,512]{2,1,0:T(8,128)(2,1)S(1)} all-gather(bf16[1,22,512]{2,1,0:T(8,128)(2,1)S(1)} %select_n.318), channel_id=1, replica_groups=mesh['pair'=2,'z'=12,'core'=2,'mp'=16] {'z'}, dimensions={0}, use_global_device_ids=true | all-gather | bytes 292864 | tf_op jit(solution)/shard_map/all_gather | solution.py:77
  60.7 1.9 %collective-permute-start.2 = (bf16[12,22,512]{2,1,0:T(8,128)(2,1)S(1)}, bf16[12,22,512]{2,1,0:T(8,128)(2,1)S(1)}, u32[]{:S(2)}, u32[]{:S(2)}) collective-permute-start(bf16[12,22,512]{2,1,0:T(8,128)(2,1)S(1)} %all_gather.3), channel_id=1, source_target_pairs={{0,16},{16,0},{1,17},{17,1},{2,18},{18,2},{3,19},{19,3},{4,20},{20... | collective-permute-start | bytes 811016 | tf_op jit(solution)/shard_map/ppermute | solution.py:16
  62.8 1.4 %collective-permute-done.2 = bf16[12,22,512]{2,1,0:T(8,128)(2,1)S(1)} collective-permute-done((bf16[12,22,512]{2,1,0:T(8,128)(2,1)S(1)}, bf16[12,22,512]{2,1,0:T(8,128)(2,1)S(1)}, u32[]{:S(2)}, u32[]{:S(2)}) %collective-permute-start.2) | collective-permute-done | bytes 270368 | tf_op jit(solution)/shard_map/ppermute | solution.py:16
  64.2 0.2 fusion
  64.4 0.2 reshape.133
  64.7 0.3 fusion.13
  65.0 0.1 pad.4
  65.1 0.2 reshape.140
  65.3 0.8 fusion.7
  66.1 2.0 %collective-permute-start.6 = (bf16[12,2,11,512]{3,2,0,1:T(8,128)(2,1)}, bf16[12,2,11,512]{3,2,0,1:T(8,128)(2,1)}, u32[]{:S(2)}, u32[]{:S(2)}) collective-permute-start(bf16[12,2,11,512]{3,2,0,1:T(8,128)(2,1)} %fusion.7), channel_id=1, source_target_pairs={{0,16},{16,0},{1,17},{17,1},{2,18},{18,2},{3,19},{19,3},{4,20},{20... | collective-permute-start | bytes 811016 | tf_op jit(solution)/shard_map/ppermute | solution.py:16
  68.2 2.0 %convolution_convert_fusion = bf16[512,256]{1,0:T(8,128)(2,1)} fusion(bf16[256,512]{1,0:T(8,128)(2,1)} %bitcast.93, bf16[528,512]{1,0:T(8,128)(2,1)S(1)} %reshape.133), kind=kOutput, calls=%fused_computation | convolution fusion | flops 134348800 | bytes 1048576 | tf_op jit(solution)/shard_map/dot_general | solution.py:106
  70.2 9.6 %all-to-all-start = ((bf16[16,32,256]{2,1,0:T(8,128)(2,1)}), bf16[16,32,256]{2,1,0:T(8,128)(2,1)S(1)}, u32[]{:S(2)}, u32[]{:S(2)}) async-start(bf16[16,32,256]{2,1,0:T(8,128)(2,1)} %bitcast.13), calls=%async_computation | async-start | bytes 524288 | tf_op jit(solution)/shard_map/all_to_all | solution.py:107
  79.8 0.4 fusion.12
  80.2 2.6 %collective-permute-start.5 = (bf16[256,512]{1,0:T(8,128)(2,1)S(1)}, bf16[256,512]{1,0:T(8,128)(2,1)S(1)}, u32[]{:S(2)}, u32[]{:S(2)}) collective-permute-start(bf16[256,512]{1,0:T(8,128)(2,1)S(1)} %get-tuple-element.25), channel_id=1, source_target_pairs={{0,384},{384,0},{1,385},{385,1},{2,386},{386,2},{3,387},{387,3},{4... | collective-permute-start | bytes 786440 | tf_op jit(solution)/shard_map/ppermute | solution.py:12
  82.8 1.2 fusion.3
  84.0 0.8 reshape.141
  84.8 8.1 %all-to-all-done = bf16[16,32,256]{2,1,0:T(8,128)(2,1)S(1)} async-done(((bf16[16,32,256]{2,1,0:T(8,128)(2,1)}), bf16[16,32,256]{2,1,0:T(8,128)(2,1)S(1)}, u32[]{:S(2)}, u32[]{:S(2)}) %all-to-all-start) | async-done | bytes 262176 | tf_op jit(solution)/shard_map/all_to_all | solution.py:107
  92.9 3.5 %all-to-all-start.2 = ((bf16[12,22,512]{2,1,0:T(8,128)(2,1)}), bf16[12,22,512]{2,1,0:T(8,128)(2,1)S(1)}, u32[]{:S(2)}, u32[]{:S(2)}) async-start(bf16[12,22,512]{2,1,0:T(8,128)(2,1)} %reshape.141), calls=%async_computation.2 | async-start | bytes 589824 | tf_op jit(solution)/shard_map/all_to_all | solution.py:93
  96.6 1.3 %select_bitcast_fusion.1 = (bf16[1,128,512]{2,1,0:T(8,128)(2,1)S(1)}, bf16[1,128,512]{2,1,0:T(8,128)(2,1)S(1)}) fusion(pred[]{:T(512)S(6)} %eq.13, pred[]{:T(512)} %bitcast, bf16[256,512]{1,0:T(8,128)(2,1)S(1)} %add_convert_fusion, pred[]{:T(512)S(6)} %eq.17, pred[]{:T(512)} %bitcast.15), kind=kLoop, calls=%fused_computation.19 | loop fusion | flops 262144 | bytes 524292 | tf_op jit(solution)/shard_map/stack | solution.py:55
  97.9 3.1 %collective-permute-start.4 = (bf16[32,256]{1,0:T(8,128)(2,1)S(1)}, bf16[32,256]{1,0:T(8,128)(2,1)S(1)}, u32[]{:S(2)}, u32[]{:S(2)}) collective-permute-start(bf16[32,256]{1,0:T(8,128)(2,1)S(1)} %reduce_sum.31), channel_id=1, source_target_pairs={{0,384},{384,0},{1,385},{385,1},{2,386},{386,2},{3,387},{387,3},{4... | collective-permute-start | bytes 49160 | tf_op jit(solution)/shard_map/ppermute | solution.py:12
  101.0 0.7 pad_maximum_fusion.1
  101.8 1.8 %collective-permute-done.4 = bf16[32,256]{1,0:T(8,128)(2,1)S(1)} collective-permute-done((bf16[32,256]{1,0:T(8,128)(2,1)S(1)}, bf16[32,256]{1,0:T(8,128)(2,1)S(1)}, u32[]{:S(2)}, u32[]{:S(2)}) %collective-permute-start.4) | collective-permute-done | bytes 16416 | tf_op jit(solution)/shard_map/ppermute | solution.py:12
  103.6 1.4 %broadcast_select_fusion.6 = (bf16[1,64,128]{2,0,1:T(2,128)(2,1)S(1)}, bf16[1,64,128]{2,0,1:T(2,128)(2,1)S(1)}) fusion(pred[]{:T(512)} %bitcast, pred[]{:T(512)S(6)} %eq.13, bf16[2,64,128]{2,0,1:T(2,128)(2,1)S(1)} %fusion.8, pred[]{:T(512)S(6)} %eq.17, pred[]{:T(512)} %bitcast.15), kind=kLoop, calls=%fused_computation.28 | loop fusion | flops 32768 | bytes 65540 | tf_op jit(solution)/shard_map/jit(_where)/select_n | solution.py:55
  105.0 9.1 %all-to-all-done.2 = bf16[12,22,512]{2,1,0:T(8,128)(2,1)S(1)} async-done(((bf16[12,22,512]{2,1,0:T(8,128)(2,1)}), bf16[12,22,512]{2,1,0:T(8,128)(2,1)S(1)}, u32[]{:S(2)}, u32[]{:S(2)}) %all-to-all-start.2) | async-done | bytes 270368 | tf_op jit(solution)/shard_map/all_to_all | solution.py:93
  114.2 1.9 %collective-permute-start.7 = (f32[11,512]{1,0:T(8,128)S(1)}, f32[11,512]{1,0:T(8,128)S(1)}, u32[]{:S(2)}, u32[]{:S(2)}) collective-permute-start(f32[11,512]{1,0:T(8,128)S(1)} %get-tuple-element.16), channel_id=1, source_target_pairs={{0,384},{384,0},{1,385},{385,1},{2,386},{386,2},{3,387},{387,3},{4... | collective-permute-start | bytes 67592 | tf_op jit(solution)/shard_map/ppermute | solution.py:12
  116.1 0.1 pad_maximum_fusion.2
  116.2 0.6 copy.58
  116.8 0.2 reshape.142
  117.0 3.0 %collective-permute-done.7 = f32[11,512]{1,0:T(8,128)S(1)} collective-permute-done((f32[11,512]{1,0:T(8,128)S(1)}, f32[11,512]{1,0:T(8,128)S(1)}, u32[]{:S(2)}, u32[]{:S(2)}) %collective-permute-start.7) | collective-permute-done | bytes 22560 | tf_op jit(solution)/shard_map/ppermute | solution.py:12
  120.0 0.2 reshape.143
  120.1 0.4 maximum_select_fusion.1
  120.5 0.9 select_n.357
  (30 shorter events, 0.7 us)
Async XLA Ops:
  0.6 22.5 %copy-start.1 = (s32[2]{0:T(128)S(1)}, s32[2]{0:T(128)}, u32[]{:S(2)}) copy-start(s32[2]{0:T(128)} %param.7) | copy-start | bytes 28
  3.6 21.7 %collective-permute-start = (bf16[2,32,128]{2,0,1:T(2,128)(2,1)S(1)}, bf16[2,32,128]{2,0,1:T(2,128)(2,1)S(1)}, u32[]{:S(2)}, u32[]{:S(2)}) collective-permute-start(bf16[2,32,128]{2,0,1:T(2,128)(2,1)S(1)} %get-tuple-element.22), channel_id=1, source_target_pairs={{0,384},{384,0},{1,385},{385,1},{2,386},{386,2},{3,387},{387,3},{4... | collective-permute-start | bytes 49160 | tf_op jit(solution)/shard_map/ppermute | solution.py:12
  16.2 9.1 %collective-permute-start.1 = (bf16[11,512]{1,0:T(8,128)(2,1)S(1)}, bf16[11,512]{1,0:T(8,128)(2,1)S(1)}, u32[]{:S(2)}, u32[]{:S(2)}) collective-permute-start(bf16[11,512]{1,0:T(8,128)(2,1)S(1)} %select_n.316), channel_id=1, source_target_pairs={{0,384},{384,0},{1,385},{385,1},{2,386},{386,2},{3,387},{387,3},{4... | collective-permute-start | bytes 33800 | tf_op jit(solution)/shard_map/ppermute | solution.py:12
  19.2 43.4 %collective-permute-start.3 = (bf16[2,128,512]{2,1,0:T(8,128)(2,1)S(1)}, bf16[2,128,512]{2,1,0:T(8,128)(2,1)S(1)}, u32[]{:S(2)}, u32[]{:S(2)}) collective-permute-start(bf16[2,128,512]{2,1,0:T(8,128)(2,1)S(1)} %reverse_select_fusion), channel_id=1, source_target_pairs={{0,384},{384,0},{1,385},{385,1},{2,386},{386,2},{3,387},{387,3},{4... | collective-permute-start | bytes 786440 | tf_op jit(solution)/shard_map/ppermute | solution.py:12
  26.2 38.5 %all-to-all-start.1 = ((bf16[16,32,256]{2,1,0:T(8,128)(2,1)}), bf16[16,32,256]{2,1,0:T(8,128)(2,1)S(1)}, u32[]{:S(2)}, u32[]{:S(2)}) async-start(bf16[16,32,256]{2,1,0:T(8,128)(2,1)} %broadcast_in_dim.14), calls=%async_computation.1 | async-start | bytes 524288 | tf_op jit(solution)/shard_map/all_to_all | solution.py:76
  60.7 3.5 %collective-permute-start.2 = (bf16[12,22,512]{2,1,0:T(8,128)(2,1)S(1)}, bf16[12,22,512]{2,1,0:T(8,128)(2,1)S(1)}, u32[]{:S(2)}, u32[]{:S(2)}) collective-permute-start(bf16[12,22,512]{2,1,0:T(8,128)(2,1)S(1)} %all_gather.3), channel_id=1, source_target_pairs={{0,16},{16,0},{1,17},{17,1},{2,18},{18,2},{3,19},{19,3},{4,20},{20... | collective-permute-start | bytes 811016 | tf_op jit(solution)/shard_map/ppermute | solution.py:16
  62.7 2.3 %copy-start = (bf16[2,128,512]{2,1,0:T(8,128)(2,1)}, bf16[2,128,512]{2,1,0:T(8,128)(2,1)S(1)}, u32[]{:S(2)}) copy-start(bf16[2,128,512]{2,1,0:T(8,128)(2,1)S(1)} %pad_maximum_fusion) | copy-start | bytes 786436
  66.1 16.7 %collective-permute-start.6 = (bf16[12,2,11,512]{3,2,0,1:T(8,128)(2,1)}, bf16[12,2,11,512]{3,2,0,1:T(8,128)(2,1)}, u32[]{:S(2)}, u32[]{:S(2)}) collective-permute-start(bf16[12,2,11,512]{3,2,0,1:T(8,128)(2,1)} %fusion.7), channel_id=1, source_target_pairs={{0,16},{16,0},{1,17},{17,1},{2,18},{18,2},{3,19},{19,3},{4,20},{20... | collective-permute-start | bytes 811016 | tf_op jit(solution)/shard_map/ppermute | solution.py:16
  70.2 22.7 %all-to-all-start = ((bf16[16,32,256]{2,1,0:T(8,128)(2,1)}), bf16[16,32,256]{2,1,0:T(8,128)(2,1)S(1)}, u32[]{:S(2)}, u32[]{:S(2)}) async-start(bf16[16,32,256]{2,1,0:T(8,128)(2,1)} %bitcast.13), calls=%async_computation | async-start | bytes 524288 | tf_op jit(solution)/shard_map/all_to_all | solution.py:107
  80.2 16.3 %collective-permute-start.5 = (bf16[256,512]{1,0:T(8,128)(2,1)S(1)}, bf16[256,512]{1,0:T(8,128)(2,1)S(1)}, u32[]{:S(2)}, u32[]{:S(2)}) collective-permute-start(bf16[256,512]{1,0:T(8,128)(2,1)S(1)} %get-tuple-element.25), channel_id=1, source_target_pairs={{0,384},{384,0},{1,385},{385,1},{2,386},{386,2},{3,387},{387,3},{4... | collective-permute-start | bytes 786440 | tf_op jit(solution)/shard_map/ppermute | solution.py:12
  92.9 21.2 %all-to-all-start.2 = ((bf16[12,22,512]{2,1,0:T(8,128)(2,1)}), bf16[12,22,512]{2,1,0:T(8,128)(2,1)S(1)}, u32[]{:S(2)}, u32[]{:S(2)}) async-start(bf16[12,22,512]{2,1,0:T(8,128)(2,1)} %reshape.141), calls=%async_computation.2 | async-start | bytes 589824 | tf_op jit(solution)/shard_map/all_to_all | solution.py:93
  97.9 5.6 %collective-permute-start.4 = (bf16[32,256]{1,0:T(8,128)(2,1)S(1)}, bf16[32,256]{1,0:T(8,128)(2,1)S(1)}, u32[]{:S(2)}, u32[]{:S(2)}) collective-permute-start(bf16[32,256]{1,0:T(8,128)(2,1)S(1)} %reduce_sum.31), channel_id=1, source_target_pairs={{0,384},{384,0},{1,385},{385,1},{2,386},{386,2},{3,387},{387,3},{4... | collective-permute-start | bytes 49160 | tf_op jit(solution)/shard_map/ppermute | solution.py:12
  114.2 5.8 %collective-permute-start.7 = (f32[11,512]{1,0:T(8,128)S(1)}, f32[11,512]{1,0:T(8,128)S(1)}, u32[]{:S(2)}, u32[]{:S(2)}) collective-permute-start(f32[11,512]{1,0:T(8,128)S(1)} %get-tuple-element.16), channel_id=1, source_target_pairs={{0,384},{384,0},{1,385},{385,1},{2,386},{386,2},{3,387},{387,3},{4... | collective-permute-start | bytes 67592 | tf_op jit(solution)/shard_map/ppermute | solution.py:12

commit v3 on v1

--- a/solution.py
+++ b/solution.py
@@ -54,56 +54,55 @@
         zero = jnp.zeros_like(rows0)
         return jnp.stack([jnp.where(alive[0], rows0, zero), jnp.where(alive[1], rows1, zero)])
 
-    w_parts = w.reshape(wrows, n_mp, 2, half)
-    w_mine = jnp.where(side == 0, w_parts[:, :, 0], w_parts[:, :, 1]).reshape(wrows, n_mp * half)
-    w_theirs = jnp.where(side == 0, w_parts[:, :, 1], w_parts[:, :, 0]).reshape(wrows, n_mp * half)
+    def pack(value):
+        lead = value.shape[:-2]
+        value = value.reshape(*lead, wrows, 2, n_mp * half // 2)
+        return jnp.swapaxes(value, -3, -2).reshape(*lead, 2 * wrows, n_mp * half // 2)
+
+    def unpack(value):
+        lead = value.shape[:-2]
+        value = value.reshape(*lead, 2, wrows, n_mp * half // 2)
+        return jnp.swapaxes(value, -3, -2).reshape(*lead, wrows, n_mp * half)
+
+    w_halves = w.reshape(wrows, n_mp, 2, half).transpose(2, 0, 1, 3).reshape(2, 1, wrows, n_mp * half)
+    w_send = pack(w_halves)
+    w_send = jnp.broadcast_to(w_send, (2, n_z) + w_send.shape[2:])
+    w_mine = lax.all_to_all(
+        w_send.reshape(2 * n_z, 2 * wrows, n_mp * half // 2), ("pair", "z"), 0, 0, tiled=True
+    )
+
     g = survivor_first(adjoint.T.reshape(2, half, seqs, span).transpose(2, 0, 1, 3))
     g_mine = jnp.where(side == 0, g[:, 0], g[:, 1])
     g_theirs = jnp.where(side == 0, g[:, 1], g[:, 0])
     xs = survivor_first(x.reshape(seqs, span, feats))
-
-    w_other = swap_pair(w_theirs)
     g_other = swap_pair(g_theirs)
     x_other = swap_pair(xs)
-
-    w_block = jnp.where(side == 0, jnp.stack([w_mine, w_other]), jnp.stack([w_other, w_mine]))
-    w_block = w_block.reshape(1, 2 * wrows, n_mp * half)
-    w_z = lax.all_to_all(jnp.broadcast_to(w_block, (n_z,) + w_block.shape[1:]), "z", 0, 0, tiled=True)
-    w_z_other = swap_core(w_z)
-
     g_pair = compact(g_mine, g_other)
     g_cols = g_pair.transpose(1, 0, 2).reshape(1, half, tokens)
-    g_all = lax.all_to_all(jnp.broadcast_to(g_cols, (n_mp, half, tokens)), "mp", 0, 0, tiled=True)
-    g_all = g_all.reshape(n_mp * half, tokens)
     x_pair = compact(xs, x_other).reshape(tokens, feats)
 
-    w_cores = jnp.where(core == 0, jnp.stack([w_z, w_z_other]), jnp.stack([w_z_other, w_z]))
-    w_full = w_cores.reshape(2, n_z, 2, wrows, n_mp * half).transpose(2, 1, 0, 3, 4)
-    w_full = w_full.reshape(4 * n_z * wrows, n_mp * half)[:feats]
+    w_theirs = swap_core(w_mine)
+    w_cores = jnp.where(core == 0, jnp.stack([w_mine, w_theirs], 1), jnp.stack([w_theirs, w_mine], 1))
+    w_full = unpack(w_cores).reshape(4 * n_z * wrows, n_mp * half)[:feats]
+
+    kv = lax.dot_general(w_full, x_pair, (((0,), (1,)), ((), ())), preferred_element_type=F32)
+    kv = kv.astype(BF16).reshape(n_mp, half, tokens)
+    both = jnp.concatenate([kv, jnp.broadcast_to(g_cols, (n_mp, half, tokens))], axis=1)
+    both = lax.all_to_all(both, "mp", 0, 0, tiled=True)
+    g_all = both[:, half:].reshape(n_mp * half, tokens)
 
     dw = lax.dot_general(x_pair, g_all, (((0,), (1,)), ((), ())), preferred_element_type=F32)
     dw = jnp.pad(dw, ((0, 4 * n_z * wrows - feats), (0, 0)))
-    dw = dw.reshape(2, n_z, 2, wrows, n_mp * half).transpose(2, 1, 0, 3, 4)
-    dw_mine = jnp.where(core == 0, dw[0], dw[1])
-    dw_theirs = jnp.where(core == 0, dw[1], dw[0]).astype(BF16)
+    dw = dw.reshape(2 * n_z, 2, wrows, n_mp * half)
+    dw_mine = pack(jnp.where(core == 0, dw[:, 0], dw[:, 1]))
+    dw_theirs = pack(jnp.where(core == 0, dw[:, 1], dw[:, 0]).astype(BF16))
     dw_sum = dw_mine + swap_core(dw_theirs).astype(F32)
-    dw_z = dw_sum.astype(BF16).reshape(n_z, 2 * wrows, n_mp * half)
-    dw_z = lax.all_to_all(dw_z, "z", 0, 0, tiled=True)
-    dw_rows = jnp.sum(dw_z.astype(F32), axis=0).reshape(2, wrows, n_mp * half)
-    dw_own = jnp.where(side == 0, dw_rows[0], dw_rows[1])
-    dw_send = jnp.where(side == 0, dw_rows[1], dw_rows[0])
-    dw_other = swap_pair(dw_send)
-    dw_own = dw_own.reshape(wrows, n_mp, 1, half)
-    dw_other = dw_other.reshape(wrows, n_mp, 1, half)
-    weight_grad = jnp.where(
-        side == 0,
-        jnp.concatenate([dw_own, dw_other], axis=2),
-        jnp.concatenate([dw_other, dw_own], axis=2),
-    ).reshape(wrows, cols)
+    dw_parts = lax.all_to_all(dw_sum.astype(BF16), ("pair", "z"), 0, 0, tiled=True)
+    dw_parts = dw_parts.reshape(2, n_z, 2 * wrows, n_mp * half // 2)
+    dw_rows = unpack(jnp.sum(dw_parts.astype(F32), axis=1)).reshape(2, wrows, n_mp, half)
+    weight_grad = dw_rows.transpose(1, 2, 0, 3).reshape(wrows, cols)
 
-    kv = lax.dot_general(w_full, x_pair, (((0,), (1,)), ((), ())), preferred_element_type=F32)
-    kv = lax.all_to_all(kv.astype(BF16).reshape(n_mp, half, tokens), "mp", 0, 0, tiled=True)
-    kv = jnp.sum(kv.astype(F32), axis=0).astype(BF16)
+    kv = jnp.sum(both[:, :half].astype(F32), axis=0).astype(BF16)
     kv_other = swap_pair(kv)
     kv_cols = jnp.where(side == 0, jnp.concatenate([kv, kv_other]), jnp.concatenate([kv_other, kv]))
     kv_home = home(kv_cols.reshape(own_cols, seqs, span).transpose(1, 0, 2))

time: 113 us -> 103 us (0.912)
  the two profiles are of different devices: /device:TPU:8 before, /device:TPU:1 now
where the time goes in v3:
time: 103 us; the launch traced here: 101 us
  starting transfers between devices  49.6 us (48%)
  waiting for transfers between devices  32.8 us (32%)
  other arithmetic  7.51 us (7%)
  local copies, waits for them, and re-layouts  7.42 us (7%)
  between operations  3.08 us (3%)
  matrix products  1.05 us (1%)
    all_to_all x1, starting transfers between devices, on_device(): lax.all_to_all(w_send.reshape(2 * n_z, 2 * wrows, n_mp * half // 2), ('pa...  16.9 us
    all_to_all x1, waiting for transfers between devices, on_device(): both = lax.all_to_all(both, 'mp', 0, 0, tiled=True)  16.8 us
    ppermute x4, starting transfers between devices, swap_pair(): return lax.ppermute(value, 'pair', SWAP)  10.8 us
    all_to_all x1, waiting for transfers between devices, on_device(): lax.all_to_all(dw_sum.astype(BF16), ('pair', 'z'), 0, 0, tiled=True)  10.7 us
    ppermute x2, starting transfers between devices, swap_core(): return lax.ppermute(value, 'core', SWAP)  9.26 us
    all_to_all x1, starting transfers between devices, on_device(): both = lax.all_to_all(both, 'mp', 0, 0, tiled=True)  8.49 us
    all_to_all x1, waiting for transfers between devices, on_device(): lax.all_to_all(w_send.reshape(2 * n_z, 2 * wrows, n_mp * half // 2), ('pa...  4.15 us
    all_to_all x1, starting transfers between devices, on_device(): lax.all_to_all(dw_sum.astype(BF16), ('pair', 'z'), 0, 0, tiled=True)  4.09 us
  transfers between devices with their start and end apart: 9, of which 4 were waited for; matrix products, arithmetic and copies ran while one was open for 9% of the time, Pallas kernels for 0%

profile of v3, /device:TPU:1, one launch (start us, length us, event | category | flops | bytes accessed | tf_op | source)
XLA Modules:
  0.0 101.4 jit_solution(2997597127436127700)
XLA Ops:
  0.7 0.9 reshape.91
  1.6 0.1 reshape_reshape.9
  1.8 0.7 broadcast_in_dim.21
  2.5 16.9 %all-to-all-start = ((bf16[24,22,256]{2,1,0:T(8,128)(2,1)}), bf16[24,22,256]{2,1,0:T(8,128)(2,1)S(1)}, u32[]{:S(2)}, u32[]{:S(2)}) async-start(bf16[24,22,256]{2,1,0:T(8,128)(2,1)} %bitcast.4), calls=%async_computation | async-start | bytes 589824 | tf_op jit(solution)/shard_map/all_to_all | solution.py:70
  19.4 0.7 broadcast_compare_fusion
  20.1 0.6 fusion.9
  21.3 0.8 reshape.96
  22.1 0.2 rev.7
  22.4 3.2 %collective-permute-start.2 = (bf16[2,32,128]{2,0,1:T(2,128)(2,1)S(1)}, bf16[2,32,128]{2,0,1:T(2,128)(2,1)S(1)}, u32[]{:S(2)}, u32[]{:S(2)}) collective-permute-start(bf16[2,32,128]{2,0,1:T(2,128)(2,1)S(1)} %get-tuple-element.16), channel_id=1, source_target_pairs={{0,384},{384,0},{1,385},{385,1},{2,386},{386,2},{3,387},{387,3},{4... | collective-permute-start | bytes 49160 | tf_op jit(solution)/shard_map/ppermute | solution.py:12
  25.6 2.1 %collective-permute-start.1 = (bf16[2,128,512]{2,1,0:T(8,128)(2,1)S(1)}, bf16[2,128,512]{2,1,0:T(8,128)(2,1)S(1)}, u32[]{:S(2)}, u32[]{:S(2)}) collective-permute-start(bf16[2,128,512]{2,1,0:T(8,128)(2,1)S(1)} %reverse_select_fusion), channel_id=1, source_target_pairs={{0,384},{384,0},{1,385},{385,1},{2,386},{386,2},{3,387},{387,3},{4... | collective-permute-start | bytes 786440 | tf_op jit(solution)/shard_map/ppermute | solution.py:12
  27.7 0.6 reduce_sum.30
  29.7 0.1 broadcast_select_fusion.15
  29.8 4.1 %all-to-all-done = bf16[24,22,256]{2,1,0:T(8,128)(2,1)S(1)} async-done(((bf16[24,22,256]{2,1,0:T(8,128)(2,1)}), bf16[24,22,256]{2,1,0:T(8,128)(2,1)S(1)}, u32[]{:S(2)}, u32[]{:S(2)}) %all-to-all-start) | async-done | bytes 270368 | tf_op jit(solution)/shard_map/all_to_all | solution.py:70
  34.0 5.6 %collective-permute-start = (bf16[24,22,256]{2,1,0:T(8,128)(2,1)S(1)}, bf16[24,22,256]{2,1,0:T(8,128)(2,1)S(1)}, u32[]{:S(2)}, u32[]{:S(2)}) collective-permute-start(bf16[24,22,256]{2,1,0:T(8,128)(2,1)S(1)} %all-to-all-done), channel_id=1, source_target_pairs={{0,16},{16,0},{1,17},{17,1},{2,18},{18,2},{3,19},{19,3},{4,20},{20... | collective-permute-start | bytes 811016 | tf_op jit(solution)/shard_map/ppermute | solution.py:16
  39.7 1.0 %collective-permute-done = bf16[24,22,256]{2,1,0:T(8,128)(2,1)S(1)} collective-permute-done((bf16[24,22,256]{2,1,0:T(8,128)(2,1)S(1)}, bf16[24,22,256]{2,1,0:T(8,128)(2,1)S(1)}, u32[]{:S(2)}, u32[]{:S(2)}) %collective-permute-start) | collective-permute-done | bytes 270368 | tf_op jit(solution)/shard_map/ppermute | solution.py:16
  40.8 0.1 fusion
  40.9 0.4 copy.59
  41.3 0.1 copy.74
  41.4 0.3 convolution_convert_fusion
  41.8 0.8 pad_maximum_fusion
  42.6 8.5 %all-to-all-start.1 = ((bf16[16,64,256]{2,1,0:T(8,128)(2,1)}), bf16[16,64,256]{2,1,0:T(8,128)(2,1)S(1)}, u32[]{:S(2)}, u32[]{:S(2)}) async-start(bf16[16,64,256]{2,1,0:T(8,128)(2,1)} %pad_maximum_fusion), calls=%async_computation.1 | async-start | bytes 1048576 | tf_op jit(solution)/shard_map/all_to_all | solution.py:91
  51.2 16.8 %all-to-all-done.1 = bf16[16,64,256]{2,1,0:T(8,128)(2,1)S(1)} async-done(((bf16[16,64,256]{2,1,0:T(8,128)(2,1)}), bf16[16,64,256]{2,1,0:T(8,128)(2,1)S(1)}, u32[]{:S(2)}, u32[]{:S(2)}) %all-to-all-start.1) | async-done | bytes 524320 | tf_op jit(solution)/shard_map/all_to_all | solution.py:91
  68.1 0.4 fusion.11
  68.4 0.1 pad.4
  68.5 0.2 reshape.100
  68.7 0.2 fusion.7
  68.9 0.6 select_convert_fusion
  69.5 0.6 copy_select_fusion
  70.1 1.9 %collective-permute-start.3 = (bf16[32,256]{1,0:T(8,128)(2,1)S(1)}, bf16[32,256]{1,0:T(8,128)(2,1)S(1)}, u32[]{:S(2)}, u32[]{:S(2)}) collective-permute-start(bf16[32,256]{1,0:T(8,128)(2,1)S(1)} %get-tuple-element.6), channel_id=1, source_target_pairs={{0,384},{384,0},{1,385},{385,1},{2,386},{386,2},{3,387},{387,3},{4... | collective-permute-start | bytes 49160 | tf_op jit(solution)/shard_map/ppermute | solution.py:12
  72.0 0.1 convert_element_type.40
  72.1 3.7 %collective-permute-start.5 = (bf16[24,22,256]{2,0,1:T(8,128)(2,1)S(1)}, bf16[24,22,256]{2,0,1:T(8,128)(2,1)S(1)}, u32[]{:S(2)}, u32[]{:S(2)}) collective-permute-start(bf16[24,22,256]{2,0,1:T(8,128)(2,1)S(1)} %bitcast.103), channel_id=1, source_target_pairs={{0,16},{16,0},{1,17},{17,1},{2,18},{18,2},{3,19},{19,3},{4,20},{20... | collective-permute-start | bytes 811016 | tf_op jit(solution)/shard_map/ppermute | solution.py:16
  75.8 0.3 fusion.10
  76.2 3.6 %collective-permute-start.4 = (bf16[256,512]{1,0:T(8,128)(2,1)S(1)}, bf16[256,512]{1,0:T(8,128)(2,1)S(1)}, u32[]{:S(2)}, u32[]{:S(2)}) collective-permute-start(bf16[256,512]{1,0:T(8,128)(2,1)S(1)} %get-tuple-element.19), channel_id=1, source_target_pairs={{0,384},{384,0},{1,385},{385,1},{2,386},{386,2},{3,387},{387,3},{4... | collective-permute-start | bytes 786440 | tf_op jit(solution)/shard_map/ppermute | solution.py:12
  79.8 0.3 select_n.276
  80.3 0.1 fusion.5
  80.3 0.1 fusion.1
  80.4 0.8 copy.68
  81.2 4.1 %all-to-all-start.2 = ((bf16[24,22,256]{2,1,0:T(8,128)(2,1)}), bf16[24,22,256]{2,1,0:T(8,128)(2,1)S(1)}, u32[]{:S(2)}, u32[]{:S(2)}) async-start(bf16[24,22,256]{2,1,0:T(8,128)(2,1)} %copy.68), calls=%async_computation.2 | async-start | bytes 589824 | tf_op jit(solution)/shard_map/all_to_all | solution.py:100
  85.3 1.4 %broadcast_select_fusion.6 = (bf16[1,64,128]{2,0,1:T(2,128)(2,1)S(1)}, bf16[1,64,128]{2,0,1:T(2,128)(2,1)S(1)}) fusion(pred[]{:T(512)} %bitcast, pred[]{:T(512)S(6)} %eq.13, bf16[2,64,128]{2,0,1:T(2,128)(2,1)S(1)} %fusion.5, pred[]{:T(512)S(6)} %eq.17, pred[]{:T(512)} %bitcast.20), kind=kLoop, calls=%fused_computation.28 | loop fusion | flops 32768 | bytes 65540 | tf_op jit(solution)/shard_map/jit(_where)/select_n | solution.py:55
  86.7 0.1 pad_maximum_fusion.3
  86.8 0.6 copy.85
  87.4 0.1 add_convert_fusion
  87.5 1.3 %select_bitcast_fusion.1 = (bf16[1,128,512]{2,1,0:T(8,128)(2,1)S(1)}, bf16[1,128,512]{2,1,0:T(8,128)(2,1)S(1)}) fusion(pred[]{:T(512)S(6)} %eq.13, pred[]{:T(512)} %bitcast, bf16[256,512]{1,0:T(8,128)(2,1)S(1)} %add_convert_fusion, pred[]{:T(512)S(6)} %eq.17, pred[]{:T(512)} %bitcast.20), kind=kLoop, calls=%fused_computation.18 | loop fusion | flops 262144 | bytes 524292 | tf_op jit(solution)/shard_map/stack | solution.py:55
  88.8 0.7 pad_maximum_fusion.2
  89.5 10.7 %all-to-all-done.2 = bf16[24,22,256]{2,1,0:T(8,128)(2,1)S(1)} async-done(((bf16[24,22,256]{2,1,0:T(8,128)(2,1)}), bf16[24,22,256]{2,1,0:T(8,128)(2,1)S(1)}, u32[]{:S(2)}, u32[]{:S(2)}) %all-to-all-start.2) | async-done | bytes 270368 | tf_op jit(solution)/shard_map/all_to_all | solution.py:100
  100.3 0.1 reshape_reshape.11
  100.5 0.1 copy.71
  100.6 0.9 reshape.104
  (30 shorter events, 0.7 us)
Async XLA Ops:
  0.6 27.1 %copy-start.1 = (s32[2]{0:T(128)S(1)}, s32[2]{0:T(128)}, u32[]{:S(2)}) copy-start(s32[2]{0:T(128)} %param.7) | copy-start | bytes 28
  0.6 24.9 %copy-start = (bf16[256,512]{1,0:T(8,128)(2,1)S(1)}, bf16[256,512]{1,0:T(8,128)(2,1)}, u32[]{:S(2)}) copy-start(bf16[256,512]{1,0:T(8,128)(2,1)} %param.4) | copy-start | bytes 786436
  2.5 31.5 %all-to-all-start = ((bf16[24,22,256]{2,1,0:T(8,128)(2,1)}), bf16[24,22,256]{2,1,0:T(8,128)(2,1)S(1)}, u32[]{:S(2)}, u32[]{:S(2)}) async-start(bf16[24,22,256]{2,1,0:T(8,128)(2,1)} %bitcast.4), calls=%async_computation | async-start | bytes 589824 | tf_op jit(solution)/shard_map/all_to_all | solution.py:70
  22.4 7.3 %collective-permute-start.2 = (bf16[2,32,128]{2,0,1:T(2,128)(2,1)S(1)}, bf16[2,32,128]{2,0,1:T(2,128)(2,1)S(1)}, u32[]{:S(2)}, u32[]{:S(2)}) collective-permute-start(bf16[2,32,128]{2,0,1:T(2,128)(2,1)S(1)} %get-tuple-element.16), channel_id=1, source_target_pairs={{0,384},{384,0},{1,385},{385,1},{2,386},{386,2},{3,387},{387,3},{4... | collective-permute-start | bytes 49160 | tf_op jit(solution)/shard_map/ppermute | solution.py:12
  25.6 13.9 %collective-permute-start.1 = (bf16[2,128,512]{2,1,0:T(8,128)(2,1)S(1)}, bf16[2,128,512]{2,1,0:T(8,128)(2,1)S(1)}, u32[]{:S(2)}, u32[]{:S(2)}) collective-permute-start(bf16[2,128,512]{2,1,0:T(8,128)(2,1)S(1)} %reverse_select_fusion), channel_id=1, source_target_pairs={{0,384},{384,0},{1,385},{385,1},{2,386},{386,2},{3,387},{387,3},{4... | collective-permute-start | bytes 786440 | tf_op jit(solution)/shard_map/ppermute | solution.py:12
  34.0 6.8 %collective-permute-start = (bf16[24,22,256]{2,1,0:T(8,128)(2,1)S(1)}, bf16[24,22,256]{2,1,0:T(8,128)(2,1)S(1)}, u32[]{:S(2)}, u32[]{:S(2)}) collective-permute-start(bf16[24,22,256]{2,1,0:T(8,128)(2,1)S(1)} %all-to-all-done), channel_id=1, source_target_pairs={{0,16},{16,0},{1,17},{17,1},{2,18},{18,2},{3,19},{19,3},{4,20},{20... | collective-permute-start | bytes 811016 | tf_op jit(solution)/shard_map/ppermute | solution.py:16
  42.6 25.4 %all-to-all-start.1 = ((bf16[16,64,256]{2,1,0:T(8,128)(2,1)}), bf16[16,64,256]{2,1,0:T(8,128)(2,1)S(1)}, u32[]{:S(2)}, u32[]{:S(2)}) async-start(bf16[16,64,256]{2,1,0:T(8,128)(2,1)} %pad_maximum_fusion), calls=%async_computation.1 | async-start | bytes 1048576 | tf_op jit(solution)/shard_map/all_to_all | solution.py:91
  70.1 10.2 %collective-permute-start.3 = (bf16[32,256]{1,0:T(8,128)(2,1)S(1)}, bf16[32,256]{1,0:T(8,128)(2,1)S(1)}, u32[]{:S(2)}, u32[]{:S(2)}) collective-permute-start(bf16[32,256]{1,0:T(8,128)(2,1)S(1)} %get-tuple-element.6), channel_id=1, source_target_pairs={{0,384},{384,0},{1,385},{385,1},{2,386},{386,2},{3,387},{387,3},{4... | collective-permute-start | bytes 49160 | tf_op jit(solution)/shard_map/ppermute | solution.py:12
  72.1 8.2 %collective-permute-start.5 = (bf16[24,22,256]{2,0,1:T(8,128)(2,1)S(1)}, bf16[24,22,256]{2,0,1:T(8,128)(2,1)S(1)}, u32[]{:S(2)}, u32[]{:S(2)}) collective-permute-start(bf16[24,22,256]{2,0,1:T(8,128)(2,1)S(1)} %bitcast.103), channel_id=1, source_target_pairs={{0,16},{16,0},{1,17},{17,1},{2,18},{18,2},{3,19},{19,3},{4,20},{20... | collective-permute-start | bytes 811016 | tf_op jit(solution)/shard_map/ppermute | solution.py:16
  76.2 11.2 %collective-permute-start.4 = (bf16[256,512]{1,0:T(8,128)(2,1)S(1)}, bf16[256,512]{1,0:T(8,128)(2,1)S(1)}, u32[]{:S(2)}, u32[]{:S(2)}) collective-permute-start(bf16[256,512]{1,0:T(8,128)(2,1)S(1)} %get-tuple-element.19), channel_id=1, source_target_pairs={{0,384},{384,0},{1,385},{385,1},{2,386},{386,2},{3,387},{387,3},{4... | collective-permute-start | bytes 786440 | tf_op jit(solution)/shard_map/ppermute | solution.py:12
  81.2 19.0 %all-to-all-start.2 = ((bf16[24,22,256]{2,1,0:T(8,128)(2,1)}), bf16[24,22,256]{2,1,0:T(8,128)(2,1)S(1)}, u32[]{:S(2)}, u32[]{:S(2)}) async-start(bf16[24,22,256]{2,1,0:T(8,128)(2,1)} %copy.68), calls=%async_computation.2 | async-start | bytes 589824 | tf_op jit(solution)/shard_map/all_to_all | solution.py:100

commit v4 on v3

--- a/solution.py
+++ b/solution.py
@@ -97,7 +97,8 @@
     dw_mine = pack(jnp.where(core == 0, dw[:, 0], dw[:, 1]))
     dw_theirs = pack(jnp.where(core == 0, dw[:, 1], dw[:, 0]).astype(BF16))
     dw_sum = dw_mine + swap_core(dw_theirs).astype(F32)
-    dw_parts = lax.all_to_all(dw_sum.astype(BF16), ("pair", "z"), 0, 0, tiled=True)
+    dw_send, both, g_all, w_full = lax.optimization_barrier((dw_sum.astype(BF16), both, g_all, w_full))
+    dw_parts = lax.all_to_all(dw_send, ("pair", "z"), 0, 0, tiled=True)
     dw_parts = dw_parts.reshape(2, n_z, 2 * wrows, n_mp * half // 2)
     dw_rows = unpack(jnp.sum(dw_parts.astype(F32), axis=1)).reshape(2, wrows, n_mp, half)
     weight_grad = dw_rows.transpose(1, 2, 0, 3).reshape(wrows, cols)

time: 103 us -> 102 us (level)
  blocking collectives: 0 us -> 25.1 us
  waiting for transfers between devices: 32.8 us -> 12.2 us
  starting transfers between devices: 49.6 us -> 41.9 us
  local copies, waits for them, and re-layouts: 7.42 us -> 9.08 us
    all_to_all x2 -> x1, waiting for transfers between devices: 27.6 us -> 1.37 us  [on_device(): dw_parts = lax.all_to_all(dw_send, ('pair', 'z'), 0, 0, tiled=True)]
    all_to_all x0 -> x1, blocking collectives: none -> 25.1 us  [on_device(): both = lax.all_to_all(both, 'mp', 0, 0, tiled=True)]
    all_to_all x2 -> x1, starting transfers between devices: 12.6 us -> 5.28 us  [on_device(): dw_parts = lax.all_to_all(dw_send, ('pair', 'z'), 0, 0, tiled=True)]
    ppermute x4, waiting for transfers between devices: 0.01 us -> 5.69 us  [swap_pair(): return lax.ppermute(value, 'pair', SWAP)]
  transfers between devices with their start and end apart: 9 -> 8, of which waited for: 4 -> 4; matrix products, arithmetic and copies ran while one was open for 9% -> 10% of each run, Pallas kernels for 0% -> 0%
where the time goes in v4:
time: 102 us; the launch traced here: 100 us
  starting transfers between devices  41.9 us (41%)
  blocking collectives  25.1 us (25%)
  waiting for transfers between devices  12.2 us (12%)
  local copies, waits for them, and re-layouts  9.08 us (9%)
  other arithmetic  7.72 us (8%)
  between operations  3.14 us (3%)
  matrix products  1.05 us (1%)
    all_to_all x1, blocking collectives, on_device(): both = lax.all_to_all(both, 'mp', 0, 0, tiled=True)  25.1 us
    all_to_all x1, starting transfers between devices, on_device(): lax.all_to_all(w_send.reshape(2 * n_z, 2 * wrows, n_mp * half // 2), ('pa...  16.9 us
    ppermute x4, starting transfers between devices, swap_pair(): return lax.ppermute(value, 'pair', SWAP)  10.4 us
    ppermute x2, starting transfers between devices, swap_core(): return lax.ppermute(value, 'core', SWAP)  9.28 us
    ppermute x4, waiting for transfers between devices, swap_pair(): return lax.ppermute(value, 'pair', SWAP)  5.69 us
    all_to_all x1, starting transfers between devices, on_device(): dw_parts = lax.all_to_all(dw_send, ('pair', 'z'), 0, 0, tiled=True)  5.28 us
    all_to_all x1, waiting for transfers between devices, on_device(): lax.all_to_all(w_send.reshape(2 * n_z, 2 * wrows, n_mp * half // 2), ('pa...  4.15 us
    another operation x3, other arithmetic, home(): jnp.stack([jnp.where(alive[0], rows0, zero), jnp.where(alive[1], rows1, z...  2.13 us
  transfers between devices with their start and end apart: 8, of which 4 were waited for; matrix products, arithmetic and copies ran while one was open for 10% of the time, Pallas kernels for 0%

profile of v4, /device:TPU:1, one launch (start us, length us, event | category | flops | bytes accessed | tf_op | source)
XLA Modules:
  0.0 100.3 jit_solution(17767561112482816280)
XLA Ops:
  0.7 0.9 reshape.93
  1.6 0.1 reshape_reshape.9
  1.8 0.7 broadcast_in_dim.21
  2.5 16.9 %all-to-all-start = ((bf16[24,22,256]{2,1,0:T(8,128)(2,1)}), bf16[24,22,256]{2,1,0:T(8,128)(2,1)S(1)}, u32[]{:S(2)}, u32[]{:S(2)}) async-start(bf16[24,22,256]{2,1,0:T(8,128)(2,1)} %bitcast.6), calls=%async_computation | async-start | bytes 589824 | tf_op jit(solution)/shard_map/all_to_all | solution.py:70
  19.5 0.7 broadcast_compare_fusion
  20.1 0.6 fusion.6
  21.4 0.8 reshape.96
  22.1 0.2 rev.7
  22.4 3.2 %collective-permute-start.2 = (bf16[2,32,128]{2,0,1:T(2,128)(2,1)S(1)}, bf16[2,32,128]{2,0,1:T(2,128)(2,1)S(1)}, u32[]{:S(2)}, u32[]{:S(2)}) collective-permute-start(bf16[2,32,128]{2,0,1:T(2,128)(2,1)S(1)} %get-tuple-element.22), channel_id=1, source_target_pairs={{0,384},{384,0},{1,385},{385,1},{2,386},{386,2},{3,387},{387,3},{4... | collective-permute-start | bytes 49160 | tf_op jit(solution)/shard_map/ppermute | solution.py:12
  25.7 2.1 %collective-permute-start = (bf16[2,128,512]{2,1,0:T(8,128)(2,1)S(1)}, bf16[2,128,512]{2,1,0:T(8,128)(2,1)S(1)}, u32[]{:S(2)}, u32[]{:S(2)}) collective-permute-start(bf16[2,128,512]{2,1,0:T(8,128)(2,1)S(1)} %reverse_select_fusion), channel_id=1, source_target_pairs={{0,384},{384,0},{1,385},{385,1},{2,386},{386,2},{3,387},{387,3},{4... | collective-permute-start | bytes 786440 | tf_op jit(solution)/shard_map/ppermute | solution.py:12
  27.8 0.6 reduce_sum.30
  29.7 0.1 broadcast_select_fusion.15
  29.9 4.1 %all-to-all-done = bf16[24,22,256]{2,1,0:T(8,128)(2,1)S(1)} async-done(((bf16[24,22,256]{2,1,0:T(8,128)(2,1)}), bf16[24,22,256]{2,1,0:T(8,128)(2,1)S(1)}, u32[]{:S(2)}, u32[]{:S(2)}) %all-to-all-start) | async-done | bytes 270368 | tf_op jit(solution)/shard_map/all_to_all | solution.py:70
  34.0 5.6 %collective-permute-start.1 = (bf16[24,22,256]{2,1,0:T(8,128)(2,1)S(1)}, bf16[24,22,256]{2,1,0:T(8,128)(2,1)S(1)}, u32[]{:S(2)}, u32[]{:S(2)}) collective-permute-start(bf16[24,22,256]{2,1,0:T(8,128)(2,1)S(1)} %all-to-all-done), channel_id=1, source_target_pairs={{0,16},{16,0},{1,17},{17,1},{2,18},{18,2},{3,19},{19,3},{4,20},{20... | collective-permute-start | bytes 811016 | tf_op jit(solution)/shard_map/ppermute | solution.py:16
  39.7 1.0 %collective-permute-done.1 = bf16[24,22,256]{2,1,0:T(8,128)(2,1)S(1)} collective-permute-done((bf16[24,22,256]{2,1,0:T(8,128)(2,1)S(1)}, bf16[24,22,256]{2,1,0:T(8,128)(2,1)S(1)}, u32[]{:S(2)}, u32[]{:S(2)}) %collective-permute-start.1) | collective-permute-done | bytes 270368 | tf_op jit(solution)/shard_map/ppermute | solution.py:16
  40.8 0.1 fusion
  40.9 0.4 copy.59
  41.3 0.1 copy.74
  41.5 0.3 convolution_convert_fusion
  41.9 25.1 %all_to_all.15 = bf16[16,64,256]{2,1,0:T(8,128)(2,1)S(1)} all-to-all(bf16[16,64,256]{2,1,0:T(8,128)(2,1)S(1)} %pad_maximum_fusion), channel_id=1, replica_groups=mesh['pair'=2,'z'=12,'core'=2,'mp'=16] {'mp'}, dimensions={0} | all-to-all | bytes 1048576 | tf_op jit(solution)/shard_map/all_to_all | solution.py:91
  67.1 0.8 copy-done.3
  67.8 0.3 fusion.8
  68.2 0.1 pad.4
  68.3 0.2 reshape.98
  68.4 0.2 fusion.5
  68.7 0.6 select_convert_fusion
  69.2 0.1 convert_element_type.37
  69.4 3.7 %collective-permute-start.3 = (bf16[24,22,256]{2,0,1:T(8,128)(2,1)S(1)}, bf16[24,22,256]{2,0,1:T(8,128)(2,1)}, u32[]{:S(2)}, u32[]{:S(2)}) collective-permute-start(bf16[24,22,256]{2,0,1:T(8,128)(2,1)S(1)} %bitcast.104), channel_id=1, source_target_pairs={{0,16},{16,0},{1,17},{17,1},{2,18},{18,2},{3,19},{19,3},{4,20},{20... | collective-permute-start | bytes 811016 | tf_op jit(solution)/shard_map/ppermute | solution.py:16
  73.1 0.8 slice.122
  74.0 0.6 copy_select_fusion
  74.6 0.3 select_n.261
  75.0 1.1 %fusion.1 = bf16[24,22,256]{2,0,1:T(8,128)(2,1)S(1)} fusion(f32[24,2,11,256]{3,0,2,1:T(8,128)S(1)} %copy.66, bf16[24,22,256]{2,0,1:T(8,128)(2,1)} %collective-permute-done.3), kind=kLoop, calls=%fused_computation.5 | loop fusion | flops 405504 | bytes 1081344 | tf_op jit(solution)/shard_map/convert_element_type | solution.py:100
  76.1 1.9 %collective-permute-start.4 = (bf16[32,256]{1,0:T(8,128)(2,1)S(1)}, bf16[32,256]{1,0:T(8,128)(2,1)S(1)}, u32[]{:S(2)}, u32[]{:S(2)}) collective-permute-start(bf16[32,256]{1,0:T(8,128)(2,1)S(1)} %slice_reduce_fusion), channel_id=1, source_target_pairs={{0,384},{384,0},{1,385},{385,1},{2,386},{386,2},{3,387},{387,3},{4... | collective-permute-start | bytes 49160 | tf_op jit(solution)/shard_map/ppermute | solution.py:12
  78.1 0.8 copy.68
  78.8 5.3 %all-to-all-start.2 = ((bf16[24,22,256]{2,1,0:T(8,128)(2,1)}), bf16[24,22,256]{2,1,0:T(8,128)(2,1)S(1)}, u32[]{:S(2)}, u32[]{:S(2)}) async-start(bf16[24,22,256]{2,1,0:T(8,128)(2,1)} %copy.68), calls=%async_computation.2 | async-start | bytes 589824 | tf_op jit(solution)/shard_map/all_to_all | solution.py:101
  84.1 0.4 fusion.7
  84.5 3.2 %collective-permute-start.5 = (bf16[256,512]{1,0:T(8,128)(2,1)S(1)}, bf16[256,512]{1,0:T(8,128)(2,1)S(1)}, u32[]{:S(2)}, u32[]{:S(2)}) collective-permute-start(bf16[256,512]{1,0:T(8,128)(2,1)S(1)} %get-tuple-element.25), channel_id=1, source_target_pairs={{0,384},{384,0},{1,385},{385,1},{2,386},{386,2},{3,387},{387,3},{4... | collective-permute-start | bytes 786440 | tf_op jit(solution)/shard_map/ppermute | solution.py:12
  87.8 1.4 %broadcast_select_fusion.6 = (bf16[1,64,128]{2,0,1:T(2,128)(2,1)S(1)}, bf16[1,64,128]{2,0,1:T(2,128)(2,1)S(1)}) fusion(pred[]{:T(512)} %bitcast, pred[]{:T(512)S(6)} %eq.13, bf16[2,64,128]{2,0,1:T(2,128)(2,1)S(1)} %fusion.2, pred[]{:T(512)S(6)} %eq.17, pred[]{:T(512)} %bitcast.25), kind=kLoop, calls=%fused_computation.25 | loop fusion | flops 32768 | bytes 65540 | tf_op jit(solution)/shard_map/jit(_where)/select_n | solution.py:55
  89.2 0.1 pad_maximum_fusion.3
  89.3 0.6 copy.85
  89.9 5.7 %collective-permute-done.5 = bf16[256,512]{1,0:T(8,128)(2,1)S(1)} collective-permute-done((bf16[256,512]{1,0:T(8,128)(2,1)S(1)}, bf16[256,512]{1,0:T(8,128)(2,1)S(1)}, u32[]{:S(2)}, u32[]{:S(2)}) %collective-permute-start.5) | collective-permute-done | bytes 262176 | tf_op jit(solution)/shard_map/ppermute | solution.py:12
  95.6 0.1 add_convert_fusion
  95.6 1.3 %select_bitcast_fusion.1 = (bf16[1,128,512]{2,1,0:T(8,128)(2,1)S(1)}, bf16[1,128,512]{2,1,0:T(8,128)(2,1)S(1)}) fusion(pred[]{:T(512)S(6)} %eq.13, pred[]{:T(512)} %bitcast, bf16[256,512]{1,0:T(8,128)(2,1)S(1)} %add_convert_fusion, pred[]{:T(512)S(6)} %eq.17, pred[]{:T(512)} %bitcast.25), kind=kLoop, calls=%fused_computation.15 | loop fusion | flops 262144 | bytes 524292 | tf_op jit(solution)/shard_map/stack | solution.py:55
  97.0 0.7 pad_maximum_fusion.2
  97.7 1.4 %all-to-all-done.2 = bf16[24,22,256]{2,1,0:T(8,128)(2,1)S(1)} async-done(((bf16[24,22,256]{2,1,0:T(8,128)(2,1)}), bf16[24,22,256]{2,1,0:T(8,128)(2,1)S(1)}, u32[]{:S(2)}, u32[]{:S(2)}) %all-to-all-start.2) | async-done | bytes 270368 | tf_op jit(solution)/shard_map/all_to_all | solution.py:101
  99.2 0.1 reshape_reshape.11
  99.3 0.1 copy.71
  99.4 0.9 reshape.104
  (41 shorter events, 0.8 us)
Async XLA Ops:
  0.6 27.1 %copy-start.6 = (s32[2]{0:T(128)S(1)}, s32[2]{0:T(128)}, u32[]{:S(2)}) copy-start(s32[2]{0:T(128)} %param.7) | copy-start | bytes 28
  0.6 24.9 %copy-start.5 = (bf16[256,512]{1,0:T(8,128)(2,1)S(1)}, bf16[256,512]{1,0:T(8,128)(2,1)}, u32[]{:S(2)}) copy-start(bf16[256,512]{1,0:T(8,128)(2,1)} %param.4) | copy-start | bytes 786436
  2.5 31.5 %all-to-all-start = ((bf16[24,22,256]{2,1,0:T(8,128)(2,1)}), bf16[24,22,256]{2,1,0:T(8,128)(2,1)S(1)}, u32[]{:S(2)}, u32[]{:S(2)}) async-start(bf16[24,22,256]{2,1,0:T(8,128)(2,1)} %bitcast.6), calls=%async_computation | async-start | bytes 589824 | tf_op jit(solution)/shard_map/all_to_all | solution.py:70
  22.4 7.3 %collective-permute-start.2 = (bf16[2,32,128]{2,0,1:T(2,128)(2,1)S(1)}, bf16[2,32,128]{2,0,1:T(2,128)(2,1)S(1)}, u32[]{:S(2)}, u32[]{:S(2)}) collective-permute-start(bf16[2,32,128]{2,0,1:T(2,128)(2,1)S(1)} %get-tuple-element.22), channel_id=1, source_target_pairs={{0,384},{384,0},{1,385},{385,1},{2,386},{386,2},{3,387},{387,3},{4... | collective-permute-start | bytes 49160 | tf_op jit(solution)/shard_map/ppermute | solution.py:12
  25.7 13.9 %collective-permute-start = (bf16[2,128,512]{2,1,0:T(8,128)(2,1)S(1)}, bf16[2,128,512]{2,1,0:T(8,128)(2,1)S(1)}, u32[]{:S(2)}, u32[]{:S(2)}) collective-permute-start(bf16[2,128,512]{2,1,0:T(8,128)(2,1)S(1)} %reverse_select_fusion), channel_id=1, source_target_pairs={{0,384},{384,0},{1,385},{385,1},{2,386},{386,2},{3,387},{387,3},{4... | collective-permute-start | bytes 786440 | tf_op jit(solution)/shard_map/ppermute | solution.py:12
  34.0 6.8 %collective-permute-start.1 = (bf16[24,22,256]{2,1,0:T(8,128)(2,1)S(1)}, bf16[24,22,256]{2,1,0:T(8,128)(2,1)S(1)}, u32[]{:S(2)}, u32[]{:S(2)}) collective-permute-start(bf16[24,22,256]{2,1,0:T(8,128)(2,1)S(1)} %all-to-all-done), channel_id=1, source_target_pairs={{0,16},{16,0},{1,17},{17,1},{2,18},{18,2},{3,19},{19,3},{4,20},{20... | collective-permute-start | bytes 811016 | tf_op jit(solution)/shard_map/ppermute | solution.py:16
  41.4 25.6 %copy-start = (bf16[66,8,2,256]{3,1,2,0:T(8,128)(2,1)}, bf16[66,8,2,256]{3,1,2,0:T(8,128)(2,1)S(1)}, u32[]{:S(2)}) copy-start(bf16[66,8,2,256]{3,1,2,0:T(8,128)(2,1)S(1)} %copy.74) | copy-start | bytes 1622020
  67.0 0.8 copy-start.3
  68.7 4.5 %copy-start.1 = (bf16[66,8,2,256]{3,1,2,0:T(8,128)(2,1)S(1)}, bf16[66,8,2,256]{3,1,2,0:T(8,128)(2,1)}, u32[]{:S(2)}) copy-start(bf16[66,8,2,256]{3,1,2,0:T(8,128)(2,1)} %copy-done) | copy-start | bytes 1622020
  69.4 5.6 %collective-permute-start.3 = (bf16[24,22,256]{2,0,1:T(8,128)(2,1)S(1)}, bf16[24,22,256]{2,0,1:T(8,128)(2,1)}, u32[]{:S(2)}, u32[]{:S(2)}) collective-permute-start(bf16[24,22,256]{2,0,1:T(8,128)(2,1)S(1)} %bitcast.104), channel_id=1, source_target_pairs={{0,16},{16,0},{1,17},{17,1},{2,18},{18,2},{3,19},{19,3},{4,20},{20... | collective-permute-start | bytes 811016 | tf_op jit(solution)/shard_map/ppermute | solution.py:16
  74.6 1.5 %copy-start.4 = (bf16[16,64,256]{2,1,0:T(8,128)(2,1)S(1)}, bf16[16,64,256]{2,1,0:T(8,128)(2,1)}, u32[]{:S(2)}) copy-start(bf16[16,64,256]{2,1,0:T(8,128)(2,1)} %copy-done.3) | copy-start | bytes 1572868
  74.9 9.2 %copy-start.2 = (bf16[512,512]{1,0:T(8,128)(2,1)S(1)}, bf16[512,512]{1,0:T(8,128)(2,1)}, u32[]{:S(2)}) copy-start(bf16[512,512]{1,0:T(8,128)(2,1)} %slice.122) | copy-start | bytes 1572868
  76.1 11.6 %collective-permute-start.4 = (bf16[32,256]{1,0:T(8,128)(2,1)S(1)}, bf16[32,256]{1,0:T(8,128)(2,1)S(1)}, u32[]{:S(2)}, u32[]{:S(2)}) collective-permute-start(bf16[32,256]{1,0:T(8,128)(2,1)S(1)} %slice_reduce_fusion), channel_id=1, source_target_pairs={{0,384},{384,0},{1,385},{385,1},{2,386},{386,2},{3,387},{387,3},{4... | collective-permute-start | bytes 49160 | tf_op jit(solution)/shard_map/ppermute | solution.py:12
  78.8 20.2 %all-to-all-start.2 = ((bf16[24,22,256]{2,1,0:T(8,128)(2,1)}), bf16[24,22,256]{2,1,0:T(8,128)(2,1)S(1)}, u32[]{:S(2)}, u32[]{:S(2)}) async-start(bf16[24,22,256]{2,1,0:T(8,128)(2,1)} %copy.68), calls=%async_computation.2 | async-start | bytes 589824 | tf_op jit(solution)/shard_map/all_to_all | solution.py:101
  84.5 11.1 %collective-permute-start.5 = (bf16[256,512]{1,0:T(8,128)(2,1)S(1)}, bf16[256,512]{1,0:T(8,128)(2,1)S(1)}, u32[]{:S(2)}, u32[]{:S(2)}) collective-permute-start(bf16[256,512]{1,0:T(8,128)(2,1)S(1)} %get-tuple-element.25), channel_id=1, source_target_pairs={{0,384},{384,0},{1,385},{385,1},{2,386},{386,2},{3,387},{387,3},{4... | collective-permute-start | bytes 786440 | tf_op jit(solution)/shard_map/ppermute | solution.py:12

commit v5 on v4

--- a/solution.py
+++ b/solution.py
@@ -14,6 +14,18 @@
 
 def swap_core(value):
     return lax.ppermute(value, "core", SWAP)
+
+
+def doubling_rounds(value, n, first, last):
+    index = lax.axis_index("mp")
+    for axis in range(first, last):
+        step = n >> (axis + 1)
+        other = lax.ppermute(value, "mp", [(i, i ^ step) for i in range(n)])
+        upper = (index & step) != 0
+        value = jnp.concatenate(
+            [jnp.where(upper, other, value), jnp.where(upper, value, other)], axis=axis
+        )
+    return value
 
 
 def on_device(x, w, adjoint, mask):
@@ -78,7 +90,10 @@
     g_other = swap_pair(g_theirs)
     x_other = swap_pair(xs)
     g_pair = compact(g_mine, g_other)
-    g_cols = g_pair.transpose(1, 0, 2).reshape(1, half, tokens)
+    g_cols = g_pair.transpose(1, 0, 2).reshape(half, tokens)
+    rounds = n_mp.bit_length() - 1
+    g_cols = g_cols.reshape((1,) * rounds + g_cols.shape)
+    g_near = doubling_rounds(g_cols, n_mp, 0, rounds // 2)
     x_pair = compact(xs, x_other).reshape(tokens, feats)
 
     w_theirs = swap_core(w_mine)
@@ -86,10 +101,9 @@
     w_full = unpack(w_cores).reshape(4 * n_z * wrows, n_mp * half)[:feats]
 
     kv = lax.dot_general(w_full, x_pair, (((0,), (1,)), ((), ())), preferred_element_type=F32)
-    kv = kv.astype(BF16).reshape(n_mp, half, tokens)
-    both = jnp.concatenate([kv, jnp.broadcast_to(g_cols, (n_mp, half, tokens))], axis=1)
-    both = lax.all_to_all(both, "mp", 0, 0, tiled=True)
-    g_all = both[:, half:].reshape(n_mp * half, tokens)
+    kv, g_near = lax.optimization_barrier((kv.astype(BF16), g_near))
+    kv_parts = lax.all_to_all(kv.reshape(n_mp, half, tokens), "mp", 0, 0, tiled=True)
+    g_all = doubling_rounds(g_near, n_mp, rounds // 2, rounds).reshape(n_mp * half, tokens)
 
     dw = lax.dot_general(x_pair, g_all, (((0,), (1,)), ((), ())), preferred_element_type=F32)
     dw = jnp.pad(dw, ((0, 4 * n_z * wrows - feats), (0, 0)))
@@ -97,13 +111,13 @@
     dw_mine = pack(jnp.where(core == 0, dw[:, 0], dw[:, 1]))
     dw_theirs = pack(jnp.where(core == 0, dw[:, 1], dw[:, 0]).astype(BF16))
     dw_sum = dw_mine + swap_core(dw_theirs).astype(F32)
-    dw_send, both, g_all, w_full = lax.optimization_barrier((dw_sum.astype(BF16), both, g_all, w_full))
+    dw_send, kv_parts = lax.optimization_barrier((dw_sum.astype(BF16), kv_parts))
     dw_parts = lax.all_to_all(dw_send, ("pair", "z"), 0, 0, tiled=True)
     dw_parts = dw_parts.reshape(2, n_z, 2 * wrows, n_mp * half // 2)
     dw_rows = unpack(jnp.sum(dw_parts.astype(F32), axis=1)).reshape(2, wrows, n_mp, half)
     weight_grad = dw_rows.transpose(1, 2, 0, 3).reshape(wrows, cols)
 
-    kv = jnp.sum(both[:, :half].astype(F32), axis=0).astype(BF16)
+    kv = jnp.sum(kv_parts.astype(F32), axis=0).astype(BF16)
     kv_other = swap_pair(kv)
     kv_cols = jnp.where(side == 0, jnp.concatenate([kv, kv_other]), jnp.concatenate([kv_other, kv]))
     kv_home = home(kv_cols.reshape(own_cols, seqs, span).transpose(1, 0, 2))

time: 102 us -> 110 us (1.078)
  the two profiles are of different devices: /device:TPU:1 before, /device:TPU:2 now
where the time goes in v5:
time: 110 us; the launch traced here: 109 us
  starting transfers between devices  61 us (55%)
  waiting for transfers between devices  26.4 us (24%)
  other arithmetic  8.46 us (8%)
  local copies, waits for them, and re-layouts  7.41 us (7%)
  between operations  3.16 us (3%)
  matrix products  2.64 us (2%)
    ppermute x4, starting transfers between devices, doubling_rounds(): other = lax.ppermute(value, 'mp', [(i, i ^ step) for i in range(n)])  16.4 us
    all_to_all x1, starting transfers between devices, on_device(): lax.all_to_all(w_send.reshape(2 * n_z, 2 * wrows, n_mp * half // 2), ('pa...  15.7 us
    ppermute x4, starting transfers between devices, swap_pair(): return lax.ppermute(value, 'pair', SWAP)  13.8 us
    all_to_all x1, waiting for transfers between devices, on_device(): lax.all_to_all(w_send.reshape(2 * n_z, 2 * wrows, n_mp * half // 2), ('pa...  9.67 us
    all_to_all x1, waiting for transfers between devices, on_device(): dw_parts = lax.all_to_all(dw_send, ('pair', 'z'), 0, 0, tiled=True)  7.05 us
    all_to_all x1, starting transfers between devices, on_device(): lax.all_to_all(kv.reshape(n_mp, half, tokens), 'mp', 0, 0, tiled=True)  5.75 us
    all_to_all x1, starting transfers between devices, on_device(): dw_parts = lax.all_to_all(dw_send, ('pair', 'z'), 0, 0, tiled=True)  5.48 us
    ppermute x4, waiting for transfers between devices, swap_pair(): return lax.ppermute(value, 'pair', SWAP)  4.5 us
  transfers between devices with their start and end apart: 13, of which 7 were waited for; matrix products, arithmetic and copies ran while one was open for 11% of the time, Pallas kernels for 0%

profile of v5, /device:TPU:2, one launch (start us, length us, event | category | flops | bytes accessed | tf_op | source)
XLA Modules:
  0.0 109.1 jit_solution(13457325725750312535)
XLA Ops:
  0.6 0.7 broadcast_compare_fusion
  1.3 0.6 fusion.8
  2.6 0.8 reshape.93
  3.4 0.2 rev.7
  3.6 3.5 %collective-permute-start.2 = (bf16[2,32,128]{2,0,1:T(2,128)(2,1)S(1)}, bf16[2,32,128]{2,0,1:T(2,128)(2,1)S(1)}, u32[]{:S(2)}, u32[]{:S(2)}) collective-permute-start(bf16[2,32,128]{2,0,1:T(2,128)(2,1)S(1)} %get-tuple-element.30), channel_id=1, source_target_pairs={{0,384},{384,0},{1,385},{385,1},{2,386},{386,2},{3,387},{387,3},{4... | collective-permute-start | bytes 49160 | tf_op jit(solution)/shard_map/ppermute | solution.py:12
  7.1 1.3 %reduce_sum.30 = s32[]{:T(128)} reduce(s32[2]{0:T(128)} %param.7, s32[]{:T(128)} %constant.11.clone.1), dimensions={0}, to_apply=%region_0.0 | reduce | flops 1 | bytes 16 | tf_op jit(solution)/shard_map/reduce_sum | solution.py:44
  9.9 7.3 %collective-permute-start.3 = (bf16[1,1,1,1,32,256]{5,4,3,2,1,0:T(8,128)(2,1)S(1)}, bf16[1,1,1,1,32,256]{5,4,3,2,1,0:T(8,128)(2,1)S(1)}, u32[]{:S(2)}, u32[]{:S(2)}) collective-permute-start(bf16[1,1,1,1,32,256]{5,4,3,2,1,0:T(8,128)(2,1)S(1)} %reshape_reshape.14), channel_id=1, source_target_pairs={{0,8},{1,9},{2,10},{3,11},{4,12},{5,13},{6,14},{7,15},{8,0},{9,1},... | collective-permute-start | bytes 49160 | tf_op jit(solution)/shard_map/ppermute | solution.py:23
  17.1 0.9 reshape.91
  18.1 0.1 reshape_reshape.12
  18.2 0.7 broadcast_in_dim.14
  19.0 15.7 %all-to-all-start = ((bf16[24,22,256]{2,1,0:T(8,128)(2,1)}), bf16[24,22,256]{2,1,0:T(8,128)(2,1)S(1)}, u32[]{:S(2)}, u32[]{:S(2)}) async-start(bf16[24,22,256]{2,1,0:T(8,128)(2,1)} %bitcast.6), calls=%async_computation | async-start | bytes 589824 | tf_op jit(solution)/shard_map/all_to_all | solution.py:82
  34.7 2.7 %collective-permute-start.4 = (bf16[2,1,1,1,32,256]{5,4,3,2,1,0:T(8,128)(2,1)S(1)}, bf16[2,1,1,1,32,256]{5,4,3,2,1,0:T(8,128)(2,1)S(1)}, u32[]{:S(2)}, u32[]{:S(2)}) collective-permute-start(bf16[2,1,1,1,32,256]{5,4,3,2,1,0:T(8,128)(2,1)S(1)} %pad_maximum_fusion.5), channel_id=1, source_target_pairs={{0,4},{1,5},{2,6},{3,7},{4,0},{5,1},{6,2},{7,3},{8,12},{9,13},{10,... | collective-permute-start | bytes 98312 | tf_op jit(solution)/shard_map/ppermute | solution.py:23
  37.5 3.8 %collective-permute-start = (bf16[2,128,512]{2,1,0:T(8,128)(2,1)S(1)}, bf16[2,128,512]{2,1,0:T(8,128)(2,1)S(1)}, u32[]{:S(2)}, u32[]{:S(2)}) collective-permute-start(bf16[2,128,512]{2,1,0:T(8,128)(2,1)S(1)} %reverse_select_fusion), channel_id=1, source_target_pairs={{0,384},{384,0},{1,385},{385,1},{2,386},{386,2},{3,387},{387,3},{4... | collective-permute-start | bytes 786440 | tf_op jit(solution)/shard_map/ppermute | solution.py:12
  41.3 0.2 collective-permute-done.4
  41.5 9.7 %all-to-all-done = bf16[24,22,256]{2,1,0:T(8,128)(2,1)S(1)} async-done(((bf16[24,22,256]{2,1,0:T(8,128)(2,1)}), bf16[24,22,256]{2,1,0:T(8,128)(2,1)S(1)}, u32[]{:S(2)}, u32[]{:S(2)}) %all-to-all-start) | async-done | bytes 270368 | tf_op jit(solution)/shard_map/all_to_all | solution.py:82
  51.2 1.9 %collective-permute-start.1 = (bf16[24,22,256]{2,1,0:T(8,128)(2,1)S(1)}, bf16[24,22,256]{2,1,0:T(8,128)(2,1)S(1)}, u32[]{:S(2)}, u32[]{:S(2)}) collective-permute-start(bf16[24,22,256]{2,1,0:T(8,128)(2,1)S(1)} %all-to-all-done), channel_id=1, source_target_pairs={{0,16},{16,0},{1,17},{17,1},{2,18},{18,2},{3,19},{19,3},{4,20},{20... | collective-permute-start | bytes 811016 | tf_op jit(solution)/shard_map/ppermute | solution.py:16
  53.3 1.4 %collective-permute-done.1 = bf16[24,22,256]{2,1,0:T(8,128)(2,1)S(1)} collective-permute-done((bf16[24,22,256]{2,1,0:T(8,128)(2,1)S(1)}, bf16[24,22,256]{2,1,0:T(8,128)(2,1)S(1)}, u32[]{:S(2)}, u32[]{:S(2)}) %collective-permute-start.1) | collective-permute-done | bytes 270368 | tf_op jit(solution)/shard_map/ppermute | solution.py:16
  54.7 0.1 fusion
  54.8 0.4 copy.59
  55.2 0.1 copy.74
  55.3 1.1 convolution_convert_fusion
  56.4 4.0 %collective-permute-start.5 = (bf16[2,2,1,1,32,256]{5,4,3,2,1,0:T(8,128)(2,1)S(1)}, bf16[2,2,1,1,32,256]{5,4,3,2,1,0:T(8,128)(2,1)S(1)}, u32[]{:S(2)}, u32[]{:S(2)}) collective-permute-start(bf16[2,2,1,1,32,256]{5,4,3,2,1,0:T(8,128)(2,1)S(1)} %pad_maximum_fusion.4), channel_id=1, source_target_pairs={{0,2},{1,3},{2,0},{3,1},{4,6},{5,7},{6,4},{7,5},{8,10},{9,11},{10,... | collective-permute-start | bytes 196616 | tf_op jit(solution)/shard_map/ppermute | solution.py:23
  60.4 3.6 %collective-permute-done.5 = bf16[2,2,1,1,32,256]{5,4,3,2,1,0:T(8,128)(2,1)S(1)} collective-permute-done((bf16[2,2,1,1,32,256]{5,4,3,2,1,0:T(8,128)(2,1)S(1)}, bf16[2,2,1,1,32,256]{5,4,3,2,1,0:T(8,128)(2,1)S(1)}, u32[]{:S(2)}, u32[]{:S(2)}) %collective-permute-start.5) | collective-permute-done | bytes 65568 | tf_op jit(solution)/shard_map/ppermute | solution.py:23
  64.1 2.4 %collective-permute-start.6 = (bf16[2,2,2,1,32,256]{5,4,3,2,1,0:T(8,128)(2,1)S(1)}, bf16[2,2,2,1,32,256]{5,4,3,2,1,0:T(8,128)(2,1)S(1)}, u32[]{:S(2)}, u32[]{:S(2)}) collective-permute-start(bf16[2,2,2,1,32,256]{5,4,3,2,1,0:T(8,128)(2,1)S(1)} %pad_maximum_fusion.3), channel_id=1, source_target_pairs={{0,1},{1,0},{2,3},{3,2},{4,5},{5,4},{6,7},{7,6},{8,9},{9,8},{10,11... | collective-permute-start | bytes 393224 | tf_op jit(solution)/shard_map/ppermute | solution.py:23
  66.6 5.7 %all-to-all-start.1 = ((bf16[16,32,256]{2,1,0:T(8,128)(2,1)}), bf16[16,32,256]{2,1,0:T(8,128)(2,1)S(1)}, u32[]{:S(2)}, u32[]{:S(2)}) async-start(bf16[16,32,256]{2,1,0:T(8,128)(2,1)} %bitcast.23), calls=%async_computation.1 | async-start | bytes 524288 | tf_op jit(solution)/shard_map/all_to_all | solution.py:105
  72.4 1.2 %fusion.9 = (bf16[256,512]{1,0:T(8,128)(2,1)}, f32[256,512]{1,0:T(8,128)}) fusion(bf16[512,256]{1,0:T(8,128)(2,1)S(1)} %bitcast.85, bf16[528,512]{1,0:T(8,128)(2,1)S(1)} %bitcast.90), kind=kOutput, calls=%fused_computation.58 | convolution fusion | flops 134348800 | bytes 1572864 | tf_op jit(solution)/shard_map/dot_general | solution.py:126
  73.7 0.3 fusion.10
  74.0 2.8 %collective-permute-start.9 = (bf16[256,512]{1,0:T(8,128)(2,1)}, bf16[256,512]{1,0:T(8,128)(2,1)}, u32[]{:S(2)}, u32[]{:S(2)}) collective-permute-start(bf16[256,512]{1,0:T(8,128)(2,1)} %get-tuple-element.33), channel_id=1, source_target_pairs={{0,384},{384,0},{1,385},{385,1},{2,386},{386,2},{3,387},{387,3},{4... | collective-permute-start | bytes 786440 | tf_op jit(solution)/shard_map/ppermute | solution.py:12
  76.9 0.2 reshape.95
  77.1 0.2 fusion.7
  77.3 0.6 select_convert_fusion
  78.0 1.9 %collective-permute-start.7 = (bf16[24,22,256]{2,0,1:T(8,128)(2,1)S(1)}, bf16[24,22,256]{2,0,1:T(8,128)(2,1)S(1)}, u32[]{:S(2)}, u32[]{:S(2)}) collective-permute-start(bf16[24,22,256]{2,0,1:T(8,128)(2,1)S(1)} %bitcast.100), channel_id=1, source_target_pairs={{0,16},{16,0},{1,17},{17,1},{2,18},{18,2},{3,19},{19,3},{4,20},{20... | collective-permute-start | bytes 811016 | tf_op jit(solution)/shard_map/ppermute | solution.py:16
  79.9 0.6 copy_select_fusion
  80.5 0.3 select_n.321
  81.0 3.2 %collective-permute-done.9 = bf16[256,512]{1,0:T(8,128)(2,1)} collective-permute-done((bf16[256,512]{1,0:T(8,128)(2,1)}, bf16[256,512]{1,0:T(8,128)(2,1)}, u32[]{:S(2)}, u32[]{:S(2)}) %collective-permute-start.9) | collective-permute-done | bytes 262176 | tf_op jit(solution)/shard_map/ppermute | solution.py:12
  84.1 1.0 add_convert_fusion
  85.3 0.8 copy.68
  86.0 5.5 %all-to-all-start.2 = ((bf16[24,22,256]{2,1,0:T(8,128)(2,1)}), bf16[24,22,256]{2,1,0:T(8,128)(2,1)S(1)}, u32[]{:S(2)}, u32[]{:S(2)}) async-start(bf16[24,22,256]{2,1,0:T(8,128)(2,1)} %copy.68), calls=%async_computation.2 | async-start | bytes 589824 | tf_op jit(solution)/shard_map/all_to_all | solution.py:115
  91.5 1.3 %select_bitcast_fusion.1 = (bf16[1,128,512]{2,1,0:T(8,128)(2,1)S(1)}, bf16[1,128,512]{2,1,0:T(8,128)(2,1)S(1)}) fusion(pred[]{:T(512)S(6)} %eq.13, pred[]{:T(512)} %bitcast, bf16[256,512]{1,0:T(8,128)(2,1)S(1)} %add_convert_fusion, pred[]{:T(512)S(6)} %eq.17, pred[]{:T(512)} %bitcast.25), kind=kLoop, calls=%fused_computation.18 | loop fusion | flops 262144 | bytes 524292 | tf_op jit(solution)/shard_map/stack | solution.py:67
  92.9 3.8 %collective-permute-start.8 = (bf16[32,256]{1,0:T(8,128)(2,1)S(1)}, bf16[32,256]{1,0:T(8,128)(2,1)S(1)}, u32[]{:S(2)}, u32[]{:S(2)}) collective-permute-start(bf16[32,256]{1,0:T(8,128)(2,1)S(1)} %reduce_sum.31), channel_id=1, source_target_pairs={{0,384},{384,0},{1,385},{385,1},{2,386},{386,2},{3,387},{387,3},{4... | collective-permute-start | bytes 49160 | tf_op jit(solution)/shard_map/ppermute | solution.py:12
  96.7 0.7 pad_maximum_fusion.2
  97.4 1.3 %collective-permute-done.8 = bf16[32,256]{1,0:T(8,128)(2,1)S(1)} collective-permute-done((bf16[32,256]{1,0:T(8,128)(2,1)S(1)}, bf16[32,256]{1,0:T(8,128)(2,1)S(1)}, u32[]{:S(2)}, u32[]{:S(2)}) %collective-permute-start.8) | collective-permute-done | bytes 16416 | tf_op jit(solution)/shard_map/ppermute | solution.py:12
  98.8 1.4 %broadcast_select_fusion.10 = (bf16[1,64,128]{2,0,1:T(2,128)(2,1)S(1)}, bf16[1,64,128]{2,0,1:T(2,128)(2,1)S(1)}) fusion(pred[]{:T(512)} %bitcast, pred[]{:T(512)S(6)} %eq.13, bf16[2,64,128]{2,0,1:T(2,128)(2,1)S(1)} %fusion.5, pred[]{:T(512)S(6)} %eq.17, pred[]{:T(512)} %bitcast.25), kind=kLoop, calls=%fused_computation.33 | loop fusion | flops 32768 | bytes 65540 | tf_op jit(solution)/shard_map/jit(_where)/select_n | solution.py:67
  100.3 0.6 copy.83
  100.9 7.1 %all-to-all-done.2 = bf16[24,22,256]{2,1,0:T(8,128)(2,1)S(1)} async-done(((bf16[24,22,256]{2,1,0:T(8,128)(2,1)}), bf16[24,22,256]{2,1,0:T(8,128)(2,1)S(1)}, u32[]{:S(2)}, u32[]{:S(2)}) %all-to-all-start.2) | async-done | bytes 270368 | tf_op jit(solution)/shard_map/all_to_all | solution.py:115
  108.1 0.1 reshape_reshape.15
  108.2 0.1 copy.71
  108.3 0.9 reshape.102
  (46 shorter events, 1.2 us)
Async XLA Ops:
  0.6 36.8 %copy-start.1 = (bf16[256,512]{1,0:T(8,128)(2,1)S(1)}, bf16[256,512]{1,0:T(8,128)(2,1)}, u32[]{:S(2)}) copy-start(bf16[256,512]{1,0:T(8,128)(2,1)} %param.4) | copy-start | bytes 786436
  3.6 6.1 %collective-permute-start.2 = (bf16[2,32,128]{2,0,1:T(2,128)(2,1)S(1)}, bf16[2,32,128]{2,0,1:T(2,128)(2,1)S(1)}, u32[]{:S(2)}, u32[]{:S(2)}) collective-permute-start(bf16[2,32,128]{2,0,1:T(2,128)(2,1)S(1)} %get-tuple-element.30), channel_id=1, source_target_pairs={{0,384},{384,0},{1,385},{385,1},{2,386},{386,2},{3,387},{387,3},{4... | collective-permute-start | bytes 49160 | tf_op jit(solution)/shard_map/ppermute | solution.py:12
  9.9 24.8 %collective-permute-start.3 = (bf16[1,1,1,1,32,256]{5,4,3,2,1,0:T(8,128)(2,1)S(1)}, bf16[1,1,1,1,32,256]{5,4,3,2,1,0:T(8,128)(2,1)S(1)}, u32[]{:S(2)}, u32[]{:S(2)}) collective-permute-start(bf16[1,1,1,1,32,256]{5,4,3,2,1,0:T(8,128)(2,1)S(1)} %reshape_reshape.14), channel_id=1, source_target_pairs={{0,8},{1,9},{2,10},{3,11},{4,12},{5,13},{6,14},{7,15},{8,0},{9,1},... | collective-permute-start | bytes 49160 | tf_op jit(solution)/shard_map/ppermute | solution.py:23
  19.0 32.2 %all-to-all-start = ((bf16[24,22,256]{2,1,0:T(8,128)(2,1)}), bf16[24,22,256]{2,1,0:T(8,128)(2,1)S(1)}, u32[]{:S(2)}, u32[]{:S(2)}) async-start(bf16[24,22,256]{2,1,0:T(8,128)(2,1)} %bitcast.6), calls=%async_computation | async-start | bytes 589824 | tf_op jit(solution)/shard_map/all_to_all | solution.py:82
  34.7 6.8 %collective-permute-start.4 = (bf16[2,1,1,1,32,256]{5,4,3,2,1,0:T(8,128)(2,1)S(1)}, bf16[2,1,1,1,32,256]{5,4,3,2,1,0:T(8,128)(2,1)S(1)}, u32[]{:S(2)}, u32[]{:S(2)}) collective-permute-start(bf16[2,1,1,1,32,256]{5,4,3,2,1,0:T(8,128)(2,1)S(1)} %pad_maximum_fusion.5), channel_id=1, source_target_pairs={{0,4},{1,5},{2,6},{3,7},{4,0},{5,1},{6,2},{7,3},{8,12},{9,13},{10,... | collective-permute-start | bytes 98312 | tf_op jit(solution)/shard_map/ppermute | solution.py:23
  37.5 15.6 %collective-permute-start = (bf16[2,128,512]{2,1,0:T(8,128)(2,1)S(1)}, bf16[2,128,512]{2,1,0:T(8,128)(2,1)S(1)}, u32[]{:S(2)}, u32[]{:S(2)}) collective-permute-start(bf16[2,128,512]{2,1,0:T(8,128)(2,1)S(1)} %reverse_select_fusion), channel_id=1, source_target_pairs={{0,384},{384,0},{1,385},{385,1},{2,386},{386,2},{3,387},{387,3},{4... | collective-permute-start | bytes 786440 | tf_op jit(solution)/shard_map/ppermute | solution.py:12
  51.2 3.5 %collective-permute-start.1 = (bf16[24,22,256]{2,1,0:T(8,128)(2,1)S(1)}, bf16[24,22,256]{2,1,0:T(8,128)(2,1)S(1)}, u32[]{:S(2)}, u32[]{:S(2)}) collective-permute-start(bf16[24,22,256]{2,1,0:T(8,128)(2,1)S(1)} %all-to-all-done), channel_id=1, source_target_pairs={{0,16},{16,0},{1,17},{17,1},{2,18},{18,2},{3,19},{19,3},{4,20},{20... | collective-permute-start | bytes 811016 | tf_op jit(solution)/shard_map/ppermute | solution.py:16
  55.2 11.3 %copy-start.2 = (s32[2]{0:T(128)S(1)}, s32[2]{0:T(128)}, u32[]{:S(2)}) copy-start(s32[2]{0:T(128)} %param.7) | copy-start | bytes 28
  56.4 7.7 %collective-permute-start.5 = (bf16[2,2,1,1,32,256]{5,4,3,2,1,0:T(8,128)(2,1)S(1)}, bf16[2,2,1,1,32,256]{5,4,3,2,1,0:T(8,128)(2,1)S(1)}, u32[]{:S(2)}, u32[]{:S(2)}) collective-permute-start(bf16[2,2,1,1,32,256]{5,4,3,2,1,0:T(8,128)(2,1)S(1)} %pad_maximum_fusion.4), channel_id=1, source_target_pairs={{0,2},{1,3},{2,0},{3,1},{4,6},{5,7},{6,4},{7,5},{8,10},{9,11},{10,... | collective-permute-start | bytes 196616 | tf_op jit(solution)/shard_map/ppermute | solution.py:23
  64.1 8.3 %collective-permute-start.6 = (bf16[2,2,2,1,32,256]{5,4,3,2,1,0:T(8,128)(2,1)S(1)}, bf16[2,2,2,1,32,256]{5,4,3,2,1,0:T(8,128)(2,1)S(1)}, u32[]{:S(2)}, u32[]{:S(2)}) collective-permute-start(bf16[2,2,2,1,32,256]{5,4,3,2,1,0:T(8,128)(2,1)S(1)} %pad_maximum_fusion.3), channel_id=1, source_target_pairs={{0,1},{1,0},{2,3},{3,2},{4,5},{5,4},{6,7},{7,6},{8,9},{9,8},{10,11... | collective-permute-start | bytes 393224 | tf_op jit(solution)/shard_map/ppermute | solution.py:23
  66.6 18.7 %all-to-all-start.1 = ((bf16[16,32,256]{2,1,0:T(8,128)(2,1)}), bf16[16,32,256]{2,1,0:T(8,128)(2,1)S(1)}, u32[]{:S(2)}, u32[]{:S(2)}) async-start(bf16[16,32,256]{2,1,0:T(8,128)(2,1)} %bitcast.23), calls=%async_computation.1 | async-start | bytes 524288 | tf_op jit(solution)/shard_map/all_to_all | solution.py:105
  74.0 10.1 %collective-permute-start.9 = (bf16[256,512]{1,0:T(8,128)(2,1)}, bf16[256,512]{1,0:T(8,128)(2,1)}, u32[]{:S(2)}, u32[]{:S(2)}) collective-permute-start(bf16[256,512]{1,0:T(8,128)(2,1)} %get-tuple-element.33), channel_id=1, source_target_pairs={{0,384},{384,0},{1,385},{385,1},{2,386},{386,2},{3,387},{387,3},{4... | collective-permute-start | bytes 786440 | tf_op jit(solution)/shard_map/ppermute | solution.py:12
  78.0 7.2 %collective-permute-start.7 = (bf16[24,22,256]{2,0,1:T(8,128)(2,1)S(1)}, bf16[24,22,256]{2,0,1:T(8,128)(2,1)S(1)}, u32[]{:S(2)}, u32[]{:S(2)}) collective-permute-start(bf16[24,22,256]{2,0,1:T(8,128)(2,1)S(1)} %bitcast.100), channel_id=1, source_target_pairs={{0,16},{16,0},{1,17},{17,1},{2,18},{18,2},{3,19},{19,3},{4,20},{20... | collective-permute-start | bytes 811016 | tf_op jit(solution)/shard_map/ppermute | solution.py:16
  80.5 3.6 %copy-start = (f32[256,512]{1,0:T(8,128)S(1)}, f32[256,512]{1,0:T(8,128)}, u32[]{:S(2)}) copy-start(f32[256,512]{1,0:T(8,128)} %get-tuple-element.34) | copy-start | bytes 1572868
  86.0 21.9 %all-to-all-start.2 = ((bf16[24,22,256]{2,1,0:T(8,128)(2,1)}), bf16[24,22,256]{2,1,0:T(8,128)(2,1)S(1)}, u32[]{:S(2)}, u32[]{:S(2)}) async-start(bf16[24,22,256]{2,1,0:T(8,128)(2,1)} %copy.68), calls=%async_computation.2 | async-start | bytes 589824 | tf_op jit(solution)/shard_map/all_to_all | solution.py:115
  92.9 5.8 %collective-permute-start.8 = (bf16[32,256]{1,0:T(8,128)(2,1)S(1)}, bf16[32,256]{1,0:T(8,128)(2,1)S(1)}, u32[]{:S(2)}, u32[]{:S(2)}) collective-permute-start(bf16[32,256]{1,0:T(8,128)(2,1)S(1)} %reduce_sum.31), channel_id=1, source_target_pairs={{0,384},{384,0},{1,385},{385,1},{2,386},{386,2},{3,387},{387,3},{4... | collective-permute-start | bytes 49160 | tf_op jit(solution)/shard_map/ppermute | solution.py:12

commit v6 on v4

--- a/solution.py
+++ b/solution.py
@@ -1,6 +1,10 @@
+import functools
+
 import jax
 import jax.numpy as jnp
 from jax import lax
+from jax.experimental import pallas as pl
+from jax.experimental.pallas import tpu as pltpu
 from jax.sharding import Mesh, PartitionSpec as P
 
 BF16 = jnp.bfloat16
@@ -14,6 +18,53 @@
 
 def swap_core(value):
     return lax.ppermute(value, "core", SWAP)
+
+
+def weight_kernel(blocks, wrows, core_ref, both_ref, x_ref, mine_ref, theirs_ref, acc_ref, stage_ref):
+    tokens, feats = x_ref.shape
+    n_mp, rows, _ = both_ref.shape
+    half = rows // 2
+    width = acc_ref.shape[2]
+    groups = width // half
+    first_core = core_ref[0] == 0
+    x_turned = x_ref[...].T
+    for part in range(2):
+        g = both_ref[part * groups : (part + 1) * groups, half:, :].reshape(width, tokens)
+        acc_ref[part, :feats] = lax.dot_general(
+            x_turned, g, (((1,), (1,)), ((), ())), preferred_element_type=F32
+        )
+        acc_ref[part, feats:] = jnp.zeros_like(acc_ref[part, feats:])
+    stage_ref[:, 2 * wrows :] = jnp.zeros_like(stage_ref[:, 2 * wrows :])
+    for block in range(blocks):
+        for part in range(2):
+            top = acc_ref[part, pl.ds(2 * block * wrows, wrows)]
+            bottom = acc_ref[part, pl.ds((2 * block + 1) * wrows, wrows)]
+            mine_ref[block, pl.ds(part * wrows, wrows)] = jnp.where(first_core, top, bottom)
+            stage_ref[block, pl.ds(part * wrows, wrows)] = jnp.where(first_core, bottom, top)
+        theirs_ref[block] = stage_ref[block, : 2 * wrows].astype(BF16)
+
+
+def weight_blocks(core, both, x_pair, blocks, wrows):
+    tokens, feats = x_pair.shape
+    n_mp, rows, _ = both.shape
+    width = n_mp * rows // 4
+    vmem = pl.BlockSpec(memory_space=pltpu.VMEM)
+    padded = -(-2 * wrows // 16) * 16
+    shape = (blocks, 2 * wrows, width)
+    return pl.pallas_call(
+        functools.partial(weight_kernel, blocks, wrows),
+        out_shape=(jax.ShapeDtypeStruct(shape, F32), jax.ShapeDtypeStruct(shape, BF16)),
+        in_specs=[pl.BlockSpec(memory_space=pltpu.SMEM), vmem, vmem],
+        out_specs=(vmem, vmem),
+        scratch_shapes=[
+            pltpu.VMEM((2, 2 * blocks * wrows, width), F32),
+            pltpu.VMEM((blocks, padded, width), F32),
+        ],
+        compiler_params=pltpu.CompilerParams(vmem_limit_bytes=32 * 2**20),
+        cost_estimate=pl.CostEstimate(
+            flops=2 * feats * tokens * 2 * width, bytes_accessed=3 * 2**20, transcendentals=0
+        ),
+    )(core.reshape(1), both, x_pair)
 
 
 def on_device(x, w, adjoint, mask):
@@ -91,13 +142,10 @@
     both = lax.all_to_all(both, "mp", 0, 0, tiled=True)
     g_all = both[:, half:].reshape(n_mp * half, tokens)
 
-    dw = lax.dot_general(x_pair, g_all, (((0,), (1,)), ((), ())), preferred_element_type=F32)
-    dw = jnp.pad(dw, ((0, 4 * n_z * wrows - feats), (0, 0)))
-    dw = dw.reshape(2 * n_z, 2, wrows, n_mp * half)
-    dw_mine = pack(jnp.where(core == 0, dw[:, 0], dw[:, 1]))
-    dw_theirs = pack(jnp.where(core == 0, dw[:, 1], dw[:, 0]).astype(BF16))
+    dw_mine, dw_theirs = weight_blocks(core, both, x_pair, 2 * n_z, wrows)
+    dw_theirs, both = lax.optimization_barrier((dw_theirs, both))
     dw_sum = dw_mine + swap_core(dw_theirs).astype(F32)
-    dw_send, both, g_all, w_full = lax.optimization_barrier((dw_sum.astype(BF16), both, g_all, w_full))
+    dw_send, g_all, w_full = lax.optimization_barrier((dw_sum.astype(BF16), g_all, w_full))
     dw_parts = lax.all_to_all(dw_send, ("pair", "z"), 0, 0, tiled=True)
     dw_parts = dw_parts.reshape(2, n_z, 2 * wrows, n_mp * half // 2)
     dw_rows = unpack(jnp.sum(dw_parts.astype(F32), axis=1)).reshape(2, wrows, n_mp, half)

time: 102 us -> 102 us (level)
  the two profiles are of different devices: /device:TPU:1 before, /device:TPU:16 now
where the time goes in v6:
time: 102 us
  starting transfers between devices  36 us (35%)
  blocking collectives  25.6 us (25%)
  waiting for transfers between devices  25 us (25%)
  other arithmetic  5.57 us (5%)
  local copies, waits for them, and re-layouts  5.14 us (5%)
  between operations  3.02 us (3%)
    all_to_all x1, blocking collectives, on_device(): both = lax.all_to_all(both, 'mp', 0, 0, tiled=True)  25.6 us
    all_to_all x1, starting transfers between devices, on_device(): lax.all_to_all(w_send.reshape(2 * n_z, 2 * wrows, n_mp * half // 2), ('pa...  16.5 us
    all_to_all x1, waiting for transfers between devices, on_device(): dw_parts = lax.all_to_all(dw_send, ('pair', 'z'), 0, 0, tiled=True)  12.3 us
    ppermute x4, starting transfers between devices, swap_pair(): return lax.ppermute(value, 'pair', SWAP)  9.68 us
    all_to_all x1, waiting for transfers between devices, on_device(): lax.all_to_all(w_send.reshape(2 * n_z, 2 * wrows, n_mp * half // 2), ('pa...  7.71 us
    all_to_all x1, starting transfers between devices, on_device(): dw_parts = lax.all_to_all(dw_send, ('pair', 'z'), 0, 0, tiled=True)  5.97 us
    ppermute x2, starting transfers between devices, swap_core(): return lax.ppermute(value, 'core', SWAP)  3.83 us
    ppermute x4, waiting for transfers between devices, swap_pair(): return lax.ppermute(value, 'pair', SWAP)  3.6 us
  transfers between devices with their start and end apart: 8, of which 4 were waited for; matrix products, arithmetic and copies ran while one was open for 6% of the time, Pallas kernels for 0%

profile of v6, /device:TPU:16, one launch (start us, length us, event | category | flops | bytes accessed | tf_op | source)
XLA Modules:
  0.0 101.6 jit_solution(2558152115395995447)
XLA Ops:
  0.6 0.9 reshape.75
  1.6 0.1 reshape_reshape.9
  1.7 0.7 broadcast_in_dim.21
  2.4 16.5 %all-to-all-start = ((bf16[24,22,256]{2,1,0:T(8,128)(2,1)}), bf16[24,22,256]{2,1,0:T(8,128)(2,1)S(1)}, u32[]{:S(2)}, u32[]{:S(2)}) async-start(bf16[24,22,256]{2,1,0:T(8,128)(2,1)} %bitcast.5), calls=%async_computation | async-start | bytes 589824 | tf_op jit(solution)/shard_map/all_to_all | solution.py:121
  19.0 0.0 copy-start.1
  19.0 0.0 copy-done.3
  19.0 0.6 fusion.4
  19.6 0.2 rev.7
  20.5 3.8 %collective-permute-start.2 = (bf16[2,32,128]{2,0,1:T(2,128)(2,1)S(1)}, bf16[2,32,128]{2,0,1:T(2,128)(2,1)S(1)}, u32[]{:S(2)}, u32[]{:S(2)}) collective-permute-start(bf16[2,32,128]{2,0,1:T(2,128)(2,1)S(1)} %get-tuple-element.26), channel_id=1, source_target_pairs={{0,384},{384,0},{1,385},{385,1},{2,386},{386,2},{3,387},{387,3},{4... | collective-permute-start | bytes 49160 | tf_op jit(solution)/shard_map/ppermute | solution.py:16
  24.3 0.1 reverse_select_fusion
  24.3 2.1 %collective-permute-start.1 = (bf16[2,128,512]{2,1,0:T(8,128)(2,1)S(1)}, bf16[2,128,512]{2,1,0:T(8,128)(2,1)S(1)}, u32[]{:S(2)}, u32[]{:S(2)}) collective-permute-start(bf16[2,128,512]{2,1,0:T(8,128)(2,1)S(1)} %reverse_select_fusion), channel_id=1, source_target_pairs={{0,384},{384,0},{1,385},{385,1},{2,386},{386,2},{3,387},{387,3},{4... | collective-permute-start | bytes 786440 | tf_op jit(solution)/shard_map/ppermute | solution.py:16
  26.4 0.6 reduce_sum.30
  28.4 0.0 collective-permute-done.2
  28.4 0.1 broadcast_select_fusion.15
  28.5 7.7 %all-to-all-done = bf16[24,22,256]{2,1,0:T(8,128)(2,1)S(1)} async-done(((bf16[24,22,256]{2,1,0:T(8,128)(2,1)}), bf16[24,22,256]{2,1,0:T(8,128)(2,1)S(1)}, u32[]{:S(2)}, u32[]{:S(2)}) %all-to-all-start) | async-done | bytes 270368 | tf_op jit(solution)/shard_map/all_to_all | solution.py:121
  36.2 1.9 %collective-permute-start = (bf16[24,22,256]{2,1,0:T(8,128)(2,1)S(1)}, bf16[24,22,256]{2,1,0:T(8,128)(2,1)S(1)}, u32[]{:S(2)}, u32[]{:S(2)}) collective-permute-start(bf16[24,22,256]{2,1,0:T(8,128)(2,1)S(1)} %all-to-all-done), channel_id=1, source_target_pairs={{0,16},{16,0},{1,17},{17,1},{2,18},{18,2},{3,19},{19,3},{4,20},{20... | collective-permute-start | bytes 811016 | tf_op jit(solution)/shard_map/ppermute | solution.py:20
  38.2 0.0 collective-permute-done.1
  38.3 0.1 copy.30
  38.3 1.4 %collective-permute-done = bf16[24,22,256]{2,1,0:T(8,128)(2,1)S(1)} collective-permute-done((bf16[24,22,256]{2,1,0:T(8,128)(2,1)S(1)}, bf16[24,22,256]{2,1,0:T(8,128)(2,1)S(1)}, u32[]{:S(2)}, u32[]{:S(2)}) %collective-permute-start) | collective-permute-done | bytes 270368 | tf_op jit(solution)/shard_map/ppermute | solution.py:20
  39.7 0.1 copy.31
  39.8 0.1 fusion
  39.8 0.4 copy.32
  40.3 0.1 copy.40
  40.4 0.4 convolution_convert_fusion
  40.8 25.6 %all_to_all.15.both_ref = bf16[16,64,256]{2,1,0:T(8,128)(2,1)S(1)} all-to-all(bf16[16,64,256]{2,1,0:T(8,128)(2,1)S(1)} %pad_maximum_fusion), channel_id=1, replica_groups=mesh['pair'=2,'z'=12,'core'=2,'mp'=16] {'mp'}, dimensions={0} | all-to-all | bytes 1048576 | tf_op jit(solution)/shard_map/all_to_all | solution.py:142
  66.4 0.5 shard_map.67
  66.9 1.9 %collective-permute-start.4 = (bf16[24,22,256]{2,1,0:T(8,128)(2,1)S(1)}, bf16[24,22,256]{2,1,0:T(8,128)(2,1)S(1)}, u32[]{:S(2)}, u32[]{:S(2)}) collective-permute-start(bf16[24,22,256]{2,1,0:T(8,128)(2,1)S(1)} %get-tuple-element.13), channel_id=1, source_target_pairs={{0,16},{16,0},{1,17},{17,1},{2,18},{18,2},{3,19},{19,3},{4,20},{20... | collective-permute-start | bytes 811016 | tf_op jit(solution)/shard_map/ppermute | solution.py:20
  68.9 1.9 %collective-permute-start.3 = (bf16[32,256]{1,0:T(8,128)(2,1)S(1)}, bf16[32,256]{1,0:T(8,128)(2,1)S(1)}, u32[]{:S(2)}, u32[]{:S(2)}) collective-permute-start(bf16[32,256]{1,0:T(8,128)(2,1)S(1)} %slice_reduce_fusion), channel_id=1, source_target_pairs={{0,384},{384,0},{1,385},{385,1},{2,386},{386,2},{3,387},{387,3},{4... | collective-permute-start | bytes 49160 | tf_op jit(solution)/shard_map/ppermute | solution.py:16
  70.9 3.6 %collective-permute-done.3 = bf16[32,256]{1,0:T(8,128)(2,1)S(1)} collective-permute-done((bf16[32,256]{1,0:T(8,128)(2,1)S(1)}, bf16[32,256]{1,0:T(8,128)(2,1)S(1)}, u32[]{:S(2)}, u32[]{:S(2)}) %collective-permute-start.3) | collective-permute-done | bytes 16416 | tf_op jit(solution)/shard_map/ppermute | solution.py:16
  74.5 0.1 fusion.1
  74.6 0.0 collective-permute-done.4
  74.6 0.0 slice-start
  74.6 0.8 add_convert_fusion
  75.4 0.2 slice-done
  75.5 0.3 fusion.5
  75.9 1.9 %collective-permute-start.5 = (bf16[256,512]{1,0:T(8,128)(2,1)S(1)}, bf16[256,512]{1,0:T(8,128)(2,1)S(1)}, u32[]{:S(2)}, u32[]{:S(2)}) collective-permute-start(bf16[256,512]{1,0:T(8,128)(2,1)S(1)} %get-tuple-element.29), channel_id=1, source_target_pairs={{0,384},{384,0},{1,385},{385,1},{2,386},{386,2},{3,387},{387,3},{4... | collective-permute-start | bytes 786440 | tf_op jit(solution)/shard_map/ppermute | solution.py:16
  77.8 6.0 %all-to-all-start.2 = ((bf16[24,22,256]{2,1,0:T(8,128)(2,1)}), bf16[24,22,256]{2,1,0:T(8,128)(2,1)S(1)}, u32[]{:S(2)}, u32[]{:S(2)}) async-start(bf16[24,22,256]{2,1,0:T(8,128)(2,1)} %add_convert_fusion), calls=%async_computation.2 | async-start | bytes 589824 | tf_op jit(solution)/shard_map/all_to_all | solution.py:149
  83.8 1.4 %broadcast_select_fusion.6 = (bf16[1,64,128]{2,0,1:T(2,128)(2,1)S(1)}, bf16[1,64,128]{2,0,1:T(2,128)(2,1)S(1)}) fusion(pred[]{:T(512)} %bitcast, pred[]{:T(512)S(6)} %eq.13, bf16[2,64,128]{2,0,1:T(2,128)(2,1)S(1)} %fusion.1, pred[]{:T(512)S(6)} %eq.17, pred[]{:T(512)} %bitcast.21), kind=kLoop, calls=%fused_computation.22 | loop fusion | flops 32768 | bytes 65540 | tf_op jit(solution)/shard_map/jit(_where)/select_n | solution.py:106
  85.2 0.1 pad_maximum_fusion.3
  85.3 0.6 copy.47
  85.9 0.0 collective-permute-done.5
  85.9 0.1 add_convert_fusion.1
  86.0 1.3 %select_bitcast_fusion.1 = (bf16[1,128,512]{2,1,0:T(8,128)(2,1)S(1)}, bf16[1,128,512]{2,1,0:T(8,128)(2,1)S(1)}) fusion(pred[]{:T(512)S(6)} %eq.13, pred[]{:T(512)} %bitcast, bf16[256,512]{1,0:T(8,128)(2,1)S(1)} %add_convert_fusion.1, pred[]{:T(512)S(6)} %eq.17, pred[]{:T(512)} %bitcast.21), kind=kLoop, calls=%fused_computation.12 | loop fusion | flops 262144 | bytes 524292 | tf_op jit(solution)/shard_map/stack | solution.py:106
  87.3 0.7 pad_maximum_fusion.2
  88.0 12.3 %all-to-all-done.2 = bf16[24,22,256]{2,1,0:T(8,128)(2,1)S(1)} async-done(((bf16[24,22,256]{2,1,0:T(8,128)(2,1)}), bf16[24,22,256]{2,1,0:T(8,128)(2,1)S(1)}, u32[]{:S(2)}, u32[]{:S(2)}) %all-to-all-start.2) | async-done | bytes 270368 | tf_op jit(solution)/shard_map/all_to_all | solution.py:149
  100.5 0.1 reshape_reshape.11
  100.6 0.1 copy.39
  100.7 0.9 reshape.85
  (26 shorter events, 0.5 us)
Async XLA Ops:
  2.4 16.5 %copy-start.3 = (s32[2]{0:T(128)S(1)}, s32[2]{0:T(128)}, u32[]{:S(2)}) copy-start(s32[2]{0:T(128)} %param.7) | copy-start | bytes 28
  2.4 17.2 %copy-start.2 = (bf16[256,64]{0,1:T(8,128)(2,1)S(1)}, bf16[256,64]{0,1:T(8,128)(2,1)}, u32[]{:S(2)}) copy-start(bf16[256,64]{0,1:T(8,128)(2,1)} %param.6) | copy-start | bytes 98308
  2.4 33.8 %all-to-all-start = ((bf16[24,22,256]{2,1,0:T(8,128)(2,1)}), bf16[24,22,256]{2,1,0:T(8,128)(2,1)S(1)}, u32[]{:S(2)}, u32[]{:S(2)}) async-start(bf16[24,22,256]{2,1,0:T(8,128)(2,1)} %bitcast.5), calls=%async_computation | async-start | bytes 589824 | tf_op jit(solution)/shard_map/all_to_all | solution.py:121
  19.0 5.3 %copy-start.1 = (bf16[256,512]{1,0:T(8,128)(2,1)S(1)}, bf16[256,512]{1,0:T(8,128)(2,1)}, u32[]{:S(2)}) copy-start(bf16[256,512]{1,0:T(8,128)(2,1)} %param.4) | copy-start | bytes 786436
  20.5 7.9 %collective-permute-start.2 = (bf16[2,32,128]{2,0,1:T(2,128)(2,1)S(1)}, bf16[2,32,128]{2,0,1:T(2,128)(2,1)S(1)}, u32[]{:S(2)}, u32[]{:S(2)}) collective-permute-start(bf16[2,32,128]{2,0,1:T(2,128)(2,1)S(1)} %get-tuple-element.26), channel_id=1, source_target_pairs={{0,384},{384,0},{1,385},{385,1},{2,386},{386,2},{3,387},{387,3},{4... | collective-permute-start | bytes 49160 | tf_op jit(solution)/shard_map/ppermute | solution.py:16
  24.3 13.8 %collective-permute-start.1 = (bf16[2,128,512]{2,1,0:T(8,128)(2,1)S(1)}, bf16[2,128,512]{2,1,0:T(8,128)(2,1)S(1)}, u32[]{:S(2)}, u32[]{:S(2)}) collective-permute-start(bf16[2,128,512]{2,1,0:T(8,128)(2,1)S(1)} %reverse_select_fusion), channel_id=1, source_target_pairs={{0,384},{384,0},{1,385},{385,1},{2,386},{386,2},{3,387},{387,3},{4... | collective-permute-start | bytes 786440 | tf_op jit(solution)/shard_map/ppermute | solution.py:16
  36.2 3.5 %collective-permute-start = (bf16[24,22,256]{2,1,0:T(8,128)(2,1)S(1)}, bf16[24,22,256]{2,1,0:T(8,128)(2,1)S(1)}, u32[]{:S(2)}, u32[]{:S(2)}) collective-permute-start(bf16[24,22,256]{2,1,0:T(8,128)(2,1)S(1)} %all-to-all-done), channel_id=1, source_target_pairs={{0,16},{16,0},{1,17},{17,1},{2,18},{18,2},{3,19},{19,3},{4,20},{20... | collective-permute-start | bytes 811016 | tf_op jit(solution)/shard_map/ppermute | solution.py:20
  66.4 4.5 %copy-start = (bf16[16,64,256]{2,1,0:T(8,128)(2,1)}, bf16[16,64,256]{2,1,0:T(8,128)(2,1)S(1)}, u32[]{:S(2)}) copy-start(bf16[16,64,256]{2,1,0:T(8,128)(2,1)S(1)} %all_to_all.15.both_ref) | copy-start | bytes 1572868
  66.9 7.7 %collective-permute-start.4 = (bf16[24,22,256]{2,1,0:T(8,128)(2,1)S(1)}, bf16[24,22,256]{2,1,0:T(8,128)(2,1)S(1)}, u32[]{:S(2)}, u32[]{:S(2)}) collective-permute-start(bf16[24,22,256]{2,1,0:T(8,128)(2,1)S(1)} %get-tuple-element.13), channel_id=1, source_target_pairs={{0,16},{16,0},{1,17},{17,1},{2,18},{18,2},{3,19},{19,3},{4,20},{20... | collective-permute-start | bytes 811016 | tf_op jit(solution)/shard_map/ppermute | solution.py:20
  68.9 5.6 %collective-permute-start.3 = (bf16[32,256]{1,0:T(8,128)(2,1)S(1)}, bf16[32,256]{1,0:T(8,128)(2,1)S(1)}, u32[]{:S(2)}, u32[]{:S(2)}) collective-permute-start(bf16[32,256]{1,0:T(8,128)(2,1)S(1)} %slice_reduce_fusion), channel_id=1, source_target_pairs={{0,384},{384,0},{1,385},{385,1},{2,386},{386,2},{3,387},{387,3},{4... | collective-permute-start | bytes 49160 | tf_op jit(solution)/shard_map/ppermute | solution.py:16
  74.6 1.0 slice-start
  75.9 10.0 %collective-permute-start.5 = (bf16[256,512]{1,0:T(8,128)(2,1)S(1)}, bf16[256,512]{1,0:T(8,128)(2,1)S(1)}, u32[]{:S(2)}, u32[]{:S(2)}) collective-permute-start(bf16[256,512]{1,0:T(8,128)(2,1)S(1)} %get-tuple-element.29), channel_id=1, source_target_pairs={{0,384},{384,0},{1,385},{385,1},{2,386},{386,2},{3,387},{387,3},{4... | collective-permute-start | bytes 786440 | tf_op jit(solution)/shard_map/ppermute | solution.py:16
  77.8 22.5 %all-to-all-start.2 = ((bf16[24,22,256]{2,1,0:T(8,128)(2,1)}), bf16[24,22,256]{2,1,0:T(8,128)(2,1)S(1)}, u32[]{:S(2)}, u32[]{:S(2)}) async-start(bf16[24,22,256]{2,1,0:T(8,128)(2,1)} %add_convert_fusion), calls=%async_computation.2 | async-start | bytes 589824 | tf_op jit(solution)/shard_map/all_to_all | solution.py:149

commit v7 on v6

--- a/solution.py
+++ b/solution.py
@@ -67,6 +67,89 @@
     )(core.reshape(1), both, x_pair)
 
 
+def return_kernel(both_ref, w_ref, send_ref, keep_ref, kv_ref):
+    n_mp, rows, tokens = both_ref.shape
+    feats = w_ref.shape[0]
+    half = rows // 2
+    g = both_ref[:, half:, :].reshape(n_mp * half, tokens)
+    dx = lax.dot_general(g.T, w_ref[...], (((1,), (1,)), ((), ())), preferred_element_type=F32)
+    keep_ref[...] = dx
+    send_ref[:tokens] = dx.astype(BF16)
+    kv = jnp.sum(both_ref[:, :half, :].astype(F32), axis=0).astype(BF16)
+    kv_ref[...] = kv
+    lanes = feats // tokens
+    deep = half // lanes
+    for part in range(lanes):
+        send_ref[tokens:, part * tokens : (part + 1) * tokens] = kv[part * deep : (part + 1) * deep]
+
+
+def return_parts(both, w_full):
+    n_mp, rows, tokens = both.shape
+    feats, width = w_full.shape
+    half = rows // 2
+    vmem = pl.BlockSpec(memory_space=pltpu.VMEM)
+    return pl.pallas_call(
+        return_kernel,
+        out_shape=(
+            jax.ShapeDtypeStruct((tokens + half * tokens // feats, feats), BF16),
+            jax.ShapeDtypeStruct((tokens, feats), F32),
+            jax.ShapeDtypeStruct((half, tokens), BF16),
+        ),
+        in_specs=[vmem, vmem],
+        out_specs=(vmem, vmem, vmem),
+        compiler_params=pltpu.CompilerParams(vmem_limit_bytes=32 * 2**20),
+        cost_estimate=pl.CostEstimate(
+            flops=2 * feats * tokens * width, bytes_accessed=2 * 2**20, transcendentals=0
+        ),
+    )(both, w_full)
+
+
+def home_kernel(seqs, place_ref, keep_ref, recv_ref, kv_ref, dx_ref, out_ref):
+    tokens, feats = keep_ref.shape
+    half = kv_ref.shape[0]
+    span = tokens // seqs
+    lanes = feats // tokens
+    deep = half // lanes
+    left = place_ref[2 * seqs] == 0
+    own = kv_ref[...].astype(F32)
+    other = jnp.concatenate(
+        [
+            recv_ref[tokens:, part * tokens : (part + 1) * tokens].astype(F32)
+            for part in range(lanes)
+        ],
+        axis=0,
+    )
+    low = jnp.where(left, own, other)
+    high = jnp.where(left, other, own)
+    for seq in range(seqs):
+        alive = place_ref[seq] != 0
+        slot = place_ref[seqs + seq]
+        rows = pl.ds(pl.multiple_of(slot * span, span), span)
+        total = keep_ref[rows] + recv_ref[rows].astype(F32)
+        here = slice(seq * span, (seq + 1) * span)
+        dx_ref[here] = jnp.where(alive, total, 0.0).astype(BF16)
+        for at, value in ((0, low), (half, high)):
+            picked = jnp.where(slot == 0, value[:, :span], value[:, span : 2 * span])
+            out_ref[at : at + half, here] = jnp.where(alive, picked, 0.0).astype(BF16)
+
+
+def bring_home(place, keep, received, kv, seqs):
+    tokens, feats = keep.shape
+    half = kv.shape[0]
+    vmem = pl.BlockSpec(memory_space=pltpu.VMEM)
+    return pl.pallas_call(
+        functools.partial(home_kernel, seqs),
+        out_shape=(
+            jax.ShapeDtypeStruct((tokens, feats), BF16),
+            jax.ShapeDtypeStruct((2 * half, tokens), BF16),
+        ),
+        in_specs=[pl.BlockSpec(memory_space=pltpu.SMEM), vmem, vmem, vmem],
+        out_specs=(vmem, vmem),
+        compiler_params=pltpu.CompilerParams(vmem_limit_bytes=32 * 2**20),
+        cost_estimate=pl.CostEstimate(flops=tokens * feats, bytes_accessed=2**20, transcendentals=0),
+    )(place, keep, received, kv)
+
+
 def on_device(x, w, adjoint, mask):
     seqs = mask.shape[0]
     tokens, feats = x.shape
@@ -74,8 +157,7 @@
     wrows, cols = w.shape
     n_z = lax.axis_size("z")
     n_mp = lax.axis_size("mp")
-    own_cols = cols // n_mp
-    half = own_cols // 2
+    half = cols // n_mp // 2
     side = lax.axis_index("pair")
     core = lax.axis_index("core")
 
@@ -95,15 +177,6 @@
         slot0 = jnp.where(first_count >= 1, a0, b0)
         slot1 = jnp.where(first_count == 2, a1, jnp.where(first_count == 1, b0, b1))
         return jnp.stack([slot0, slot1])
-
-    start = jnp.where(side == 0, 0, 2 - count)
-
-    def home(slots):
-        second = start + mask[0]
-        rows0 = jnp.where(start == 0, slots[0], slots[1])
-        rows1 = jnp.where(second == 0, slots[0], slots[1])
-        zero = jnp.zeros_like(rows0)
-        return jnp.stack([jnp.where(alive[0], rows0, zero), jnp.where(alive[1], rows1, zero)])
 
     def pack(value):
         lead = value.shape[:-2]
@@ -140,28 +213,24 @@
     kv = kv.astype(BF16).reshape(n_mp, half, tokens)
     both = jnp.concatenate([kv, jnp.broadcast_to(g_cols, (n_mp, half, tokens))], axis=1)
     both = lax.all_to_all(both, "mp", 0, 0, tiled=True)
-    g_all = both[:, half:].reshape(n_mp * half, tokens)
 
     dw_mine, dw_theirs = weight_blocks(core, both, x_pair, 2 * n_z, wrows)
     dw_theirs, both = lax.optimization_barrier((dw_theirs, both))
     dw_sum = dw_mine + swap_core(dw_theirs).astype(F32)
-    dw_send, g_all, w_full = lax.optimization_barrier((dw_sum.astype(BF16), g_all, w_full))
+
+    send, keep, kv = return_parts(both, w_full)
+    received = swap_pair(send)
+    dw_send, keep = lax.optimization_barrier((dw_sum.astype(BF16), keep))
     dw_parts = lax.all_to_all(dw_send, ("pair", "z"), 0, 0, tiled=True)
     dw_parts = dw_parts.reshape(2, n_z, 2 * wrows, n_mp * half // 2)
     dw_rows = unpack(jnp.sum(dw_parts.astype(F32), axis=1)).reshape(2, wrows, n_mp, half)
     weight_grad = dw_rows.transpose(1, 2, 0, 3).reshape(wrows, cols)
 
-    kv = jnp.sum(both[:, :half].astype(F32), axis=0).astype(BF16)
-    kv_other = swap_pair(kv)
-    kv_cols = jnp.where(side == 0, jnp.concatenate([kv, kv_other]), jnp.concatenate([kv_other, kv]))
-    kv_home = home(kv_cols.reshape(own_cols, seqs, span).transpose(1, 0, 2))
-    kv_values = kv_home.transpose(0, 2, 1).reshape(tokens, own_cols)
-
-    dx = lax.dot_general(g_all, w_full, (((0,), (1,)), ((), ())), preferred_element_type=F32)
-    dx_other = swap_pair(dx.astype(BF16))
-    dx = (dx + dx_other.astype(F32)).astype(BF16)
-    activation_grad = home(dx.reshape(seqs, span, feats)).reshape(tokens, feats)
-    return kv_values, activation_grad, weight_grad
+    start = jnp.where(side == 0, 0, 2 - count)
+    slots = jnp.minimum(jnp.stack([start, start + mask[0]]), 1)
+    place = jnp.concatenate([mask, slots, side.reshape(1)])
+    activation_grad, kv_home = bring_home(place, keep, received, kv, seqs)
+    return kv_home.T, activation_grad, weight_grad
 
 
 def solution(mesh):

time: 102 us -> 95 us (0.931)
  the two profiles are of different devices: /device:TPU:16 before, /device:TPU:1 now
where the time goes in v7:
time: 95 us; the launch traced here: 93.7 us
  starting transfers between devices  39.1 us (41%)
  blocking collectives  25.1 us (26%)
  waiting for transfers between devices  18.8 us (20%)
  local copies, waits for them, and re-layouts  3.76 us (4%)
  between operations  2.35 us (2%)
  Pallas kernels  2.17 us (2%)
  other arithmetic  2.08 us (2%)
    all_to_all x1, blocking collectives, on_device(): both = lax.all_to_all(both, 'mp', 0, 0, tiled=True)  25.1 us
    all_to_all x1, starting transfers between devices, on_device(): lax.all_to_all(w_send.reshape(2 * n_z, 2 * wrows, n_mp * half // 2), ('pa...  17.1 us
    ppermute x2, starting transfers between devices, swap_core(): return lax.ppermute(value, 'core', SWAP)  9.34 us
    ppermute x3, starting transfers between devices, swap_pair(): return lax.ppermute(value, 'pair', SWAP)  8.48 us
    ppermute x3, waiting for transfers between devices, swap_pair(): return lax.ppermute(value, 'pair', SWAP)  7.84 us
    all_to_all x1, waiting for transfers between devices, on_device(): lax.all_to_all(w_send.reshape(2 * n_z, 2 * wrows, n_mp * half // 2), ('pa...  6.73 us
    all_to_all x1, starting transfers between devices, on_device(): dw_parts = lax.all_to_all(dw_send, ('pair', 'z'), 0, 0, tiled=True)  4.26 us
    all_to_all x1, waiting for transfers between devices, on_device(): dw_parts = lax.all_to_all(dw_send, ('pair', 'z'), 0, 0, tiled=True)  2.36 us
  transfers between devices with their start and end apart: 7, of which 5 were waited for; matrix products, arithmetic and copies ran while one was open for 1% of the time, Pallas kernels for 2%

profile of v7, /device:TPU:1, one launch (start us, length us, event | category | flops | bytes accessed | tf_op | source)
XLA Modules:
  0.0 93.7 jit_solution(3448570393169778864)
XLA Ops:
  0.6 0.9 reshape.61
  1.6 0.1 reshape_reshape.9
  1.7 0.7 broadcast_in_dim.15
  2.5 0.0 copy-start.1
  2.5 0.0 copy-start.2
  2.5 17.1 %all-to-all-start = ((bf16[24,22,256]{2,1,0:T(8,128)(2,1)}), bf16[24,22,256]{2,1,0:T(8,128)(2,1)S(1)}, u32[]{:S(2)}, u32[]{:S(2)}) async-start(bf16[24,22,256]{2,1,0:T(8,128)(2,1)} %bitcast.8), calls=%async_computation | async-start | bytes 589824 | tf_op jit(solution)/shard_map/all_to_all | solution.py:194
  19.5 0.0 copy-start
  19.5 0.0 copy-done.1
  19.6 0.2 rev.7
  19.7 0.0 copy-done.2
  19.9 3.2 %collective-permute-start.2 = (bf16[2,32,128]{2,0,1:T(2,128)(2,1)S(1)}, bf16[2,32,128]{2,0,1:T(2,128)(2,1)S(1)}, u32[]{:S(2)}, u32[]{:S(2)}) collective-permute-start(bf16[2,32,128]{2,0,1:T(2,128)(2,1)S(1)} %get-tuple-element.30), channel_id=1, source_target_pairs={{0,384},{384,0},{1,385},{385,1},{2,386},{386,2},{3,387},{387,3},{4... | collective-permute-start | bytes 49160 | tf_op jit(solution)/shard_map/ppermute | solution.py:16
  23.1 0.0 copy-done
  23.1 0.1 reverse_select_fusion
  23.2 2.1 %collective-permute-start.1 = (bf16[2,128,512]{2,1,0:T(8,128)(2,1)S(1)}, bf16[2,128,512]{2,1,0:T(8,128)(2,1)S(1)}, u32[]{:S(2)}, u32[]{:S(2)}) collective-permute-start(bf16[2,128,512]{2,1,0:T(8,128)(2,1)S(1)} %reverse_select_fusion), channel_id=1, source_target_pairs={{0,384},{384,0},{1,385},{385,1},{2,386},{386,2},{3,387},{387,3},{4... | collective-permute-start | bytes 786440 | tf_op jit(solution)/shard_map/ppermute | solution.py:16
  25.3 0.6 reduce_sum.18
  27.2 0.0 collective-permute-done.2
  27.2 0.1 broadcast_select_fusion.10
  27.4 6.7 %all-to-all-done = bf16[24,22,256]{2,1,0:T(8,128)(2,1)S(1)} async-done(((bf16[24,22,256]{2,1,0:T(8,128)(2,1)}), bf16[24,22,256]{2,1,0:T(8,128)(2,1)S(1)}, u32[]{:S(2)}, u32[]{:S(2)}) %all-to-all-start) | async-done | bytes 270368 | tf_op jit(solution)/shard_map/all_to_all | solution.py:194
  34.1 5.6 %collective-permute-start = (bf16[24,22,256]{2,1,0:T(8,128)(2,1)S(1)}, bf16[24,22,256]{2,1,0:T(8,128)(2,1)S(1)}, u32[]{:S(2)}, u32[]{:S(2)}) collective-permute-start(bf16[24,22,256]{2,1,0:T(8,128)(2,1)S(1)} %all-to-all-done), channel_id=1, source_target_pairs={{0,16},{16,0},{1,17},{17,1},{2,18},{18,2},{3,19},{19,3},{4,20},{20... | collective-permute-start | bytes 811016 | tf_op jit(solution)/shard_map/ppermute | solution.py:20
  39.7 0.0 collective-permute-done.1
  39.8 0.1 copy.30
  39.8 1.0 %collective-permute-done = bf16[24,22,256]{2,1,0:T(8,128)(2,1)S(1)} collective-permute-done((bf16[24,22,256]{2,1,0:T(8,128)(2,1)S(1)}, bf16[24,22,256]{2,1,0:T(8,128)(2,1)S(1)}, u32[]{:S(2)}, u32[]{:S(2)}) %collective-permute-start) | collective-permute-done | bytes 270368 | tf_op jit(solution)/shard_map/ppermute | solution.py:20
  40.9 0.1 copy.31
  40.9 0.1 fusion
  41.0 0.4 copy.32
  41.4 0.1 copy.40
  41.5 0.4 convolution_convert_fusion
  42.0 25.1 %all_to_all.15.both_ref = bf16[16,64,256]{2,1,0:T(8,128)(2,1)S(1)} all-to-all(bf16[16,64,256]{2,1,0:T(8,128)(2,1)S(1)} %pad_maximum_fusion), channel_id=1, replica_groups=mesh['pair'=2,'z'=12,'core'=2,'mp'=16] {'mp'}, dimensions={0} | all-to-all | bytes 1048576 | tf_op jit(solution)/shard_map/all_to_all | solution.py:215
  67.0 0.5 shard_map.67
  67.6 3.8 %collective-permute-start.3 = (bf16[24,22,256]{2,1,0:T(8,128)(2,1)S(1)}, bf16[24,22,256]{2,1,0:T(8,128)(2,1)S(1)}, u32[]{:S(2)}, u32[]{:S(2)}) collective-permute-start(bf16[24,22,256]{2,1,0:T(8,128)(2,1)S(1)} %get-tuple-element.16), channel_id=1, source_target_pairs={{0,16},{16,0},{1,17},{17,1},{2,18},{18,2},{3,19},{19,3},{4,20},{20... | collective-permute-start | bytes 811016 | tf_op jit(solution)/shard_map/ppermute | solution.py:20
  71.4 0.3 shard_map.68
  71.7 0.8 collective-permute-done.3
  72.5 0.8 add_convert_fusion
  73.3 4.3 %all-to-all-start.2 = ((bf16[24,22,256]{2,1,0:T(8,128)(2,1)}), bf16[24,22,256]{2,1,0:T(8,128)(2,1)S(1)}, u32[]{:S(2)}, u32[]{:S(2)}) async-start(bf16[24,22,256]{2,1,0:T(8,128)(2,1)} %add_convert_fusion), calls=%async_computation.2 | async-start | bytes 589824 | tf_op jit(solution)/shard_map/all_to_all | solution.py:224
  77.6 3.2 %collective-permute-start.4 = (bf16[272,512]{1,0:T(8,128)(2,1)S(1)}, bf16[272,512]{1,0:T(8,128)(2,1)S(1)}, u32[]{:S(2)}, u32[]{:S(2)}) collective-permute-start(bf16[272,512]{1,0:T(8,128)(2,1)S(1)} %get-tuple-element.20), channel_id=1, source_target_pairs={{0,384},{384,0},{1,385},{385,1},{2,386},{386,2},{3,387},{387,3},{4... | collective-permute-start | bytes 835592 | tf_op jit(solution)/shard_map/ppermute | solution.py:16
  80.8 0.1 add_minimum_fusion
  80.9 0.1 pad_add_fusion.place_ref
  81.0 7.8 %collective-permute-done.4.recv_ref = bf16[272,512]{1,0:T(8,128)(2,1)S(1)} collective-permute-done((bf16[272,512]{1,0:T(8,128)(2,1)S(1)}, bf16[272,512]{1,0:T(8,128)(2,1)S(1)}, u32[]{:S(2)}, u32[]{:S(2)}) %collective-permute-start.4) | collective-permute-done | bytes 278560 | tf_op jit(solution)/shard_map/ppermute | solution.py:16
  88.8 1.3 %shard_map.69 = (bf16[256,512]{1,0:T(8,128)(2,1)}, bf16[64,256]{1,0:T(8,128)(2,1)}) custom-call(s32[5]{0:T(128)S(1)} %pad_add_fusion.place_ref, f32[256,512]{1,0:T(8,128)S(1)} %get-tuple-element.19.keep_ref, bf16[272,512]{1,0:T(8,128)(2,1)S(1)} %collective-permute-done.4.recv_ref, bf16[32,256]{1,0:T(8,128)(2,1)S(1)} %get-tuple-element.21.kv_ref), custom_call_target="tpu_custom_call" | custom-call | flops 131072 | bytes 1048576 | tf_op jit(solution)/shard_map/pallas_call | solution.py:140
  90.1 2.4 %all-to-all-done.2 = bf16[24,22,256]{2,1,0:T(8,128)(2,1)S(1)} async-done(((bf16[24,22,256]{2,1,0:T(8,128)(2,1)}), bf16[24,22,256]{2,1,0:T(8,128)(2,1)S(1)}, u32[]{:S(2)}, u32[]{:S(2)}) %all-to-all-start.2) | async-done | bytes 270368 | tf_op jit(solution)/shard_map/all_to_all | solution.py:224
  92.6 0.1 reshape_reshape.11
  92.7 0.1 copy.39
  92.9 0.9 reshape.68
  (17 shorter events, 0.4 us)
Async XLA Ops:
  2.5 17.1 %copy-start.1 = (bf16[256,64]{0,1:T(8,128)(2,1)S(1)}, bf16[256,64]{0,1:T(8,128)(2,1)}, u32[]{:S(2)}) copy-start(bf16[256,64]{0,1:T(8,128)(2,1)} %param.6) | copy-start | bytes 98308
  2.5 17.3 %copy-start.2 = (s32[2]{0:T(128)S(1)}, s32[2]{0:T(128)}, u32[]{:S(2)}) copy-start(s32[2]{0:T(128)} %param.7) | copy-start | bytes 28
  2.5 31.6 %all-to-all-start = ((bf16[24,22,256]{2,1,0:T(8,128)(2,1)}), bf16[24,22,256]{2,1,0:T(8,128)(2,1)S(1)}, u32[]{:S(2)}, u32[]{:S(2)}) async-start(bf16[24,22,256]{2,1,0:T(8,128)(2,1)} %bitcast.8), calls=%async_computation | async-start | bytes 589824 | tf_op jit(solution)/shard_map/all_to_all | solution.py:194
  19.5 3.6 %copy-start = (bf16[256,512]{1,0:T(8,128)(2,1)S(1)}, bf16[256,512]{1,0:T(8,128)(2,1)}, u32[]{:S(2)}) copy-start(bf16[256,512]{1,0:T(8,128)(2,1)} %param.4) | copy-start | bytes 786436
  19.9 7.3 %collective-permute-start.2 = (bf16[2,32,128]{2,0,1:T(2,128)(2,1)S(1)}, bf16[2,32,128]{2,0,1:T(2,128)(2,1)S(1)}, u32[]{:S(2)}, u32[]{:S(2)}) collective-permute-start(bf16[2,32,128]{2,0,1:T(2,128)(2,1)S(1)} %get-tuple-element.30), channel_id=1, source_target_pairs={{0,384},{384,0},{1,385},{385,1},{2,386},{386,2},{3,387},{387,3},{4... | collective-permute-start | bytes 49160 | tf_op jit(solution)/shard_map/ppermute | solution.py:16
  23.2 16.5 %collective-permute-start.1 = (bf16[2,128,512]{2,1,0:T(8,128)(2,1)S(1)}, bf16[2,128,512]{2,1,0:T(8,128)(2,1)S(1)}, u32[]{:S(2)}, u32[]{:S(2)}) collective-permute-start(bf16[2,128,512]{2,1,0:T(8,128)(2,1)S(1)} %reverse_select_fusion), channel_id=1, source_target_pairs={{0,384},{384,0},{1,385},{385,1},{2,386},{386,2},{3,387},{387,3},{4... | collective-permute-start | bytes 786440 | tf_op jit(solution)/shard_map/ppermute | solution.py:16
  34.1 6.8 %collective-permute-start = (bf16[24,22,256]{2,1,0:T(8,128)(2,1)S(1)}, bf16[24,22,256]{2,1,0:T(8,128)(2,1)S(1)}, u32[]{:S(2)}, u32[]{:S(2)}) collective-permute-start(bf16[24,22,256]{2,1,0:T(8,128)(2,1)S(1)} %all-to-all-done), channel_id=1, source_target_pairs={{0,16},{16,0},{1,17},{17,1},{2,18},{18,2},{3,19},{19,3},{4,20},{20... | collective-permute-start | bytes 811016 | tf_op jit(solution)/shard_map/ppermute | solution.py:20
  67.6 5.0 %collective-permute-start.3 = (bf16[24,22,256]{2,1,0:T(8,128)(2,1)S(1)}, bf16[24,22,256]{2,1,0:T(8,128)(2,1)S(1)}, u32[]{:S(2)}, u32[]{:S(2)}) collective-permute-start(bf16[24,22,256]{2,1,0:T(8,128)(2,1)S(1)} %get-tuple-element.16), channel_id=1, source_target_pairs={{0,16},{16,0},{1,17},{17,1},{2,18},{18,2},{3,19},{19,3},{4,20},{20... | collective-permute-start | bytes 811016 | tf_op jit(solution)/shard_map/ppermute | solution.py:20
  73.3 19.2 %all-to-all-start.2 = ((bf16[24,22,256]{2,1,0:T(8,128)(2,1)}), bf16[24,22,256]{2,1,0:T(8,128)(2,1)S(1)}, u32[]{:S(2)}, u32[]{:S(2)}) async-start(bf16[24,22,256]{2,1,0:T(8,128)(2,1)} %add_convert_fusion), calls=%async_computation.2 | async-start | bytes 589824 | tf_op jit(solution)/shard_map/all_to_all | solution.py:224
  77.6 11.2 %collective-permute-start.4 = (bf16[272,512]{1,0:T(8,128)(2,1)S(1)}, bf16[272,512]{1,0:T(8,128)(2,1)S(1)}, u32[]{:S(2)}, u32[]{:S(2)}) collective-permute-start(bf16[272,512]{1,0:T(8,128)(2,1)S(1)} %get-tuple-element.20), channel_id=1, source_target_pairs={{0,384},{384,0},{1,385},{385,1},{2,386},{386,2},{3,387},{387,3},{4... | collective-permute-start | bytes 835592 | tf_op jit(solution)/shard_map/ppermute | solution.py:16

commit v8 on v7

--- a/solution.py
+++ b/solution.py
@@ -150,6 +150,98 @@
     )(place, keep, received, kv)
 
 
+def halves_matrix(size, half, transposed):
+    here = lax.broadcasted_iota(jnp.int32, (size, size), 1 if transposed else 0)
+    there = lax.broadcasted_iota(jnp.int32, (size, size), 0 if transposed else 1)
+    rest = there % (size // 2)
+    source = (rest // half) * (2 * half) + (there // (size // 2)) * half + rest % half
+    return (here == source).astype(F32).astype(BF16)
+
+
+def spread_kernel(half, n_z, w_ref, out_ref, stage_ref):
+    wrows, cols = w_ref.shape
+    width = cols // 4
+    size = min(256, 2 * width)
+    matrix = halves_matrix(size, half, False)
+    stage_ref[:, 2 * wrows :] = jnp.zeros_like(stage_ref[:, 2 * wrows :])
+    for part in range(2):
+        for group in range(2 * width // size):
+            at = part * 2 * width + group * size
+            split = jnp.dot(w_ref[:, at : at + size], matrix, preferred_element_type=F32)
+            lanes = slice(group * size // 2, (group + 1) * size // 2)
+            for side in range(2):
+                stage_ref[side, pl.ds(part * wrows, wrows), lanes] = split[
+                    :, side * size // 2 : (side + 1) * size // 2
+                ]
+    for side in range(2):
+        block = stage_ref[side, : 2 * wrows].astype(BF16)
+        for z in range(n_z):
+            out_ref[side * n_z + z] = block
+
+
+def spread_weight(w, half, n_z):
+    wrows, cols = w.shape
+    vmem = pl.BlockSpec(memory_space=pltpu.VMEM)
+    padded = -(-2 * wrows // 16) * 16
+    return pl.pallas_call(
+        functools.partial(spread_kernel, half, n_z),
+        out_shape=jax.ShapeDtypeStruct((2 * n_z, 2 * wrows, cols // 4), BF16),
+        in_specs=[vmem],
+        out_specs=vmem,
+        scratch_shapes=[pltpu.VMEM((2, padded, cols // 4), F32)],
+        compiler_params=pltpu.CompilerParams(vmem_limit_bytes=32 * 2**20),
+        cost_estimate=pl.CostEstimate(
+            flops=2 * wrows * cols * 256, bytes_accessed=2**19, transcendentals=0
+        ),
+    )(w)
+
+
+def sum_kernel(half, parts_ref, out_ref, stage_ref):
+    blocks = parts_ref.shape[0]
+    wrows, cols = out_ref.shape
+    width = cols // 4
+    size = min(256, 2 * width)
+    matrix = halves_matrix(size, half, True)
+    for side in range(2):
+        first = side * blocks // 2
+        total = parts_ref[first].astype(F32)
+        for block in range(first + 1, first + blocks // 2):
+            total = total + parts_ref[block].astype(F32)
+        stage_ref[side, pl.ds(0, 2 * wrows)] = total
+    for part in range(2):
+        for group in range(2 * width // size):
+            lanes = slice(group * size // 2, (group + 1) * size // 2)
+            both = jnp.concatenate(
+                [stage_ref[side, pl.ds(part * wrows, wrows), lanes] for side in range(2)], axis=1
+            )
+            top = both.astype(BF16)
+            rest = both - top.astype(F32)
+            middle = rest.astype(BF16)
+            bottom = (rest - middle.astype(F32)).astype(BF16)
+            value = jnp.dot(top, matrix, preferred_element_type=F32)
+            value = value + jnp.dot(middle, matrix, preferred_element_type=F32)
+            value = value + jnp.dot(bottom, matrix, preferred_element_type=F32)
+            at = part * 2 * width + group * size
+            out_ref[:, at : at + size] = value
+
+
+def sum_blocks(parts, half, wrows):
+    width = parts.shape[2]
+    vmem = pl.BlockSpec(memory_space=pltpu.VMEM)
+    padded = -(-2 * wrows // 16) * 16
+    return pl.pallas_call(
+        functools.partial(sum_kernel, half),
+        out_shape=jax.ShapeDtypeStruct((wrows, 4 * width), F32),
+        in_specs=[vmem],
+        out_specs=vmem,
+        scratch_shapes=[pltpu.VMEM((2, padded, width), F32)],
+        compiler_params=pltpu.CompilerParams(vmem_limit_bytes=32 * 2**20),
+        cost_estimate=pl.CostEstimate(
+            flops=6 * wrows * 4 * width * 256, bytes_accessed=2**19, transcendentals=0
+        ),
+    )(parts)
+
+
 def on_device(x, w, adjoint, mask):
     seqs = mask.shape[0]
     tokens, feats = x.shape
@@ -178,22 +270,12 @@
         slot1 = jnp.where(first_count == 2, a1, jnp.where(first_count == 1, b0, b1))
         return jnp.stack([slot0, slot1])
 
-    def pack(value):
-        lead = value.shape[:-2]
-        value = value.reshape(*lead, wrows, 2, n_mp * half // 2)
-        return jnp.swapaxes(value, -3, -2).reshape(*lead, 2 * wrows, n_mp * half // 2)
-
     def unpack(value):
         lead = value.shape[:-2]
         value = value.reshape(*lead, 2, wrows, n_mp * half // 2)
         return jnp.swapaxes(value, -3, -2).reshape(*lead, wrows, n_mp * half)
 
-    w_halves = w.reshape(wrows, n_mp, 2, half).transpose(2, 0, 1, 3).reshape(2, 1, wrows, n_mp * half)
-    w_send = pack(w_halves)
-    w_send = jnp.broadcast_to(w_send, (2, n_z) + w_send.shape[2:])
-    w_mine = lax.all_to_all(
-        w_send.reshape(2 * n_z, 2 * wrows, n_mp * half // 2), ("pair", "z"), 0, 0, tiled=True
-    )
+    w_mine = lax.all_to_all(spread_weight(w, half, n_z), ("pair", "z"), 0, 0, tiled=True)
 
     g = survivor_first(adjoint.T.reshape(2, half, seqs, span).transpose(2, 0, 1, 3))
     g_mine = jnp.where(side == 0, g[:, 0], g[:, 1])
@@ -222,9 +304,7 @@
     received = swap_pair(send)
     dw_send, keep = lax.optimization_barrier((dw_sum.astype(BF16), keep))
     dw_parts = lax.all_to_all(dw_send, ("pair", "z"), 0, 0, tiled=True)
-    dw_parts = dw_parts.reshape(2, n_z, 2 * wrows, n_mp * half // 2)
-    dw_rows = unpack(jnp.sum(dw_parts.astype(F32), axis=1)).reshape(2, wrows, n_mp, half)
-    weight_grad = dw_rows.transpose(1, 2, 0, 3).reshape(wrows, cols)
+    weight_grad = sum_blocks(dw_parts, half, wrows)
 
     start = jnp.where(side == 0, 0, 2 - count)
     slots = jnp.minimum(jnp.stack([start, start + mask[0]]), 1)

time: 95 us -> 94.7 us (level)
  local copies, waits for them, and re-layouts: 3.76 us -> 1.6 us
  Pallas kernels: 2.17 us -> 4.11 us
    pallas_call x0 -> x2, Pallas kernels: none -> 1.94 us  [the longest x1 1.02 us: sum_blocks(): pl.pallas_call(functools.partial(sum_kernel, half), out_shape=jax.ShapeDt...]
    reshape x3 -> x0, local copies, waits for them, and re-layouts: 1.76 us -> none  [the longest x2 0.9 us: on_device(): w.reshape(wrows, n_mp, 2, half).transpose(2, 0, 1, 3)]
where the time goes in v8:
time: 94.7 us; the launch traced here: 93.4 us
  starting transfers between devices  39.1 us (41%)
  blocking collectives  25.1 us (27%)
  waiting for transfers between devices  18.8 us (20%)
  Pallas kernels  4.11 us (4%)
  between operations  2.29 us (2%)
  other arithmetic  2.02 us (2%)
  local copies, waits for them, and re-layouts  1.6 us (2%)
    all_to_all x1, blocking collectives, on_device(): both = lax.all_to_all(both, 'mp', 0, 0, tiled=True)  25.1 us
    all_to_all x1, starting transfers between devices, on_device(): lax.all_to_all(spread_weight(w, half, n_z), ('pair', 'z'), 0, 0, tiled=True)  17.1 us
    ppermute x2, starting transfers between devices, swap_core(): return lax.ppermute(value, 'core', SWAP)  9.28 us
    ppermute x3, starting transfers between devices, swap_pair(): return lax.ppermute(value, 'pair', SWAP)  8.48 us
    ppermute x3, waiting for transfers between devices, swap_pair(): return lax.ppermute(value, 'pair', SWAP)  7.84 us
    all_to_all x1, waiting for transfers between devices, on_device(): lax.all_to_all(spread_weight(w, half, n_z), ('pair', 'z'), 0, 0, tiled=True)  6.73 us
    all_to_all x1, starting transfers between devices, on_device(): dw_parts = lax.all_to_all(dw_send, ('pair', 'z'), 0, 0, tiled=True)  4.26 us
    all_to_all x1, waiting for transfers between devices, on_device(): dw_parts = lax.all_to_all(dw_send, ('pair', 'z'), 0, 0, tiled=True)  2.36 us
  transfers between devices with their start and end apart: 7, of which 5 were waited for; matrix products, arithmetic and copies ran while one was open for 1% of the time, Pallas kernels for 2%

profile of v8, /device:TPU:1, one launch (start us, length us, event | category | flops | bytes accessed | tf_op | source)
XLA Modules:
  0.0 93.4 jit_solution(17765260526675550615)
XLA Ops:
  0.6 0.0 copy-start
  0.6 0.7 copy-done
  1.4 0.9 shard_map.67
  2.3 0.0 copy-start.2
  2.3 0.0 copy-start.3
  2.3 17.1 %all-to-all-start = ((bf16[24,22,256]{2,1,0:T(8,128)(2,1)}), bf16[24,22,256]{2,1,0:T(8,128)(2,1)S(1)}, u32[]{:S(2)}, u32[]{:S(2)}) async-start(bf16[24,22,256]{2,1,0:T(8,128)(2,1)} %shard_map.67), calls=%async_computation | async-start | bytes 589824 | tf_op jit(solution)/shard_map/all_to_all | solution.py:278
  19.4 0.0 copy-start.1
  19.4 0.0 copy-done.2
  19.4 0.2 rev.7
  19.6 0.0 copy-done.3
  19.7 3.2 %collective-permute-start.2 = (bf16[2,32,128]{2,0,1:T(2,128)(2,1)S(1)}, bf16[2,32,128]{2,0,1:T(2,128)(2,1)S(1)}, u32[]{:S(2)}, u32[]{:S(2)}) collective-permute-start(bf16[2,32,128]{2,0,1:T(2,128)(2,1)S(1)} %get-tuple-element.30), channel_id=1, source_target_pairs={{0,384},{384,0},{1,385},{385,1},{2,386},{386,2},{3,387},{387,3},{4... | collective-permute-start | bytes 49160 | tf_op jit(solution)/shard_map/ppermute | solution.py:16
  23.0 0.0 copy-done.1
  23.0 0.1 reverse_select_fusion
  23.0 2.1 %collective-permute-start.1 = (bf16[2,128,512]{2,1,0:T(8,128)(2,1)S(1)}, bf16[2,128,512]{2,1,0:T(8,128)(2,1)S(1)}, u32[]{:S(2)}, u32[]{:S(2)}) collective-permute-start(bf16[2,128,512]{2,1,0:T(8,128)(2,1)S(1)} %reverse_select_fusion), channel_id=1, source_target_pairs={{0,384},{384,0},{1,385},{385,1},{2,386},{386,2},{3,387},{387,3},{4... | collective-permute-start | bytes 786440 | tf_op jit(solution)/shard_map/ppermute | solution.py:16
  25.1 0.6 reduce_sum.9
  27.1 0.0 collective-permute-done.2
  27.1 0.1 broadcast_select_fusion.10
  27.2 6.7 %all-to-all-done = bf16[24,22,256]{2,1,0:T(8,128)(2,1)S(1)} async-done(((bf16[24,22,256]{2,1,0:T(8,128)(2,1)}), bf16[24,22,256]{2,1,0:T(8,128)(2,1)S(1)}, u32[]{:S(2)}, u32[]{:S(2)}) %all-to-all-start) | async-done | bytes 270368 | tf_op jit(solution)/shard_map/all_to_all | solution.py:278
  33.9 5.6 %collective-permute-start = (bf16[24,22,256]{2,1,0:T(8,128)(2,1)S(1)}, bf16[24,22,256]{2,1,0:T(8,128)(2,1)S(1)}, u32[]{:S(2)}, u32[]{:S(2)}) collective-permute-start(bf16[24,22,256]{2,1,0:T(8,128)(2,1)S(1)} %all-to-all-done), channel_id=1, source_target_pairs={{0,16},{16,0},{1,17},{17,1},{2,18},{18,2},{3,19},{19,3},{4,20},{20... | collective-permute-start | bytes 811016 | tf_op jit(solution)/shard_map/ppermute | solution.py:20
  39.5 0.0 collective-permute-done.1
  39.6 0.1 copy.18
  39.7 1.0 %collective-permute-done = bf16[24,22,256]{2,1,0:T(8,128)(2,1)S(1)} collective-permute-done((bf16[24,22,256]{2,1,0:T(8,128)(2,1)S(1)}, bf16[24,22,256]{2,1,0:T(8,128)(2,1)S(1)}, u32[]{:S(2)}, u32[]{:S(2)}) %collective-permute-start) | collective-permute-done | bytes 270368 | tf_op jit(solution)/shard_map/ppermute | solution.py:20
  40.7 0.1 copy.19
  40.8 0.1 fusion
  40.9 0.4 copy.20
  41.3 0.1 copy.25
  41.4 0.4 convolution_convert_fusion
  41.8 25.1 %all_to_all.15.both_ref = bf16[16,64,256]{2,1,0:T(8,128)(2,1)S(1)} all-to-all(bf16[16,64,256]{2,1,0:T(8,128)(2,1)S(1)} %pad_maximum_fusion), channel_id=1, replica_groups=mesh['pair'=2,'z'=12,'core'=2,'mp'=16] {'mp'}, dimensions={0} | all-to-all | bytes 1048576 | tf_op jit(solution)/shard_map/all_to_all | solution.py:297
  67.0 0.5 shard_map.68
  67.5 3.7 %collective-permute-start.3 = (bf16[24,22,256]{2,1,0:T(8,128)(2,1)S(1)}, bf16[24,22,256]{2,1,0:T(8,128)(2,1)S(1)}, u32[]{:S(2)}, u32[]{:S(2)}) collective-permute-start(bf16[24,22,256]{2,1,0:T(8,128)(2,1)S(1)} %get-tuple-element.16), channel_id=1, source_target_pairs={{0,16},{16,0},{1,17},{17,1},{2,18},{18,2},{3,19},{19,3},{4,20},{20... | collective-permute-start | bytes 811016 | tf_op jit(solution)/shard_map/ppermute | solution.py:20
  71.2 0.3 shard_map.69
  71.6 0.8 collective-permute-done.3
  72.4 0.8 add_convert_fusion
  73.2 4.3 %all-to-all-start.2 = ((bf16[24,22,256]{2,1,0:T(8,128)(2,1)}), bf16[24,22,256]{2,1,0:T(8,128)(2,1)S(1)}, u32[]{:S(2)}, u32[]{:S(2)}) async-start(bf16[24,22,256]{2,1,0:T(8,128)(2,1)} %add_convert_fusion), calls=%async_computation.2 | async-start | bytes 589824 | tf_op jit(solution)/shard_map/all_to_all | solution.py:306
  77.4 3.2 %collective-permute-start.4 = (bf16[272,512]{1,0:T(8,128)(2,1)S(1)}, bf16[272,512]{1,0:T(8,128)(2,1)S(1)}, u32[]{:S(2)}, u32[]{:S(2)}) collective-permute-start(bf16[272,512]{1,0:T(8,128)(2,1)S(1)} %get-tuple-element.20), channel_id=1, source_target_pairs={{0,384},{384,0},{1,385},{385,1},{2,386},{386,2},{3,387},{387,3},{4... | collective-permute-start | bytes 835592 | tf_op jit(solution)/shard_map/ppermute | solution.py:16
  80.7 0.1 add_minimum_fusion
  80.8 0.1 pad_add_fusion.place_ref
  80.8 7.8 %collective-permute-done.4.recv_ref = bf16[272,512]{1,0:T(8,128)(2,1)S(1)} collective-permute-done((bf16[272,512]{1,0:T(8,128)(2,1)S(1)}, bf16[272,512]{1,0:T(8,128)(2,1)S(1)}, u32[]{:S(2)}, u32[]{:S(2)}) %collective-permute-start.4) | collective-permute-done | bytes 278560 | tf_op jit(solution)/shard_map/ppermute | solution.py:16
  88.7 1.3 %shard_map.70 = (bf16[256,512]{1,0:T(8,128)(2,1)}, bf16[64,256]{1,0:T(8,128)(2,1)}) custom-call(s32[5]{0:T(128)S(1)} %pad_add_fusion.place_ref, f32[256,512]{1,0:T(8,128)S(1)} %get-tuple-element.19.keep_ref, bf16[272,512]{1,0:T(8,128)(2,1)S(1)} %collective-permute-done.4.recv_ref, bf16[32,256]{1,0:T(8,128)(2,1)S(1)} %get-tuple-element.21.kv_ref), custom_call_target="tpu_custom_call" | custom-call | flops 131072 | bytes 1048576 | tf_op jit(solution)/shard_map/pallas_call | solution.py:140
  90.0 2.4 %all-to-all-done.2.parts_ref = bf16[24,22,256]{2,1,0:T(8,128)(2,1)S(1)} async-done(((bf16[24,22,256]{2,1,0:T(8,128)(2,1)}), bf16[24,22,256]{2,1,0:T(8,128)(2,1)S(1)}, u32[]{:S(2)}, u32[]{:S(2)}) %all-to-all-start.2) | async-done | bytes 270368 | tf_op jit(solution)/shard_map/all_to_all | solution.py:306
  92.4 1.0 %shard_map.71 = f32[11,1024]{1,0:T(8,128)} custom-call(bf16[24,22,256]{2,1,0:T(8,128)(2,1)S(1)} %all-to-all-done.2.parts_ref), custom_call_target="tpu_custom_call" | custom-call | flops 17301504 | bytes 524288 | tf_op jit(solution)/shard_map/pallas_call | solution.py:232
  (11 shorter events, 0.3 us)
Async XLA Ops:
  0.6 0.8 copy-start
  2.3 17.1 %copy-start.2 = (bf16[256,64]{0,1:T(8,128)(2,1)S(1)}, bf16[256,64]{0,1:T(8,128)(2,1)}, u32[]{:S(2)}) copy-start(bf16[256,64]{0,1:T(8,128)(2,1)} %param.6) | copy-start | bytes 98308
  2.3 17.3 %copy-start.3 = (s32[2]{0:T(128)S(1)}, s32[2]{0:T(128)}, u32[]{:S(2)}) copy-start(s32[2]{0:T(128)} %param.7) | copy-start | bytes 28
  2.3 31.6 %all-to-all-start = ((bf16[24,22,256]{2,1,0:T(8,128)(2,1)}), bf16[24,22,256]{2,1,0:T(8,128)(2,1)S(1)}, u32[]{:S(2)}, u32[]{:S(2)}) async-start(bf16[24,22,256]{2,1,0:T(8,128)(2,1)} %shard_map.67), calls=%async_computation | async-start | bytes 589824 | tf_op jit(solution)/shard_map/all_to_all | solution.py:278
  19.4 3.6 %copy-start.1 = (bf16[256,512]{1,0:T(8,128)(2,1)S(1)}, bf16[256,512]{1,0:T(8,128)(2,1)}, u32[]{:S(2)}) copy-start(bf16[256,512]{1,0:T(8,128)(2,1)} %param.4) | copy-start | bytes 786436
  19.7 7.3 %collective-permute-start.2 = (bf16[2,32,128]{2,0,1:T(2,128)(2,1)S(1)}, bf16[2,32,128]{2,0,1:T(2,128)(2,1)S(1)}, u32[]{:S(2)}, u32[]{:S(2)}) collective-permute-start(bf16[2,32,128]{2,0,1:T(2,128)(2,1)S(1)} %get-tuple-element.30), channel_id=1, source_target_pairs={{0,384},{384,0},{1,385},{385,1},{2,386},{386,2},{3,387},{387,3},{4... | collective-permute-start | bytes 49160 | tf_op jit(solution)/shard_map/ppermute | solution.py:16
  23.0 16.5 %collective-permute-start.1 = (bf16[2,128,512]{2,1,0:T(8,128)(2,1)S(1)}, bf16[2,128,512]{2,1,0:T(8,128)(2,1)S(1)}, u32[]{:S(2)}, u32[]{:S(2)}) collective-permute-start(bf16[2,128,512]{2,1,0:T(8,128)(2,1)S(1)} %reverse_select_fusion), channel_id=1, source_target_pairs={{0,384},{384,0},{1,385},{385,1},{2,386},{386,2},{3,387},{387,3},{4... | collective-permute-start | bytes 786440 | tf_op jit(solution)/shard_map/ppermute | solution.py:16
  33.9 6.8 %collective-permute-start = (bf16[24,22,256]{2,1,0:T(8,128)(2,1)S(1)}, bf16[24,22,256]{2,1,0:T(8,128)(2,1)S(1)}, u32[]{:S(2)}, u32[]{:S(2)}) collective-permute-start(bf16[24,22,256]{2,1,0:T(8,128)(2,1)S(1)} %all-to-all-done), channel_id=1, source_target_pairs={{0,16},{16,0},{1,17},{17,1},{2,18},{18,2},{3,19},{19,3},{4,20},{20... | collective-permute-start | bytes 811016 | tf_op jit(solution)/shard_map/ppermute | solution.py:20
  67.5 4.9 %collective-permute-start.3 = (bf16[24,22,256]{2,1,0:T(8,128)(2,1)S(1)}, bf16[24,22,256]{2,1,0:T(8,128)(2,1)S(1)}, u32[]{:S(2)}, u32[]{:S(2)}) collective-permute-start(bf16[24,22,256]{2,1,0:T(8,128)(2,1)S(1)} %get-tuple-element.16), channel_id=1, source_target_pairs={{0,16},{16,0},{1,17},{17,1},{2,18},{18,2},{3,19},{19,3},{4,20},{20... | collective-permute-start | bytes 811016 | tf_op jit(solution)/shard_map/ppermute | solution.py:20
  73.2 19.2 %all-to-all-start.2 = ((bf16[24,22,256]{2,1,0:T(8,128)(2,1)}), bf16[24,22,256]{2,1,0:T(8,128)(2,1)S(1)}, u32[]{:S(2)}, u32[]{:S(2)}) async-start(bf16[24,22,256]{2,1,0:T(8,128)(2,1)} %add_convert_fusion), calls=%async_computation.2 | async-start | bytes 589824 | tf_op jit(solution)/shard_map/all_to_all | solution.py:306
  77.4 11.2 %collective-permute-start.4 = (bf16[272,512]{1,0:T(8,128)(2,1)S(1)}, bf16[272,512]{1,0:T(8,128)(2,1)S(1)}, u32[]{:S(2)}, u32[]{:S(2)}) collective-permute-start(bf16[272,512]{1,0:T(8,128)(2,1)S(1)} %get-tuple-element.20), channel_id=1, source_target_pairs={{0,384},{384,0},{1,385},{385,1},{2,386},{386,2},{3,387},{387,3},{4... | collective-permute-start | bytes 835592 | tf_op jit(solution)/shard_map/ppermute | solution.py:16

commit v9 on v8

--- a/solution.py
+++ b/solution.py
@@ -10,6 +10,7 @@
 BF16 = jnp.bfloat16
 F32 = jnp.float32
 SWAP = [(0, 1), (1, 0)]
+HALF = 32
 
 
 def swap_pair(value):
@@ -20,16 +21,28 @@
     return lax.ppermute(value, "core", SWAP)
 
 
+def ordered(both_ref):
+    n_x, rows, _ = both_ref.shape
+    half = rows // 2
+    n_y = half // HALF
+    return jnp.concatenate(
+        [
+            both_ref[ix, half + iy * HALF : half + (iy + 1) * HALF]
+            for iy in range(n_y)
+            for ix in range(n_x)
+        ],
+        axis=0,
+    )
+
+
 def weight_kernel(blocks, wrows, core_ref, both_ref, x_ref, mine_ref, theirs_ref, acc_ref, stage_ref):
     tokens, feats = x_ref.shape
-    n_mp, rows, _ = both_ref.shape
-    half = rows // 2
     width = acc_ref.shape[2]
-    groups = width // half
     first_core = core_ref[0] == 0
     x_turned = x_ref[...].T
+    g_all = ordered(both_ref)
     for part in range(2):
-        g = both_ref[part * groups : (part + 1) * groups, half:, :].reshape(width, tokens)
+        g = g_all[part * width : (part + 1) * width]
         acc_ref[part, :feats] = lax.dot_general(
             x_turned, g, (((1,), (1,)), ((), ())), preferred_element_type=F32
         )
@@ -46,8 +59,7 @@
 
 def weight_blocks(core, both, x_pair, blocks, wrows):
     tokens, feats = x_pair.shape
-    n_mp, rows, _ = both.shape
-    width = n_mp * rows // 4
+    width = both.shape[0] * both.shape[1] // 4
     vmem = pl.BlockSpec(memory_space=pltpu.VMEM)
     padded = -(-2 * wrows // 16) * 16
     shape = (blocks, 2 * wrows, width)
@@ -67,36 +79,25 @@
     )(core.reshape(1), both, x_pair)
 
 
-def return_kernel(both_ref, w_ref, send_ref, keep_ref, kv_ref):
-    n_mp, rows, tokens = both_ref.shape
-    feats = w_ref.shape[0]
-    half = rows // 2
-    g = both_ref[:, half:, :].reshape(n_mp * half, tokens)
+def return_kernel(both_ref, w_ref, send_ref, keep_ref):
+    g = ordered(both_ref)
     dx = lax.dot_general(g.T, w_ref[...], (((1,), (1,)), ((), ())), preferred_element_type=F32)
     keep_ref[...] = dx
-    send_ref[:tokens] = dx.astype(BF16)
-    kv = jnp.sum(both_ref[:, :half, :].astype(F32), axis=0).astype(BF16)
-    kv_ref[...] = kv
-    lanes = feats // tokens
-    deep = half // lanes
-    for part in range(lanes):
-        send_ref[tokens:, part * tokens : (part + 1) * tokens] = kv[part * deep : (part + 1) * deep]
+    send_ref[...] = dx.astype(BF16)
 
 
 def return_parts(both, w_full):
-    n_mp, rows, tokens = both.shape
+    tokens = both.shape[2]
     feats, width = w_full.shape
-    half = rows // 2
     vmem = pl.BlockSpec(memory_space=pltpu.VMEM)
     return pl.pallas_call(
         return_kernel,
         out_shape=(
-            jax.ShapeDtypeStruct((tokens + half * tokens // feats, feats), BF16),
+            jax.ShapeDtypeStruct((tokens, feats), BF16),
             jax.ShapeDtypeStruct((tokens, feats), F32),
-            jax.ShapeDtypeStruct((half, tokens), BF16),
         ),
         in_specs=[vmem, vmem],
-        out_specs=(vmem, vmem, vmem),
+        out_specs=(vmem, vmem),
         compiler_params=pltpu.CompilerParams(vmem_limit_bytes=32 * 2**20),
         cost_estimate=pl.CostEstimate(
             flops=2 * feats * tokens * width, bytes_accessed=2 * 2**20, transcendentals=0
@@ -104,21 +105,13 @@
     )(both, w_full)
 
 
-def home_kernel(seqs, place_ref, keep_ref, recv_ref, kv_ref, dx_ref, out_ref):
+def home_kernel(seqs, place_ref, keep_ref, recv_ref, kv_ref, other_ref, dx_ref, out_ref):
     tokens, feats = keep_ref.shape
     half = kv_ref.shape[0]
     span = tokens // seqs
-    lanes = feats // tokens
-    deep = half // lanes
     left = place_ref[2 * seqs] == 0
     own = kv_ref[...].astype(F32)
-    other = jnp.concatenate(
-        [
-            recv_ref[tokens:, part * tokens : (part + 1) * tokens].astype(F32)
-            for part in range(lanes)
-        ],
-        axis=0,
-    )
+    other = other_ref[...].astype(F32)
     low = jnp.where(left, own, other)
     high = jnp.where(left, other, own)
     for seq in range(seqs):
@@ -133,7 +126,7 @@
             out_ref[at : at + half, here] = jnp.where(alive, picked, 0.0).astype(BF16)
 
 
-def bring_home(place, keep, received, kv, seqs):
+def bring_home(place, keep, received, kv, kv_other, seqs):
     tokens, feats = keep.shape
     half = kv.shape[0]
     vmem = pl.BlockSpec(memory_space=pltpu.VMEM)
@@ -143,11 +136,11 @@
             jax.ShapeDtypeStruct((tokens, feats), BF16),
             jax.ShapeDtypeStruct((2 * half, tokens), BF16),
         ),
-        in_specs=[pl.BlockSpec(memory_space=pltpu.SMEM), vmem, vmem, vmem],
+        in_specs=[pl.BlockSpec(memory_space=pltpu.SMEM), vmem, vmem, vmem, vmem],
         out_specs=(vmem, vmem),
         compiler_params=pltpu.CompilerParams(vmem_limit_bytes=32 * 2**20),
         cost_estimate=pl.CostEstimate(flops=tokens * feats, bytes_accessed=2**20, transcendentals=0),
-    )(place, keep, received, kv)
+    )(place, keep, received, kv, kv_other)
 
 
 def halves_matrix(size, half, transposed):
@@ -242,33 +235,116 @@
     )(parts)
 
 
+def swap_kernel(mask_ref, x_ref, g_ref, send_ref):
+    tokens, feats = x_ref.shape
+    span = tokens // 2
+    lanes = feats // tokens
+    deep = HALF // lanes
+    skip = mask_ref[0] == 0
+    left = mask_ref[2] == 0
+    for seq in range(2):
+        source = jnp.where(skip, 1 - seq, seq)
+        rows = pl.ds(pl.multiple_of(source * span, span), span)
+        send_ref[seq * span : (seq + 1) * span] = x_ref[rows]
+    g = jnp.where(left, g_ref[HALF:].astype(F32), g_ref[:HALF].astype(F32))
+    g0 = jnp.where(skip, g[:, span:], g[:, :span])
+    g1 = jnp.where(skip, g[:, :span], g[:, span:])
+    g = jnp.concatenate([g0, g1], axis=1).astype(BF16)
+    for part in range(lanes):
+        send_ref[tokens:, part * tokens : (part + 1) * tokens] = g[part * deep : (part + 1) * deep]
+
+
+def prepare_swap(state, x, g):
+    tokens, feats = x.shape
+    vmem = pl.BlockSpec(memory_space=pltpu.VMEM)
+    return pl.pallas_call(
+        swap_kernel,
+        out_shape=jax.ShapeDtypeStruct((tokens + HALF * tokens // feats, feats), BF16),
+        in_specs=[pl.BlockSpec(memory_space=pltpu.SMEM), vmem, vmem],
+        out_specs=vmem,
+        compiler_params=pltpu.CompilerParams(vmem_limit_bytes=32 * 2**20),
+        cost_estimate=pl.CostEstimate(flops=2**18, bytes_accessed=2**19, transcendentals=0),
+    )(state, x, g)
+
+
+def compact_kernel(mask_ref, x_ref, g_ref, recv_ref, x_out, g_out):
+    tokens, feats = x_ref.shape
+    span = tokens // 2
+    lanes = feats // tokens
+    deep = HALF // lanes
+    count = mask_ref[0] + mask_ref[1]
+    skip = jnp.where(mask_ref[0] == 0, 1, 0)
+    left = mask_ref[2] == 0
+    two = count == 2
+    some = count >= 1
+    mine = (jnp.logical_or(jnp.logical_and(left, some), two), jnp.logical_or(jnp.logical_and(left, two), jnp.logical_and(jnp.logical_not(left), some)))
+    own_at = (jnp.where(two, 0, skip), jnp.where(jnp.logical_or(left, two), 1, skip))
+    other_at = (0, jnp.where(count == 1, 0, 1))
+    own = jnp.where(left, g_ref[:HALF].astype(F32), g_ref[HALF:].astype(F32))
+    other = jnp.concatenate(
+        [
+            recv_ref[tokens:, part * tokens : (part + 1) * tokens].astype(F32)
+            for part in range(lanes)
+        ],
+        axis=0,
+    )
+    for slot in range(2):
+        here = slice(slot * span, (slot + 1) * span)
+        own_rows = pl.ds(pl.multiple_of(own_at[slot] * span, span), span)
+        other_rows = pl.ds(pl.multiple_of(other_at[slot] * span, span), span)
+
+        @pl.when(mine[slot])
+        def _():
+            x_out[here] = x_ref[own_rows]
+            g_out[:, here] = jnp.where(own_at[slot] == 0, own[:, :span], own[:, span:]).astype(BF16)
+
+        @pl.when(jnp.logical_not(mine[slot]))
+        def _():
+            x_out[here] = recv_ref[other_rows]
+            g_out[:, here] = jnp.where(other_at[slot] == 0, other[:, :span], other[:, span:]).astype(BF16)
+
+
+def compact_pair(state, x, g, received):
+    tokens, feats = x.shape
+    vmem = pl.BlockSpec(memory_space=pltpu.VMEM)
+    return pl.pallas_call(
+        compact_kernel,
+        out_shape=(
+            jax.ShapeDtypeStruct((tokens, feats), BF16),
+            jax.ShapeDtypeStruct((HALF, tokens), BF16),
+        ),
+        in_specs=[pl.BlockSpec(memory_space=pltpu.SMEM), vmem, vmem, vmem],
+        out_specs=(vmem, vmem),
+        compiler_params=pltpu.CompilerParams(vmem_limit_bytes=32 * 2**20),
+        cost_estimate=pl.CostEstimate(flops=2**18, bytes_accessed=2**19, transcendentals=0),
+    )(state, x, g, received)
+
+
+def gather_doubling(value, axis_name, n):
+    index = lax.axis_index(axis_name)
+    bits = n.bit_length() - 1
+    value = value.reshape((1,) * bits + value.shape)
+    for axis in range(bits):
+        step = n >> (axis + 1)
+        other = lax.ppermute(value, axis_name, [(i, i ^ step) for i in range(n)])
+        upper = (index & step) != 0
+        value = jnp.concatenate(
+            [jnp.where(upper, other, value), jnp.where(upper, value, other)], axis=axis
+        )
+    return value
+
+
 def on_device(x, w, adjoint, mask):
     seqs = mask.shape[0]
     tokens, feats = x.shape
-    span = tokens // seqs
     wrows, cols = w.shape
     n_z = lax.axis_size("z")
-    n_mp = lax.axis_size("mp")
+    n_y, n_x = lax.axis_size("y_hi"), lax.axis_size("x")
+    n_mp = n_y * n_x
     half = cols // n_mp // 2
     side = lax.axis_index("pair")
     core = lax.axis_index("core")
-
-    alive = mask != 0
     count = jnp.sum(mask)
-    first_count = jnp.where(side == 0, count, 2 - count)
-    skip_first = jnp.logical_not(alive[0])
-
-    def survivor_first(value):
-        return jnp.where(skip_first, value[::-1], value)
-
-    def compact(own, other):
-        a0 = jnp.where(side == 0, own[0], other[0])
-        a1 = jnp.where(side == 0, own[1], other[1])
-        b0 = jnp.where(side == 0, other[0], own[0])
-        b1 = jnp.where(side == 0, other[1], own[1])
-        slot0 = jnp.where(first_count >= 1, a0, b0)
-        slot1 = jnp.where(first_count == 2, a1, jnp.where(first_count == 1, b0, b1))
-        return jnp.stack([slot0, slot1])
 
     def unpack(value):
         lead = value.shape[:-2]
@@ -277,51 +353,52 @@
 
     w_mine = lax.all_to_all(spread_weight(w, half, n_z), ("pair", "z"), 0, 0, tiled=True)
 
-    g = survivor_first(adjoint.T.reshape(2, half, seqs, span).transpose(2, 0, 1, 3))
-    g_mine = jnp.where(side == 0, g[:, 0], g[:, 1])
-    g_theirs = jnp.where(side == 0, g[:, 1], g[:, 0])
-    xs = survivor_first(x.reshape(seqs, span, feats))
-    g_other = swap_pair(g_theirs)
-    x_other = swap_pair(xs)
-    g_pair = compact(g_mine, g_other)
-    g_cols = g_pair.transpose(1, 0, 2).reshape(1, half, tokens)
-    x_pair = compact(xs, x_other).reshape(tokens, feats)
+    state = jnp.concatenate([mask, side.reshape(1)])
+    g = adjoint.T
+    received = swap_pair(prepare_swap(state, x, g))
+    x_pair, g_cols = compact_pair(state, x, g, received)
+    g_rows = gather_doubling(g_cols, "y_hi", n_y).reshape(1, n_y * half, tokens)
 
     w_theirs = swap_core(w_mine)
     w_cores = jnp.where(core == 0, jnp.stack([w_mine, w_theirs], 1), jnp.stack([w_theirs, w_mine], 1))
     w_full = unpack(w_cores).reshape(4 * n_z * wrows, n_mp * half)[:feats]
 
     kv = lax.dot_general(w_full, x_pair, (((0,), (1,)), ((), ())), preferred_element_type=F32)
-    kv = kv.astype(BF16).reshape(n_mp, half, tokens)
-    both = jnp.concatenate([kv, jnp.broadcast_to(g_cols, (n_mp, half, tokens))], axis=1)
-    both = lax.all_to_all(both, "mp", 0, 0, tiled=True)
+    kv = kv.astype(BF16).reshape(n_y, n_x, half, tokens).transpose(1, 0, 2, 3)
+    kv = kv.reshape(n_x, n_y * half, tokens)
+    both = jnp.concatenate([kv, jnp.broadcast_to(g_rows, kv.shape)], axis=1)
+    both = lax.all_to_all(both, "x", 0, 0, tiled=True)
+    kv = jnp.sum(both[:, : n_y * half].astype(F32), axis=0).astype(BF16)
+    kv_parts = lax.all_to_all(kv.reshape(n_y, half, tokens), "y_hi", 0, 0, tiled=True)
 
     dw_mine, dw_theirs = weight_blocks(core, both, x_pair, 2 * n_z, wrows)
     dw_theirs, both = lax.optimization_barrier((dw_theirs, both))
     dw_sum = dw_mine + swap_core(dw_theirs).astype(F32)
 
-    send, keep, kv = return_parts(both, w_full)
+    send, keep = return_parts(both, w_full)
     received = swap_pair(send)
-    dw_send, keep = lax.optimization_barrier((dw_sum.astype(BF16), keep))
+    dw_send, kv_parts = lax.optimization_barrier((dw_sum.astype(BF16), kv_parts))
     dw_parts = lax.all_to_all(dw_send, ("pair", "z"), 0, 0, tiled=True)
     weight_grad = sum_blocks(dw_parts, half, wrows)
 
     start = jnp.where(side == 0, 0, 2 - count)
     slots = jnp.minimum(jnp.stack([start, start + mask[0]]), 1)
     place = jnp.concatenate([mask, slots, side.reshape(1)])
-    activation_grad, kv_home = bring_home(place, keep, received, kv, seqs)
+    kv = jnp.sum(kv_parts.astype(F32), axis=0).astype(BF16)
+    activation_grad, kv_home = bring_home(place, keep, received, kv, swap_pair(kv), seqs)
     return kv_home.T, activation_grad, weight_grad
 
 
 def solution(mesh):
     n_dp, n_mp = mesh.devices.shape
-    names = ("pair", "z", "core", "mp")
-    split = Mesh(mesh.devices.reshape(2, n_dp // 4, 2, n_mp), names)
-    dp = ("pair", "z", "core")
+    n_y = 1 << ((n_mp.bit_length() - 1) // 2)
+    names = ("pair", "z", "core", "y_hi", "x")
+    split = Mesh(mesh.devices.reshape(2, n_dp // 4, 2, n_y, n_mp // n_y), names)
+    dp, mp = names[:3], names[3:]
     return jax.shard_map(
         on_device,
         mesh=split,
-        in_specs=(P(dp, "mp"), P((*dp, "mp"), None), P(dp, "mp"), P(dp)),
-        out_specs=(P(dp, "mp"), P(dp, "mp"), P((*dp, "mp"), None)),
+        in_specs=(P(dp, mp), P((*dp, *mp), None), P(dp, mp), P(dp)),
+        out_specs=(P(dp, mp), P(dp, mp), P((*dp, *mp), None)),
         check_vma=False,
     )

time: 94.7 us -> 108 us (1.14)
  the two profiles are of different devices: /device:TPU:1 before, /device:TPU:2 now
where the time goes in v9:
time: 108 us
  starting transfers between devices  55.2 us (51%)
  waiting for transfers between devices  27.9 us (26%)
  blocking collectives  12.9 us (12%)
  Pallas kernels  5.25 us (5%)
  other arithmetic  2.46 us (2%)
  local copies, waits for them, and re-layouts  2.09 us (2%)
  between operations  1.57 us (1%)
    all_to_all x1, starting transfers between devices, on_device(): lax.all_to_all(spread_weight(w, half, n_z), ('pair', 'z'), 0, 0, tiled=True)  16.5 us
    ppermute x3, waiting for transfers between devices, swap_pair(): return lax.ppermute(value, 'pair', SWAP)  13.3 us
    all_to_all x1, blocking collectives, on_device(): both = lax.all_to_all(both, 'x', 0, 0, tiled=True)  12.9 us
    ppermute x2, starting transfers between devices, gather_doubling(): other = lax.ppermute(value, axis_name, [(i, i ^ step) for i in range(n)])  11.3 us
    ppermute x3, starting transfers between devices, swap_pair(): return lax.ppermute(value, 'pair', SWAP)  9.6 us
    all_to_all x1, starting transfers between devices, on_device(): dw_parts = lax.all_to_all(dw_send, ('pair', 'z'), 0, 0, tiled=True)  9.48 us
    all_to_all x1, waiting for transfers between devices, on_device(): lax.all_to_all(kv.reshape(n_y, half, tokens), 'y_hi', 0, 0, tiled=True)  7.62 us
    all_to_all x1, starting transfers between devices, on_device(): lax.all_to_all(kv.reshape(n_y, half, tokens), 'y_hi', 0, 0, tiled=True)  4.4 us
  transfers between devices with their start and end apart: 10, of which 8 were waited for; matrix products, arithmetic and copies ran while one was open for 2% of the time, Pallas kernels for 3%

profile of v9, /device:TPU:2, one launch (start us, length us, event | category | flops | bytes accessed | tf_op | source)
XLA Modules:
  0.0 107.8 jit_solution(14212641613993780977)
XLA Ops:
  0.6 0.0 copy-start.2
  0.6 0.7 copy-done.2
  1.4 0.9 shard_map.67
  2.3 0.0 copy-start
  2.3 0.0 copy-start.1
  2.3 16.5 %all-to-all-start = ((bf16[24,22,256]{2,1,0:T(8,128)(2,1)}), bf16[24,22,256]{2,1,0:T(8,128)(2,1)S(1)}, u32[]{:S(2)}, u32[]{:S(2)}) async-start(bf16[24,22,256]{2,1,0:T(8,128)(2,1)} %shard_map.67), calls=%async_computation | async-start | bytes 589824 | tf_op jit(solution)/shard_map/all_to_all | solution.py:354
  18.8 0.0 copy-start.3
  18.9 0.6 copy-done.3
  19.5 0.1 pad_add_fusion.1.mask_ref
  19.6 0.0 copy-done
  19.6 0.0 copy-done.1
  19.6 0.6 shard_map.68
  20.2 3.8 %collective-permute-start.1 = (bf16[272,512]{1,0:T(8,128)(2,1)S(1)}, bf16[272,512]{1,0:T(8,128)(2,1)S(1)}, u32[]{:S(2)}, u32[]{:S(2)}) collective-permute-start(bf16[272,512]{1,0:T(8,128)(2,1)S(1)} %shard_map.68), channel_id=1, source_target_pairs={{0,384},{384,0},{1,385},{385,1},{2,386},{386,2},{3,387},{387,3},{4... | collective-permute-start | bytes 835592 | tf_op jit(solution)/shard_map/ppermute | solution.py:17
  23.9 8.8 %collective-permute-done.1.recv_ref = bf16[272,512]{1,0:T(8,128)(2,1)S(1)} collective-permute-done((bf16[272,512]{1,0:T(8,128)(2,1)S(1)}, bf16[272,512]{1,0:T(8,128)(2,1)S(1)}, u32[]{:S(2)}, u32[]{:S(2)}) %collective-permute-start.1) | collective-permute-done | bytes 278560 | tf_op jit(solution)/shard_map/ppermute | solution.py:17
  32.7 0.6 shard_map.69
  33.3 6.8 %collective-permute-start.2 = (bf16[1,1,32,256]{3,2,1,0:T(8,128)(2,1)S(1)}, bf16[1,1,32,256]{3,2,1,0:T(8,128)(2,1)S(1)}, u32[]{:S(2)}, u32[]{:S(2)}) collective-permute-start(bf16[1,1,32,256]{3,2,1,0:T(8,128)(2,1)S(1)} %bitcast.27), channel_id=1, source_target_pairs={{0,8},{4,12},{8,0},{12,4},{1,9},{5,13},{9,1},{13,5},{2,10},{6,14},... | collective-permute-start | bytes 49160 | tf_op jit(solution)/shard_map/ppermute | solution.py:329
  40.2 2.7 %collective-permute-done.2 = bf16[1,1,32,256]{3,2,1,0:T(8,128)(2,1)S(1)} collective-permute-done((bf16[1,1,32,256]{3,2,1,0:T(8,128)(2,1)S(1)}, bf16[1,1,32,256]{3,2,1,0:T(8,128)(2,1)S(1)}, u32[]{:S(2)}, u32[]{:S(2)}) %collective-permute-start.2) | collective-permute-done | bytes 16416 | tf_op jit(solution)/shard_map/ppermute | solution.py:329
  42.9 4.5 %collective-permute-start.3 = (bf16[2,1,32,256]{3,2,1,0:T(8,128)(2,1)S(1)}, bf16[2,1,32,256]{3,2,1,0:T(8,128)(2,1)S(1)}, u32[]{:S(2)}, u32[]{:S(2)}) collective-permute-start(bf16[2,1,32,256]{3,2,1,0:T(8,128)(2,1)S(1)} %pad_maximum_fusion.2), channel_id=1, source_target_pairs={{0,4},{4,0},{8,12},{12,8},{1,5},{5,1},{9,13},{13,9},{2,6},{6,2},{1... | collective-permute-start | bytes 98312 | tf_op jit(solution)/shard_map/ppermute | solution.py:329
  47.4 0.0 all-to-all-done
  47.4 1.9 %collective-permute-start = (bf16[24,22,256]{2,1,0:T(8,128)(2,1)S(1)}, bf16[24,22,256]{2,1,0:T(8,128)(2,1)S(1)}, u32[]{:S(2)}, u32[]{:S(2)}) collective-permute-start(bf16[24,22,256]{2,1,0:T(8,128)(2,1)S(1)} %all-to-all-done), channel_id=1, source_target_pairs={{0,16},{16,0},{1,17},{17,1},{2,18},{18,2},{3,19},{19,3},{4,20},{20... | collective-permute-start | bytes 811016 | tf_op jit(solution)/shard_map/ppermute | solution.py:21
  49.3 0.3 collective-permute-done.3
  49.6 0.1 copy.12
  49.7 1.2 %collective-permute-done = bf16[24,22,256]{2,1,0:T(8,128)(2,1)S(1)} collective-permute-done((bf16[24,22,256]{2,1,0:T(8,128)(2,1)S(1)}, bf16[24,22,256]{2,1,0:T(8,128)(2,1)S(1)}, u32[]{:S(2)}, u32[]{:S(2)}) %collective-permute-start) | collective-permute-done | bytes 270368 | tf_op jit(solution)/shard_map/ppermute | solution.py:21
  50.9 0.1 copy.13
  50.9 0.1 fusion
  51.0 0.4 copy.14
  51.5 0.1 copy.16
  51.6 0.3 convolution_convert_fusion
  52.0 12.9 %all_to_all.20.both_ref = bf16[4,256,256]{2,1,0:T(8,128)(2,1)S(1)} all-to-all(bf16[4,256,256]{2,1,0:T(8,128)(2,1)S(1)} %pad_maximum_fusion), channel_id=1, replica_groups=mesh['pair'=2,'z'=12,'core'=2,'y_hi'=4,'x'=4] {'x'}, dimensions={0} | all-to-all | bytes 1048576 | tf_op jit(solution)/shard_map/all_to_all | solution.py:370
  65.0 0.5 shard_map.70
  65.5 1.9 %collective-permute-start.5 = (bf16[24,22,256]{2,1,0:T(8,128)(2,1)S(1)}, bf16[24,22,256]{2,1,0:T(8,128)(2,1)S(1)}, u32[]{:S(2)}, u32[]{:S(2)}) collective-permute-start(bf16[24,22,256]{2,1,0:T(8,128)(2,1)S(1)} %get-tuple-element.22), channel_id=1, source_target_pairs={{0,16},{16,0},{1,17},{17,1},{2,18},{18,2},{3,19},{19,3},{4,20},{20... | collective-permute-start | bytes 811016 | tf_op jit(solution)/shard_map/ppermute | solution.py:21
  67.4 0.7 slice_reduce_fusion
  68.1 4.4 %all-to-all-start.2 = ((bf16[4,32,256]{2,1,0:T(8,128)(2,1)}), bf16[4,32,256]{2,1,0:T(8,128)(2,1)S(1)}, u32[]{:S(2)}, u32[]{:S(2)}) async-start(bf16[4,32,256]{2,1,0:T(8,128)(2,1)} %bitcast.14), calls=%async_computation.2 | async-start | bytes 131072 | tf_op jit(solution)/shard_map/all_to_all | solution.py:372
  72.5 0.0 collective-permute-done.5
  72.5 0.8 add_convert_fusion
  73.2 7.6 %all-to-all-done.2 = bf16[4,32,256]{2,1,0:T(8,128)(2,1)S(1)} async-done(((bf16[4,32,256]{2,1,0:T(8,128)(2,1)}), bf16[4,32,256]{2,1,0:T(8,128)(2,1)S(1)}, u32[]{:S(2)}, u32[]{:S(2)}) %all-to-all-start.2) | async-done | bytes 65568 | tf_op jit(solution)/shard_map/all_to_all | solution.py:372
  80.9 9.5 %all-to-all-start.3 = ((bf16[24,22,256]{2,1,0:T(8,128)(2,1)}), bf16[24,22,256]{2,1,0:T(8,128)(2,1)S(1)}, u32[]{:S(2)}, u32[]{:S(2)}) async-start(bf16[24,22,256]{2,1,0:T(8,128)(2,1)} %add_convert_fusion), calls=%async_computation.3 | async-start | bytes 589824 | tf_op jit(solution)/shard_map/all_to_all | solution.py:381
  90.4 0.3 shard_map.71
  90.7 3.8 %collective-permute-start.4 = (bf16[256,512]{1,0:T(8,128)(2,1)S(1)}, bf16[256,512]{1,0:T(8,128)(2,1)S(1)}, u32[]{:S(2)}, u32[]{:S(2)}) collective-permute-start(bf16[256,512]{1,0:T(8,128)(2,1)S(1)} %get-tuple-element.20), channel_id=1, source_target_pairs={{0,384},{384,0},{1,385},{385,1},{2,386},{386,2},{3,387},{387,3},{4... | collective-permute-start | bytes 786440 | tf_op jit(solution)/shard_map/ppermute | solution.py:17
  94.5 0.6 reduce_sum.33
  95.8 0.1 add_minimum_fusion
  95.9 2.1 %collective-permute-start.6 = (bf16[32,256]{1,0:T(8,128)(2,1)S(1)}, bf16[32,256]{1,0:T(8,128)(2,1)S(1)}, u32[]{:S(2)}, u32[]{:S(2)}) collective-permute-start(bf16[32,256]{1,0:T(8,128)(2,1)S(1)} %reduce_sum.35.kv_ref), channel_id=1, source_target_pairs={{0,384},{384,0},{1,385},{385,1},{2,386},{386,2},{3,387},{387,3},{4... | collective-permute-start | bytes 49160 | tf_op jit(solution)/shard_map/ppermute | solution.py:17
  98.0 0.1 pad_add_fusion.place_ref
  98.1 4.3 %collective-permute-done.4.recv_ref = bf16[256,512]{1,0:T(8,128)(2,1)S(1)} collective-permute-done((bf16[256,512]{1,0:T(8,128)(2,1)S(1)}, bf16[256,512]{1,0:T(8,128)(2,1)S(1)}, u32[]{:S(2)}, u32[]{:S(2)}) %collective-permute-start.4) | collective-permute-done | bytes 262176 | tf_op jit(solution)/shard_map/ppermute | solution.py:17
  102.4 0.2 collective-permute-done.6.other_ref
  102.6 1.3 %shard_map.72 = (bf16[256,512]{1,0:T(8,128)(2,1)}, bf16[64,256]{1,0:T(8,128)(2,1)}) custom-call(s32[5]{0:T(128)S(1)} %pad_add_fusion.place_ref, f32[256,512]{1,0:T(8,128)S(1)} %get-tuple-element.19.keep_ref, bf16[256,512]{1,0:T(8,128)(2,1)S(1)} %collective-permute-done.4.recv_ref, bf16[32,256]{1,0:T(8,128)(2,1)S(1)} %reduce_sum.35.kv_ref, ...), custom_call_target="tpu_custom_call" | custom-call | flops 131072 | bytes 1048576 | tf_op jit(solution)/shard_map/pallas_call | solution.py:133
  103.9 2.8 %all-to-all-done.3.parts_ref = bf16[24,22,256]{2,1,0:T(8,128)(2,1)S(1)} async-done(((bf16[24,22,256]{2,1,0:T(8,128)(2,1)}), bf16[24,22,256]{2,1,0:T(8,128)(2,1)S(1)}, u32[]{:S(2)}, u32[]{:S(2)}) %all-to-all-start.3) | async-done | bytes 270368 | tf_op jit(solution)/shard_map/all_to_all | solution.py:381
  106.8 1.0 shard_map.73
  (9 shorter events, 0.2 us)
Async XLA Ops:
  0.6 0.8 copy-start.2
  2.3 17.3 %copy-start = (bf16[256,512]{1,0:T(8,128)(2,1)S(1)}, bf16[256,512]{1,0:T(8,128)(2,1)}, u32[]{:S(2)}) copy-start(bf16[256,512]{1,0:T(8,128)(2,1)} %x_ref.3) | copy-start | bytes 786436
  2.3 17.3 %copy-start.1 = (bf16[256,64]{0,1:T(8,128)(2,1)S(1)}, bf16[256,64]{0,1:T(8,128)(2,1)}, u32[]{:S(2)}) copy-start(bf16[256,64]{0,1:T(8,128)(2,1)} %param.6) | copy-start | bytes 98308
  2.3 45.1 %all-to-all-start = ((bf16[24,22,256]{2,1,0:T(8,128)(2,1)}), bf16[24,22,256]{2,1,0:T(8,128)(2,1)S(1)}, u32[]{:S(2)}, u32[]{:S(2)}) async-start(bf16[24,22,256]{2,1,0:T(8,128)(2,1)} %shard_map.67), calls=%async_computation | async-start | bytes 589824 | tf_op jit(solution)/shard_map/all_to_all | solution.py:354
  18.8 0.7 copy-start.3
  20.2 12.6 %collective-permute-start.1 = (bf16[272,512]{1,0:T(8,128)(2,1)S(1)}, bf16[272,512]{1,0:T(8,128)(2,1)S(1)}, u32[]{:S(2)}, u32[]{:S(2)}) collective-permute-start(bf16[272,512]{1,0:T(8,128)(2,1)S(1)} %shard_map.68), channel_id=1, source_target_pairs={{0,384},{384,0},{1,385},{385,1},{2,386},{386,2},{3,387},{387,3},{4... | collective-permute-start | bytes 835592 | tf_op jit(solution)/shard_map/ppermute | solution.py:17
  33.3 9.5 %collective-permute-start.2 = (bf16[1,1,32,256]{3,2,1,0:T(8,128)(2,1)S(1)}, bf16[1,1,32,256]{3,2,1,0:T(8,128)(2,1)S(1)}, u32[]{:S(2)}, u32[]{:S(2)}) collective-permute-start(bf16[1,1,32,256]{3,2,1,0:T(8,128)(2,1)S(1)} %bitcast.27), channel_id=1, source_target_pairs={{0,8},{4,12},{8,0},{12,4},{1,9},{5,13},{9,1},{13,5},{2,10},{6,14},... | collective-permute-start | bytes 49160 | tf_op jit(solution)/shard_map/ppermute | solution.py:329
  42.9 6.7 %collective-permute-start.3 = (bf16[2,1,32,256]{3,2,1,0:T(8,128)(2,1)S(1)}, bf16[2,1,32,256]{3,2,1,0:T(8,128)(2,1)S(1)}, u32[]{:S(2)}, u32[]{:S(2)}) collective-permute-start(bf16[2,1,32,256]{3,2,1,0:T(8,128)(2,1)S(1)} %pad_maximum_fusion.2), channel_id=1, source_target_pairs={{0,4},{4,0},{8,12},{12,8},{1,5},{5,1},{9,13},{13,9},{2,6},{6,2},{1... | collective-permute-start | bytes 98312 | tf_op jit(solution)/shard_map/ppermute | solution.py:329
  47.4 3.5 %collective-permute-start = (bf16[24,22,256]{2,1,0:T(8,128)(2,1)S(1)}, bf16[24,22,256]{2,1,0:T(8,128)(2,1)S(1)}, u32[]{:S(2)}, u32[]{:S(2)}) collective-permute-start(bf16[24,22,256]{2,1,0:T(8,128)(2,1)S(1)} %all-to-all-done), channel_id=1, source_target_pairs={{0,16},{16,0},{1,17},{17,1},{2,18},{18,2},{3,19},{19,3},{4,20},{20... | collective-permute-start | bytes 811016 | tf_op jit(solution)/shard_map/ppermute | solution.py:21
  65.5 7.0 %collective-permute-start.5 = (bf16[24,22,256]{2,1,0:T(8,128)(2,1)S(1)}, bf16[24,22,256]{2,1,0:T(8,128)(2,1)S(1)}, u32[]{:S(2)}, u32[]{:S(2)}) collective-permute-start(bf16[24,22,256]{2,1,0:T(8,128)(2,1)S(1)} %get-tuple-element.22), channel_id=1, source_target_pairs={{0,16},{16,0},{1,17},{17,1},{2,18},{18,2},{3,19},{19,3},{4,20},{20... | collective-permute-start | bytes 811016 | tf_op jit(solution)/shard_map/ppermute | solution.py:21
  68.1 12.8 %all-to-all-start.2 = ((bf16[4,32,256]{2,1,0:T(8,128)(2,1)}), bf16[4,32,256]{2,1,0:T(8,128)(2,1)S(1)}, u32[]{:S(2)}, u32[]{:S(2)}) async-start(bf16[4,32,256]{2,1,0:T(8,128)(2,1)} %bitcast.14), calls=%async_computation.2 | async-start | bytes 131072 | tf_op jit(solution)/shard_map/all_to_all | solution.py:372
  80.9 25.9 %all-to-all-start.3 = ((bf16[24,22,256]{2,1,0:T(8,128)(2,1)}), bf16[24,22,256]{2,1,0:T(8,128)(2,1)S(1)}, u32[]{:S(2)}, u32[]{:S(2)}) async-start(bf16[24,22,256]{2,1,0:T(8,128)(2,1)} %add_convert_fusion), calls=%async_computation.3 | async-start | bytes 589824 | tf_op jit(solution)/shard_map/all_to_all | solution.py:381
  90.7 11.7 %collective-permute-start.4 = (bf16[256,512]{1,0:T(8,128)(2,1)S(1)}, bf16[256,512]{1,0:T(8,128)(2,1)S(1)}, u32[]{:S(2)}, u32[]{:S(2)}) collective-permute-start(bf16[256,512]{1,0:T(8,128)(2,1)S(1)} %get-tuple-element.20), channel_id=1, source_target_pairs={{0,384},{384,0},{1,385},{385,1},{2,386},{386,2},{3,387},{387,3},{4... | collective-permute-start | bytes 786440 | tf_op jit(solution)/shard_map/ppermute | solution.py:17
  95.9 6.7 %collective-permute-start.6 = (bf16[32,256]{1,0:T(8,128)(2,1)S(1)}, bf16[32,256]{1,0:T(8,128)(2,1)S(1)}, u32[]{:S(2)}, u32[]{:S(2)}) collective-permute-start(bf16[32,256]{1,0:T(8,128)(2,1)S(1)} %reduce_sum.35.kv_ref), channel_id=1, source_target_pairs={{0,384},{384,0},{1,385},{385,1},{2,386},{386,2},{3,387},{387,3},{4... | collective-permute-start | bytes 49160 | tf_op jit(solution)/shard_map/ppermute | solution.py:17

commit v10 on v9

--- a/solution.py
+++ b/solution.py
@@ -235,59 +235,43 @@
     )(parts)
 
 
-def swap_kernel(mask_ref, x_ref, g_ref, send_ref):
-    tokens, feats = x_ref.shape
-    span = tokens // 2
-    lanes = feats // tokens
-    deep = HALF // lanes
+def first_kernel(mask_ref, x_ref, send_ref):
+    span = x_ref.shape[0] // 2
     skip = mask_ref[0] == 0
-    left = mask_ref[2] == 0
     for seq in range(2):
         source = jnp.where(skip, 1 - seq, seq)
         rows = pl.ds(pl.multiple_of(source * span, span), span)
         send_ref[seq * span : (seq + 1) * span] = x_ref[rows]
+
+
+def theirs_kernel(mask_ref, g_ref, send_ref):
+    span = g_ref.shape[1] // 2
+    skip = mask_ref[0] == 0
+    left = mask_ref[2] == 0
     g = jnp.where(left, g_ref[HALF:].astype(F32), g_ref[:HALF].astype(F32))
-    g0 = jnp.where(skip, g[:, span:], g[:, :span])
-    g1 = jnp.where(skip, g[:, :span], g[:, span:])
-    g = jnp.concatenate([g0, g1], axis=1).astype(BF16)
-    for part in range(lanes):
-        send_ref[tokens:, part * tokens : (part + 1) * tokens] = g[part * deep : (part + 1) * deep]
-
-
-def prepare_swap(state, x, g):
-    tokens, feats = x.shape
-    vmem = pl.BlockSpec(memory_space=pltpu.VMEM)
-    return pl.pallas_call(
-        swap_kernel,
-        out_shape=jax.ShapeDtypeStruct((tokens + HALF * tokens // feats, feats), BF16),
-        in_specs=[pl.BlockSpec(memory_space=pltpu.SMEM), vmem, vmem],
-        out_specs=vmem,
-        compiler_params=pltpu.CompilerParams(vmem_limit_bytes=32 * 2**20),
-        cost_estimate=pl.CostEstimate(flops=2**18, bytes_accessed=2**19, transcendentals=0),
-    )(state, x, g)
-
-
-def compact_kernel(mask_ref, x_ref, g_ref, recv_ref, x_out, g_out):
-    tokens, feats = x_ref.shape
-    span = tokens // 2
-    lanes = feats // tokens
-    deep = HALF // lanes
+    send_ref[:, :span] = jnp.where(skip, g[:, span:], g[:, :span]).astype(BF16)
+    send_ref[:, span:] = jnp.where(skip, g[:, :span], g[:, span:]).astype(BF16)
+
+
+def places(mask_ref):
     count = mask_ref[0] + mask_ref[1]
     skip = jnp.where(mask_ref[0] == 0, 1, 0)
     left = mask_ref[2] == 0
     two = count == 2
     some = count >= 1
-    mine = (jnp.logical_or(jnp.logical_and(left, some), two), jnp.logical_or(jnp.logical_and(left, two), jnp.logical_and(jnp.logical_not(left), some)))
+    right_some = jnp.logical_and(jnp.logical_not(left), some)
+    mine = (
+        jnp.logical_or(jnp.logical_and(left, some), two),
+        jnp.logical_or(two, right_some),
+    )
     own_at = (jnp.where(two, 0, skip), jnp.where(jnp.logical_or(left, two), 1, skip))
     other_at = (0, jnp.where(count == 1, 0, 1))
-    own = jnp.where(left, g_ref[:HALF].astype(F32), g_ref[HALF:].astype(F32))
-    other = jnp.concatenate(
-        [
-            recv_ref[tokens:, part * tokens : (part + 1) * tokens].astype(F32)
-            for part in range(lanes)
-        ],
-        axis=0,
-    )
+    return mine, own_at, other_at
+
+
+def rows_kernel(mask_ref, x_ref, recv_ref, out_ref):
+    span = x_ref.shape[0] // 2
+    mine, own_at, other_at = places(mask_ref)
     for slot in range(2):
         here = slice(slot * span, (slot + 1) * span)
         own_rows = pl.ds(pl.multiple_of(own_at[slot] * span, span), span)
@@ -295,43 +279,62 @@
 
         @pl.when(mine[slot])
         def _():
-            x_out[here] = x_ref[own_rows]
-            g_out[:, here] = jnp.where(own_at[slot] == 0, own[:, :span], own[:, span:]).astype(BF16)
+            out_ref[here] = x_ref[own_rows]
 
         @pl.when(jnp.logical_not(mine[slot]))
         def _():
-            x_out[here] = recv_ref[other_rows]
-            g_out[:, here] = jnp.where(other_at[slot] == 0, other[:, :span], other[:, span:]).astype(BF16)
-
-
-def compact_pair(state, x, g, received):
-    tokens, feats = x.shape
-    vmem = pl.BlockSpec(memory_space=pltpu.VMEM)
-    return pl.pallas_call(
-        compact_kernel,
-        out_shape=(
-            jax.ShapeDtypeStruct((tokens, feats), BF16),
-            jax.ShapeDtypeStruct((HALF, tokens), BF16),
-        ),
-        in_specs=[pl.BlockSpec(memory_space=pltpu.SMEM), vmem, vmem, vmem],
-        out_specs=(vmem, vmem),
-        compiler_params=pltpu.CompilerParams(vmem_limit_bytes=32 * 2**20),
-        cost_estimate=pl.CostEstimate(flops=2**18, bytes_accessed=2**19, transcendentals=0),
-    )(state, x, g, received)
-
-
-def gather_doubling(value, axis_name, n):
+            out_ref[here] = recv_ref[other_rows]
+
+
+def columns_kernel(mask_ref, g_ref, recv_ref, out_ref):
+    span = g_ref.shape[1] // 2
+    left = mask_ref[2] == 0
+    mine, own_at, other_at = places(mask_ref)
+    own = jnp.where(left, g_ref[:HALF].astype(F32), g_ref[HALF:].astype(F32))
+    other = recv_ref[...].astype(F32)
+    for slot in range(2):
+        here = slice(slot * span, (slot + 1) * span)
+        a = jnp.where(own_at[slot] == 0, own[:, :span], own[:, span:])
+        b = jnp.where(other_at[slot] == 0, other[:, :span], other[:, span:])
+        out_ref[:, here] = jnp.where(mine[slot], a, b).astype(BF16)
+
+
+def small_call(kernel, shape, state, *operands):
+    vmem = pl.BlockSpec(memory_space=pltpu.VMEM)
+    return pl.pallas_call(
+        kernel,
+        out_shape=jax.ShapeDtypeStruct(shape, BF16),
+        in_specs=[pl.BlockSpec(memory_space=pltpu.SMEM)] + [vmem] * len(operands),
+        out_specs=vmem,
+        compiler_params=pltpu.CompilerParams(vmem_limit_bytes=32 * 2**20),
+        cost_estimate=pl.CostEstimate(flops=2**18, bytes_accessed=2**18, transcendentals=0),
+    )(state, *operands)
+
+
+def gather_doubling(value, axis_name, n, early):
     index = lax.axis_index(axis_name)
     bits = n.bit_length() - 1
     value = value.reshape((1,) * bits + value.shape)
     for axis in range(bits):
         step = n >> (axis + 1)
+        if axis == bits - 1:
+            value, early = lax.optimization_barrier((value, early))
         other = lax.ppermute(value, axis_name, [(i, i ^ step) for i in range(n)])
         upper = (index & step) != 0
         value = jnp.concatenate(
             [jnp.where(upper, other, value), jnp.where(upper, value, other)], axis=axis
         )
-    return value
+    return value, early
+
+
+def scatter_sum(value, axis_name, n):
+    index = lax.axis_index(axis_name)
+    total = lax.dynamic_index_in_dim(value, index, keepdims=False)
+    narrow = value.astype(BF16)
+    for step in range(1, n):
+        block = lax.dynamic_index_in_dim(narrow, index ^ step, keepdims=False)
+        total = total + lax.ppermute(block, axis_name, [(i, i ^ step) for i in range(n)]).astype(F32)
+    return total
 
 
 def on_device(x, w, adjoint, mask):
@@ -355,9 +358,12 @@
 
     state = jnp.concatenate([mask, side.reshape(1)])
     g = adjoint.T
-    received = swap_pair(prepare_swap(state, x, g))
-    x_pair, g_cols = compact_pair(state, x, g, received)
-    g_rows = gather_doubling(g_cols, "y_hi", n_y).reshape(1, n_y * half, tokens)
+    g_other = swap_pair(small_call(theirs_kernel, (half, tokens), state, g))
+    g_cols = small_call(columns_kernel, (half, tokens), state, g, g_other)
+    x_other = swap_pair(small_call(first_kernel, (tokens, feats), state, x))
+    x_pair = small_call(rows_kernel, (tokens, feats), state, x, x_other)
+    g_rows, x_pair = gather_doubling(g_cols, "y_hi", n_y, x_pair)
+    g_rows = g_rows.reshape(1, n_y * half, tokens)
 
     w_theirs = swap_core(w_mine)
     w_cores = jnp.where(core == 0, jnp.stack([w_mine, w_theirs], 1), jnp.stack([w_theirs, w_mine], 1))
@@ -368,8 +374,6 @@
     kv = kv.reshape(n_x, n_y * half, tokens)
     both = jnp.concatenate([kv, jnp.broadcast_to(g_rows, kv.shape)], axis=1)
     both = lax.all_to_all(both, "x", 0, 0, tiled=True)
-    kv = jnp.sum(both[:, : n_y * half].astype(F32), axis=0).astype(BF16)
-    kv_parts = lax.all_to_all(kv.reshape(n_y, half, tokens), "y_hi", 0, 0, tiled=True)
 
     dw_mine, dw_theirs = weight_blocks(core, both, x_pair, 2 * n_z, wrows)
     dw_theirs, both = lax.optimization_barrier((dw_theirs, both))
@@ -377,14 +381,15 @@
 
     send, keep = return_parts(both, w_full)
     received = swap_pair(send)
-    dw_send, kv_parts = lax.optimization_barrier((dw_sum.astype(BF16), kv_parts))
+    dw_send, both = lax.optimization_barrier((dw_sum.astype(BF16), both))
     dw_parts = lax.all_to_all(dw_send, ("pair", "z"), 0, 0, tiled=True)
     weight_grad = sum_blocks(dw_parts, half, wrows)
 
     start = jnp.where(side == 0, 0, 2 - count)
     slots = jnp.minimum(jnp.stack([start, start + mask[0]]), 1)
     place = jnp.concatenate([mask, slots, side.reshape(1)])
-    kv = jnp.sum(kv_parts.astype(F32), axis=0).astype(BF16)
+    kv = jnp.sum(both[:, : n_y * half].astype(F32), axis=0).reshape(n_y, half, tokens)
+    kv = scatter_sum(kv, "y_hi", n_y).astype(BF16)
     activation_grad, kv_home = bring_home(place, keep, received, kv, swap_pair(kv), seqs)
     return kv_home.T, activation_grad, weight_grad
 

time: 108 us -> 106 us (0.981)
  the two profiles are of different devices: /device:TPU:2 before, /device:TPU:1 now
where the time goes in v10:
time: 106 us; the launch traced here: 105 us
  starting transfers between devices  68.3 us (64%)
  blocking collectives  12.2 us (12%)
  waiting for transfers between devices  11.9 us (11%)
  Pallas kernels  6.37 us (6%)
  local copies, waits for them, and re-layouts  2.1 us (2%)
  other arithmetic  1.88 us (2%)
  between operations  1.73 us (2%)
    all_to_all x1, starting transfers between devices, on_device(): lax.all_to_all(spread_weight(w, half, n_z), ('pair', 'z'), 0, 0, tiled=True)  17.1 us
    all_to_all x1, blocking collectives, on_device(): both = lax.all_to_all(both, 'x', 0, 0, tiled=True)  12.2 us
    ppermute x4, starting transfers between devices, swap_pair(): return lax.ppermute(value, 'pair', SWAP)  11.7 us
    ppermute x3, starting transfers between devices, scatter_sum(): lax.ppermute(block, axis_name, [(i, i ^ step) for i in range(n)])  11.4 us
    all_to_all x1, starting transfers between devices, on_device(): dw_parts = lax.all_to_all(dw_send, ('pair', 'z'), 0, 0, tiled=True)  10.2 us
    ppermute x4, waiting for transfers between devices, swap_pair(): return lax.ppermute(value, 'pair', SWAP)  9.57 us
    ppermute x2, starting transfers between devices, gather_doubling(): other = lax.ppermute(value, axis_name, [(i, i ^ step) for i in range(n)])  9.24 us
    ppermute x2, starting transfers between devices, swap_core(): return lax.ppermute(value, 'core', SWAP)  8.8 us
  transfers between devices with their start and end apart: 13, of which 6 were waited for; matrix products, arithmetic and copies ran while one was open for 1% of the time, Pallas kernels for 4%

profile of v10, /device:TPU:1, one launch (start us, length us, event | category | flops | bytes accessed | tf_op | source)
XLA Modules:
  0.0 104.8 jit_solution(9310869721073111307)
XLA Ops:
  0.6 0.7 copy-done.2
  1.4 0.9 shard_map.67
  2.3 17.1 %all-to-all-start = ((bf16[24,22,256]{2,1,0:T(8,128)(2,1)}), bf16[24,22,256]{2,1,0:T(8,128)(2,1)S(1)}, u32[]{:S(2)}, u32[]{:S(2)}) async-start(bf16[24,22,256]{2,1,0:T(8,128)(2,1)} %shard_map.67), calls=%async_computation | async-start | bytes 589824 | tf_op jit(solution)/shard_map/all_to_all | solution.py:357
  19.4 0.0 copy-start.3
  19.4 0.6 copy-done.3
  20.1 0.1 pad_add_fusion.1.mask_ref
  20.1 0.6 shard_map.68
  20.7 3.2 %collective-permute-start.1 = (bf16[32,256]{1,0:T(8,128)(2,1)S(1)}, bf16[32,256]{1,0:T(8,128)(2,1)S(1)}, u32[]{:S(2)}, u32[]{:S(2)}) collective-permute-start(bf16[32,256]{1,0:T(8,128)(2,1)S(1)} %shard_map.68), channel_id=1, source_target_pairs={{0,384},{384,0},{1,385},{385,1},{2,386},{386,2},{3,387},{387,3},{4... | collective-permute-start | bytes 49160 | tf_op jit(solution)/shard_map/ppermute | solution.py:17
  23.9 1.7 %collective-permute-done.1.recv_ref = bf16[32,256]{1,0:T(8,128)(2,1)S(1)} collective-permute-done((bf16[32,256]{1,0:T(8,128)(2,1)S(1)}, bf16[32,256]{1,0:T(8,128)(2,1)S(1)}, u32[]{:S(2)}, u32[]{:S(2)}) %collective-permute-start.1) | collective-permute-done | bytes 16416 | tf_op jit(solution)/shard_map/ppermute | solution.py:17
  25.6 0.6 shard_map.69
  26.2 6.6 %collective-permute-start.2 = (bf16[1,1,32,256]{3,2,1,0:T(8,128)(2,1)S(1)}, bf16[1,1,32,256]{3,2,1,0:T(8,128)(2,1)S(1)}, u32[]{:S(2)}, u32[]{:S(2)}) collective-permute-start(bf16[1,1,32,256]{3,2,1,0:T(8,128)(2,1)S(1)} %bitcast.41), channel_id=1, source_target_pairs={{0,8},{4,12},{8,0},{12,4},{1,9},{5,13},{9,1},{13,5},{2,10},{6,14},... | collective-permute-start | bytes 49160 | tf_op jit(solution)/shard_map/ppermute | solution.py:322
  32.7 0.6 shard_map.70
  33.3 3.2 %collective-permute-start.3 = (bf16[256,512]{1,0:T(8,128)(2,1)S(1)}, bf16[256,512]{1,0:T(8,128)(2,1)S(1)}, u32[]{:S(2)}, u32[]{:S(2)}) collective-permute-start(bf16[256,512]{1,0:T(8,128)(2,1)S(1)} %shard_map.70), channel_id=1, source_target_pairs={{0,384},{384,0},{1,385},{385,1},{2,386},{386,2},{3,387},{387,3},{4... | collective-permute-start | bytes 786440 | tf_op jit(solution)/shard_map/ppermute | solution.py:17
  36.5 0.0 collective-permute-done.2
  36.6 4.8 %collective-permute-done.3.recv_ref = bf16[256,512]{1,0:T(8,128)(2,1)S(1)} collective-permute-done((bf16[256,512]{1,0:T(8,128)(2,1)S(1)}, bf16[256,512]{1,0:T(8,128)(2,1)S(1)}, u32[]{:S(2)}, u32[]{:S(2)}) %collective-permute-start.3) | collective-permute-done | bytes 262176 | tf_op jit(solution)/shard_map/ppermute | solution.py:17
  41.3 0.6 shard_map.71.x_ref
  41.9 2.7 %collective-permute-start.4 = (bf16[2,1,32,256]{3,2,1,0:T(8,128)(2,1)S(1)}, bf16[2,1,32,256]{3,2,1,0:T(8,128)(2,1)S(1)}, u32[]{:S(2)}, u32[]{:S(2)}) collective-permute-start(bf16[2,1,32,256]{3,2,1,0:T(8,128)(2,1)S(1)} %pad_maximum_fusion.2), channel_id=1, source_target_pairs={{0,4},{4,0},{8,12},{12,8},{1,5},{5,1},{9,13},{13,9},{2,6},{6,2},{1... | collective-permute-start | bytes 98312 | tf_op jit(solution)/shard_map/ppermute | solution.py:322
  44.6 0.0 all-to-all-done
  44.6 4.8 %collective-permute-start = (bf16[24,22,256]{2,1,0:T(8,128)(2,1)S(1)}, bf16[24,22,256]{2,1,0:T(8,128)(2,1)S(1)}, u32[]{:S(2)}, u32[]{:S(2)}) collective-permute-start(bf16[24,22,256]{2,1,0:T(8,128)(2,1)S(1)} %all-to-all-done), channel_id=1, source_target_pairs={{0,16},{16,0},{1,17},{17,1},{2,18},{18,2},{3,19},{19,3},{4,20},{20... | collective-permute-start | bytes 811016 | tf_op jit(solution)/shard_map/ppermute | solution.py:21
  49.5 0.0 collective-permute-done.4
  49.5 0.1 copy.12
  49.6 1.1 %collective-permute-done = bf16[24,22,256]{2,1,0:T(8,128)(2,1)S(1)} collective-permute-done((bf16[24,22,256]{2,1,0:T(8,128)(2,1)S(1)}, bf16[24,22,256]{2,1,0:T(8,128)(2,1)S(1)}, u32[]{:S(2)}, u32[]{:S(2)}) %collective-permute-start) | collective-permute-done | bytes 270368 | tf_op jit(solution)/shard_map/ppermute | solution.py:21
  50.7 0.1 copy.13
  50.7 0.1 fusion
  50.8 0.4 copy.14
  51.2 0.1 copy.16
  51.3 0.3 convolution_convert_fusion
  51.8 12.2 %all_to_all.15.both_ref = bf16[4,256,256]{2,1,0:T(8,128)(2,1)S(1)} all-to-all(bf16[4,256,256]{2,1,0:T(8,128)(2,1)S(1)} %pad_maximum_fusion), channel_id=1, replica_groups=mesh['pair'=2,'z'=12,'core'=2,'y_hi'=4,'x'=4] {'x'}, dimensions={0} | all-to-all | bytes 1048576 | tf_op jit(solution)/shard_map/all_to_all | solution.py:376
  64.0 0.5 shard_map.72
  64.5 4.0 %collective-permute-start.6 = (bf16[24,22,256]{2,1,0:T(8,128)(2,1)S(1)}, bf16[24,22,256]{2,1,0:T(8,128)(2,1)S(1)}, u32[]{:S(2)}, u32[]{:S(2)}) collective-permute-start(bf16[24,22,256]{2,1,0:T(8,128)(2,1)S(1)} %get-tuple-element.22), channel_id=1, source_target_pairs={{0,16},{16,0},{1,17},{17,1},{2,18},{18,2},{3,19},{19,3},{4,20},{20... | collective-permute-start | bytes 811016 | tf_op jit(solution)/shard_map/ppermute | solution.py:21
  68.4 1.2 %collective-permute-done.6 = bf16[24,22,256]{2,1,0:T(8,128)(2,1)S(1)} collective-permute-done((bf16[24,22,256]{2,1,0:T(8,128)(2,1)S(1)}, bf16[24,22,256]{2,1,0:T(8,128)(2,1)S(1)}, u32[]{:S(2)}, u32[]{:S(2)}) %collective-permute-start.6) | collective-permute-done | bytes 270368 | tf_op jit(solution)/shard_map/ppermute | solution.py:21
  69.6 0.8 add_convert_fusion
  70.4 10.2 %all-to-all-start.2 = ((bf16[24,22,256]{2,1,0:T(8,128)(2,1)}), bf16[24,22,256]{2,1,0:T(8,128)(2,1)S(1)}, u32[]{:S(2)}, u32[]{:S(2)}) async-start(bf16[24,22,256]{2,1,0:T(8,128)(2,1)} %add_convert_fusion), calls=%async_computation.2 | async-start | bytes 589824 | tf_op jit(solution)/shard_map/all_to_all | solution.py:385
  80.6 0.6 reduce_sum.18
  82.0 3.6 %collective-permute-start.7 = (bf16[32,256]{1,0:T(8,128)(2,1)S(1)}, bf16[32,256]{1,0:T(8,128)(2,1)S(1)}, u32[]{:S(2)}, u32[]{:S(2)}) collective-permute-start(bf16[32,256]{1,0:T(8,128)(2,1)S(1)} %get-tuple-element.27), channel_id=1, source_target_pairs={{0,4},{4,0},{8,12},{12,8},{1,5},{5,1},{9,13},{13,9},{2,6},{6,2},{1... | collective-permute-start | bytes 49160 | tf_op jit(solution)/shard_map/ppermute | solution.py:336
  85.6 2.8 %collective-permute-start.8 = (bf16[32,256]{1,0:T(8,128)(2,1)S(1)}, bf16[32,256]{1,0:T(8,128)(2,1)S(1)}, u32[]{:S(2)}, u32[]{:S(2)}) collective-permute-start(bf16[32,256]{1,0:T(8,128)(2,1)S(1)} %get-tuple-element.29), channel_id=1, source_target_pairs={{0,8},{4,12},{8,0},{12,4},{1,9},{5,13},{9,1},{13,5},{2,10},{6,14},... | collective-permute-start | bytes 49160 | tf_op jit(solution)/shard_map/ppermute | solution.py:336
  88.5 5.0 %collective-permute-start.9 = (bf16[32,256]{1,0:T(8,128)(2,1)S(1)}, bf16[32,256]{1,0:T(8,128)(2,1)S(1)}, u32[]{:S(2)}, u32[]{:S(2)}) collective-permute-start(bf16[32,256]{1,0:T(8,128)(2,1)S(1)} %get-tuple-element.28), channel_id=1, source_target_pairs={{0,12},{4,8},{8,4},{12,0},{1,13},{5,9},{9,5},{13,1},{2,14},{6,10},... | collective-permute-start | bytes 49160 | tf_op jit(solution)/shard_map/ppermute | solution.py:336
  93.4 0.1 add_minimum_fusion
  93.6 0.3 shard_map.73
  93.9 3.2 %collective-permute-start.5 = (bf16[256,512]{1,0:T(8,128)(2,1)S(1)}, bf16[256,512]{1,0:T(8,128)(2,1)S(1)}, u32[]{:S(2)}, u32[]{:S(2)}) collective-permute-start(bf16[256,512]{1,0:T(8,128)(2,1)S(1)} %get-tuple-element.20), channel_id=1, source_target_pairs={{0,384},{384,0},{1,385},{385,1},{2,386},{386,2},{3,387},{387,3},{4... | collective-permute-start | bytes 786440 | tf_op jit(solution)/shard_map/ppermute | solution.py:17
  97.1 0.0 collective-permute-done.8
  97.2 2.1 %collective-permute-start.10 = (bf16[32,256]{1,0:T(8,128)(2,1)S(1)}, bf16[32,256]{1,0:T(8,128)(2,1)S(1)}, u32[]{:S(2)}, u32[]{:S(2)}) collective-permute-start(bf16[32,256]{1,0:T(8,128)(2,1)S(1)} %fusion.3.kv_ref), channel_id=1, source_target_pairs={{0,384},{384,0},{1,385},{385,1},{2,386},{386,2},{3,387},{387,3},{4... | collective-permute-start | bytes 49160 | tf_op jit(solution)/shard_map/ppermute | solution.py:17
  99.3 0.1 pad_add_fusion.place_ref
  99.3 2.8 %collective-permute-done.5.recv_ref = bf16[256,512]{1,0:T(8,128)(2,1)S(1)} collective-permute-done((bf16[256,512]{1,0:T(8,128)(2,1)S(1)}, bf16[256,512]{1,0:T(8,128)(2,1)S(1)}, u32[]{:S(2)}, u32[]{:S(2)}) %collective-permute-start.5) | collective-permute-done | bytes 262176 | tf_op jit(solution)/shard_map/ppermute | solution.py:17
  102.1 0.4 collective-permute-done.10.other_ref
  102.5 1.3 %shard_map.74 = (bf16[256,512]{1,0:T(8,128)(2,1)}, bf16[64,256]{1,0:T(8,128)(2,1)}) custom-call(s32[5]{0:T(128)S(1)} %pad_add_fusion.place_ref, f32[256,512]{1,0:T(8,128)S(1)} %get-tuple-element.19.keep_ref, bf16[256,512]{1,0:T(8,128)(2,1)S(1)} %collective-permute-done.5.recv_ref, bf16[32,256]{1,0:T(8,128)(2,1)S(1)} %fusion.3.kv_ref, ...), custom_call_target="tpu_custom_call" | custom-call | flops 131072 | bytes 1048576 | tf_op jit(solution)/shard_map/pallas_call | solution.py:133
  103.8 0.0 all-to-all-done.2.parts_ref
  103.8 1.0 shard_map.75
  (19 shorter events, 0.2 us)
Async XLA Ops:
  0.6 0.8 copy-start.2
  2.3 17.8 %copy-start.1 = (bf16[256,64]{0,1:T(8,128)(2,1)S(1)}, bf16[256,64]{0,1:T(8,128)(2,1)}, u32[]{:S(2)}) copy-start(bf16[256,64]{0,1:T(8,128)(2,1)} %param.6) | copy-start | bytes 98308
  2.3 30.4 %copy-start = (bf16[256,512]{1,0:T(8,128)(2,1)S(1)}, bf16[256,512]{1,0:T(8,128)(2,1)}, u32[]{:S(2)}) copy-start(bf16[256,512]{1,0:T(8,128)(2,1)} %x_ref.3) | copy-start | bytes 786436
  2.3 42.3 %all-to-all-start = ((bf16[24,22,256]{2,1,0:T(8,128)(2,1)}), bf16[24,22,256]{2,1,0:T(8,128)(2,1)S(1)}, u32[]{:S(2)}, u32[]{:S(2)}) async-start(bf16[24,22,256]{2,1,0:T(8,128)(2,1)} %shard_map.67), calls=%async_computation | async-start | bytes 589824 | tf_op jit(solution)/shard_map/all_to_all | solution.py:357
  19.4 0.7 copy-start.3
  20.7 4.9 %collective-permute-start.1 = (bf16[32,256]{1,0:T(8,128)(2,1)S(1)}, bf16[32,256]{1,0:T(8,128)(2,1)S(1)}, u32[]{:S(2)}, u32[]{:S(2)}) collective-permute-start(bf16[32,256]{1,0:T(8,128)(2,1)S(1)} %shard_map.68), channel_id=1, source_target_pairs={{0,384},{384,0},{1,385},{385,1},{2,386},{386,2},{3,387},{387,3},{4... | collective-permute-start | bytes 49160 | tf_op jit(solution)/shard_map/ppermute | solution.py:17
  26.2 10.4 %collective-permute-start.2 = (bf16[1,1,32,256]{3,2,1,0:T(8,128)(2,1)S(1)}, bf16[1,1,32,256]{3,2,1,0:T(8,128)(2,1)S(1)}, u32[]{:S(2)}, u32[]{:S(2)}) collective-permute-start(bf16[1,1,32,256]{3,2,1,0:T(8,128)(2,1)S(1)} %bitcast.41), channel_id=1, source_target_pairs={{0,8},{4,12},{8,0},{12,4},{1,9},{5,13},{9,1},{13,5},{2,10},{6,14},... | collective-permute-start | bytes 49160 | tf_op jit(solution)/shard_map/ppermute | solution.py:322
  33.3 8.0 %collective-permute-start.3 = (bf16[256,512]{1,0:T(8,128)(2,1)S(1)}, bf16[256,512]{1,0:T(8,128)(2,1)S(1)}, u32[]{:S(2)}, u32[]{:S(2)}) collective-permute-start(bf16[256,512]{1,0:T(8,128)(2,1)S(1)} %shard_map.70), channel_id=1, source_target_pairs={{0,384},{384,0},{1,385},{385,1},{2,386},{386,2},{3,387},{387,3},{4... | collective-permute-start | bytes 786440 | tf_op jit(solution)/shard_map/ppermute | solution.py:17
  41.9 7.6 %collective-permute-start.4 = (bf16[2,1,32,256]{3,2,1,0:T(8,128)(2,1)S(1)}, bf16[2,1,32,256]{3,2,1,0:T(8,128)(2,1)S(1)}, u32[]{:S(2)}, u32[]{:S(2)}) collective-permute-start(bf16[2,1,32,256]{3,2,1,0:T(8,128)(2,1)S(1)} %pad_maximum_fusion.2), channel_id=1, source_target_pairs={{0,4},{4,0},{8,12},{12,8},{1,5},{5,1},{9,13},{13,9},{2,6},{6,2},{1... | collective-permute-start | bytes 98312 | tf_op jit(solution)/shard_map/ppermute | solution.py:322
  44.6 6.0 %collective-permute-start = (bf16[24,22,256]{2,1,0:T(8,128)(2,1)S(1)}, bf16[24,22,256]{2,1,0:T(8,128)(2,1)S(1)}, u32[]{:S(2)}, u32[]{:S(2)}) collective-permute-start(bf16[24,22,256]{2,1,0:T(8,128)(2,1)S(1)} %all-to-all-done), channel_id=1, source_target_pairs={{0,16},{16,0},{1,17},{17,1},{2,18},{18,2},{3,19},{19,3},{4,20},{20... | collective-permute-start | bytes 811016 | tf_op jit(solution)/shard_map/ppermute | solution.py:21
  64.5 5.2 %collective-permute-start.6 = (bf16[24,22,256]{2,1,0:T(8,128)(2,1)S(1)}, bf16[24,22,256]{2,1,0:T(8,128)(2,1)S(1)}, u32[]{:S(2)}, u32[]{:S(2)}) collective-permute-start(bf16[24,22,256]{2,1,0:T(8,128)(2,1)S(1)} %get-tuple-element.22), channel_id=1, source_target_pairs={{0,16},{16,0},{1,17},{17,1},{2,18},{18,2},{3,19},{19,3},{4,20},{20... | collective-permute-start | bytes 811016 | tf_op jit(solution)/shard_map/ppermute | solution.py:21
  70.4 33.4 %all-to-all-start.2 = ((bf16[24,22,256]{2,1,0:T(8,128)(2,1)}), bf16[24,22,256]{2,1,0:T(8,128)(2,1)S(1)}, u32[]{:S(2)}, u32[]{:S(2)}) async-start(bf16[24,22,256]{2,1,0:T(8,128)(2,1)} %add_convert_fusion), calls=%async_computation.2 | async-start | bytes 589824 | tf_op jit(solution)/shard_map/all_to_all | solution.py:385
  82.0 15.1 %collective-permute-start.7 = (bf16[32,256]{1,0:T(8,128)(2,1)S(1)}, bf16[32,256]{1,0:T(8,128)(2,1)S(1)}, u32[]{:S(2)}, u32[]{:S(2)}) collective-permute-start(bf16[32,256]{1,0:T(8,128)(2,1)S(1)} %get-tuple-element.27), channel_id=1, source_target_pairs={{0,4},{4,0},{8,12},{12,8},{1,5},{5,1},{9,13},{13,9},{2,6},{6,2},{1... | collective-permute-start | bytes 49160 | tf_op jit(solution)/shard_map/ppermute | solution.py:336
  85.6 11.5 %collective-permute-start.8 = (bf16[32,256]{1,0:T(8,128)(2,1)S(1)}, bf16[32,256]{1,0:T(8,128)(2,1)S(1)}, u32[]{:S(2)}, u32[]{:S(2)}) collective-permute-start(bf16[32,256]{1,0:T(8,128)(2,1)S(1)} %get-tuple-element.29), channel_id=1, source_target_pairs={{0,8},{4,12},{8,0},{12,4},{1,9},{5,13},{9,1},{13,5},{2,10},{6,14},... | collective-permute-start | bytes 49160 | tf_op jit(solution)/shard_map/ppermute | solution.py:336
  88.5 8.7 %collective-permute-start.9 = (bf16[32,256]{1,0:T(8,128)(2,1)S(1)}, bf16[32,256]{1,0:T(8,128)(2,1)S(1)}, u32[]{:S(2)}, u32[]{:S(2)}) collective-permute-start(bf16[32,256]{1,0:T(8,128)(2,1)S(1)} %get-tuple-element.28), channel_id=1, source_target_pairs={{0,12},{4,8},{8,4},{12,0},{1,13},{5,9},{9,5},{13,1},{2,14},{6,10},... | collective-permute-start | bytes 49160 | tf_op jit(solution)/shard_map/ppermute | solution.py:336
  93.9 8.2 %collective-permute-start.5 = (bf16[256,512]{1,0:T(8,128)(2,1)S(1)}, bf16[256,512]{1,0:T(8,128)(2,1)S(1)}, u32[]{:S(2)}, u32[]{:S(2)}) collective-permute-start(bf16[256,512]{1,0:T(8,128)(2,1)S(1)} %get-tuple-element.20), channel_id=1, source_target_pairs={{0,384},{384,0},{1,385},{385,1},{2,386},{386,2},{3,387},{387,3},{4... | collective-permute-start | bytes 786440 | tf_op jit(solution)/shard_map/ppermute | solution.py:17
  97.2 5.3 %collective-permute-start.10 = (bf16[32,256]{1,0:T(8,128)(2,1)S(1)}, bf16[32,256]{1,0:T(8,128)(2,1)S(1)}, u32[]{:S(2)}, u32[]{:S(2)}) collective-permute-start(bf16[32,256]{1,0:T(8,128)(2,1)S(1)} %fusion.3.kv_ref), channel_id=1, source_target_pairs={{0,384},{384,0},{1,385},{385,1},{2,386},{386,2},{3,387},{387,3},{4... | collective-permute-start | bytes 49160 | tf_op jit(solution)/shard_map/ppermute | solution.py:17

commit v11 on v8

--- a/solution.py
+++ b/solution.py
@@ -158,7 +158,7 @@
     return (here == source).astype(F32).astype(BF16)
 
 
-def spread_kernel(half, n_z, w_ref, out_ref, stage_ref):
+def spread_kernel(half, n_z, turn_ref, w_ref, out_ref, stage_ref):
     wrows, cols = w_ref.shape
     width = cols // 4
     size = min(256, 2 * width)
@@ -173,41 +173,47 @@
                 stage_ref[side, pl.ds(part * wrows, wrows), lanes] = split[
                     :, side * size // 2 : (side + 1) * size // 2
                 ]
-    for side in range(2):
-        block = stage_ref[side, : 2 * wrows].astype(BF16)
+    turned = turn_ref[0] != 0
+    low, high = stage_ref[0, : 2 * wrows], stage_ref[1, : 2 * wrows]
+    for side, block in enumerate((jnp.where(turned, high, low), jnp.where(turned, low, high))):
+        block = block.astype(BF16)
         for z in range(n_z):
             out_ref[side * n_z + z] = block
 
 
-def spread_weight(w, half, n_z):
+def spread_weight(turn, w, half, n_z):
     wrows, cols = w.shape
     vmem = pl.BlockSpec(memory_space=pltpu.VMEM)
     padded = -(-2 * wrows // 16) * 16
     return pl.pallas_call(
         functools.partial(spread_kernel, half, n_z),
         out_shape=jax.ShapeDtypeStruct((2 * n_z, 2 * wrows, cols // 4), BF16),
-        in_specs=[vmem],
+        in_specs=[pl.BlockSpec(memory_space=pltpu.SMEM), vmem],
         out_specs=vmem,
         scratch_shapes=[pltpu.VMEM((2, padded, cols // 4), F32)],
         compiler_params=pltpu.CompilerParams(vmem_limit_bytes=32 * 2**20),
         cost_estimate=pl.CostEstimate(
             flops=2 * wrows * cols * 256, bytes_accessed=2**19, transcendentals=0
         ),
-    )(w)
-
-
-def sum_kernel(half, parts_ref, out_ref, stage_ref):
+    )(turn.reshape(1), w)
+
+
+def sum_kernel(half, turn_ref, parts_ref, out_ref, stage_ref):
     blocks = parts_ref.shape[0]
     wrows, cols = out_ref.shape
     width = cols // 4
     size = min(256, 2 * width)
     matrix = halves_matrix(size, half, True)
+    sums = []
     for side in range(2):
         first = side * blocks // 2
         total = parts_ref[first].astype(F32)
         for block in range(first + 1, first + blocks // 2):
             total = total + parts_ref[block].astype(F32)
-        stage_ref[side, pl.ds(0, 2 * wrows)] = total
+        sums.append(total)
+    turned = turn_ref[0] != 0
+    stage_ref[0, pl.ds(0, 2 * wrows)] = jnp.where(turned, sums[1], sums[0])
+    stage_ref[1, pl.ds(0, 2 * wrows)] = jnp.where(turned, sums[0], sums[1])
     for part in range(2):
         for group in range(2 * width // size):
             lanes = slice(group * size // 2, (group + 1) * size // 2)
@@ -225,21 +231,21 @@
             out_ref[:, at : at + size] = value
 
 
-def sum_blocks(parts, half, wrows):
+def sum_blocks(turn, parts, half, wrows):
     width = parts.shape[2]
     vmem = pl.BlockSpec(memory_space=pltpu.VMEM)
     padded = -(-2 * wrows // 16) * 16
     return pl.pallas_call(
         functools.partial(sum_kernel, half),
         out_shape=jax.ShapeDtypeStruct((wrows, 4 * width), F32),
-        in_specs=[vmem],
+        in_specs=[pl.BlockSpec(memory_space=pltpu.SMEM), vmem],
         out_specs=vmem,
         scratch_shapes=[pltpu.VMEM((2, padded, width), F32)],
         compiler_params=pltpu.CompilerParams(vmem_limit_bytes=32 * 2**20),
         cost_estimate=pl.CostEstimate(
             flops=6 * wrows * 4 * width * 256, bytes_accessed=2**19, transcendentals=0
         ),
-    )(parts)
+    )(turn.reshape(1), parts)
 
 
 def on_device(x, w, adjoint, mask):
@@ -252,6 +258,11 @@
     half = cols // n_mp // 2
     side = lax.axis_index("pair")
     core = lax.axis_index("core")
+    turn = lax.axis_index("mp") // (n_mp // 2)
+    hand = jnp.bitwise_xor(side, turn)
+    groups = [
+        [(s ^ (g // (n_mp // 2))) * n_mp + g for g in range(n_mp)] for s in range(2)
+    ]
 
     alive = mask != 0
     count = jnp.sum(mask)
@@ -275,11 +286,11 @@
         value = value.reshape(*lead, 2, wrows, n_mp * half // 2)
         return jnp.swapaxes(value, -3, -2).reshape(*lead, wrows, n_mp * half)
 
-    w_mine = lax.all_to_all(spread_weight(w, half, n_z), ("pair", "z"), 0, 0, tiled=True)
+    w_mine = lax.all_to_all(spread_weight(turn, w, half, n_z), ("pair", "z"), 0, 0, tiled=True)
 
     g = survivor_first(adjoint.T.reshape(2, half, seqs, span).transpose(2, 0, 1, 3))
-    g_mine = jnp.where(side == 0, g[:, 0], g[:, 1])
-    g_theirs = jnp.where(side == 0, g[:, 1], g[:, 0])
+    g_mine = jnp.where(hand == 0, g[:, 0], g[:, 1])
+    g_theirs = jnp.where(hand == 0, g[:, 1], g[:, 0])
     xs = survivor_first(x.reshape(seqs, span, feats))
     g_other = swap_pair(g_theirs)
     x_other = swap_pair(xs)
@@ -294,7 +305,7 @@
     kv = lax.dot_general(w_full, x_pair, (((0,), (1,)), ((), ())), preferred_element_type=F32)
     kv = kv.astype(BF16).reshape(n_mp, half, tokens)
     both = jnp.concatenate([kv, jnp.broadcast_to(g_cols, (n_mp, half, tokens))], axis=1)
-    both = lax.all_to_all(both, "mp", 0, 0, tiled=True)
+    both = lax.all_to_all(both, ("pair", "mp"), 0, 0, axis_index_groups=groups, tiled=True)
 
     dw_mine, dw_theirs = weight_blocks(core, both, x_pair, 2 * n_z, wrows)
     dw_theirs, both = lax.optimization_barrier((dw_theirs, both))
@@ -304,11 +315,11 @@
     received = swap_pair(send)
     dw_send, keep = lax.optimization_barrier((dw_sum.astype(BF16), keep))
     dw_parts = lax.all_to_all(dw_send, ("pair", "z"), 0, 0, tiled=True)
-    weight_grad = sum_blocks(dw_parts, half, wrows)
+    weight_grad = sum_blocks(turn, dw_parts, half, wrows)
 
     start = jnp.where(side == 0, 0, 2 - count)
     slots = jnp.minimum(jnp.stack([start, start + mask[0]]), 1)
-    place = jnp.concatenate([mask, slots, side.reshape(1)])
+    place = jnp.concatenate([mask, slots, hand.reshape(1)])
     activation_grad, kv_home = bring_home(place, keep, received, kv, seqs)
     return kv_home.T, activation_grad, weight_grad
 

time: 94.7 us -> 93.5 us (0.987)
  blocking collectives: 25.1 us -> 22.9 us
    all_to_all x1, blocking collectives: 25.1 us -> 22.9 us  [on_device(): lax.all_to_all(both, ('pair', 'mp'), 0, 0, axis_index_groups=groups, tile...]
where the time goes in v11:
time: 93.5 us; the launch traced here: 91.7 us
  starting transfers between devices  39.6 us (42%)
  blocking collectives  22.9 us (24%)
  waiting for transfers between devices  18.7 us (20%)
  Pallas kernels  4.11 us (4%)
  between operations  2.31 us (2%)
  other arithmetic  2.02 us (2%)
  local copies, waits for them, and re-layouts  1.59 us (2%)
    all_to_all x1, blocking collectives, on_device(): lax.all_to_all(both, ('pair', 'mp'), 0, 0, axis_index_groups=groups, tile...  22.9 us
    all_to_all x1, starting transfers between devices, on_device(): lax.all_to_all(spread_weight(turn, w, half, n_z), ('pair', 'z'), 0, 0, ti...  17.1 us
    ppermute x2, starting transfers between devices, swap_core(): return lax.ppermute(value, 'core', SWAP)  9.89 us
    ppermute x3, starting transfers between devices, swap_pair(): return lax.ppermute(value, 'pair', SWAP)  8.48 us
    ppermute x3, waiting for transfers between devices, swap_pair(): return lax.ppermute(value, 'pair', SWAP)  7.84 us
    all_to_all x1, waiting for transfers between devices, on_device(): lax.all_to_all(spread_weight(turn, w, half, n_z), ('pair', 'z'), 0, 0, ti...  6.72 us
    all_to_all x1, starting transfers between devices, on_device(): dw_parts = lax.all_to_all(dw_send, ('pair', 'z'), 0, 0, tiled=True)  4.2 us
    all_to_all x1, waiting for transfers between devices, on_device(): dw_parts = lax.all_to_all(dw_send, ('pair', 'z'), 0, 0, tiled=True)  2.36 us
  transfers between devices with their start and end apart: 7, of which 5 were waited for; matrix products, arithmetic and copies ran while one was open for 1% of the time, Pallas kernels for 2%

profile of v11, /device:TPU:1, one launch (start us, length us, event | category | flops | bytes accessed | tf_op | source)
XLA Modules:
  0.0 91.7 jit_solution(13693048513927960424)
XLA Ops:
  0.6 0.0 copy-start
  0.7 0.7 copy-done
  1.4 0.9 %shard_map.67 = bf16[24,22,256]{2,1,0:T(8,128)(2,1)} custom-call(s32[1]{0:T(128)} %bitcast.5.turn_ref, bf16[11,1024]{1,0:T(8,128)(2,1)S(1)} %copy-done), custom_call_target="tpu_custom_call" | custom-call | flops 5767168 | bytes 524288 | tf_op jit(solution)/shard_map/pallas_call | solution.py:188
  2.3 0.0 copy-start.2
  2.3 0.0 copy-start.3
  2.3 17.1 %all-to-all-start = ((bf16[24,22,256]{2,1,0:T(8,128)(2,1)}), bf16[24,22,256]{2,1,0:T(8,128)(2,1)S(1)}, u32[]{:S(2)}, u32[]{:S(2)}) async-start(bf16[24,22,256]{2,1,0:T(8,128)(2,1)} %shard_map.67), calls=%async_computation | async-start | bytes 589824 | tf_op jit(solution)/shard_map/all_to_all | solution.py:289
  19.4 0.0 copy-start.1
  19.4 0.0 copy-done.2
  19.4 0.2 rev.7
  19.6 0.0 copy-done.3
  19.8 3.2 %collective-permute-start.2 = (bf16[2,32,128]{2,0,1:T(2,128)(2,1)S(1)}, bf16[2,32,128]{2,0,1:T(2,128)(2,1)S(1)}, u32[]{:S(2)}, u32[]{:S(2)}) collective-permute-start(bf16[2,32,128]{2,0,1:T(2,128)(2,1)S(1)} %get-tuple-element.30), channel_id=1, source_target_pairs={{0,384},{384,0},{1,385},{385,1},{2,386},{386,2},{3,387},{387,3},{4... | collective-permute-start | bytes 49160 | tf_op jit(solution)/shard_map/ppermute | solution.py:16
  23.0 0.0 copy-done.1
  23.0 0.1 reverse_select_fusion
  23.0 2.1 %collective-permute-start.1 = (bf16[2,128,512]{2,1,0:T(8,128)(2,1)S(1)}, bf16[2,128,512]{2,1,0:T(8,128)(2,1)S(1)}, u32[]{:S(2)}, u32[]{:S(2)}) collective-permute-start(bf16[2,128,512]{2,1,0:T(8,128)(2,1)S(1)} %reverse_select_fusion), channel_id=1, source_target_pairs={{0,384},{384,0},{1,385},{385,1},{2,386},{386,2},{3,387},{387,3},{4... | collective-permute-start | bytes 786440 | tf_op jit(solution)/shard_map/ppermute | solution.py:16
  25.1 0.6 reduce_sum.9
  27.1 0.0 collective-permute-done.2
  27.1 0.1 broadcast_select_fusion.10
  27.2 6.7 %all-to-all-done = bf16[24,22,256]{2,1,0:T(8,128)(2,1)S(1)} async-done(((bf16[24,22,256]{2,1,0:T(8,128)(2,1)}), bf16[24,22,256]{2,1,0:T(8,128)(2,1)S(1)}, u32[]{:S(2)}, u32[]{:S(2)}) %all-to-all-start) | async-done | bytes 270368 | tf_op jit(solution)/shard_map/all_to_all | solution.py:289
  33.9 5.6 %collective-permute-start = (bf16[24,22,256]{2,1,0:T(8,128)(2,1)S(1)}, bf16[24,22,256]{2,1,0:T(8,128)(2,1)S(1)}, u32[]{:S(2)}, u32[]{:S(2)}) collective-permute-start(bf16[24,22,256]{2,1,0:T(8,128)(2,1)S(1)} %all-to-all-done), channel_id=1, source_target_pairs={{0,16},{16,0},{1,17},{17,1},{2,18},{18,2},{3,19},{19,3},{4,20},{20... | collective-permute-start | bytes 811016 | tf_op jit(solution)/shard_map/ppermute | solution.py:20
  39.5 0.0 collective-permute-done.1
  39.6 0.1 copy.18
  39.7 1.0 %collective-permute-done = bf16[24,22,256]{2,1,0:T(8,128)(2,1)S(1)} collective-permute-done((bf16[24,22,256]{2,1,0:T(8,128)(2,1)S(1)}, bf16[24,22,256]{2,1,0:T(8,128)(2,1)S(1)}, u32[]{:S(2)}, u32[]{:S(2)}) %collective-permute-start) | collective-permute-done | bytes 270368 | tf_op jit(solution)/shard_map/ppermute | solution.py:20
  40.7 0.1 copy.19
  40.8 0.1 fusion
  40.9 0.4 copy.20
  41.3 0.1 copy.25
  41.4 0.4 convolution_convert_fusion
  41.8 22.9 %all_to_all.15.both_ref = bf16[16,64,256]{2,1,0:T(8,128)(2,1)S(1)} all-to-all(bf16[16,64,256]{2,1,0:T(8,128)(2,1)S(1)} %pad_maximum_fusion), channel_id=1, replica_groups={{0,1,2,3,4,5,6,7,392,393,394,395,396,397,398,399},{384,385,386,387,388,..., dimensions={0} | all-to-all | bytes 1048576 | tf_op jit(solution)/shard_map/all_to_all | solution.py:308
  64.8 0.5 shard_map.68
  65.3 4.3 %collective-permute-start.3 = (bf16[24,22,256]{2,1,0:T(8,128)(2,1)S(1)}, bf16[24,22,256]{2,1,0:T(8,128)(2,1)S(1)}, u32[]{:S(2)}, u32[]{:S(2)}) collective-permute-start(bf16[24,22,256]{2,1,0:T(8,128)(2,1)S(1)} %get-tuple-element.16), channel_id=1, source_target_pairs={{0,16},{16,0},{1,17},{17,1},{2,18},{18,2},{3,19},{19,3},{4,20},{20... | collective-permute-start | bytes 811016 | tf_op jit(solution)/shard_map/ppermute | solution.py:20
  69.6 0.3 shard_map.69
  70.0 0.8 collective-permute-done.3
  70.8 0.8 add_convert_fusion
  71.6 4.2 %all-to-all-start.2 = ((bf16[24,22,256]{2,1,0:T(8,128)(2,1)}), bf16[24,22,256]{2,1,0:T(8,128)(2,1)S(1)}, u32[]{:S(2)}, u32[]{:S(2)}) async-start(bf16[24,22,256]{2,1,0:T(8,128)(2,1)} %add_convert_fusion), calls=%async_computation.2 | async-start | bytes 589824 | tf_op jit(solution)/shard_map/all_to_all | solution.py:317
  75.8 3.2 %collective-permute-start.4 = (bf16[272,512]{1,0:T(8,128)(2,1)S(1)}, bf16[272,512]{1,0:T(8,128)(2,1)S(1)}, u32[]{:S(2)}, u32[]{:S(2)}) collective-permute-start(bf16[272,512]{1,0:T(8,128)(2,1)S(1)} %get-tuple-element.20), channel_id=1, source_target_pairs={{0,384},{384,0},{1,385},{385,1},{2,386},{386,2},{3,387},{387,3},{4... | collective-permute-start | bytes 835592 | tf_op jit(solution)/shard_map/ppermute | solution.py:16
  79.0 0.1 add_minimum_fusion
  79.1 0.1 pad_add_fusion.place_ref
  79.2 7.8 %collective-permute-done.4.recv_ref = bf16[272,512]{1,0:T(8,128)(2,1)S(1)} collective-permute-done((bf16[272,512]{1,0:T(8,128)(2,1)S(1)}, bf16[272,512]{1,0:T(8,128)(2,1)S(1)}, u32[]{:S(2)}, u32[]{:S(2)}) %collective-permute-start.4) | collective-permute-done | bytes 278560 | tf_op jit(solution)/shard_map/ppermute | solution.py:16
  87.0 1.3 %shard_map.70 = (bf16[256,512]{1,0:T(8,128)(2,1)}, bf16[64,256]{1,0:T(8,128)(2,1)}) custom-call(s32[5]{0:T(128)S(1)} %pad_add_fusion.place_ref, f32[256,512]{1,0:T(8,128)S(1)} %get-tuple-element.19.keep_ref, bf16[272,512]{1,0:T(8,128)(2,1)S(1)} %collective-permute-done.4.recv_ref, bf16[32,256]{1,0:T(8,128)(2,1)S(1)} %get-tuple-element.21.kv_ref), custom_call_target="tpu_custom_call" | custom-call | flops 131072 | bytes 1048576 | tf_op jit(solution)/shard_map/pallas_call | solution.py:140
  88.3 2.4 %all-to-all-done.2.parts_ref = bf16[24,22,256]{2,1,0:T(8,128)(2,1)S(1)} async-done(((bf16[24,22,256]{2,1,0:T(8,128)(2,1)}), bf16[24,22,256]{2,1,0:T(8,128)(2,1)S(1)}, u32[]{:S(2)}, u32[]{:S(2)}) %all-to-all-start.2) | async-done | bytes 270368 | tf_op jit(solution)/shard_map/all_to_all | solution.py:317
  90.7 1.0 %shard_map.71 = f32[11,1024]{1,0:T(8,128)} custom-call(s32[1]{0:T(128)} %bitcast.5.turn_ref, bf16[24,22,256]{2,1,0:T(8,128)(2,1)S(1)} %all-to-all-done.2.parts_ref), custom_call_target="tpu_custom_call" | custom-call | flops 17301504 | bytes 524288 | tf_op jit(solution)/shard_map/pallas_call | solution.py:238
  (11 shorter events, 0.3 us)
Async XLA Ops:
  0.6 0.8 copy-start
  2.3 17.1 %copy-start.2 = (bf16[256,64]{0,1:T(8,128)(2,1)S(1)}, bf16[256,64]{0,1:T(8,128)(2,1)}, u32[]{:S(2)}) copy-start(bf16[256,64]{0,1:T(8,128)(2,1)} %param.6) | copy-start | bytes 98308
  2.3 17.3 %copy-start.3 = (s32[2]{0:T(128)S(1)}, s32[2]{0:T(128)}, u32[]{:S(2)}) copy-start(s32[2]{0:T(128)} %param.7) | copy-start | bytes 28
  2.3 31.6 %all-to-all-start = ((bf16[24,22,256]{2,1,0:T(8,128)(2,1)}), bf16[24,22,256]{2,1,0:T(8,128)(2,1)S(1)}, u32[]{:S(2)}, u32[]{:S(2)}) async-start(bf16[24,22,256]{2,1,0:T(8,128)(2,1)} %shard_map.67), calls=%async_computation | async-start | bytes 589824 | tf_op jit(solution)/shard_map/all_to_all | solution.py:289
  19.4 3.6 %copy-start.1 = (bf16[256,512]{1,0:T(8,128)(2,1)S(1)}, bf16[256,512]{1,0:T(8,128)(2,1)}, u32[]{:S(2)}) copy-start(bf16[256,512]{1,0:T(8,128)(2,1)} %param.4) | copy-start | bytes 786436
  19.8 7.3 %collective-permute-start.2 = (bf16[2,32,128]{2,0,1:T(2,128)(2,1)S(1)}, bf16[2,32,128]{2,0,1:T(2,128)(2,1)S(1)}, u32[]{:S(2)}, u32[]{:S(2)}) collective-permute-start(bf16[2,32,128]{2,0,1:T(2,128)(2,1)S(1)} %get-tuple-element.30), channel_id=1, source_target_pairs={{0,384},{384,0},{1,385},{385,1},{2,386},{386,2},{3,387},{387,3},{4... | collective-permute-start | bytes 49160 | tf_op jit(solution)/shard_map/ppermute | solution.py:16
  23.0 16.5 %collective-permute-start.1 = (bf16[2,128,512]{2,1,0:T(8,128)(2,1)S(1)}, bf16[2,128,512]{2,1,0:T(8,128)(2,1)S(1)}, u32[]{:S(2)}, u32[]{:S(2)}) collective-permute-start(bf16[2,128,512]{2,1,0:T(8,128)(2,1)S(1)} %reverse_select_fusion), channel_id=1, source_target_pairs={{0,384},{384,0},{1,385},{385,1},{2,386},{386,2},{3,387},{387,3},{4... | collective-permute-start | bytes 786440 | tf_op jit(solution)/shard_map/ppermute | solution.py:16
  33.9 6.8 %collective-permute-start = (bf16[24,22,256]{2,1,0:T(8,128)(2,1)S(1)}, bf16[24,22,256]{2,1,0:T(8,128)(2,1)S(1)}, u32[]{:S(2)}, u32[]{:S(2)}) collective-permute-start(bf16[24,22,256]{2,1,0:T(8,128)(2,1)S(1)} %all-to-all-done), channel_id=1, source_target_pairs={{0,16},{16,0},{1,17},{17,1},{2,18},{18,2},{3,19},{19,3},{4,20},{20... | collective-permute-start | bytes 811016 | tf_op jit(solution)/shard_map/ppermute | solution.py:20
  65.3 5.5 %collective-permute-start.3 = (bf16[24,22,256]{2,1,0:T(8,128)(2,1)S(1)}, bf16[24,22,256]{2,1,0:T(8,128)(2,1)S(1)}, u32[]{:S(2)}, u32[]{:S(2)}) collective-permute-start(bf16[24,22,256]{2,1,0:T(8,128)(2,1)S(1)} %get-tuple-element.16), channel_id=1, source_target_pairs={{0,16},{16,0},{1,17},{17,1},{2,18},{18,2},{3,19},{19,3},{4,20},{20... | collective-permute-start | bytes 811016 | tf_op jit(solution)/shard_map/ppermute | solution.py:20
  71.6 19.1 %all-to-all-start.2 = ((bf16[24,22,256]{2,1,0:T(8,128)(2,1)}), bf16[24,22,256]{2,1,0:T(8,128)(2,1)S(1)}, u32[]{:S(2)}, u32[]{:S(2)}) async-start(bf16[24,22,256]{2,1,0:T(8,128)(2,1)} %add_convert_fusion), calls=%async_computation.2 | async-start | bytes 589824 | tf_op jit(solution)/shard_map/all_to_all | solution.py:317
  75.8 11.2 %collective-permute-start.4 = (bf16[272,512]{1,0:T(8,128)(2,1)S(1)}, bf16[272,512]{1,0:T(8,128)(2,1)S(1)}, u32[]{:S(2)}, u32[]{:S(2)}) collective-permute-start(bf16[272,512]{1,0:T(8,128)(2,1)S(1)} %get-tuple-element.20), channel_id=1, source_target_pairs={{0,384},{384,0},{1,385},{385,1},{2,386},{386,2},{3,387},{387,3},{4... | collective-permute-start | bytes 835592 | tf_op jit(solution)/shard_map/ppermute | solution.py:16

commit v12 on v11

--- a/solution.py
+++ b/solution.py
@@ -10,6 +10,7 @@
 BF16 = jnp.bfloat16
 F32 = jnp.float32
 SWAP = [(0, 1), (1, 0)]
+HALF = 32
 
 
 def swap_pair(value):
@@ -248,10 +249,96 @@
     )(turn.reshape(1), parts)
 
 
+def swap_kernel(mask_ref, x_ref, g_ref, send_ref):
+    tokens, feats = x_ref.shape
+    span = tokens // 2
+    lanes = feats // tokens
+    deep = HALF // lanes
+    skip = mask_ref[0] == 0
+    low_half = mask_ref[3] == 0
+    for seq in range(2):
+        source = jnp.where(skip, 1 - seq, seq)
+        rows = pl.ds(pl.multiple_of(source * span, span), span)
+        send_ref[seq * span : (seq + 1) * span] = x_ref[rows]
+    g = jnp.where(low_half, g_ref[HALF:].astype(F32), g_ref[:HALF].astype(F32))
+    g0 = jnp.where(skip, g[:, span:], g[:, :span])
+    g1 = jnp.where(skip, g[:, :span], g[:, span:])
+    g = jnp.concatenate([g0, g1], axis=1).astype(BF16)
+    for part in range(lanes):
+        send_ref[tokens:, part * tokens : (part + 1) * tokens] = g[part * deep : (part + 1) * deep]
+
+
+def prepare_swap(state, x, g):
+    tokens, feats = x.shape
+    vmem = pl.BlockSpec(memory_space=pltpu.VMEM)
+    return pl.pallas_call(
+        swap_kernel,
+        out_shape=jax.ShapeDtypeStruct((tokens + HALF * tokens // feats, feats), BF16),
+        in_specs=[pl.BlockSpec(memory_space=pltpu.SMEM), vmem, vmem],
+        out_specs=vmem,
+        compiler_params=pltpu.CompilerParams(vmem_limit_bytes=32 * 2**20),
+        cost_estimate=pl.CostEstimate(flops=2**18, bytes_accessed=2**19, transcendentals=0),
+    )(state, x, g)
+
+
+def compact_kernel(mask_ref, x_ref, g_ref, recv_ref, x_out, g_out):
+    tokens, feats = x_ref.shape
+    span = tokens // 2
+    lanes = feats // tokens
+    deep = HALF // lanes
+    count = mask_ref[0] + mask_ref[1]
+    skip = jnp.where(mask_ref[0] == 0, 1, 0)
+    left = mask_ref[2] == 0
+    two = count == 2
+    some = count >= 1
+    right_some = jnp.logical_and(jnp.logical_not(left), some)
+    mine = (jnp.logical_or(jnp.logical_and(left, some), two), jnp.logical_or(two, right_some))
+    own_at = (jnp.where(two, 0, skip), jnp.where(jnp.logical_or(left, two), 1, skip))
+    other_at = (0, jnp.where(count == 1, 0, 1))
+    low_half = mask_ref[3] == 0
+    own = jnp.where(low_half, g_ref[:HALF].astype(F32), g_ref[HALF:].astype(F32))
+    other = jnp.concatenate(
+        [
+            recv_ref[tokens:, part * tokens : (part + 1) * tokens].astype(F32)
+            for part in range(lanes)
+        ],
+        axis=0,
+    )
+    for slot in range(2):
+        here = slice(slot * span, (slot + 1) * span)
+        own_rows = pl.ds(pl.multiple_of(own_at[slot] * span, span), span)
+        other_rows = pl.ds(pl.multiple_of(other_at[slot] * span, span), span)
+
+        @pl.when(mine[slot])
+        def _():
+            x_out[here] = x_ref[own_rows]
+            g_out[:, here] = jnp.where(own_at[slot] == 0, own[:, :span], own[:, span:]).astype(BF16)
+
+        @pl.when(jnp.logical_not(mine[slot]))
+        def _():
+            x_out[here] = recv_ref[other_rows]
+            g_out[:, here] = jnp.where(other_at[slot] == 0, other[:, :span], other[:, span:]).astype(BF16)
+
+
+def compact_pair(state, x, g, received):
+    tokens, feats = x.shape
+    vmem = pl.BlockSpec(memory_space=pltpu.VMEM)
+    return pl.pallas_call(
+        compact_kernel,
+        out_shape=(
+            jax.ShapeDtypeStruct((tokens, feats), BF16),
+            jax.ShapeDtypeStruct((HALF, tokens), BF16),
+        ),
+        in_specs=[pl.BlockSpec(memory_space=pltpu.SMEM), vmem, vmem, vmem],
+        out_specs=(vmem, vmem),
+        compiler_params=pltpu.CompilerParams(vmem_limit_bytes=32 * 2**20),
+        cost_estimate=pl.CostEstimate(flops=2**18, bytes_accessed=2**19, transcendentals=0),
+    )(state, x, g, received)
+
+
 def on_device(x, w, adjoint, mask):
     seqs = mask.shape[0]
     tokens, feats = x.shape
-    span = tokens // seqs
     wrows, cols = w.shape
     n_z = lax.axis_size("z")
     n_mp = lax.axis_size("mp")
@@ -264,22 +351,7 @@
         [(s ^ (g // (n_mp // 2))) * n_mp + g for g in range(n_mp)] for s in range(2)
     ]
 
-    alive = mask != 0
     count = jnp.sum(mask)
-    first_count = jnp.where(side == 0, count, 2 - count)
-    skip_first = jnp.logical_not(alive[0])
-
-    def survivor_first(value):
-        return jnp.where(skip_first, value[::-1], value)
-
-    def compact(own, other):
-        a0 = jnp.where(side == 0, own[0], other[0])
-        a1 = jnp.where(side == 0, own[1], other[1])
-        b0 = jnp.where(side == 0, other[0], own[0])
-        b1 = jnp.where(side == 0, other[1], own[1])
-        slot0 = jnp.where(first_count >= 1, a0, b0)
-        slot1 = jnp.where(first_count == 2, a1, jnp.where(first_count == 1, b0, b1))
-        return jnp.stack([slot0, slot1])
 
     def unpack(value):
         lead = value.shape[:-2]
@@ -288,15 +360,10 @@
 
     w_mine = lax.all_to_all(spread_weight(turn, w, half, n_z), ("pair", "z"), 0, 0, tiled=True)
 
-    g = survivor_first(adjoint.T.reshape(2, half, seqs, span).transpose(2, 0, 1, 3))
-    g_mine = jnp.where(hand == 0, g[:, 0], g[:, 1])
-    g_theirs = jnp.where(hand == 0, g[:, 1], g[:, 0])
-    xs = survivor_first(x.reshape(seqs, span, feats))
-    g_other = swap_pair(g_theirs)
-    x_other = swap_pair(xs)
-    g_pair = compact(g_mine, g_other)
-    g_cols = g_pair.transpose(1, 0, 2).reshape(1, half, tokens)
-    x_pair = compact(xs, x_other).reshape(tokens, feats)
+    state = jnp.concatenate([mask, jnp.stack([side, hand])])
+    g = adjoint.T
+    received = swap_pair(prepare_swap(state, x, g))
+    x_pair, g_cols = compact_pair(state, x, g, received)
 
     w_theirs = swap_core(w_mine)
     w_cores = jnp.where(core == 0, jnp.stack([w_mine, w_theirs], 1), jnp.stack([w_theirs, w_mine], 1))

time: 93.5 us -> 93.4 us (level)
  starting transfers between devices: 39.6 us -> 37.5 us
  waiting for transfers between devices: 18.7 us -> 20.2 us
  Pallas kernels: 4.11 us -> 5.26 us
    all_to_all x1, waiting for transfers between devices: 6.72 us -> 10 us  [on_device(): lax.all_to_all(spread_weight(turn, w, half, n_z), ('pair', 'z'), 0, 0, ti...]
    ppermute x3 -> x2, starting transfers between devices: 8.48 us -> 6.4 us  [swap_pair(): return lax.ppermute(value, 'pair', SWAP)]
    ppermute x3 -> x2, waiting for transfers between devices: 7.84 us -> 6.55 us  [swap_pair(): return lax.ppermute(value, 'pair', SWAP)]
    pallas_call x0 -> x2, Pallas kernels: none -> 1.15 us  [the longest x1 0.58 us: compact_pair(): pl.pallas_call(compact_kernel, out_shape=(jax.ShapeDtypeStruct((tokens, f...]
  transfers between devices with their start and end apart: 7 -> 6, of which waited for: 5 -> 5; matrix products, arithmetic and copies ran while one was open for 1% -> 1% of each run, Pallas kernels for 2% -> 3%
where the time goes in v12:
time: 93.4 us; the launch traced here: 91.7 us
  starting transfers between devices  37.5 us (40%)
  blocking collectives  23 us (25%)
  waiting for transfers between devices  20.2 us (22%)
  Pallas kernels  5.26 us (6%)
  local copies, waits for them, and re-layouts  2.06 us (2%)
  other arithmetic  1.76 us (2%)
  between operations  1.53 us (2%)
    all_to_all x1, blocking collectives, on_device(): lax.all_to_all(both, ('pair', 'mp'), 0, 0, axis_index_groups=groups, tile...  23 us
    all_to_all x1, starting transfers between devices, on_device(): lax.all_to_all(spread_weight(turn, w, half, n_z), ('pair', 'z'), 0, 0, ti...  17.1 us
    all_to_all x1, waiting for transfers between devices, on_device(): lax.all_to_all(spread_weight(turn, w, half, n_z), ('pair', 'z'), 0, 0, ti...  10 us
    ppermute x2, starting transfers between devices, swap_core(): return lax.ppermute(value, 'core', SWAP)  9.86 us
    ppermute x2, waiting for transfers between devices, swap_pair(): return lax.ppermute(value, 'pair', SWAP)  6.55 us
    ppermute x2, starting transfers between devices, swap_pair(): return lax.ppermute(value, 'pair', SWAP)  6.4 us
    all_to_all x1, starting transfers between devices, on_device(): dw_parts = lax.all_to_all(dw_send, ('pair', 'z'), 0, 0, tiled=True)  4.2 us
    all_to_all x1, waiting for transfers between devices, on_device(): dw_parts = lax.all_to_all(dw_send, ('pair', 'z'), 0, 0, tiled=True)  2.36 us
  transfers between devices with their start and end apart: 6, of which 5 were waited for; matrix products, arithmetic and copies ran while one was open for 1% of the time, Pallas kernels for 3%

profile of v12, /device:TPU:1, one launch (start us, length us, event | category | flops | bytes accessed | tf_op | source)
XLA Modules:
  0.0 91.7 jit_solution(5000251471645468866)
XLA Ops:
  0.6 0.0 copy-start.2
  0.7 0.7 copy-done.2
  1.4 0.9 %shard_map.67 = bf16[24,22,256]{2,1,0:T(8,128)(2,1)} custom-call(s32[1]{0:T(128)} %bitcast.5.turn_ref, bf16[11,1024]{1,0:T(8,128)(2,1)S(1)} %copy-done.2), custom_call_target="tpu_custom_call" | custom-call | flops 5767168 | bytes 524288 | tf_op jit(solution)/shard_map/pallas_call | solution.py:189
  2.3 0.0 copy-start
  2.3 0.0 copy-start.1
  2.3 17.1 %all-to-all-start = ((bf16[24,22,256]{2,1,0:T(8,128)(2,1)}), bf16[24,22,256]{2,1,0:T(8,128)(2,1)S(1)}, u32[]{:S(2)}, u32[]{:S(2)}) async-start(bf16[24,22,256]{2,1,0:T(8,128)(2,1)} %shard_map.67), calls=%async_computation | async-start | bytes 589824 | tf_op jit(solution)/shard_map/all_to_all | solution.py:361
  19.4 0.0 copy-start.3
  19.4 0.6 copy-done.3
  20.1 0.1 pad_add_fusion.1.mask_ref
  20.1 0.0 copy-done
  20.1 0.0 copy-done.1
  20.1 0.6 shard_map.68
  20.7 3.2 %collective-permute-start.1 = (bf16[272,512]{1,0:T(8,128)(2,1)S(1)}, bf16[272,512]{1,0:T(8,128)(2,1)S(1)}, u32[]{:S(2)}, u32[]{:S(2)}) collective-permute-start(bf16[272,512]{1,0:T(8,128)(2,1)S(1)} %shard_map.68), channel_id=1, source_target_pairs={{0,384},{384,0},{1,385},{385,1},{2,386},{386,2},{3,387},{387,3},{4... | collective-permute-start | bytes 835592 | tf_op jit(solution)/shard_map/ppermute | solution.py:17
  23.9 10.0 %all-to-all-done = bf16[24,22,256]{2,1,0:T(8,128)(2,1)S(1)} async-done(((bf16[24,22,256]{2,1,0:T(8,128)(2,1)}), bf16[24,22,256]{2,1,0:T(8,128)(2,1)S(1)}, u32[]{:S(2)}, u32[]{:S(2)}) %all-to-all-start) | async-done | bytes 270368 | tf_op jit(solution)/shard_map/all_to_all | solution.py:361
  33.9 5.6 %collective-permute-start = (bf16[24,22,256]{2,1,0:T(8,128)(2,1)S(1)}, bf16[24,22,256]{2,1,0:T(8,128)(2,1)S(1)}, u32[]{:S(2)}, u32[]{:S(2)}) collective-permute-start(bf16[24,22,256]{2,1,0:T(8,128)(2,1)S(1)} %all-to-all-done), channel_id=1, source_target_pairs={{0,16},{16,0},{1,17},{17,1},{2,18},{18,2},{3,19},{19,3},{4,20},{20... | collective-permute-start | bytes 811016 | tf_op jit(solution)/shard_map/ppermute | solution.py:21
  39.5 0.0 collective-permute-done.1.recv_ref
  39.6 0.6 shard_map.69
  40.1 0.1 copy.11
  40.2 0.5 collective-permute-done
  40.7 0.1 copy.12
  40.8 0.1 fusion
  40.9 0.4 copy.13
  41.3 0.1 copy.14
  41.4 0.4 convolution_convert_fusion
  41.8 23.0 %all_to_all.15.both_ref = bf16[16,64,256]{2,1,0:T(8,128)(2,1)S(1)} all-to-all(bf16[16,64,256]{2,1,0:T(8,128)(2,1)S(1)} %pad_maximum_fusion), channel_id=1, replica_groups={{0,1,2,3,4,5,6,7,392,393,394,395,396,397,398,399},{384,385,386,387,388,..., dimensions={0} | all-to-all | bytes 1048576 | tf_op jit(solution)/shard_map/all_to_all | solution.py:375
  64.8 0.5 shard_map.70
  65.3 4.3 %collective-permute-start.2 = (bf16[24,22,256]{2,1,0:T(8,128)(2,1)S(1)}, bf16[24,22,256]{2,1,0:T(8,128)(2,1)S(1)}, u32[]{:S(2)}, u32[]{:S(2)}) collective-permute-start(bf16[24,22,256]{2,1,0:T(8,128)(2,1)S(1)} %get-tuple-element.20), channel_id=1, source_target_pairs={{0,16},{16,0},{1,17},{17,1},{2,18},{18,2},{3,19},{19,3},{4,20},{20... | collective-permute-start | bytes 811016 | tf_op jit(solution)/shard_map/ppermute | solution.py:21
  69.6 0.3 shard_map.71
  70.0 0.8 collective-permute-done.2
  70.8 0.8 add_convert_fusion
  71.6 4.2 %all-to-all-start.2 = ((bf16[24,22,256]{2,1,0:T(8,128)(2,1)}), bf16[24,22,256]{2,1,0:T(8,128)(2,1)S(1)}, u32[]{:S(2)}, u32[]{:S(2)}) async-start(bf16[24,22,256]{2,1,0:T(8,128)(2,1)} %add_convert_fusion), calls=%async_computation.2 | async-start | bytes 589824 | tf_op jit(solution)/shard_map/all_to_all | solution.py:384
  75.8 3.2 %collective-permute-start.3 = (bf16[272,512]{1,0:T(8,128)(2,1)S(1)}, bf16[272,512]{1,0:T(8,128)(2,1)S(1)}, u32[]{:S(2)}, u32[]{:S(2)}) collective-permute-start(bf16[272,512]{1,0:T(8,128)(2,1)S(1)} %get-tuple-element.24), channel_id=1, source_target_pairs={{0,384},{384,0},{1,385},{385,1},{2,386},{386,2},{3,387},{387,3},{4... | collective-permute-start | bytes 835592 | tf_op jit(solution)/shard_map/ppermute | solution.py:17
  79.0 0.6 reduce_sum.9
  80.3 0.1 add_minimum_fusion
  80.4 0.1 pad_add_fusion.place_ref
  80.5 6.5 %collective-permute-done.3.recv_ref = bf16[272,512]{1,0:T(8,128)(2,1)S(1)} collective-permute-done((bf16[272,512]{1,0:T(8,128)(2,1)S(1)}, bf16[272,512]{1,0:T(8,128)(2,1)S(1)}, u32[]{:S(2)}, u32[]{:S(2)}) %collective-permute-start.3) | collective-permute-done | bytes 278560 | tf_op jit(solution)/shard_map/ppermute | solution.py:17
  87.0 1.3 %shard_map.72 = (bf16[256,512]{1,0:T(8,128)(2,1)}, bf16[64,256]{1,0:T(8,128)(2,1)}) custom-call(s32[5]{0:T(128)S(1)} %pad_add_fusion.place_ref, f32[256,512]{1,0:T(8,128)S(1)} %get-tuple-element.23.keep_ref, bf16[272,512]{1,0:T(8,128)(2,1)S(1)} %collective-permute-done.3.recv_ref, bf16[32,256]{1,0:T(8,128)(2,1)S(1)} %get-tuple-element.25.kv_ref), custom_call_target="tpu_custom_call" | custom-call | flops 131072 | bytes 1048576 | tf_op jit(solution)/shard_map/pallas_call | solution.py:141
  88.3 2.4 %all-to-all-done.2.parts_ref = bf16[24,22,256]{2,1,0:T(8,128)(2,1)S(1)} async-done(((bf16[24,22,256]{2,1,0:T(8,128)(2,1)}), bf16[24,22,256]{2,1,0:T(8,128)(2,1)S(1)}, u32[]{:S(2)}, u32[]{:S(2)}) %all-to-all-start.2) | async-done | bytes 270368 | tf_op jit(solution)/shard_map/all_to_all | solution.py:384
  90.7 1.0 %shard_map.73 = f32[11,1024]{1,0:T(8,128)} custom-call(s32[1]{0:T(128)} %bitcast.5.turn_ref, bf16[24,22,256]{2,1,0:T(8,128)(2,1)S(1)} %all-to-all-done.2.parts_ref), custom_call_target="tpu_custom_call" | custom-call | flops 17301504 | bytes 524288 | tf_op jit(solution)/shard_map/pallas_call | solution.py:239
  (3 shorter events, 0.1 us)
Async XLA Ops:
  0.6 0.8 copy-start.2
  2.3 17.8 %copy-start = (bf16[256,512]{1,0:T(8,128)(2,1)S(1)}, bf16[256,512]{1,0:T(8,128)(2,1)}, u32[]{:S(2)}) copy-start(bf16[256,512]{1,0:T(8,128)(2,1)} %x_ref.3) | copy-start | bytes 786436
  2.3 17.8 %copy-start.1 = (bf16[256,64]{0,1:T(8,128)(2,1)S(1)}, bf16[256,64]{0,1:T(8,128)(2,1)}, u32[]{:S(2)}) copy-start(bf16[256,64]{0,1:T(8,128)(2,1)} %param.6) | copy-start | bytes 98308
  2.3 31.6 %all-to-all-start = ((bf16[24,22,256]{2,1,0:T(8,128)(2,1)}), bf16[24,22,256]{2,1,0:T(8,128)(2,1)S(1)}, u32[]{:S(2)}, u32[]{:S(2)}) async-start(bf16[24,22,256]{2,1,0:T(8,128)(2,1)} %shard_map.67), calls=%async_computation | async-start | bytes 589824 | tf_op jit(solution)/shard_map/all_to_all | solution.py:361
  19.4 0.7 copy-start.3
  20.7 18.8 %collective-permute-start.1 = (bf16[272,512]{1,0:T(8,128)(2,1)S(1)}, bf16[272,512]{1,0:T(8,128)(2,1)S(1)}, u32[]{:S(2)}, u32[]{:S(2)}) collective-permute-start(bf16[272,512]{1,0:T(8,128)(2,1)S(1)} %shard_map.68), channel_id=1, source_target_pairs={{0,384},{384,0},{1,385},{385,1},{2,386},{386,2},{3,387},{387,3},{4... | collective-permute-start | bytes 835592 | tf_op jit(solution)/shard_map/ppermute | solution.py:17
  33.9 6.8 %collective-permute-start = (bf16[24,22,256]{2,1,0:T(8,128)(2,1)S(1)}, bf16[24,22,256]{2,1,0:T(8,128)(2,1)S(1)}, u32[]{:S(2)}, u32[]{:S(2)}) collective-permute-start(bf16[24,22,256]{2,1,0:T(8,128)(2,1)S(1)} %all-to-all-done), channel_id=1, source_target_pairs={{0,16},{16,0},{1,17},{17,1},{2,18},{18,2},{3,19},{19,3},{4,20},{20... | collective-permute-start | bytes 811016 | tf_op jit(solution)/shard_map/ppermute | solution.py:21
  65.3 5.5 %collective-permute-start.2 = (bf16[24,22,256]{2,1,0:T(8,128)(2,1)S(1)}, bf16[24,22,256]{2,1,0:T(8,128)(2,1)S(1)}, u32[]{:S(2)}, u32[]{:S(2)}) collective-permute-start(bf16[24,22,256]{2,1,0:T(8,128)(2,1)S(1)} %get-tuple-element.20), channel_id=1, source_target_pairs={{0,16},{16,0},{1,17},{17,1},{2,18},{18,2},{3,19},{19,3},{4,20},{20... | collective-permute-start | bytes 811016 | tf_op jit(solution)/shard_map/ppermute | solution.py:21
  71.6 19.1 %all-to-all-start.2 = ((bf16[24,22,256]{2,1,0:T(8,128)(2,1)}), bf16[24,22,256]{2,1,0:T(8,128)(2,1)S(1)}, u32[]{:S(2)}, u32[]{:S(2)}) async-start(bf16[24,22,256]{2,1,0:T(8,128)(2,1)} %add_convert_fusion), calls=%async_computation.2 | async-start | bytes 589824 | tf_op jit(solution)/shard_map/all_to_all | solution.py:384
  75.8 11.2 %collective-permute-start.3 = (bf16[272,512]{1,0:T(8,128)(2,1)S(1)}, bf16[272,512]{1,0:T(8,128)(2,1)S(1)}, u32[]{:S(2)}, u32[]{:S(2)}) collective-permute-start(bf16[272,512]{1,0:T(8,128)(2,1)S(1)} %get-tuple-element.24), channel_id=1, source_target_pairs={{0,384},{384,0},{1,385},{385,1},{2,386},{386,2},{3,387},{387,3},{4... | collective-permute-start | bytes 835592 | tf_op jit(solution)/shard_map/ppermute | solution.py:17

commit v13 on v12

--- a/solution.py
+++ b/solution.py
@@ -21,7 +21,7 @@
     return lax.ppermute(value, "core", SWAP)
 
 
-def weight_kernel(blocks, wrows, core_ref, both_ref, x_ref, mine_ref, theirs_ref, acc_ref, stage_ref):
+def weight_kernel(blocks, wrows, core_ref, both_ref, x_ref, mine_ref, theirs_ref, acc_ref, own_ref, stage_ref):
     tokens, feats = x_ref.shape
     n_mp, rows, _ = both_ref.shape
     half = rows // 2
@@ -40,8 +40,9 @@
         for part in range(2):
             top = acc_ref[part, pl.ds(2 * block * wrows, wrows)]
             bottom = acc_ref[part, pl.ds((2 * block + 1) * wrows, wrows)]
-            mine_ref[block, pl.ds(part * wrows, wrows)] = jnp.where(first_core, top, bottom)
+            own_ref[block, pl.ds(part * wrows, wrows)] = jnp.where(first_core, top, bottom)
             stage_ref[block, pl.ds(part * wrows, wrows)] = jnp.where(first_core, bottom, top)
+        mine_ref[block] = own_ref[block, : 2 * wrows].astype(BF16)
         theirs_ref[block] = stage_ref[block, : 2 * wrows].astype(BF16)
 
 
@@ -54,11 +55,12 @@
     shape = (blocks, 2 * wrows, width)
     return pl.pallas_call(
         functools.partial(weight_kernel, blocks, wrows),
-        out_shape=(jax.ShapeDtypeStruct(shape, F32), jax.ShapeDtypeStruct(shape, BF16)),
+        out_shape=(jax.ShapeDtypeStruct(shape, BF16), jax.ShapeDtypeStruct(shape, BF16)),
         in_specs=[pl.BlockSpec(memory_space=pltpu.SMEM), vmem, vmem],
         out_specs=(vmem, vmem),
         scratch_shapes=[
             pltpu.VMEM((2, 2 * blocks * wrows, width), F32),
+            pltpu.VMEM((blocks, padded, width), F32),
             pltpu.VMEM((blocks, padded, width), F32),
         ],
         compiler_params=pltpu.CompilerParams(vmem_limit_bytes=32 * 2**20),
@@ -74,8 +76,9 @@
     half = rows // 2
     g = both_ref[:, half:, :].reshape(n_mp * half, tokens)
     dx = lax.dot_general(g.T, w_ref[...], (((1,), (1,)), ((), ())), preferred_element_type=F32)
+    dx = dx.astype(BF16)
     keep_ref[...] = dx
-    send_ref[:tokens] = dx.astype(BF16)
+    send_ref[:tokens] = dx
     kv = jnp.sum(both_ref[:, :half, :].astype(F32), axis=0).astype(BF16)
     kv_ref[...] = kv
     lanes = feats // tokens
@@ -93,7 +96,7 @@
         return_kernel,
         out_shape=(
             jax.ShapeDtypeStruct((tokens + half * tokens // feats, feats), BF16),
-            jax.ShapeDtypeStruct((tokens, feats), F32),
+            jax.ShapeDtypeStruct((tokens, feats), BF16),
             jax.ShapeDtypeStruct((half, tokens), BF16),
         ),
         in_specs=[vmem, vmem],
@@ -126,7 +129,7 @@
         alive = place_ref[seq] != 0
         slot = place_ref[seqs + seq]
         rows = pl.ds(pl.multiple_of(slot * span, span), span)
-        total = keep_ref[rows] + recv_ref[rows].astype(F32)
+        total = keep_ref[rows].astype(F32) + recv_ref[rows].astype(F32)
         here = slice(seq * span, (seq + 1) * span)
         dx_ref[here] = jnp.where(alive, total, 0.0).astype(BF16)
         for at, value in ((0, low), (half, high)):
@@ -376,7 +379,7 @@
 
     dw_mine, dw_theirs = weight_blocks(core, both, x_pair, 2 * n_z, wrows)
     dw_theirs, both = lax.optimization_barrier((dw_theirs, both))
-    dw_sum = dw_mine + swap_core(dw_theirs).astype(F32)
+    dw_sum = dw_mine.astype(F32) + swap_core(dw_theirs).astype(F32)
 
     send, keep, kv = return_parts(both, w_full)
     received = swap_pair(send)

time: 93.4 us -> 93.4 us (level)
  no operation moved by 1% of the time
where the time goes in v13:
time: 93.4 us; the launch traced here: 91.7 us
  starting transfers between devices  37.5 us (40%)
  blocking collectives  23 us (25%)
  waiting for transfers between devices  20.2 us (22%)
  Pallas kernels  5.3 us (6%)
  local copies, waits for them, and re-layouts  2.06 us (2%)
  other arithmetic  1.76 us (2%)
  between operations  1.53 us (2%)
    all_to_all x1, blocking collectives, on_device(): lax.all_to_all(both, ('pair', 'mp'), 0, 0, axis_index_groups=groups, tile...  23 us
    all_to_all x1, starting transfers between devices, on_device(): lax.all_to_all(spread_weight(turn, w, half, n_z), ('pair', 'z'), 0, 0, ti...  17.1 us
    all_to_all x1, waiting for transfers between devices, on_device(): lax.all_to_all(spread_weight(turn, w, half, n_z), ('pair', 'z'), 0, 0, ti...  10 us
    ppermute x2, starting transfers between devices, swap_core(): return lax.ppermute(value, 'core', SWAP)  9.87 us
    ppermute x2, waiting for transfers between devices, swap_pair(): return lax.ppermute(value, 'pair', SWAP)  6.55 us
    ppermute x2, starting transfers between devices, swap_pair(): return lax.ppermute(value, 'pair', SWAP)  6.4 us
    all_to_all x1, starting transfers between devices, on_device(): dw_parts = lax.all_to_all(dw_send, ('pair', 'z'), 0, 0, tiled=True)  4.2 us
    all_to_all x1, waiting for transfers between devices, on_device(): dw_parts = lax.all_to_all(dw_send, ('pair', 'z'), 0, 0, tiled=True)  2.34 us
  transfers between devices with their start and end apart: 6, of which 5 were waited for; matrix products, arithmetic and copies ran while one was open for 1% of the time, Pallas kernels for 3%

profile of v13, /device:TPU:1, one launch (start us, length us, event | category | flops | bytes accessed | tf_op | source)
XLA Modules:
  0.0 91.7 jit_solution(9439870712926419853)
XLA Ops:
  0.6 0.0 copy-start.2
  0.7 0.7 copy-done.2
  1.4 0.9 %shard_map.67 = bf16[24,22,256]{2,1,0:T(8,128)(2,1)} custom-call(s32[1]{0:T(128)} %bitcast.5.turn_ref, bf16[11,1024]{1,0:T(8,128)(2,1)S(1)} %copy-done.2), custom_call_target="tpu_custom_call" | custom-call | flops 5767168 | bytes 524288 | tf_op jit(solution)/shard_map/pallas_call | solution.py:192
  2.3 0.0 copy-start
  2.3 0.0 copy-start.1
  2.3 17.1 %all-to-all-start = ((bf16[24,22,256]{2,1,0:T(8,128)(2,1)}), bf16[24,22,256]{2,1,0:T(8,128)(2,1)S(1)}, u32[]{:S(2)}, u32[]{:S(2)}) async-start(bf16[24,22,256]{2,1,0:T(8,128)(2,1)} %shard_map.67), calls=%async_computation | async-start | bytes 589824 | tf_op jit(solution)/shard_map/all_to_all | solution.py:364
  19.4 0.0 copy-start.3
  19.4 0.6 copy-done.3
  20.1 0.1 pad_add_fusion.1.mask_ref
  20.1 0.0 copy-done
  20.1 0.0 copy-done.1
  20.1 0.6 shard_map.68
  20.7 3.2 %collective-permute-start.1 = (bf16[272,512]{1,0:T(8,128)(2,1)S(1)}, bf16[272,512]{1,0:T(8,128)(2,1)S(1)}, u32[]{:S(2)}, u32[]{:S(2)}) collective-permute-start(bf16[272,512]{1,0:T(8,128)(2,1)S(1)} %shard_map.68), channel_id=1, source_target_pairs={{0,384},{384,0},{1,385},{385,1},{2,386},{386,2},{3,387},{387,3},{4... | collective-permute-start | bytes 835592 | tf_op jit(solution)/shard_map/ppermute | solution.py:17
  23.9 10.0 %all-to-all-done = bf16[24,22,256]{2,1,0:T(8,128)(2,1)S(1)} async-done(((bf16[24,22,256]{2,1,0:T(8,128)(2,1)}), bf16[24,22,256]{2,1,0:T(8,128)(2,1)S(1)}, u32[]{:S(2)}, u32[]{:S(2)}) %all-to-all-start) | async-done | bytes 270368 | tf_op jit(solution)/shard_map/all_to_all | solution.py:364
  33.9 5.6 %collective-permute-start = (bf16[24,22,256]{2,1,0:T(8,128)(2,1)S(1)}, bf16[24,22,256]{2,1,0:T(8,128)(2,1)S(1)}, u32[]{:S(2)}, u32[]{:S(2)}) collective-permute-start(bf16[24,22,256]{2,1,0:T(8,128)(2,1)S(1)} %all-to-all-done), channel_id=1, source_target_pairs={{0,16},{16,0},{1,17},{17,1},{2,18},{18,2},{3,19},{19,3},{4,20},{20... | collective-permute-start | bytes 811016 | tf_op jit(solution)/shard_map/ppermute | solution.py:21
  39.5 0.0 collective-permute-done.1.recv_ref
  39.6 0.6 shard_map.69
  40.1 0.1 copy.11
  40.2 0.5 collective-permute-done
  40.7 0.1 copy.12
  40.8 0.1 fusion
  40.9 0.4 copy.13
  41.3 0.1 copy.14
  41.4 0.3 convolution_convert_fusion
  41.8 23.0 %all_to_all.15.both_ref = bf16[16,64,256]{2,1,0:T(8,128)(2,1)S(1)} all-to-all(bf16[16,64,256]{2,1,0:T(8,128)(2,1)S(1)} %pad_maximum_fusion), channel_id=1, replica_groups={{0,1,2,3,4,5,6,7,392,393,394,395,396,397,398,399},{384,385,386,387,388,..., dimensions={0} | all-to-all | bytes 1048576 | tf_op jit(solution)/shard_map/all_to_all | solution.py:378
  64.8 0.5 shard_map.70
  65.3 4.3 %collective-permute-start.2 = (bf16[24,22,256]{2,1,0:T(8,128)(2,1)S(1)}, bf16[24,22,256]{2,1,0:T(8,128)(2,1)S(1)}, u32[]{:S(2)}, u32[]{:S(2)}) collective-permute-start(bf16[24,22,256]{2,1,0:T(8,128)(2,1)S(1)} %get-tuple-element.20), channel_id=1, source_target_pairs={{0,16},{16,0},{1,17},{17,1},{2,18},{18,2},{3,19},{19,3},{4,20},{20... | collective-permute-start | bytes 811016 | tf_op jit(solution)/shard_map/ppermute | solution.py:21
  69.7 0.3 shard_map.71
  70.0 0.8 collective-permute-done.2
  70.8 0.8 add_convert_fusion
  71.6 4.2 %all-to-all-start.2 = ((bf16[24,22,256]{2,1,0:T(8,128)(2,1)}), bf16[24,22,256]{2,1,0:T(8,128)(2,1)S(1)}, u32[]{:S(2)}, u32[]{:S(2)}) async-start(bf16[24,22,256]{2,1,0:T(8,128)(2,1)} %add_convert_fusion), calls=%async_computation.2 | async-start | bytes 589824 | tf_op jit(solution)/shard_map/all_to_all | solution.py:387
  75.8 3.2 %collective-permute-start.3 = (bf16[272,512]{1,0:T(8,128)(2,1)S(1)}, bf16[272,512]{1,0:T(8,128)(2,1)S(1)}, u32[]{:S(2)}, u32[]{:S(2)}) collective-permute-start(bf16[272,512]{1,0:T(8,128)(2,1)S(1)} %get-tuple-element.24), channel_id=1, source_target_pairs={{0,384},{384,0},{1,385},{385,1},{2,386},{386,2},{3,387},{387,3},{4... | collective-permute-start | bytes 835592 | tf_op jit(solution)/shard_map/ppermute | solution.py:17
  79.0 0.6 reduce_sum.9
  80.3 0.1 add_minimum_fusion
  80.4 0.1 pad_add_fusion.place_ref
  80.5 6.5 %collective-permute-done.3.recv_ref = bf16[272,512]{1,0:T(8,128)(2,1)S(1)} collective-permute-done((bf16[272,512]{1,0:T(8,128)(2,1)S(1)}, bf16[272,512]{1,0:T(8,128)(2,1)S(1)}, u32[]{:S(2)}, u32[]{:S(2)}) %collective-permute-start.3) | collective-permute-done | bytes 278560 | tf_op jit(solution)/shard_map/ppermute | solution.py:17
  87.0 1.3 %shard_map.72 = (bf16[256,512]{1,0:T(8,128)(2,1)}, bf16[64,256]{1,0:T(8,128)(2,1)}) custom-call(s32[5]{0:T(128)S(1)} %pad_add_fusion.place_ref, bf16[256,512]{1,0:T(8,128)(2,1)S(1)} %get-tuple-element.23.keep_ref, bf16[272,512]{1,0:T(8,128)(2,1)S(1)} %collective-permute-done.3.recv_ref, bf16[32,256]{1,0:T(8,128)(2,1)S(1)} %get-tuple-element.25.kv_ref), custom_call_target="tpu_custom_call" | custom-call | flops 131072 | bytes 1048576 | tf_op jit(solution)/shard_map/pallas_call | solution.py:144
  88.4 2.3 %all-to-all-done.2.parts_ref = bf16[24,22,256]{2,1,0:T(8,128)(2,1)S(1)} async-done(((bf16[24,22,256]{2,1,0:T(8,128)(2,1)}), bf16[24,22,256]{2,1,0:T(8,128)(2,1)S(1)}, u32[]{:S(2)}, u32[]{:S(2)}) %all-to-all-start.2) | async-done | bytes 270368 | tf_op jit(solution)/shard_map/all_to_all | solution.py:387
  90.7 1.0 %shard_map.73 = f32[11,1024]{1,0:T(8,128)} custom-call(s32[1]{0:T(128)} %bitcast.5.turn_ref, bf16[24,22,256]{2,1,0:T(8,128)(2,1)S(1)} %all-to-all-done.2.parts_ref), custom_call_target="tpu_custom_call" | custom-call | flops 17301504 | bytes 524288 | tf_op jit(solution)/shard_map/pallas_call | solution.py:242
  (3 shorter events, 0.1 us)
Async XLA Ops:
  0.6 0.8 copy-start.2
  2.3 17.8 %copy-start = (bf16[256,512]{1,0:T(8,128)(2,1)S(1)}, bf16[256,512]{1,0:T(8,128)(2,1)}, u32[]{:S(2)}) copy-start(bf16[256,512]{1,0:T(8,128)(2,1)} %x_ref.3) | copy-start | bytes 786436
  2.3 17.8 %copy-start.1 = (bf16[256,64]{0,1:T(8,128)(2,1)S(1)}, bf16[256,64]{0,1:T(8,128)(2,1)}, u32[]{:S(2)}) copy-start(bf16[256,64]{0,1:T(8,128)(2,1)} %param.6) | copy-start | bytes 98308
  2.3 31.6 %all-to-all-start = ((bf16[24,22,256]{2,1,0:T(8,128)(2,1)}), bf16[24,22,256]{2,1,0:T(8,128)(2,1)S(1)}, u32[]{:S(2)}, u32[]{:S(2)}) async-start(bf16[24,22,256]{2,1,0:T(8,128)(2,1)} %shard_map.67), calls=%async_computation | async-start | bytes 589824 | tf_op jit(solution)/shard_map/all_to_all | solution.py:364
  19.4 0.7 copy-start.3
  20.7 18.8 %collective-permute-start.1 = (bf16[272,512]{1,0:T(8,128)(2,1)S(1)}, bf16[272,512]{1,0:T(8,128)(2,1)S(1)}, u32[]{:S(2)}, u32[]{:S(2)}) collective-permute-start(bf16[272,512]{1,0:T(8,128)(2,1)S(1)} %shard_map.68), channel_id=1, source_target_pairs={{0,384},{384,0},{1,385},{385,1},{2,386},{386,2},{3,387},{387,3},{4... | collective-permute-start | bytes 835592 | tf_op jit(solution)/shard_map/ppermute | solution.py:17
  33.9 6.8 %collective-permute-start = (bf16[24,22,256]{2,1,0:T(8,128)(2,1)S(1)}, bf16[24,22,256]{2,1,0:T(8,128)(2,1)S(1)}, u32[]{:S(2)}, u32[]{:S(2)}) collective-permute-start(bf16[24,22,256]{2,1,0:T(8,128)(2,1)S(1)} %all-to-all-done), channel_id=1, source_target_pairs={{0,16},{16,0},{1,17},{17,1},{2,18},{18,2},{3,19},{19,3},{4,20},{20... | collective-permute-start | bytes 811016 | tf_op jit(solution)/shard_map/ppermute | solution.py:21
  65.3 5.5 %collective-permute-start.2 = (bf16[24,22,256]{2,1,0:T(8,128)(2,1)S(1)}, bf16[24,22,256]{2,1,0:T(8,128)(2,1)S(1)}, u32[]{:S(2)}, u32[]{:S(2)}) collective-permute-start(bf16[24,22,256]{2,1,0:T(8,128)(2,1)S(1)} %get-tuple-element.20), channel_id=1, source_target_pairs={{0,16},{16,0},{1,17},{17,1},{2,18},{18,2},{3,19},{19,3},{4,20},{20... | collective-permute-start | bytes 811016 | tf_op jit(solution)/shard_map/ppermute | solution.py:21
  71.6 19.1 %all-to-all-start.2 = ((bf16[24,22,256]{2,1,0:T(8,128)(2,1)}), bf16[24,22,256]{2,1,0:T(8,128)(2,1)S(1)}, u32[]{:S(2)}, u32[]{:S(2)}) async-start(bf16[24,22,256]{2,1,0:T(8,128)(2,1)} %add_convert_fusion), calls=%async_computation.2 | async-start | bytes 589824 | tf_op jit(solution)/shard_map/all_to_all | solution.py:387
  75.8 11.2 %collective-permute-start.3 = (bf16[272,512]{1,0:T(8,128)(2,1)S(1)}, bf16[272,512]{1,0:T(8,128)(2,1)S(1)}, u32[]{:S(2)}, u32[]{:S(2)}) collective-permute-start(bf16[272,512]{1,0:T(8,128)(2,1)S(1)} %get-tuple-element.24), channel_id=1, source_target_pairs={{0,384},{384,0},{1,385},{385,1},{2,386},{386,2},{3,387},{387,3},{4... | collective-permute-start | bytes 835592 | tf_op jit(solution)/shard_map/ppermute | solution.py:17

commit v14 on v12

--- a/solution.py
+++ b/solution.py
@@ -37,12 +37,15 @@
         acc_ref[part, feats:] = jnp.zeros_like(acc_ref[part, feats:])
     stage_ref[:, 2 * wrows :] = jnp.zeros_like(stage_ref[:, 2 * wrows :])
     for block in range(blocks):
+        ahead, back = block, blocks - 1 - block
+        mine = jnp.where(first_core, ahead, back)
+        theirs = jnp.where(first_core, back, ahead)
         for part in range(2):
             top = acc_ref[part, pl.ds(2 * block * wrows, wrows)]
             bottom = acc_ref[part, pl.ds((2 * block + 1) * wrows, wrows)]
-            mine_ref[block, pl.ds(part * wrows, wrows)] = jnp.where(first_core, top, bottom)
+            mine_ref[mine, pl.ds(part * wrows, wrows)] = jnp.where(first_core, top, bottom)
             stage_ref[block, pl.ds(part * wrows, wrows)] = jnp.where(first_core, bottom, top)
-        theirs_ref[block] = stage_ref[block, : 2 * wrows].astype(BF16)
+        theirs_ref[theirs] = stage_ref[block, : 2 * wrows].astype(BF16)
 
 
 def weight_blocks(core, both, x_pair, blocks, wrows):
@@ -381,8 +384,12 @@
     send, keep, kv = return_parts(both, w_full)
     received = swap_pair(send)
     dw_send, keep = lax.optimization_barrier((dw_sum.astype(BF16), keep))
-    dw_parts = lax.all_to_all(dw_send, ("pair", "z"), 0, 0, tiled=True)
-    weight_grad = sum_blocks(turn, dw_parts, half, wrows)
+    ahead = [2 * k for k in range(2 * n_z)]
+    back = [2 * k + 1 for k in reversed(range(2 * n_z))]
+    dw_parts = lax.all_to_all(
+        dw_send, ("pair", "z", "core"), 0, 0, axis_index_groups=[ahead, back], tiled=True
+    )
+    weight_grad = sum_blocks(jnp.bitwise_xor(turn, core), dw_parts, half, wrows)
 
     start = jnp.where(side == 0, 0, 2 - count)
     slots = jnp.minimum(jnp.stack([start, start + mask[0]]), 1)

time: 93.4 us -> 93.9 us (level); the launches traced: 91.7 us -> 93.4 us
  starting transfers between devices: 37.5 us -> 38.7 us
    all_to_all x1, starting transfers between devices: 4.2 us -> 6.4 us  [on_device(): lax.all_to_all(dw_send, ('pair', 'z', 'core'), 0, 0, axis_index_groups=[a...]
    ppermute x2, waiting for transfers between devices: 6.55 us -> 8.2 us  [swap_pair(): return lax.ppermute(value, 'pair', SWAP)]
    all_to_all x1, waiting for transfers between devices: 2.36 us -> 1.22 us  [on_device(): lax.all_to_all(dw_send, ('pair', 'z', 'core'), 0, 0, axis_index_groups=[a...]
    ppermute x2, starting transfers between devices: 6.4 us -> 5.36 us  [swap_pair(): return lax.ppermute(value, 'pair', SWAP)]
where the time goes in v14:
time: 93.9 us; the launch traced here: 93.4 us
  starting transfers between devices  38.7 us (41%)
  blocking collectives  23 us (24%)
  waiting for transfers between devices  20.8 us (22%)
  Pallas kernels  5.27 us (6%)
  local copies, waits for them, and re-layouts  2.06 us (2%)
  other arithmetic  1.76 us (2%)
  between operations  1.53 us (2%)
    all_to_all x1, blocking collectives, on_device(): lax.all_to_all(both, ('pair', 'mp'), 0, 0, axis_index_groups=groups, tile...  23 us
    all_to_all x1, starting transfers between devices, on_device(): lax.all_to_all(spread_weight(turn, w, half, n_z), ('pair', 'z'), 0, 0, ti...  17.1 us
    all_to_all x1, waiting for transfers between devices, on_device(): lax.all_to_all(spread_weight(turn, w, half, n_z), ('pair', 'z'), 0, 0, ti...  10 us
    ppermute x2, starting transfers between devices, swap_core(): return lax.ppermute(value, 'core', SWAP)  9.86 us
    ppermute x2, waiting for transfers between devices, swap_pair(): return lax.ppermute(value, 'pair', SWAP)  8.2 us
    all_to_all x1, starting transfers between devices, on_device(): lax.all_to_all(dw_send, ('pair', 'z', 'core'), 0, 0, axis_index_groups=[a...  6.4 us
    ppermute x2, starting transfers between devices, swap_pair(): return lax.ppermute(value, 'pair', SWAP)  5.36 us
  transfers between devices with their start and end apart: 6, of which 5 were waited for; matrix products, arithmetic and copies ran while one was open for 1% of the time, Pallas kernels for 3%

profile of v14, /device:TPU:1, one launch (start us, length us, event | category | flops | bytes accessed | tf_op | source)
XLA Modules:
  0.0 93.4 jit_solution(11327339503994105158)
XLA Ops:
  0.6 0.0 copy-start.2
  0.7 0.7 copy-done.2
  1.4 0.9 shard_map.67
  2.3 0.0 copy-start
  2.3 0.0 copy-start.1
  2.3 17.1 %all-to-all-start = ((bf16[24,22,256]{2,1,0:T(8,128)(2,1)}), bf16[24,22,256]{2,1,0:T(8,128)(2,1)S(1)}, u32[]{:S(2)}, u32[]{:S(2)}) async-start(bf16[24,22,256]{2,1,0:T(8,128)(2,1)} %shard_map.67), calls=%async_computation | async-start | bytes 589824 | tf_op jit(solution)/shard_map/all_to_all | solution.py:364
  19.4 0.0 copy-start.3
  19.4 0.6 copy-done.3
  20.1 0.1 pad_add_fusion.1.mask_ref
  20.1 0.0 copy-done
  20.1 0.0 copy-done.1
  20.1 0.6 shard_map.68
  20.7 3.2 %collective-permute-start.1 = (bf16[272,512]{1,0:T(8,128)(2,1)S(1)}, bf16[272,512]{1,0:T(8,128)(2,1)S(1)}, u32[]{:S(2)}, u32[]{:S(2)}) collective-permute-start(bf16[272,512]{1,0:T(8,128)(2,1)S(1)} %shard_map.68), channel_id=1, source_target_pairs={{0,384},{384,0},{1,385},{385,1},{2,386},{386,2},{3,387},{387,3},{4... | collective-permute-start | bytes 835592 | tf_op jit(solution)/shard_map/ppermute | solution.py:17
  23.9 10.0 %all-to-all-done = bf16[24,22,256]{2,1,0:T(8,128)(2,1)S(1)} async-done(((bf16[24,22,256]{2,1,0:T(8,128)(2,1)}), bf16[24,22,256]{2,1,0:T(8,128)(2,1)S(1)}, u32[]{:S(2)}, u32[]{:S(2)}) %all-to-all-start) | async-done | bytes 270368 | tf_op jit(solution)/shard_map/all_to_all | solution.py:364
  33.9 5.6 %collective-permute-start = (bf16[24,22,256]{2,1,0:T(8,128)(2,1)S(1)}, bf16[24,22,256]{2,1,0:T(8,128)(2,1)S(1)}, u32[]{:S(2)}, u32[]{:S(2)}) collective-permute-start(bf16[24,22,256]{2,1,0:T(8,128)(2,1)S(1)} %all-to-all-done), channel_id=1, source_target_pairs={{0,16},{16,0},{1,17},{17,1},{2,18},{18,2},{3,19},{19,3},{4,20},{20... | collective-permute-start | bytes 811016 | tf_op jit(solution)/shard_map/ppermute | solution.py:21
  39.5 0.0 collective-permute-done.1.recv_ref
  39.6 0.6 shard_map.69
  40.1 0.1 copy.11
  40.2 0.5 collective-permute-done
  40.7 0.1 copy.12
  40.8 0.1 fusion
  40.9 0.4 copy.13
  41.3 0.1 copy.14
  41.4 0.4 convolution_convert_fusion
  41.8 23.0 %all_to_all.15.both_ref = bf16[16,64,256]{2,1,0:T(8,128)(2,1)S(1)} all-to-all(bf16[16,64,256]{2,1,0:T(8,128)(2,1)S(1)} %pad_maximum_fusion), channel_id=1, replica_groups={{0,1,2,3,4,5,6,7,392,393,394,395,396,397,398,399},{384,385,386,387,388,..., dimensions={0} | all-to-all | bytes 1048576 | tf_op jit(solution)/shard_map/all_to_all | solution.py:378
  64.8 0.5 shard_map.70
  65.3 4.3 %collective-permute-start.2 = (bf16[24,22,256]{2,1,0:T(8,128)(2,1)S(1)}, bf16[24,22,256]{2,1,0:T(8,128)(2,1)S(1)}, u32[]{:S(2)}, u32[]{:S(2)}) collective-permute-start(bf16[24,22,256]{2,1,0:T(8,128)(2,1)S(1)} %get-tuple-element.20), channel_id=1, source_target_pairs={{0,16},{16,0},{1,17},{17,1},{2,18},{18,2},{3,19},{19,3},{4,20},{20... | collective-permute-start | bytes 811016 | tf_op jit(solution)/shard_map/ppermute | solution.py:21
  69.6 0.3 shard_map.71
  70.0 0.8 collective-permute-done.2
  70.8 0.8 add_convert_fusion
  71.6 6.4 %all-to-all-start.2 = ((bf16[24,22,256]{2,1,0:T(8,128)(2,1)}), bf16[24,22,256]{2,1,0:T(8,128)(2,1)S(1)}, u32[]{:S(2)}, u32[]{:S(2)}) async-start(bf16[24,22,256]{2,1,0:T(8,128)(2,1)} %add_convert_fusion), calls=%async_computation.2 | async-start | bytes 589824 | tf_op jit(solution)/shard_map/all_to_all | solution.py:389
  78.0 2.2 %collective-permute-start.3 = (bf16[272,512]{1,0:T(8,128)(2,1)S(1)}, bf16[272,512]{1,0:T(8,128)(2,1)S(1)}, u32[]{:S(2)}, u32[]{:S(2)}) collective-permute-start(bf16[272,512]{1,0:T(8,128)(2,1)S(1)} %get-tuple-element.24), channel_id=1, source_target_pairs={{0,384},{384,0},{1,385},{385,1},{2,386},{386,2},{3,387},{387,3},{4... | collective-permute-start | bytes 835592 | tf_op jit(solution)/shard_map/ppermute | solution.py:17
  80.1 0.6 reduce_sum.9
  81.5 0.1 add_minimum_fusion
  81.5 0.1 pad_add_fusion.place_ref
  81.6 8.2 %collective-permute-done.3.recv_ref = bf16[272,512]{1,0:T(8,128)(2,1)S(1)} collective-permute-done((bf16[272,512]{1,0:T(8,128)(2,1)S(1)}, bf16[272,512]{1,0:T(8,128)(2,1)S(1)}, u32[]{:S(2)}, u32[]{:S(2)}) %collective-permute-start.3) | collective-permute-done | bytes 278560 | tf_op jit(solution)/shard_map/ppermute | solution.py:17
  89.8 1.3 %shard_map.72 = (bf16[256,512]{1,0:T(8,128)(2,1)}, bf16[64,256]{1,0:T(8,128)(2,1)}) custom-call(s32[5]{0:T(128)S(1)} %pad_add_fusion.place_ref, f32[256,512]{1,0:T(8,128)S(1)} %get-tuple-element.23.keep_ref, bf16[272,512]{1,0:T(8,128)(2,1)S(1)} %collective-permute-done.3.recv_ref, bf16[32,256]{1,0:T(8,128)(2,1)S(1)} %get-tuple-element.25.kv_ref), custom_call_target="tpu_custom_call" | custom-call | flops 131072 | bytes 1048576 | tf_op jit(solution)/shard_map/pallas_call | solution.py:144
  91.1 1.2 %all-to-all-done.2.parts_ref = bf16[24,22,256]{2,1,0:T(8,128)(2,1)S(1)} async-done(((bf16[24,22,256]{2,1,0:T(8,128)(2,1)}), bf16[24,22,256]{2,1,0:T(8,128)(2,1)S(1)}, u32[]{:S(2)}, u32[]{:S(2)}) %all-to-all-start.2) | async-done | bytes 270368 | tf_op jit(solution)/shard_map/all_to_all | solution.py:389
  92.4 1.0 %shard_map.73 = f32[11,1024]{1,0:T(8,128)} custom-call(s32[1]{0:T(128)} %bitcast.13.turn_ref, bf16[24,22,256]{2,1,0:T(8,128)(2,1)S(1)} %all-to-all-done.2.parts_ref), custom_call_target="tpu_custom_call" | custom-call | flops 17301504 | bytes 524288 | tf_op jit(solution)/shard_map/pallas_call | solution.py:242
  (3 shorter events, 0.1 us)
Async XLA Ops:
  0.6 0.8 copy-start.2
  2.3 17.8 %copy-start = (bf16[256,512]{1,0:T(8,128)(2,1)S(1)}, bf16[256,512]{1,0:T(8,128)(2,1)}, u32[]{:S(2)}) copy-start(bf16[256,512]{1,0:T(8,128)(2,1)} %x_ref.3) | copy-start | bytes 786436
  2.3 17.8 %copy-start.1 = (bf16[256,64]{0,1:T(8,128)(2,1)S(1)}, bf16[256,64]{0,1:T(8,128)(2,1)}, u32[]{:S(2)}) copy-start(bf16[256,64]{0,1:T(8,128)(2,1)} %param.6) | copy-start | bytes 98308
  2.3 31.6 %all-to-all-start = ((bf16[24,22,256]{2,1,0:T(8,128)(2,1)}), bf16[24,22,256]{2,1,0:T(8,128)(2,1)S(1)}, u32[]{:S(2)}, u32[]{:S(2)}) async-start(bf16[24,22,256]{2,1,0:T(8,128)(2,1)} %shard_map.67), calls=%async_computation | async-start | bytes 589824 | tf_op jit(solution)/shard_map/all_to_all | solution.py:364
  19.4 0.7 copy-start.3
  20.7 18.8 %collective-permute-start.1 = (bf16[272,512]{1,0:T(8,128)(2,1)S(1)}, bf16[272,512]{1,0:T(8,128)(2,1)S(1)}, u32[]{:S(2)}, u32[]{:S(2)}) collective-permute-start(bf16[272,512]{1,0:T(8,128)(2,1)S(1)} %shard_map.68), channel_id=1, source_target_pairs={{0,384},{384,0},{1,385},{385,1},{2,386},{386,2},{3,387},{387,3},{4... | collective-permute-start | bytes 835592 | tf_op jit(solution)/shard_map/ppermute | solution.py:17
  33.9 6.8 %collective-permute-start = (bf16[24,22,256]{2,1,0:T(8,128)(2,1)S(1)}, bf16[24,22,256]{2,1,0:T(8,128)(2,1)S(1)}, u32[]{:S(2)}, u32[]{:S(2)}) collective-permute-start(bf16[24,22,256]{2,1,0:T(8,128)(2,1)S(1)} %all-to-all-done), channel_id=1, source_target_pairs={{0,16},{16,0},{1,17},{17,1},{2,18},{18,2},{3,19},{19,3},{4,20},{20... | collective-permute-start | bytes 811016 | tf_op jit(solution)/shard_map/ppermute | solution.py:21
  65.3 5.5 %collective-permute-start.2 = (bf16[24,22,256]{2,1,0:T(8,128)(2,1)S(1)}, bf16[24,22,256]{2,1,0:T(8,128)(2,1)S(1)}, u32[]{:S(2)}, u32[]{:S(2)}) collective-permute-start(bf16[24,22,256]{2,1,0:T(8,128)(2,1)S(1)} %get-tuple-element.20), channel_id=1, source_target_pairs={{0,16},{16,0},{1,17},{17,1},{2,18},{18,2},{3,19},{19,3},{4,20},{20... | collective-permute-start | bytes 811016 | tf_op jit(solution)/shard_map/ppermute | solution.py:21
  71.6 20.8 %all-to-all-start.2 = ((bf16[24,22,256]{2,1,0:T(8,128)(2,1)}), bf16[24,22,256]{2,1,0:T(8,128)(2,1)S(1)}, u32[]{:S(2)}, u32[]{:S(2)}) async-start(bf16[24,22,256]{2,1,0:T(8,128)(2,1)} %add_convert_fusion), calls=%async_computation.2 | async-start | bytes 589824 | tf_op jit(solution)/shard_map/all_to_all | solution.py:389
  78.0 11.9 %collective-permute-start.3 = (bf16[272,512]{1,0:T(8,128)(2,1)S(1)}, bf16[272,512]{1,0:T(8,128)(2,1)S(1)}, u32[]{:S(2)}, u32[]{:S(2)}) collective-permute-start(bf16[272,512]{1,0:T(8,128)(2,1)S(1)} %get-tuple-element.24), channel_id=1, source_target_pairs={{0,384},{384,0},{1,385},{385,1},{2,386},{386,2},{3,387},{387,3},{4... | collective-permute-start | bytes 835592 | tf_op jit(solution)/shard_map/ppermute | solution.py:17

commit v15 on v13

--- a/solution.py
+++ b/solution.py
@@ -339,6 +339,72 @@
     )(state, x, g, received)
 
 
+def keys_kernel(blocks, wrows, core_ref, mine_ref, theirs_ref, x_ref, g_ref, both_ref, w_ref, acc_ref, stage_ref):
+    feats, cols = w_ref.shape
+    width = cols // 2
+    n_mp, _, tokens = both_ref.shape
+    groups = n_mp // 2
+    first_core = core_ref[0] == 0
+    for block in range(blocks):
+        mine = mine_ref[block].astype(F32)
+        theirs = theirs_ref[block].astype(F32)
+        stage_ref[2 * block, : 2 * wrows] = jnp.where(first_core, mine, theirs)
+        stage_ref[2 * block + 1, : 2 * wrows] = jnp.where(first_core, theirs, mine)
+    for block in range(2 * blocks):
+        for part in range(2):
+            rows = pl.ds(block * wrows, wrows)
+            acc_ref[part, rows] = stage_ref[block, pl.ds(part * wrows, wrows)]
+    x = x_ref[...]
+    for part in range(2):
+        w = acc_ref[part, :feats].astype(BF16)
+        w_ref[:, part * width : (part + 1) * width] = w
+        kv = lax.dot_general(w.T, x, (((1,), (1,)), ((), ())), preferred_element_type=F32)
+        both_ref[part * groups : (part + 1) * groups, :HALF, :] = kv.astype(BF16).reshape(
+            groups, HALF, tokens
+        )
+    both_ref[:, HALF:, :] = jnp.broadcast_to(g_ref[...][None], (n_mp, HALF, tokens))
+
+
+def make_keys(core, w_mine, w_theirs, x_pair, g_cols, wrows, n_mp):
+    blocks, _, width = w_mine.shape
+    tokens, feats = x_pair.shape
+    vmem = pl.BlockSpec(memory_space=pltpu.VMEM)
+    padded = -(-2 * wrows // 16) * 16
+    return pl.pallas_call(
+        functools.partial(keys_kernel, blocks, wrows),
+        out_shape=(
+            jax.ShapeDtypeStruct((n_mp, 2 * HALF, tokens), BF16),
+            jax.ShapeDtypeStruct((feats, 2 * width), BF16),
+        ),
+        in_specs=[pl.BlockSpec(memory_space=pltpu.SMEM), vmem, vmem, vmem, vmem],
+        out_specs=(vmem, vmem),
+        scratch_shapes=[
+            pltpu.VMEM((2, 2 * blocks * wrows, width), F32),
+            pltpu.VMEM((2 * blocks, padded, width), F32),
+        ],
+        compiler_params=pltpu.CompilerParams(vmem_limit_bytes=32 * 2**20),
+        cost_estimate=pl.CostEstimate(
+            flops=4 * feats * tokens * width, bytes_accessed=2 * 2**20, transcendentals=0
+        ),
+    )(core.reshape(1), w_mine, w_theirs, x_pair, g_cols)
+
+
+def add_kernel(mine_ref, theirs_ref, out_ref):
+    out_ref[...] = (mine_ref[...].astype(F32) + theirs_ref[...].astype(F32)).astype(BF16)
+
+
+def add_blocks(mine, theirs):
+    vmem = pl.BlockSpec(memory_space=pltpu.VMEM)
+    return pl.pallas_call(
+        add_kernel,
+        out_shape=jax.ShapeDtypeStruct(mine.shape, BF16),
+        in_specs=[vmem, vmem],
+        out_specs=vmem,
+        compiler_params=pltpu.CompilerParams(vmem_limit_bytes=32 * 2**20),
+        cost_estimate=pl.CostEstimate(flops=2**18, bytes_accessed=2**20, transcendentals=0),
+    )(mine, theirs)
+
+
 def on_device(x, w, adjoint, mask):
     seqs = mask.shape[0]
     tokens, feats = x.shape
@@ -356,11 +422,6 @@
 
     count = jnp.sum(mask)
 
-    def unpack(value):
-        lead = value.shape[:-2]
-        value = value.reshape(*lead, 2, wrows, n_mp * half // 2)
-        return jnp.swapaxes(value, -3, -2).reshape(*lead, wrows, n_mp * half)
-
     w_mine = lax.all_to_all(spread_weight(turn, w, half, n_z), ("pair", "z"), 0, 0, tiled=True)
 
     state = jnp.concatenate([mask, jnp.stack([side, hand])])
@@ -368,22 +429,16 @@
     received = swap_pair(prepare_swap(state, x, g))
     x_pair, g_cols = compact_pair(state, x, g, received)
 
-    w_theirs = swap_core(w_mine)
-    w_cores = jnp.where(core == 0, jnp.stack([w_mine, w_theirs], 1), jnp.stack([w_theirs, w_mine], 1))
-    w_full = unpack(w_cores).reshape(4 * n_z * wrows, n_mp * half)[:feats]
-
-    kv = lax.dot_general(w_full, x_pair, (((0,), (1,)), ((), ())), preferred_element_type=F32)
-    kv = kv.astype(BF16).reshape(n_mp, half, tokens)
-    both = jnp.concatenate([kv, jnp.broadcast_to(g_cols, (n_mp, half, tokens))], axis=1)
+    both, w_full = make_keys(core, w_mine, swap_core(w_mine), x_pair, g_cols, wrows, n_mp)
     both = lax.all_to_all(both, ("pair", "mp"), 0, 0, axis_index_groups=groups, tiled=True)
 
     dw_mine, dw_theirs = weight_blocks(core, both, x_pair, 2 * n_z, wrows)
     dw_theirs, both = lax.optimization_barrier((dw_theirs, both))
-    dw_sum = dw_mine.astype(F32) + swap_core(dw_theirs).astype(F32)
+    dw_sum = add_blocks(dw_mine, swap_core(dw_theirs))
 
     send, keep, kv = return_parts(both, w_full)
     received = swap_pair(send)
-    dw_send, keep = lax.optimization_barrier((dw_sum.astype(BF16), keep))
+    dw_send, keep = lax.optimization_barrier((dw_sum, keep))
     dw_parts = lax.all_to_all(dw_send, ("pair", "z"), 0, 0, tiled=True)
     weight_grad = sum_blocks(turn, dw_parts, half, wrows)
 

time: 93.4 us -> 92.8 us (level)
  Pallas kernels: 5.3 us -> 6.6 us
    pallas_call x0 -> x2, Pallas kernels: none -> 1.31 us  [the longest x1 0.77 us: add_blocks(): pl.pallas_call(add_kernel, out_shape=jax.ShapeDtypeStruct(mine.shape, BF1...]
where the time goes in v15:
time: 92.8 us; the launch traced here: 91.1 us
  starting transfers between devices  37.5 us (40%)
  blocking collectives  23 us (25%)
  waiting for transfers between devices  20.3 us (22%)
  Pallas kernels  6.6 us (7%)
  between operations  1.47 us (2%)
  local copies, waits for them, and re-layouts  1.39 us (1%)
    all_to_all x1, blocking collectives, on_device(): lax.all_to_all(both, ('pair', 'mp'), 0, 0, axis_index_groups=groups, tile...  23 us
    all_to_all x1, starting transfers between devices, on_device(): lax.all_to_all(spread_weight(turn, w, half, n_z), ('pair', 'z'), 0, 0, ti...  17.1 us
    all_to_all x1, waiting for transfers between devices, on_device(): lax.all_to_all(spread_weight(turn, w, half, n_z), ('pair', 'z'), 0, 0, ti...  10 us
    ppermute x2, starting transfers between devices, swap_core(): return lax.ppermute(value, 'core', SWAP)  9.86 us
    ppermute x2, waiting for transfers between devices, swap_pair(): return lax.ppermute(value, 'pair', SWAP)  6.55 us
    ppermute x2, starting transfers between devices, swap_pair(): return lax.ppermute(value, 'pair', SWAP)  6.4 us
    all_to_all x1, starting transfers between devices, on_device(): dw_parts = lax.all_to_all(dw_send, ('pair', 'z'), 0, 0, tiled=True)  4.2 us
    all_to_all x1, waiting for transfers between devices, on_device(): dw_parts = lax.all_to_all(dw_send, ('pair', 'z'), 0, 0, tiled=True)  2.34 us
  transfers between devices with their start and end apart: 6, of which 5 were waited for; matrix products, arithmetic and copies ran while one was open for 1% of the time, Pallas kernels for 3%

profile of v15, /device:TPU:1, one launch (start us, length us, event | category | flops | bytes accessed | tf_op | source)
XLA Modules:
  0.0 91.1 jit_solution(15052693403025901614)
XLA Ops:
  0.6 0.0 copy-start.2
  0.7 0.7 copy-done.2
  1.4 0.9 %shard_map.67 = bf16[24,22,256]{2,1,0:T(8,128)(2,1)} custom-call(s32[1]{0:T(128)} %bitcast.5.turn_ref, bf16[11,1024]{1,0:T(8,128)(2,1)S(1)} %copy-done.2), custom_call_target="tpu_custom_call" | custom-call | flops 5767168 | bytes 524288 | tf_op jit(solution)/shard_map/pallas_call | solution.py:192
  2.3 0.0 copy-start
  2.3 0.0 copy-start.1
  2.3 17.1 %all-to-all-start = ((bf16[24,22,256]{2,1,0:T(8,128)(2,1)}), bf16[24,22,256]{2,1,0:T(8,128)(2,1)S(1)}, u32[]{:S(2)}, u32[]{:S(2)}) async-start(bf16[24,22,256]{2,1,0:T(8,128)(2,1)} %shard_map.67), calls=%async_computation | async-start | bytes 589824 | tf_op jit(solution)/shard_map/all_to_all | solution.py:425
  19.4 0.0 copy-start.3
  19.4 0.6 copy-done.3
  20.1 0.1 pad_add_fusion.1.mask_ref
  20.1 0.0 copy-done
  20.1 0.0 copy-done.1
  20.1 0.6 shard_map.68
  20.7 3.2 %collective-permute-start.1 = (bf16[272,512]{1,0:T(8,128)(2,1)S(1)}, bf16[272,512]{1,0:T(8,128)(2,1)S(1)}, u32[]{:S(2)}, u32[]{:S(2)}) collective-permute-start(bf16[272,512]{1,0:T(8,128)(2,1)S(1)} %shard_map.68), channel_id=1, source_target_pairs={{0,384},{384,0},{1,385},{385,1},{2,386},{386,2},{3,387},{387,3},{4... | collective-permute-start | bytes 835592 | tf_op jit(solution)/shard_map/ppermute | solution.py:17
  23.9 10.0 %all-to-all-done.mine_ref = bf16[24,22,256]{2,1,0:T(8,128)(2,1)S(1)} async-done(((bf16[24,22,256]{2,1,0:T(8,128)(2,1)}), bf16[24,22,256]{2,1,0:T(8,128)(2,1)S(1)}, u32[]{:S(2)}, u32[]{:S(2)}) %all-to-all-start) | async-done | bytes 270368 | tf_op jit(solution)/shard_map/all_to_all | solution.py:425
  33.9 5.6 %collective-permute-start = (bf16[24,22,256]{2,1,0:T(8,128)(2,1)S(1)}, bf16[24,22,256]{2,1,0:T(8,128)(2,1)S(1)}, u32[]{:S(2)}, u32[]{:S(2)}) collective-permute-start(bf16[24,22,256]{2,1,0:T(8,128)(2,1)S(1)} %all-to-all-done.mine_ref), channel_id=1, source_target_pairs={{0,16},{16,0},{1,17},{17,1},{2,18},{18,2},{3,19},{19,3},{4,20},{20... | collective-permute-start | bytes 811016 | tf_op jit(solution)/shard_map/ppermute | solution.py:21
  39.5 0.0 collective-permute-done.1.recv_ref
  39.5 0.6 shard_map.69
  40.1 0.6 collective-permute-done.theirs_ref
  40.7 0.5 shard_map.70
  41.3 23.0 %all_to_all.15.both_ref = bf16[16,64,256]{2,1,0:T(8,128)(2,1)S(1)} all-to-all(bf16[16,64,256]{2,1,0:T(8,128)(2,1)S(1)} %get-tuple-element.20), channel_id=1, replica_groups={{0,1,2,3,4,5,6,7,392,393,394,395,396,397,398,399},{384,385,386,387,388,..., dimensions={0} | all-to-all | bytes 1048576 | tf_op jit(solution)/shard_map/all_to_all | solution.py:433
  64.2 0.5 shard_map.71
  64.8 4.3 %collective-permute-start.2 = (bf16[24,22,256]{2,1,0:T(8,128)(2,1)S(1)}, bf16[24,22,256]{2,1,0:T(8,128)(2,1)S(1)}, u32[]{:S(2)}, u32[]{:S(2)}) collective-permute-start(bf16[24,22,256]{2,1,0:T(8,128)(2,1)S(1)} %get-tuple-element.23), channel_id=1, source_target_pairs={{0,16},{16,0},{1,17},{17,1},{2,18},{18,2},{3,19},{19,3},{4,20},{20... | collective-permute-start | bytes 811016 | tf_op jit(solution)/shard_map/ppermute | solution.py:21
  69.0 0.3 shard_map.73
  69.4 0.8 collective-permute-done.2.theirs_ref
  70.2 0.8 shard_map.72
  71.0 4.2 %all-to-all-start.2 = ((bf16[24,22,256]{2,1,0:T(8,128)(2,1)}), bf16[24,22,256]{2,1,0:T(8,128)(2,1)S(1)}, u32[]{:S(2)}, u32[]{:S(2)}) async-start(bf16[24,22,256]{2,1,0:T(8,128)(2,1)} %shard_map.72), calls=%async_computation.2 | async-start | bytes 589824 | tf_op jit(solution)/shard_map/all_to_all | solution.py:442
  75.2 3.2 %collective-permute-start.3 = (bf16[272,512]{1,0:T(8,128)(2,1)S(1)}, bf16[272,512]{1,0:T(8,128)(2,1)S(1)}, u32[]{:S(2)}, u32[]{:S(2)}) collective-permute-start(bf16[272,512]{1,0:T(8,128)(2,1)S(1)} %get-tuple-element.28), channel_id=1, source_target_pairs={{0,384},{384,0},{1,385},{385,1},{2,386},{386,2},{3,387},{387,3},{4... | collective-permute-start | bytes 835592 | tf_op jit(solution)/shard_map/ppermute | solution.py:17
  78.4 0.6 reduce_sum.9
  79.8 0.1 add_minimum_fusion
  79.8 0.1 pad_add_fusion.place_ref
  79.9 6.5 %collective-permute-done.3.recv_ref = bf16[272,512]{1,0:T(8,128)(2,1)S(1)} collective-permute-done((bf16[272,512]{1,0:T(8,128)(2,1)S(1)}, bf16[272,512]{1,0:T(8,128)(2,1)S(1)}, u32[]{:S(2)}, u32[]{:S(2)}) %collective-permute-start.3) | collective-permute-done | bytes 278560 | tf_op jit(solution)/shard_map/ppermute | solution.py:17
  86.5 1.3 %shard_map.74 = (bf16[256,512]{1,0:T(8,128)(2,1)}, bf16[64,256]{1,0:T(8,128)(2,1)}) custom-call(s32[5]{0:T(128)S(1)} %pad_add_fusion.place_ref, bf16[256,512]{1,0:T(8,128)(2,1)S(1)} %get-tuple-element.27.keep_ref, bf16[272,512]{1,0:T(8,128)(2,1)S(1)} %collective-permute-done.3.recv_ref, bf16[32,256]{1,0:T(8,128)(2,1)S(1)} %get-tuple-element.29.kv_ref), custom_call_target="tpu_custom_call" | custom-call | flops 131072 | bytes 1048576 | tf_op jit(solution)/shard_map/pallas_call | solution.py:144
  87.8 2.3 %all-to-all-done.2.parts_ref = bf16[24,22,256]{2,1,0:T(8,128)(2,1)S(1)} async-done(((bf16[24,22,256]{2,1,0:T(8,128)(2,1)}), bf16[24,22,256]{2,1,0:T(8,128)(2,1)S(1)}, u32[]{:S(2)}, u32[]{:S(2)}) %all-to-all-start.2) | async-done | bytes 270368 | tf_op jit(solution)/shard_map/all_to_all | solution.py:442
  90.1 1.0 %shard_map.75 = f32[11,1024]{1,0:T(8,128)} custom-call(s32[1]{0:T(128)} %bitcast.5.turn_ref, bf16[24,22,256]{2,1,0:T(8,128)(2,1)S(1)} %all-to-all-done.2.parts_ref), custom_call_target="tpu_custom_call" | custom-call | flops 17301504 | bytes 524288 | tf_op jit(solution)/shard_map/pallas_call | solution.py:242
Async XLA Ops:
  0.6 0.8 copy-start.2
  2.3 17.8 %copy-start = (bf16[256,512]{1,0:T(8,128)(2,1)S(1)}, bf16[256,512]{1,0:T(8,128)(2,1)}, u32[]{:S(2)}) copy-start(bf16[256,512]{1,0:T(8,128)(2,1)} %x_ref.3) | copy-start | bytes 786436
  2.3 17.8 %copy-start.1 = (bf16[256,64]{0,1:T(8,128)(2,1)S(1)}, bf16[256,64]{0,1:T(8,128)(2,1)}, u32[]{:S(2)}) copy-start(bf16[256,64]{0,1:T(8,128)(2,1)} %param.6) | copy-start | bytes 98308
  2.3 31.6 %all-to-all-start = ((bf16[24,22,256]{2,1,0:T(8,128)(2,1)}), bf16[24,22,256]{2,1,0:T(8,128)(2,1)S(1)}, u32[]{:S(2)}, u32[]{:S(2)}) async-start(bf16[24,22,256]{2,1,0:T(8,128)(2,1)} %shard_map.67), calls=%async_computation | async-start | bytes 589824 | tf_op jit(solution)/shard_map/all_to_all | solution.py:425
  19.4 0.7 copy-start.3
  20.7 18.8 %collective-permute-start.1 = (bf16[272,512]{1,0:T(8,128)(2,1)S(1)}, bf16[272,512]{1,0:T(8,128)(2,1)S(1)}, u32[]{:S(2)}, u32[]{:S(2)}) collective-permute-start(bf16[272,512]{1,0:T(8,128)(2,1)S(1)} %shard_map.68), channel_id=1, source_target_pairs={{0,384},{384,0},{1,385},{385,1},{2,386},{386,2},{3,387},{387,3},{4... | collective-permute-start | bytes 835592 | tf_op jit(solution)/shard_map/ppermute | solution.py:17
  33.9 6.8 %collective-permute-start = (bf16[24,22,256]{2,1,0:T(8,128)(2,1)S(1)}, bf16[24,22,256]{2,1,0:T(8,128)(2,1)S(1)}, u32[]{:S(2)}, u32[]{:S(2)}) collective-permute-start(bf16[24,22,256]{2,1,0:T(8,128)(2,1)S(1)} %all-to-all-done.mine_ref), channel_id=1, source_target_pairs={{0,16},{16,0},{1,17},{17,1},{2,18},{18,2},{3,19},{19,3},{4,20},{20... | collective-permute-start | bytes 811016 | tf_op jit(solution)/shard_map/ppermute | solution.py:21
  64.8 5.5 %collective-permute-start.2 = (bf16[24,22,256]{2,1,0:T(8,128)(2,1)S(1)}, bf16[24,22,256]{2,1,0:T(8,128)(2,1)S(1)}, u32[]{:S(2)}, u32[]{:S(2)}) collective-permute-start(bf16[24,22,256]{2,1,0:T(8,128)(2,1)S(1)} %get-tuple-element.23), channel_id=1, source_target_pairs={{0,16},{16,0},{1,17},{17,1},{2,18},{18,2},{3,19},{19,3},{4,20},{20... | collective-permute-start | bytes 811016 | tf_op jit(solution)/shard_map/ppermute | solution.py:21
  71.0 19.1 %all-to-all-start.2 = ((bf16[24,22,256]{2,1,0:T(8,128)(2,1)}), bf16[24,22,256]{2,1,0:T(8,128)(2,1)S(1)}, u32[]{:S(2)}, u32[]{:S(2)}) async-start(bf16[24,22,256]{2,1,0:T(8,128)(2,1)} %shard_map.72), calls=%async_computation.2 | async-start | bytes 589824 | tf_op jit(solution)/shard_map/all_to_all | solution.py:442
  75.2 11.2 %collective-permute-start.3 = (bf16[272,512]{1,0:T(8,128)(2,1)S(1)}, bf16[272,512]{1,0:T(8,128)(2,1)S(1)}, u32[]{:S(2)}, u32[]{:S(2)}) collective-permute-start(bf16[272,512]{1,0:T(8,128)(2,1)S(1)} %get-tuple-element.28), channel_id=1, source_target_pairs={{0,384},{384,0},{1,385},{385,1},{2,386},{386,2},{3,387},{387,3},{4... | collective-permute-start | bytes 835592 | tf_op jit(solution)/shard_map/ppermute | solution.py:17

commit v16 on v15

--- a/solution.py
+++ b/solution.py
@@ -108,7 +108,7 @@
     )(both, w_full)
 
 
-def home_kernel(seqs, place_ref, keep_ref, recv_ref, kv_ref, dx_ref, out_ref):
+def home_kernel(seqs, place_ref, keep_ref, recv_ref, kv_ref, dx_ref, out_ref, held_ref, sems):
     tokens, feats = keep_ref.shape
     half = kv_ref.shape[0]
     span = tokens // seqs
@@ -125,16 +125,22 @@
     )
     low = jnp.where(left, own, other)
     high = jnp.where(left, other, own)
+    copies = []
     for seq in range(seqs):
         alive = place_ref[seq] != 0
         slot = place_ref[seqs + seq]
         rows = pl.ds(pl.multiple_of(slot * span, span), span)
         total = keep_ref[rows].astype(F32) + recv_ref[rows].astype(F32)
         here = slice(seq * span, (seq + 1) * span)
-        dx_ref[here] = jnp.where(alive, total, 0.0).astype(BF16)
+        held_ref[here] = jnp.where(alive, total, 0.0).astype(BF16)
+        rows = pl.ds(seq * span, span)
+        copies.append(pltpu.make_async_copy(held_ref.at[rows], dx_ref.at[rows], sems.at[seq]))
+        copies[-1].start()
         for at, value in ((0, low), (half, high)):
             picked = jnp.where(slot == 0, value[:, :span], value[:, span : 2 * span])
             out_ref[at : at + half, here] = jnp.where(alive, picked, 0.0).astype(BF16)
+    for copy in copies:
+        copy.wait()
 
 
 def bring_home(place, keep, received, kv, seqs):
@@ -148,7 +154,8 @@
             jax.ShapeDtypeStruct((2 * half, tokens), BF16),
         ),
         in_specs=[pl.BlockSpec(memory_space=pltpu.SMEM), vmem, vmem, vmem],
-        out_specs=(vmem, vmem),
+        out_specs=(pl.BlockSpec(memory_space=pl.ANY), vmem),
+        scratch_shapes=[pltpu.VMEM((tokens, feats), BF16), pltpu.SemaphoreType.DMA((seqs,))],
         compiler_params=pltpu.CompilerParams(vmem_limit_bytes=32 * 2**20),
         cost_estimate=pl.CostEstimate(flops=tokens * feats, bytes_accessed=2**20, transcendentals=0),
     )(place, keep, received, kv)
@@ -389,17 +396,27 @@
     )(core.reshape(1), w_mine, w_theirs, x_pair, g_cols)
 
 
-def add_kernel(mine_ref, theirs_ref, out_ref):
-    out_ref[...] = (mine_ref[...].astype(F32) + theirs_ref[...].astype(F32)).astype(BF16)
+def add_kernel(steps, mine_ref, theirs_ref, out_ref, held_ref, sems):
+    size = mine_ref.shape[0] // steps
+    copies = []
+    for step in range(steps):
+        part = slice(step * size, (step + 1) * size)
+        held_ref[part] = (mine_ref[part].astype(F32) + theirs_ref[part].astype(F32)).astype(BF16)
+        rows = pl.ds(step * size, size)
+        copies.append(pltpu.make_async_copy(held_ref.at[rows], out_ref.at[rows], sems.at[step]))
+        copies[-1].start()
+    for copy in copies:
+        copy.wait()
 
 
 def add_blocks(mine, theirs):
     vmem = pl.BlockSpec(memory_space=pltpu.VMEM)
     return pl.pallas_call(
-        add_kernel,
+        functools.partial(add_kernel, 3),
         out_shape=jax.ShapeDtypeStruct(mine.shape, BF16),
         in_specs=[vmem, vmem],
-        out_specs=vmem,
+        out_specs=pl.BlockSpec(memory_space=pl.ANY),
+        scratch_shapes=[pltpu.VMEM(mine.shape, BF16), pltpu.SemaphoreType.DMA((3,))],
         compiler_params=pltpu.CompilerParams(vmem_limit_bytes=32 * 2**20),
         cost_estimate=pl.CostEstimate(flops=2**18, bytes_accessed=2**20, transcendentals=0),
     )(mine, theirs)

time: 92.8 us -> 92.8 us (level)
  transfers between devices with their start and end apart: 6 -> 6, of which waited for: 5 -> 5; matrix products, arithmetic and copies ran while one was open for 1% -> 1% of each run, Pallas kernels for 3% -> 4%
where the time goes in v16:
time: 92.8 us; the launch traced here: 91.1 us
  starting transfers between devices  37.5 us (40%)
  blocking collectives  23 us (25%)
  waiting for transfers between devices  19.7 us (21%)
  Pallas kernels  7.16 us (8%)
  between operations  1.49 us (2%)
  local copies, waits for them, and re-layouts  1.39 us (1%)
    all_to_all x1, blocking collectives, on_device(): lax.all_to_all(both, ('pair', 'mp'), 0, 0, axis_index_groups=groups, tile...  23 us
    all_to_all x1, starting transfers between devices, on_device(): lax.all_to_all(spread_weight(turn, w, half, n_z), ('pair', 'z'), 0, 0, ti...  17.1 us
    all_to_all x1, waiting for transfers between devices, on_device(): lax.all_to_all(spread_weight(turn, w, half, n_z), ('pair', 'z'), 0, 0, ti...  10 us
    ppermute x2, starting transfers between devices, swap_core(): return lax.ppermute(value, 'core', SWAP)  9.86 us
    ppermute x2, waiting for transfers between devices, swap_pair(): return lax.ppermute(value, 'pair', SWAP)  6.55 us
    ppermute x2, starting transfers between devices, swap_pair(): return lax.ppermute(value, 'pair', SWAP)  6.4 us
    all_to_all x1, starting transfers between devices, on_device(): dw_parts = lax.all_to_all(dw_send, ('pair', 'z'), 0, 0, tiled=True)  4.21 us
    pallas_call x1, Pallas kernels, bring_home(): pl.pallas_call(functools.partial(home_kernel, seqs), out_shape=(jax.Shape...  1.91 us
  transfers between devices with their start and end apart: 6, of which 5 were waited for; matrix products, arithmetic and copies ran while one was open for 1% of the time, Pallas kernels for 4%

profile of v16, /device:TPU:1, one launch (start us, length us, event | category | flops | bytes accessed | tf_op | source)
XLA Modules:
  0.0 91.1 jit_solution(5336311962437547326)
XLA Ops:
  0.6 0.0 copy-start.2
  0.7 0.7 copy-done.2
  1.4 0.9 %shard_map.67 = bf16[24,22,256]{2,1,0:T(8,128)(2,1)} custom-call(s32[1]{0:T(128)} %bitcast.5.turn_ref, bf16[11,1024]{1,0:T(8,128)(2,1)S(1)} %copy-done.2), custom_call_target="tpu_custom_call" | custom-call | flops 5767168 | bytes 524288 | tf_op jit(solution)/shard_map/pallas_call | solution.py:199
  2.3 0.0 copy-start
  2.3 0.0 copy-start.1
  2.3 17.1 %all-to-all-start = ((bf16[24,22,256]{2,1,0:T(8,128)(2,1)}), bf16[24,22,256]{2,1,0:T(8,128)(2,1)S(1)}, u32[]{:S(2)}, u32[]{:S(2)}) async-start(bf16[24,22,256]{2,1,0:T(8,128)(2,1)} %shard_map.67), calls=%async_computation | async-start | bytes 589824 | tf_op jit(solution)/shard_map/all_to_all | solution.py:442
  19.4 0.0 copy-start.3
  19.4 0.6 copy-done.3
  20.1 0.1 pad_add_fusion.1.mask_ref
  20.1 0.0 copy-done
  20.1 0.0 copy-done.1
  20.1 0.6 shard_map.68
  20.7 3.2 %collective-permute-start.1 = (bf16[272,512]{1,0:T(8,128)(2,1)S(1)}, bf16[272,512]{1,0:T(8,128)(2,1)S(1)}, u32[]{:S(2)}, u32[]{:S(2)}) collective-permute-start(bf16[272,512]{1,0:T(8,128)(2,1)S(1)} %shard_map.68), channel_id=1, source_target_pairs={{0,384},{384,0},{1,385},{385,1},{2,386},{386,2},{3,387},{387,3},{4... | collective-permute-start | bytes 835592 | tf_op jit(solution)/shard_map/ppermute | solution.py:17
  23.9 10.0 %all-to-all-done.mine_ref = bf16[24,22,256]{2,1,0:T(8,128)(2,1)S(1)} async-done(((bf16[24,22,256]{2,1,0:T(8,128)(2,1)}), bf16[24,22,256]{2,1,0:T(8,128)(2,1)S(1)}, u32[]{:S(2)}, u32[]{:S(2)}) %all-to-all-start) | async-done | bytes 270368 | tf_op jit(solution)/shard_map/all_to_all | solution.py:442
  33.9 5.6 %collective-permute-start = (bf16[24,22,256]{2,1,0:T(8,128)(2,1)S(1)}, bf16[24,22,256]{2,1,0:T(8,128)(2,1)S(1)}, u32[]{:S(2)}, u32[]{:S(2)}) collective-permute-start(bf16[24,22,256]{2,1,0:T(8,128)(2,1)S(1)} %all-to-all-done.mine_ref), channel_id=1, source_target_pairs={{0,16},{16,0},{1,17},{17,1},{2,18},{18,2},{3,19},{19,3},{4,20},{20... | collective-permute-start | bytes 811016 | tf_op jit(solution)/shard_map/ppermute | solution.py:21
  39.5 0.0 collective-permute-done.1.recv_ref
  39.5 0.6 shard_map.69
  40.1 0.6 collective-permute-done.theirs_ref
  40.7 0.5 shard_map.70
  41.3 23.0 %all_to_all.15.both_ref = bf16[16,64,256]{2,1,0:T(8,128)(2,1)S(1)} all-to-all(bf16[16,64,256]{2,1,0:T(8,128)(2,1)S(1)} %get-tuple-element.20), channel_id=1, replica_groups={{0,1,2,3,4,5,6,7,392,393,394,395,396,397,398,399},{384,385,386,387,388,..., dimensions={0} | all-to-all | bytes 1048576 | tf_op jit(solution)/shard_map/all_to_all | solution.py:450
  64.2 0.5 shard_map.71
  64.8 4.3 %collective-permute-start.2 = (bf16[24,22,256]{2,1,0:T(8,128)(2,1)S(1)}, bf16[24,22,256]{2,1,0:T(8,128)(2,1)S(1)}, u32[]{:S(2)}, u32[]{:S(2)}) collective-permute-start(bf16[24,22,256]{2,1,0:T(8,128)(2,1)S(1)} %get-tuple-element.23), channel_id=1, source_target_pairs={{0,16},{16,0},{1,17},{17,1},{2,18},{18,2},{3,19},{19,3},{4,20},{20... | collective-permute-start | bytes 811016 | tf_op jit(solution)/shard_map/ppermute | solution.py:21
  69.0 0.3 shard_map.73
  69.4 0.8 collective-permute-done.2.theirs_ref
  70.2 0.8 shard_map.72
  71.0 4.2 %all-to-all-start.2 = ((bf16[24,22,256]{2,1,0:T(8,128)(2,1)}), bf16[24,22,256]{2,1,0:T(8,128)(2,1)S(1)}, u32[]{:S(2)}, u32[]{:S(2)}) async-start(bf16[24,22,256]{2,1,0:T(8,128)(2,1)} %shard_map.72), calls=%async_computation.2 | async-start | bytes 589824 | tf_op jit(solution)/shard_map/all_to_all | solution.py:459
  75.2 3.2 %collective-permute-start.3 = (bf16[272,512]{1,0:T(8,128)(2,1)S(1)}, bf16[272,512]{1,0:T(8,128)(2,1)S(1)}, u32[]{:S(2)}, u32[]{:S(2)}) collective-permute-start(bf16[272,512]{1,0:T(8,128)(2,1)S(1)} %get-tuple-element.28), channel_id=1, source_target_pairs={{0,384},{384,0},{1,385},{385,1},{2,386},{386,2},{3,387},{387,3},{4... | collective-permute-start | bytes 835592 | tf_op jit(solution)/shard_map/ppermute | solution.py:17
  78.4 0.6 reduce_sum.9
  79.8 0.1 add_minimum_fusion
  79.8 0.1 pad_add_fusion.place_ref
  79.9 6.5 %collective-permute-done.3.recv_ref = bf16[272,512]{1,0:T(8,128)(2,1)S(1)} collective-permute-done((bf16[272,512]{1,0:T(8,128)(2,1)S(1)}, bf16[272,512]{1,0:T(8,128)(2,1)S(1)}, u32[]{:S(2)}, u32[]{:S(2)}) %collective-permute-start.3) | collective-permute-done | bytes 278560 | tf_op jit(solution)/shard_map/ppermute | solution.py:17
  86.5 1.9 %shard_map.74 = (bf16[256,512]{1,0:T(8,128)(2,1)}, bf16[64,256]{1,0:T(8,128)(2,1)}) custom-call(s32[5]{0:T(128)S(1)} %pad_add_fusion.place_ref, bf16[256,512]{1,0:T(8,128)(2,1)S(1)} %get-tuple-element.27.keep_ref, bf16[272,512]{1,0:T(8,128)(2,1)S(1)} %collective-permute-done.3.recv_ref, bf16[32,256]{1,0:T(8,128)(2,1)S(1)} %get-tuple-element.29.kv_ref), custom_call_target="tpu_custom_call" | custom-call | flops 131072 | bytes 1048576 | tf_op jit(solution)/shard_map/pallas_call | solution.py:150
  88.4 1.8 %all-to-all-done.2.parts_ref = bf16[24,22,256]{2,1,0:T(8,128)(2,1)S(1)} async-done(((bf16[24,22,256]{2,1,0:T(8,128)(2,1)}), bf16[24,22,256]{2,1,0:T(8,128)(2,1)S(1)}, u32[]{:S(2)}, u32[]{:S(2)}) %all-to-all-start.2) | async-done | bytes 270368 | tf_op jit(solution)/shard_map/all_to_all | solution.py:459
  90.1 1.0 %shard_map.75 = f32[11,1024]{1,0:T(8,128)} custom-call(s32[1]{0:T(128)} %bitcast.5.turn_ref, bf16[24,22,256]{2,1,0:T(8,128)(2,1)S(1)} %all-to-all-done.2.parts_ref), custom_call_target="tpu_custom_call" | custom-call | flops 17301504 | bytes 524288 | tf_op jit(solution)/shard_map/pallas_call | solution.py:249
Async XLA Ops:
  0.6 0.8 copy-start.2
  2.3 17.8 %copy-start = (bf16[256,512]{1,0:T(8,128)(2,1)S(1)}, bf16[256,512]{1,0:T(8,128)(2,1)}, u32[]{:S(2)}) copy-start(bf16[256,512]{1,0:T(8,128)(2,1)} %x_ref.3) | copy-start | bytes 786436
  2.3 17.8 %copy-start.1 = (bf16[256,64]{0,1:T(8,128)(2,1)S(1)}, bf16[256,64]{0,1:T(8,128)(2,1)}, u32[]{:S(2)}) copy-start(bf16[256,64]{0,1:T(8,128)(2,1)} %param.6) | copy-start | bytes 98308
  2.3 31.6 %all-to-all-start = ((bf16[24,22,256]{2,1,0:T(8,128)(2,1)}), bf16[24,22,256]{2,1,0:T(8,128)(2,1)S(1)}, u32[]{:S(2)}, u32[]{:S(2)}) async-start(bf16[24,22,256]{2,1,0:T(8,128)(2,1)} %shard_map.67), calls=%async_computation | async-start | bytes 589824 | tf_op jit(solution)/shard_map/all_to_all | solution.py:442
  19.4 0.7 copy-start.3
  20.7 18.8 %collective-permute-start.1 = (bf16[272,512]{1,0:T(8,128)(2,1)S(1)}, bf16[272,512]{1,0:T(8,128)(2,1)S(1)}, u32[]{:S(2)}, u32[]{:S(2)}) collective-permute-start(bf16[272,512]{1,0:T(8,128)(2,1)S(1)} %shard_map.68), channel_id=1, source_target_pairs={{0,384},{384,0},{1,385},{385,1},{2,386},{386,2},{3,387},{387,3},{4... | collective-permute-start | bytes 835592 | tf_op jit(solution)/shard_map/ppermute | solution.py:17
  33.9 6.8 %collective-permute-start = (bf16[24,22,256]{2,1,0:T(8,128)(2,1)S(1)}, bf16[24,22,256]{2,1,0:T(8,128)(2,1)S(1)}, u32[]{:S(2)}, u32[]{:S(2)}) collective-permute-start(bf16[24,22,256]{2,1,0:T(8,128)(2,1)S(1)} %all-to-all-done.mine_ref), channel_id=1, source_target_pairs={{0,16},{16,0},{1,17},{17,1},{2,18},{18,2},{3,19},{19,3},{4,20},{20... | collective-permute-start | bytes 811016 | tf_op jit(solution)/shard_map/ppermute | solution.py:21
  64.8 5.5 %collective-permute-start.2 = (bf16[24,22,256]{2,1,0:T(8,128)(2,1)S(1)}, bf16[24,22,256]{2,1,0:T(8,128)(2,1)S(1)}, u32[]{:S(2)}, u32[]{:S(2)}) collective-permute-start(bf16[24,22,256]{2,1,0:T(8,128)(2,1)S(1)} %get-tuple-element.23), channel_id=1, source_target_pairs={{0,16},{16,0},{1,17},{17,1},{2,18},{18,2},{3,19},{19,3},{4,20},{20... | collective-permute-start | bytes 811016 | tf_op jit(solution)/shard_map/ppermute | solution.py:21
  71.0 19.1 %all-to-all-start.2 = ((bf16[24,22,256]{2,1,0:T(8,128)(2,1)}), bf16[24,22,256]{2,1,0:T(8,128)(2,1)S(1)}, u32[]{:S(2)}, u32[]{:S(2)}) async-start(bf16[24,22,256]{2,1,0:T(8,128)(2,1)} %shard_map.72), calls=%async_computation.2 | async-start | bytes 589824 | tf_op jit(solution)/shard_map/all_to_all | solution.py:459
  75.2 11.2 %collective-permute-start.3 = (bf16[272,512]{1,0:T(8,128)(2,1)S(1)}, bf16[272,512]{1,0:T(8,128)(2,1)S(1)}, u32[]{:S(2)}, u32[]{:S(2)}) collective-permute-start(bf16[272,512]{1,0:T(8,128)(2,1)S(1)} %get-tuple-element.28), channel_id=1, source_target_pairs={{0,384},{384,0},{1,385},{385,1},{2,386},{386,2},{3,387},{387,3},{4... | collective-permute-start | bytes 835592 | tf_op jit(solution)/shard_map/ppermute | solution.py:17

commit v17 on v15

--- a/solution.py
+++ b/solution.py
@@ -125,11 +125,14 @@
     )
     low = jnp.where(left, own, other)
     high = jnp.where(left, other, own)
+    totals = [
+        keep_ref[at : at + span].astype(F32) + recv_ref[at : at + span].astype(F32)
+        for at in (0, span)
+    ]
     for seq in range(seqs):
         alive = place_ref[seq] != 0
         slot = place_ref[seqs + seq]
-        rows = pl.ds(pl.multiple_of(slot * span, span), span)
-        total = keep_ref[rows].astype(F32) + recv_ref[rows].astype(F32)
+        total = jnp.where(slot == 0, totals[0], totals[1])
         here = slice(seq * span, (seq + 1) * span)
         dx_ref[here] = jnp.where(alive, total, 0.0).astype(BF16)
         for at, value in ((0, low), (half, high)):

time: 92.8 us -> 92.8 us (level)
  no operation moved by 1% of the time
where the time goes in v17:
time: 92.8 us; the launch traced here: 91.1 us
  starting transfers between devices  37.5 us (40%)
  blocking collectives  23 us (25%)
  waiting for transfers between devices  20.3 us (22%)
  Pallas kernels  6.61 us (7%)
  between operations  1.47 us (2%)
  local copies, waits for them, and re-layouts  1.39 us (1%)
    all_to_all x1, blocking collectives, on_device(): lax.all_to_all(both, ('pair', 'mp'), 0, 0, axis_index_groups=groups, tile...  23 us
    all_to_all x1, starting transfers between devices, on_device(): lax.all_to_all(spread_weight(turn, w, half, n_z), ('pair', 'z'), 0, 0, ti...  17.1 us
    all_to_all x1, waiting for transfers between devices, on_device(): lax.all_to_all(spread_weight(turn, w, half, n_z), ('pair', 'z'), 0, 0, ti...  10 us
    ppermute x2, starting transfers between devices, swap_core(): return lax.ppermute(value, 'core', SWAP)  9.86 us
    ppermute x2, waiting for transfers between devices, swap_pair(): return lax.ppermute(value, 'pair', SWAP)  6.55 us
    ppermute x2, starting transfers between devices, swap_pair(): return lax.ppermute(value, 'pair', SWAP)  6.4 us
    all_to_all x1, starting transfers between devices, on_device(): dw_parts = lax.all_to_all(dw_send, ('pair', 'z'), 0, 0, tiled=True)  4.2 us
    all_to_all x1, waiting for transfers between devices, on_device(): dw_parts = lax.all_to_all(dw_send, ('pair', 'z'), 0, 0, tiled=True)  2.33 us
  transfers between devices with their start and end apart: 6, of which 5 were waited for; matrix products, arithmetic and copies ran while one was open for 1% of the time, Pallas kernels for 3%

profile of v17, /device:TPU:1, one launch (start us, length us, event | category | flops | bytes accessed | tf_op | source)
XLA Modules:
  0.0 91.1 jit_solution(3359830876987422330)
XLA Ops:
  0.6 0.0 copy-start.2
  0.7 0.7 copy-done.2
  1.4 0.9 %shard_map.67 = bf16[24,22,256]{2,1,0:T(8,128)(2,1)} custom-call(s32[1]{0:T(128)} %bitcast.5.turn_ref, bf16[11,1024]{1,0:T(8,128)(2,1)S(1)} %copy-done.2), custom_call_target="tpu_custom_call" | custom-call | flops 5767168 | bytes 524288 | tf_op jit(solution)/shard_map/pallas_call | solution.py:195
  2.3 0.0 copy-start
  2.3 0.0 copy-start.1
  2.3 17.1 %all-to-all-start = ((bf16[24,22,256]{2,1,0:T(8,128)(2,1)}), bf16[24,22,256]{2,1,0:T(8,128)(2,1)S(1)}, u32[]{:S(2)}, u32[]{:S(2)}) async-start(bf16[24,22,256]{2,1,0:T(8,128)(2,1)} %shard_map.67), calls=%async_computation | async-start | bytes 589824 | tf_op jit(solution)/shard_map/all_to_all | solution.py:428
  19.4 0.0 copy-start.3
  19.4 0.6 copy-done.3
  20.1 0.1 pad_add_fusion.1.mask_ref
  20.1 0.0 copy-done
  20.1 0.0 copy-done.1
  20.1 0.6 shard_map.68
  20.7 3.2 %collective-permute-start.1 = (bf16[272,512]{1,0:T(8,128)(2,1)S(1)}, bf16[272,512]{1,0:T(8,128)(2,1)S(1)}, u32[]{:S(2)}, u32[]{:S(2)}) collective-permute-start(bf16[272,512]{1,0:T(8,128)(2,1)S(1)} %shard_map.68), channel_id=1, source_target_pairs={{0,384},{384,0},{1,385},{385,1},{2,386},{386,2},{3,387},{387,3},{4... | collective-permute-start | bytes 835592 | tf_op jit(solution)/shard_map/ppermute | solution.py:17
  23.9 10.0 %all-to-all-done.mine_ref = bf16[24,22,256]{2,1,0:T(8,128)(2,1)S(1)} async-done(((bf16[24,22,256]{2,1,0:T(8,128)(2,1)}), bf16[24,22,256]{2,1,0:T(8,128)(2,1)S(1)}, u32[]{:S(2)}, u32[]{:S(2)}) %all-to-all-start) | async-done | bytes 270368 | tf_op jit(solution)/shard_map/all_to_all | solution.py:428
  33.9 5.6 %collective-permute-start = (bf16[24,22,256]{2,1,0:T(8,128)(2,1)S(1)}, bf16[24,22,256]{2,1,0:T(8,128)(2,1)S(1)}, u32[]{:S(2)}, u32[]{:S(2)}) collective-permute-start(bf16[24,22,256]{2,1,0:T(8,128)(2,1)S(1)} %all-to-all-done.mine_ref), channel_id=1, source_target_pairs={{0,16},{16,0},{1,17},{17,1},{2,18},{18,2},{3,19},{19,3},{4,20},{20... | collective-permute-start | bytes 811016 | tf_op jit(solution)/shard_map/ppermute | solution.py:21
  39.5 0.0 collective-permute-done.1.recv_ref
  39.5 0.6 shard_map.69
  40.1 0.6 collective-permute-done.theirs_ref
  40.7 0.5 shard_map.70
  41.3 23.0 %all_to_all.15.both_ref = bf16[16,64,256]{2,1,0:T(8,128)(2,1)S(1)} all-to-all(bf16[16,64,256]{2,1,0:T(8,128)(2,1)S(1)} %get-tuple-element.20), channel_id=1, replica_groups={{0,1,2,3,4,5,6,7,392,393,394,395,396,397,398,399},{384,385,386,387,388,..., dimensions={0} | all-to-all | bytes 1048576 | tf_op jit(solution)/shard_map/all_to_all | solution.py:436
  64.2 0.5 shard_map.71
  64.8 4.3 %collective-permute-start.2 = (bf16[24,22,256]{2,1,0:T(8,128)(2,1)S(1)}, bf16[24,22,256]{2,1,0:T(8,128)(2,1)S(1)}, u32[]{:S(2)}, u32[]{:S(2)}) collective-permute-start(bf16[24,22,256]{2,1,0:T(8,128)(2,1)S(1)} %get-tuple-element.23), channel_id=1, source_target_pairs={{0,16},{16,0},{1,17},{17,1},{2,18},{18,2},{3,19},{19,3},{4,20},{20... | collective-permute-start | bytes 811016 | tf_op jit(solution)/shard_map/ppermute | solution.py:21
  69.0 0.3 shard_map.73
  69.4 0.8 collective-permute-done.2.theirs_ref
  70.2 0.8 shard_map.72
  71.0 4.2 %all-to-all-start.2 = ((bf16[24,22,256]{2,1,0:T(8,128)(2,1)}), bf16[24,22,256]{2,1,0:T(8,128)(2,1)S(1)}, u32[]{:S(2)}, u32[]{:S(2)}) async-start(bf16[24,22,256]{2,1,0:T(8,128)(2,1)} %shard_map.72), calls=%async_computation.2 | async-start | bytes 589824 | tf_op jit(solution)/shard_map/all_to_all | solution.py:445
  75.2 3.2 %collective-permute-start.3 = (bf16[272,512]{1,0:T(8,128)(2,1)S(1)}, bf16[272,512]{1,0:T(8,128)(2,1)S(1)}, u32[]{:S(2)}, u32[]{:S(2)}) collective-permute-start(bf16[272,512]{1,0:T(8,128)(2,1)S(1)} %get-tuple-element.28), channel_id=1, source_target_pairs={{0,384},{384,0},{1,385},{385,1},{2,386},{386,2},{3,387},{387,3},{4... | collective-permute-start | bytes 835592 | tf_op jit(solution)/shard_map/ppermute | solution.py:17
  78.4 0.6 reduce_sum.9
  79.8 0.1 add_minimum_fusion
  79.8 0.1 pad_add_fusion.place_ref
  79.9 6.5 %collective-permute-done.3.recv_ref = bf16[272,512]{1,0:T(8,128)(2,1)S(1)} collective-permute-done((bf16[272,512]{1,0:T(8,128)(2,1)S(1)}, bf16[272,512]{1,0:T(8,128)(2,1)S(1)}, u32[]{:S(2)}, u32[]{:S(2)}) %collective-permute-start.3) | collective-permute-done | bytes 278560 | tf_op jit(solution)/shard_map/ppermute | solution.py:17
  86.5 1.3 %shard_map.74 = (bf16[256,512]{1,0:T(8,128)(2,1)}, bf16[64,256]{1,0:T(8,128)(2,1)}) custom-call(s32[5]{0:T(128)S(1)} %pad_add_fusion.place_ref, bf16[256,512]{1,0:T(8,128)(2,1)S(1)} %get-tuple-element.27.keep_ref, bf16[272,512]{1,0:T(8,128)(2,1)S(1)} %collective-permute-done.3.recv_ref, bf16[32,256]{1,0:T(8,128)(2,1)S(1)} %get-tuple-element.29.kv_ref), custom_call_target="tpu_custom_call" | custom-call | flops 131072 | bytes 1048576 | tf_op jit(solution)/shard_map/pallas_call | solution.py:147
  87.8 2.3 %all-to-all-done.2.parts_ref = bf16[24,22,256]{2,1,0:T(8,128)(2,1)S(1)} async-done(((bf16[24,22,256]{2,1,0:T(8,128)(2,1)}), bf16[24,22,256]{2,1,0:T(8,128)(2,1)S(1)}, u32[]{:S(2)}, u32[]{:S(2)}) %all-to-all-start.2) | async-done | bytes 270368 | tf_op jit(solution)/shard_map/all_to_all | solution.py:445
  90.1 1.0 %shard_map.75 = f32[11,1024]{1,0:T(8,128)} custom-call(s32[1]{0:T(128)} %bitcast.5.turn_ref, bf16[24,22,256]{2,1,0:T(8,128)(2,1)S(1)} %all-to-all-done.2.parts_ref), custom_call_target="tpu_custom_call" | custom-call | flops 17301504 | bytes 524288 | tf_op jit(solution)/shard_map/pallas_call | solution.py:245
Async XLA Ops:
  0.6 0.8 copy-start.2
  2.3 17.8 %copy-start = (bf16[256,512]{1,0:T(8,128)(2,1)S(1)}, bf16[256,512]{1,0:T(8,128)(2,1)}, u32[]{:S(2)}) copy-start(bf16[256,512]{1,0:T(8,128)(2,1)} %x_ref.3) | copy-start | bytes 786436
  2.3 17.8 %copy-start.1 = (bf16[256,64]{0,1:T(8,128)(2,1)S(1)}, bf16[256,64]{0,1:T(8,128)(2,1)}, u32[]{:S(2)}) copy-start(bf16[256,64]{0,1:T(8,128)(2,1)} %param.6) | copy-start | bytes 98308
  2.3 31.6 %all-to-all-start = ((bf16[24,22,256]{2,1,0:T(8,128)(2,1)}), bf16[24,22,256]{2,1,0:T(8,128)(2,1)S(1)}, u32[]{:S(2)}, u32[]{:S(2)}) async-start(bf16[24,22,256]{2,1,0:T(8,128)(2,1)} %shard_map.67), calls=%async_computation | async-start | bytes 589824 | tf_op jit(solution)/shard_map/all_to_all | solution.py:428
  19.4 0.7 copy-start.3
  20.7 18.8 %collective-permute-start.1 = (bf16[272,512]{1,0:T(8,128)(2,1)S(1)}, bf16[272,512]{1,0:T(8,128)(2,1)S(1)}, u32[]{:S(2)}, u32[]{:S(2)}) collective-permute-start(bf16[272,512]{1,0:T(8,128)(2,1)S(1)} %shard_map.68), channel_id=1, source_target_pairs={{0,384},{384,0},{1,385},{385,1},{2,386},{386,2},{3,387},{387,3},{4... | collective-permute-start | bytes 835592 | tf_op jit(solution)/shard_map/ppermute | solution.py:17
  33.9 6.8 %collective-permute-start = (bf16[24,22,256]{2,1,0:T(8,128)(2,1)S(1)}, bf16[24,22,256]{2,1,0:T(8,128)(2,1)S(1)}, u32[]{:S(2)}, u32[]{:S(2)}) collective-permute-start(bf16[24,22,256]{2,1,0:T(8,128)(2,1)S(1)} %all-to-all-done.mine_ref), channel_id=1, source_target_pairs={{0,16},{16,0},{1,17},{17,1},{2,18},{18,2},{3,19},{19,3},{4,20},{20... | collective-permute-start | bytes 811016 | tf_op jit(solution)/shard_map/ppermute | solution.py:21
  64.8 5.5 %collective-permute-start.2 = (bf16[24,22,256]{2,1,0:T(8,128)(2,1)S(1)}, bf16[24,22,256]{2,1,0:T(8,128)(2,1)S(1)}, u32[]{:S(2)}, u32[]{:S(2)}) collective-permute-start(bf16[24,22,256]{2,1,0:T(8,128)(2,1)S(1)} %get-tuple-element.23), channel_id=1, source_target_pairs={{0,16},{16,0},{1,17},{17,1},{2,18},{18,2},{3,19},{19,3},{4,20},{20... | collective-permute-start | bytes 811016 | tf_op jit(solution)/shard_map/ppermute | solution.py:21
  71.0 19.1 %all-to-all-start.2 = ((bf16[24,22,256]{2,1,0:T(8,128)(2,1)}), bf16[24,22,256]{2,1,0:T(8,128)(2,1)S(1)}, u32[]{:S(2)}, u32[]{:S(2)}) async-start(bf16[24,22,256]{2,1,0:T(8,128)(2,1)} %shard_map.72), calls=%async_computation.2 | async-start | bytes 589824 | tf_op jit(solution)/shard_map/all_to_all | solution.py:445
  75.2 11.2 %collective-permute-start.3 = (bf16[272,512]{1,0:T(8,128)(2,1)S(1)}, bf16[272,512]{1,0:T(8,128)(2,1)S(1)}, u32[]{:S(2)}, u32[]{:S(2)}) collective-permute-start(bf16[272,512]{1,0:T(8,128)(2,1)S(1)} %get-tuple-element.28), channel_id=1, source_target_pairs={{0,384},{384,0},{1,385},{385,1},{2,386},{386,2},{3,387},{387,3},{4... | collective-permute-start | bytes 835592 | tf_op jit(solution)/shard_map/ppermute | solution.py:17
